TPU v7x, 32 devices: a whole 2x2x4 slice. The times are simulated.
32 devices in a mesh: mesh: 16 (over z, x, core), state: 2 (over y).
Axes of the slice: x: 2, y: 2, z: 4, core: 2. Of those that a mesh axis runs over, the one named last changes fastest.
Arguments:
- subspace: float32 [2048, 4096], P('state', 'mesh'), may hold values from -6 to 6
- ritz: float32 [1024, 2048], P('state'), may hold values from -0.125 to 0.125
- element_ham: float32 [256, 125, 125], P('mesh'), may hold values from -0.6 to 0.6
- connect: int32 [256, 125], P('mesh'), may hold values from 0 to 383, as said below
- send_rows: int32 [16, 4, 32], P('mesh'), may hold values from 0 to 255, as said below
Outputs:
- filtered: float32 [1024, 4096], P('state', 'mesh')
Inputs may be any that keep to these rules, and one draw needn't show every extreme that they name: send_rows[p][k] lists nodes of partition p, local numbering, that neighbour k of p uses; only a leading part of each list, of 32 entries or fewer, is used, and some partition uses a whole list. `connect`: entries below 256 are the partition's own nodes; an entry 256 + k * 32 + j is entry j of the list that neighbour k keeps for this partition.
All inputs are finite; a program needn't handle non-finite values.
Results may differ from a plain program's by a relative error of at most 0.0001.
Values sent between devices are 32-bit elements; how exact they have to be, the bound alone decides.
No kernel may reach another device: no remote copies, remote signals or barrier semaphores. Data moves between devices by JAX's collectives and lax.ppermute only.
A program may use at most 64 MiB of HBM per device.

v0:
```python
import jax
import jax.numpy as jnp
from jax import lax
from jax.sharding import PartitionSpec as P


def per_device(subspace, ritz, element_ham, connect, send_rows):
    block_rows = ritz.shape[0]
    node_count = subspace.shape[1]
    partitions = lax.axis_size("mesh")
    slot_count = send_rows.shape[1]
    halo_width = send_rows.shape[2]
    across = partitions // 2
    offsets = (1, -1, across, -across)
    start_block = jnp.dot(
        ritz,
        lax.all_gather(subspace, "state", axis=0, tiled=True),
        precision=lax.Precision.HIGHEST,
        preferred_element_type=jnp.float32,
    )
    own_index = lax.axis_index("mesh")
    neighbour_ids = (own_index + jnp.array(offsets, jnp.int32) + partitions) % partitions
    selector = (neighbour_ids[:, None] == jnp.arange(partitions, dtype=jnp.int32)[None, :]).astype(
        jnp.float32
    )
    slot_ids = jnp.arange(4, dtype=jnp.int32)
    parity_ids = jnp.arange(2, dtype=jnp.int32)
    send_parity = ((slot_ids % 2)[:, None] == parity_ids[None, :]).astype(jnp.float32)
    take_parity = (((slot_ids ^ 1) % 2)[:, None] == parity_ids[None, :]).astype(jnp.float32)
    send_route = selector[:, :, None] * send_parity[:, None, :]
    take_route = selector[:, :, None] * take_parity[:, None, :]
    list_rows = send_rows[0].reshape(-1)

    def fetch_ghosts(packed):
        outgoing = jnp.einsum("kpr,ckj->pcrj", send_route, packed, precision=lax.Precision.HIGHEST)
        incoming = lax.all_to_all(
            outgoing.reshape(partitions, block_rows * 2 * halo_width),
            "mesh",
            split_axis=0,
            concat_axis=0,
            tiled=True,
        )
        return jnp.einsum(
            "kpr,pcrj->ckj",
            take_route,
            incoming.reshape(partitions, block_rows, 2, halo_width),
            precision=lax.Precision.HIGHEST,
        )

    def return_sums(returned_part):
        going_back = jnp.einsum(
            "kpr,ckj->pcrj", send_route, returned_part, precision=lax.Precision.HIGHEST
        )
        arrived = lax.all_to_all(
            going_back.reshape(partitions, block_rows * 2 * halo_width),
            "mesh",
            split_axis=0,
            concat_axis=0,
            tiled=True,
        )
        return jnp.einsum(
            "kpr,pcrj->ckj",
            take_route,
            arrived.reshape(partitions, block_rows, 2, halo_width),
            precision=lax.Precision.HIGHEST,
        )

    def apply_ham(values_in):
        packed = values_in[:, list_rows].reshape(block_rows, slot_count, halo_width)
        ghosts = fetch_ghosts(packed)
        extended = jnp.concatenate(
            [values_in, ghosts.reshape(block_rows, slot_count * halo_width)], 1
        )
        element_values = extended[:, connect]
        products = jnp.einsum(
            "eab,ceb->cea", element_ham, element_values, precision=lax.Precision.HIGHEST
        )
        summed = jnp.zeros(extended.shape, jnp.float32).at[:, connect].add(products)
        returned_part = summed[:, node_count:].reshape(block_rows, slot_count, halo_width)
        owner_terms = return_sums(returned_part)
        return (
            summed[:, :node_count]
            .at[:, list_rows]
            .add(owner_terms.reshape(block_rows, slot_count * halo_width))
        )

    half = 1.5
    centre = 2.5
    sigma_one = half / (-1.0 - centre)
    sigma_two = 1.0 / (2.0 / sigma_one - sigma_one)
    first = sigma_one / half * (apply_ham(start_block) - centre * start_block)
    second = 2.0 * sigma_two / half * (apply_ham(first) - centre * first)
    return second - sigma_one * sigma_two * start_block


def solution(mesh):
    in_specs = (
        P("state", "mesh"),
        P("state", None),
        P("mesh", None, None),
        P("mesh", None),
        P("mesh", None, None),
    )
    out_specs = P("state", "mesh")
    return jax.shard_map(
        per_device, mesh=mesh, in_specs=in_specs, out_specs=out_specs, check_vma=False
    )
```

profile of v0, /device:TPU:11, one launch (start us, length us, event | category | flops | bytes accessed | tf_op | source)
XLA Modules:
  0.0 562.0 jit_solution(6650308787093833255)
XLA Ops:
  8.8 34.4 %all-gather.2.cloned.1.call-done = f32[2048,256]{1,0:T(8,128)} async-done(((f32[1024,256]{1,0:T(8,128)}), f32[2048,256]{1,0:T(8,128)}) %all-gather.2.cloned.1.call-update) | async-done | bytes 2097168 | tf_op jit(solution)/shard_map/all_gather | solution.py:17
  43.2 9.2 %fusion.57 = f32[512,256]{0,1:T(8,128)S(1)} fusion(f32[512,2048]{1,0:T(8,128)} %param.7, f32[2048,256]{1,0:T(8,128)} %all-gather.2.cloned.1.call-done), kind=kOutput, calls=%fused_computation.87 | convolution fusion | flops 3221225472 | bytes 6815744 | tf_op jit(solution)/shard_map/dot_general | solution.py:15
  64.4 11.4 %all_to_all.32 = f32[16,1,32768]{2,1,0:T(1,128)} reshape(f32[16,512,2,32]{3,2,1,0:T(2,128)} %copy.38) | data formatting | bytes 4194304 | tf_op jit(solution)/shard_map/all_to_all | solution.py:36
  82.8 47.2 %all-to-all-done = f32[16,1,32768]{2,1,0:T(1,128)} async-done(((f32[16,1,32768]{2,1,0:T(1,128)}), f32[16,1,32768]{2,1,0:T(1,128)}, u32[]{:S(2)}, u32[]{:S(2)}) %all-to-all-start) | async-done | bytes 2097184 | tf_op jit(solution)/shard_map/all_to_all | solution.py:36
  138.0 10.2 %reshape.167 = f32[16,512,2,32]{3,2,1,0:T(2,128)} reshape(f32[16,32768]{1,0:T(8,128)} %reduce) | data formatting | bytes 4194304 | tf_op jit(solution)/shard_map/reshape | solution.py:46
  148.2 8.1 %copy.40 = f32[16,512,2,32]{1,0,2,3:T(8,128)} copy(f32[16,512,2,32]{3,2,1,0:T(2,128)} %reshape.167) | data formatting | bytes 4194304 | tf_op jit(solution)/shard_map/reshape | solution.py:46
  159.3 8.9 %gather_fusion.1 = f32[2000,512]{1,0:T(8,128)} fusion(f32[512,384]{0,1:T(8,128)S(1)} %pad_maximum_fusion, s32[2048]{0:T(1024)S(1)} %pad_clamp_fusion), kind=kCustom, calls=%fused_computation.1 | custom fusion | bytes 8200000 | tf_op jit(solution)/shard_map/gather | solution.py:74
  172.1 8.2 %fusion.4 = f32[16,125,512]{2,1,0:T(8,128)} fusion(f32[16,125,512]{2,1,0:T(8,128)} %reshape.191, f32[16,125,125]{2,0,1:T(8,128)S(1)} %copy-done), kind=kOutput, calls=%fused_computation.12 | convolution fusion | flops 1536000000 | bytes 9192000 | tf_op jit(solution)/shard_map/eab,ceb->cea/dot_general | solution.py:75
  184.1 13.4 %scatter_custom_fusion = f32[512,384]{0,1:T(8,128)S(1)} fusion(s32[2000]{0:T(1024)S(1)} %reshape.228, f32[2000,512]{1,0:T(8,128)} %reshape.214, f32[]{:T(128)} %constant.45.clone.1), kind=kCustom, calls=%fused_computation.31 | custom fusion | flops 1024000 | bytes 786944 | tf_op jit(solution)/shard_map/scatter-add | solution.py:78
  208.7 11.4 %all_to_all.33 = f32[16,1,32768]{2,1,0:T(1,128)} reshape(f32[16,512,2,32]{3,2,1,0:T(2,128)} %copy.45) | data formatting | bytes 4194304 | tf_op jit(solution)/shard_map/all_to_all | solution.py:54
  225.6 47.3 %all-to-all-done.1 = f32[16,1,32768]{2,1,0:T(1,128)} async-done(((f32[16,1,32768]{2,1,0:T(1,128)}), f32[16,1,32768]{2,1,0:T(1,128)}, u32[]{:S(2)}, u32[]{:S(2)}) %all-to-all-start.1) | async-done | bytes 2097184 | tf_op jit(solution)/shard_map/all_to_all | solution.py:54
  281.0 10.2 %reshape.170 = f32[16,512,2,32]{3,2,1,0:T(2,128)} reshape(f32[16,32768]{1,0:T(8,128)} %reduce.1) | data formatting | bytes 4194304 | tf_op jit(solution)/shard_map/reshape | solution.py:64
  291.2 8.1 %copy.47 = f32[16,512,2,32]{1,0,2,3:T(8,128)} copy(f32[16,512,2,32]{3,2,1,0:T(2,128)} %reshape.170) | data formatting | bytes 4194304 | tf_op jit(solution)/shard_map/reshape | solution.py:64
  316.1 11.4 %all_to_all.34 = f32[16,1,32768]{2,1,0:T(1,128)} reshape(f32[16,512,2,32]{3,2,1,0:T(2,128)} %copy.50) | data formatting | bytes 4194304 | tf_op jit(solution)/shard_map/all_to_all | solution.py:36
  327.4 52.3 %all_to_all.40 = f32[16,1,32768]{2,1,0:T(1,128)} all-to-all(f32[16,1,32768]{2,1,0:T(1,128)} %all_to_all.34), channel_id=1, replica_groups=mesh['mesh'=16,'state'=2] {'mesh'}, dimensions={0} | all-to-all | bytes 4194304 | tf_op jit(solution)/shard_map/all_to_all | solution.py:36
  387.8 10.2 %reshape.173 = f32[16,512,2,32]{3,2,1,0:T(2,128)} reshape(f32[16,32768]{1,0:T(8,128)} %reduce.2) | data formatting | bytes 4194304 | tf_op jit(solution)/shard_map/reshape | solution.py:46
  398.0 8.1 %copy.52 = f32[16,512,2,32]{1,0,2,3:T(8,128)} copy(f32[16,512,2,32]{3,2,1,0:T(2,128)} %reshape.173) | data formatting | bytes 4194304 | tf_op jit(solution)/shard_map/reshape | solution.py:46
  409.1 8.9 %gather_fusion.3 = f32[2000,512]{1,0:T(8,128)} fusion(f32[512,384]{0,1:T(8,128)S(1)} %pad_maximum_fusion.1, s32[2048]{0:T(1024)S(1)} %pad_clamp_fusion), kind=kCustom, calls=%fused_computation.3 | custom fusion | bytes 8200000 | tf_op jit(solution)/shard_map/gather | solution.py:74
  421.9 8.2 %fusion.7 = f32[16,125,512]{2,1,0:T(8,128)} fusion(f32[16,125,512]{2,1,0:T(8,128)} %reshape.207, f32[16,125,125]{2,0,1:T(8,128)S(1)} %copy-done), kind=kOutput, calls=%fused_computation.13 | convolution fusion | flops 1536000000 | bytes 9192000 | tf_op jit(solution)/shard_map/eab,ceb->cea/dot_general | solution.py:75
  433.8 13.4 %scatter_custom_fusion.2 = f32[512,384]{0,1:T(8,128)S(1)} fusion(s32[2000]{0:T(1024)S(1)} %reshape.228, f32[2000,512]{1,0:T(8,128)} %reshape.230, f32[]{:T(128)} %constant.45.clone.1), kind=kCustom, calls=%fused_computation.29 | custom fusion | flops 1024000 | bytes 786944 | tf_op jit(solution)/shard_map/scatter-add | solution.py:78
  458.5 11.4 %all_to_all.35 = f32[16,1,32768]{2,1,0:T(1,128)} reshape(f32[16,512,2,32]{3,2,1,0:T(2,128)} %copy.57) | data formatting | bytes 4194304 | tf_op jit(solution)/shard_map/all_to_all | solution.py:54
  475.6 47.3 %all-to-all-done.3 = f32[16,1,32768]{2,1,0:T(1,128)} async-done(((f32[16,1,32768]{2,1,0:T(1,128)}), f32[16,1,32768]{2,1,0:T(1,128)}, u32[]{:S(2)}, u32[]{:S(2)}) %all-to-all-start.3) | async-done | bytes 2097184 | tf_op jit(solution)/shard_map/all_to_all | solution.py:54
  530.9 10.2 %reshape.176 = f32[16,512,2,32]{3,2,1,0:T(2,128)} reshape(f32[16,32768]{1,0:T(8,128)} %reduce.3) | data formatting | bytes 4194304 | tf_op jit(solution)/shard_map/reshape | solution.py:64
  541.1 8.1 %copy.59 = f32[16,512,2,32]{1,0,2,3:T(8,128)} copy(f32[16,512,2,32]{3,2,1,0:T(2,128)} %reshape.176) | data formatting | bytes 4194304 | tf_op jit(solution)/shard_map/reshape | solution.py:64
  (64 shorter events, 130.5 us)
Async XLA Ops:
  6.5 165.6 %copy-start = (f32[16,125,125]{2,0,1:T(8,128)S(1)}, f32[16,125,125]{2,0,1:T(8,128)}, u32[]{:S(2)}) copy-start(f32[16,125,125]{2,0,1:T(8,128)} %param.8) | copy-start | bytes 3000004
  6.5 36.7 %all-gather.2.cloned.1.call-start = ((), (), s32[]{:S(2)}) async-start(), calls=%async_computation.4 | async-start | bytes 3145728 | tf_op jit(solution)/shard_map/all_gather | solution.py:17
  75.8 6.8 %copy-start.3 = (s32[16,125]{1,0:T(8,128)S(1)}, s32[16,125]{1,0:T(8,128)}, u32[]{:S(2)}) copy-start(s32[16,125]{1,0:T(8,128)} %param.9) | copy-start | bytes 24004
  75.8 54.2 %all-to-all-start = ((f32[16,1,32768]{2,1,0:T(1,128)}), f32[16,1,32768]{2,1,0:T(1,128)}, u32[]{:S(2)}, u32[]{:S(2)}) async-start(f32[16,1,32768]{2,1,0:T(1,128)} %all_to_all.32), calls=%async_computation | async-start | bytes 4194304 | tf_op jit(solution)/shard_map/all_to_all | solution.py:36
  197.5 28.1 %copy-start.1 = (f32[512,384]{0,1:T(8,128)}, f32[512,384]{0,1:T(8,128)S(1)}, u32[]{:S(2)}) copy-start(f32[512,384]{0,1:T(8,128)S(1)} %scatter_custom_fusion) | copy-start | bytes 2359300
  220.1 52.8 %all-to-all-start.1 = ((f32[16,1,32768]{2,1,0:T(1,128)}), f32[16,1,32768]{2,1,0:T(1,128)}, u32[]{:S(2)}, u32[]{:S(2)}) async-start(f32[16,1,32768]{2,1,0:T(1,128)} %all_to_all.33), calls=%async_computation.1 | async-start | bytes 4194304 | tf_op jit(solution)/shard_map/all_to_all | solution.py:54
  291.2 11.1 %slice-start = ((f32[512,384]{0,1:T(8,128)}), f32[512,256]{0,1:T(8,128)S(1)}, s32[]{:S(2)}) async-start(f32[512,384]{0,1:T(8,128)} %copy-done.1), calls=%async_computation.5 | async-start | bytes 1048576 | tf_op jit(solution)/shard_map/slice | solution.py:82
  447.2 28.3 %copy-start.2 = (f32[512,384]{0,1:T(8,128)}, f32[512,384]{0,1:T(8,128)S(1)}, u32[]{:S(2)}) copy-start(f32[512,384]{0,1:T(8,128)S(1)} %scatter_custom_fusion.2) | copy-start | bytes 2359300
  469.9 53.0 %all-to-all-start.3 = ((f32[16,1,32768]{2,1,0:T(1,128)}), f32[16,1,32768]{2,1,0:T(1,128)}, u32[]{:S(2)}, u32[]{:S(2)}) async-start(f32[16,1,32768]{2,1,0:T(1,128)} %all_to_all.35), calls=%async_computation.3 | async-start | bytes 4194304 | tf_op jit(solution)/shard_map/all_to_all | solution.py:54
  541.1 11.1 %slice-start.1 = ((f32[512,384]{0,1:T(8,128)}), f32[512,256]{0,1:T(8,128)S(1)}, s32[]{:S(2)}) async-start(f32[512,384]{0,1:T(8,128)} %copy-done.2), calls=%async_computation.6 | async-start | bytes 1048576 | tf_op jit(solution)/shard_map/slice | solution.py:82
Sparse Core Ops, SparseCore 0:
  8.9 34.2 all-gather.1
where the time goes:
time: 570 us; the launch traced here: 562 us
  local copies, waits for them, and re-layouts  187 us (33%)
  waiting for transfers between devices  177 us (31%)
  other arithmetic  63.4 us (11%)
  blocking collectives  52.3 us (9%)
  matrix products  50.6 us (9%)
  starting transfers between devices  18 us (3%)
  between operations  13.9 us (2%)
    all_to_all x2, waiting for transfers between devices, return_sums(): lax.all_to_all(going_back.reshape(partitions, block_rows * 2 * halo_width...  94.7 us
    all_to_all x1, blocking collectives, fetch_ghosts(): lax.all_to_all(outgoing.reshape(partitions, block_rows * 2 * halo_width),...  52.3 us
    all_to_all x1, waiting for transfers between devices, fetch_ghosts(): lax.all_to_all(outgoing.reshape(partitions, block_rows * 2 * halo_width),...  47.2 us
    reshape x4, local copies, waits for them, and re-layouts, return_sums(): arrived.reshape(partitions, block_rows, 2, halo_width)  36.7 us
    reshape x4, local copies, waits for them, and re-layouts, fetch_ghosts(): incoming.reshape(partitions, block_rows, 2, halo_width)  36.6 us
    all_gather x1, waiting for transfers between devices, per_device(): lax.all_gather(subspace, 'state', axis=0, tiled=True)  34.4 us
    scatter-add x2, other arithmetic, apply_ham(): summed = jnp.zeros(extended.shape, jnp.float32).at[:, connect].add(products)  26.8 us
    gather x4, local copies, waits for them, and re-layouts, apply_ham(): element_values = extended[:, connect]  25.6 us
  transfers between devices with their start and end apart: 4, of which 4 were waited for; matrix products, arithmetic and copies ran while one was open for 0% of the time, Pallas kernels for 0%

commit v1 on v0

v1 whole, which is shorter than its diff:
```python
import jax
import jax.numpy as jnp
from jax import lax
from jax.sharding import PartitionSpec as P

F32 = jnp.float32
HIGH = lax.Precision.HIGH


def mm(a, b, dims=((1,), (0,))):
    return lax.dot_general(a, b, (dims, ((), ())), precision=HIGH, preferred_element_type=F32)


def per_device(subspace, ritz, element_ham, connect, send_rows):
    depth, nodes = subspace.shape
    elems, size = connect.shape
    slots, halo = send_rows.shape[1:]
    partitions = lax.axis_size("mesh")
    groups = lax.axis_size("state")
    across = partitions // 2
    wide = slots * halo
    half_nodes = wide

    odd = lax.axis_index("mesh") % 2
    group = lax.axis_index("state")
    pairs_far = [(i, (i + across) % partitions) for i in range(partitions)]
    pairs_in = [(i, i ^ 1) for i in range(partitions)]
    pairs_out = [
        (i, (i + 1) % partitions if i % 2 else (i - 1) % partitions) for i in range(partitions)
    ]

    lists = send_rows[0]
    outer = jnp.where(odd == 1, lists[0], lists[1])
    inner = jnp.where(odd == 1, lists[1], lists[0])
    sent = jnp.concatenate([lists[2], lists[3], outer, inner])
    ids = jnp.arange(nodes, dtype=jnp.int32)
    hits = (sent[:, None] == ids[None, :]).astype(F32)
    edge = jnp.max(hits, axis=0).astype(jnp.int32)
    count = jnp.sum(jnp.where(ids[:, None] <= ids[None, :], edge[:, None], 0), axis=0)
    place = jnp.where(edge == 1, count - 1, jnp.sum(edge) + ids - count)
    shuffle = place[None, :] == ids[:, None]
    origin = jnp.sum(jnp.where(shuffle, ids[None, :], 0), axis=1)
    shuffle = shuffle.astype(F32)
    lane = jnp.arange(halo, dtype=jnp.int32)
    ghost_ids = nodes + jnp.concatenate(
        [3 * halo + lane, 2 * halo + lane, (1 - odd) * halo + lane, odd * halo + lane]
    )
    pick = (sent[:, None] == origin[None, :half_nodes]).astype(F32)

    turned = mm(shuffle, subspace, ((1,), (1,)))
    first_rows = turned[:half_nodes]
    other_rows = turned[half_nodes:]

    def from_group(rows, step):
        return lax.ppermute(rows, "state", [(i, (i + step) % groups) for i in range(groups)])

    edge_in = [from_group(first_rows, step) for step in range(1, groups)]
    rest_in = [from_group(other_rows, step) for step in range(1, groups)]

    def ritz_part(step):
        return lax.dynamic_slice_in_dim(ritz, ((group - step) % groups) * depth, depth, 1)

    columns = jnp.concatenate([origin, ghost_ids])
    spread = (connect.reshape(-1)[:, None] == columns[None, :]).astype(F32)
    blocks = lax.dot_general(
        element_ham,
        spread.reshape(elems, size, nodes + wide),
        (((2,), (1,)), ((0,), (0,))),
        precision=HIGH,
        preferred_element_type=F32,
    )
    ham = mm(spread, blocks.reshape(elems * size, nodes + wide), ((0,), (0,)))

    def exchange(packed):
        far = lax.ppermute(packed[: 2 * halo], "mesh", pairs_far)
        out = lax.ppermute(packed[2 * halo : 3 * halo], "mesh", pairs_out)
        near = lax.ppermute(packed[3 * halo :], "mesh", pairs_in)
        return jnp.concatenate([far, out, near], 0)

    own_start = mm(turned, ritz_part(0), ((1,), (1,)))
    start_edge = own_start[:half_nodes]
    for step in range(1, groups):
        start_edge = start_edge + mm(edge_in[step - 1], ritz_part(step), ((1,), (1,)))
    ghosts = exchange(mm(pick, start_edge))
    start_rest = own_start[half_nodes:]
    for step in range(1, groups):
        start_rest = start_rest + mm(rest_in[step - 1], ritz_part(step), ((1,), (1,)))

    half = 1.5
    centre = 2.5
    sigma_one = half / (-1.0 - centre)
    sigma_two = 1.0 / (2.0 / sigma_one - sigma_one)
    scale_one = sigma_one / half
    scale_two = 2.0 * sigma_two / half

    extended = jnp.concatenate([start_edge, start_rest, ghosts], 0)
    start = extended[:nodes]
    returned = exchange(mm(ham[nodes:], extended))
    base = scale_one * (mm(ham[:nodes], extended) - centre * start)
    packed = mm(pick, base[:half_nodes]) + mm(scale_one * mm(pick, pick, ((1,), (1,))), returned)
    ghosts = exchange(packed)
    first = jnp.concatenate(
        [
            base[:half_nodes] + scale_one * mm(pick, returned, ((0,), (0,))),
            base[half_nodes:],
        ],
        0,
    )
    own_part = mm(ham[:, :nodes], first)
    returned = exchange(own_part[nodes:] + mm(ham[nodes:, nodes:], ghosts))
    second = (
        scale_two * (own_part[:nodes] + mm(ham[:nodes, nodes:], ghosts) - centre * first)
        - sigma_one * sigma_two * start
    )
    return mm(second, shuffle, ((0,), (0,))) + mm(returned, scale_two * hits, ((0,), (0,)))


def solution(mesh):
    in_specs = (
        P("state", "mesh"),
        P("state", None),
        P("mesh", None, None),
        P("mesh", None),
        P("mesh", None, None),
    )
    out_specs = P("state", "mesh")
    return jax.shard_map(
        per_device, mesh=mesh, in_specs=in_specs, out_specs=out_specs, check_vma=False
    )
```

time: 570 us -> 65.4 us (0.11)
  the two profiles are of different devices: /device:TPU:11 before, /device:TPU:0 now
where the time goes in v1:
time: 65.4 us; the launch traced here: 65.1 us
  waiting for transfers between devices  21 us (32%)
  matrix products  19.8 us (30%)
  starting transfers between devices  16.7 us (26%)
  local copies, waits for them, and re-layouts  4.53 us (7%)
  other arithmetic  2.68 us (4%)
    dot_general x17, matrix products, mm(): lax.dot_general(a, b, (dims, ((), ())), precision=HIGH, preferred_element...  17.1 us
    ppermute x4, waiting for transfers between devices, exchange(): far = lax.ppermute(packed[:2 * halo], 'mesh', pairs_far)  10.1 us
    ppermute x4, starting transfers between devices, exchange(): far = lax.ppermute(packed[:2 * halo], 'mesh', pairs_far)  9.23 us
    ppermute x4, waiting for transfers between devices, exchange(): out = lax.ppermute(packed[2 * halo:3 * halo], 'mesh', pairs_out)  8.24 us
    reshape x1, local copies, waits for them, and re-layouts, per_device(): ham = mm(spread, blocks.reshape(elems * size, nodes + wide), ((0,), (0,)))  3.21 us
    ppermute x2, starting transfers between devices, from_group(): lax.ppermute(rows, 'state', [(i, (i + step) % groups) for i in range(grou...  3.02 us
    dot_general x1, matrix products, per_device(): lax.dot_general(element_ham, spread.reshape(elems, size, nodes + wide), (...  2.73 us
    ppermute x4, starting transfers between devices, exchange(): out = lax.ppermute(packed[2 * halo:3 * halo], 'mesh', pairs_out)  2.64 us
  transfers between devices with their start and end apart: 14, of which 7 were waited for; matrix products, arithmetic and copies ran while one was open for 30% of the time, Pallas kernels for 0%

profile of v1, /device:TPU:0, one launch (start us, length us, event | category | flops | bytes accessed | tf_op | source)
XLA Modules:
  0.0 65.1 jit_solution(1420325099190122776)
XLA Ops:
  0.0 0.9 %slice_bitcast_fusion.1 = (s32[32]{0:T(128)S(1)}, s32[32]{0:T(128)S(1)}, s32[32]{0:T(128)S(1)}, s32[32]{0:T(128)S(1)}) fusion(s32[1,4,32]{2,1,0:T(4,128)} %param.9, pred[]{:T(512)S(6)} %eq.77), kind=kLoop, calls=%fused_computation.100 | loop fusion | flops 64 | bytes 1025 | tf_op jit(solution)/shard_map/squeeze | solution.py:35
  3.0 1.0 %fusion.73 = (f32[128,1024]{1,0:T(8,128)}, f32[128,1024]{1,0:T(8,128)}) fusion(f32[256,1024]{1,0:T(8,128)S(1)} %fusion.38), kind=kLoop, calls=%fused_computation.106 | loop fusion | bytes 2097152 | tf_op jit(solution)/shard_map/slice | solution.py:52
  4.0 3.0 %collective-permute-start = (f32[128,1024]{1,0:T(8,128)}, f32[128,1024]{1,0:T(8,128)}, u32[]{:S(2)}, u32[]{:S(2)}) collective-permute-start(f32[128,1024]{1,0:T(8,128)} %get-tuple-element.6), channel_id=1, source_target_pairs={{0,1},{1,0},{2,3},{3,2},{4,5},{5,4},{6,7},{7,6},{8,9},{9,8},{10,11... | collective-permute-start | bytes 1572872 | tf_op jit(solution)/shard_map/ppermute | solution.py:55
  7.4 2.7 %fusion.10 = f32[16,125,384]{2,1,0:T(8,128)} fusion(s32[384]{0:T(512)S(1)} %pad_add_fusion, s32[16,125]{1,0:T(8,128)S(1)} %copy-done.3, f32[16,125,125]{2,0,1:T(8,128)S(1)} %copy-done.2), kind=kOutput, calls=%fused_computation.10 | convolution fusion | flops 576768000 | bytes 4081536 | tf_op jit(solution)/shard_map/dot_general | solution.py:65
  10.1 3.2 %reshape.45 = f32[2000,384]{1,0:T(8,128)} reshape(f32[16,125,384]{2,1,0:T(8,128)} %fusion.10) | data formatting | bytes 6144000 | tf_op jit(solution)/shard_map/reshape | solution.py:72
  13.4 2.8 %fusion.4 = f32[256,512]{1,0:T(8,128)S(1)} fusion(f32[256,1024]{1,0:T(8,128)S(1)} %fusion.38, f32[512,2048]{1,0:T(8,128)} %param.6, s32[]{:T(128)S(6)} %select_n.68), kind=kOutput, calls=%fused_computation.4 | convolution fusion | flops 805306368 | bytes 3670020 | tf_op jit(solution)/shard_map/dot_general | solution.py:11
  16.3 4.1 %fusion.2 = f32[384,384]{1,0:T(8,128)S(1)} fusion(f32[2000,384]{1,0:T(8,128)} %reshape.45, s32[384]{0:T(512)S(1)} %pad_add_fusion, s32[2000]{0:T(1024)S(1)} %eq.75), kind=kOutput, calls=%fused_computation.2 | convolution fusion | flops 1770240000 | bytes 3671360 | tf_op jit(solution)/shard_map/dot_general | solution.py:11
  20.5 2.3 %constant_dynamic-update-slice_fusion.4 = (f32[384,512]{1,0:T(8,128)S(1)}, f32[128,512]{1,0:T(8,128)S(1)}) fusion(f32[128,1024]{1,0:T(8,128)} %collective-permute-done, f32[512,2048]{1,0:T(8,128)S(1)} %copy-done.1, s32[]{:T(128)S(6)} %select_n.70, f32[256,512]{1,0:T(8,128)S(1)} %fusion.4), kind=kOutput, calls=%fused_computation.77 | convolution fusion | flops 402718720 | bytes 3407876 | tf_op jit(solution)/shard_map/dot_general | solution.py:11
  23.0 3.1 %collective-permute-start.2 = (f32[64,512]{1,0:T(8,128)S(1)}, f32[64,512]{1,0:T(8,128)S(1)}, u32[]{:S(2)}, u32[]{:S(2)}) collective-permute-start(f32[64,512]{1,0:T(8,128)S(1)} %slice.135), channel_id=1, source_target_pairs={{0,16},{2,18},{4,20},{6,22},{8,24},{10,26},{12,28},{14,30},{16,0},... | collective-permute-start | bytes 393224 | tf_op jit(solution)/shard_map/ppermute | solution.py:75
  26.2 0.9 %collective-permute-start.3 = (f32[32,512]{1,0:T(8,128)S(1)}, f32[32,512]{1,0:T(8,128)S(1)}, u32[]{:S(2)}, u32[]{:S(2)}) collective-permute-start(f32[32,512]{1,0:T(8,128)S(1)} %get-tuple-element.14), channel_id=1, source_target_pairs={{0,30},{2,4},{4,2},{6,8},{8,6},{10,12},{12,10},{14,16},{16,14},{18... | collective-permute-start | bytes 196616 | tf_op jit(solution)/shard_map/ppermute | solution.py:76
  27.1 0.7 %collective-permute-start.4 = (f32[32,512]{1,0:T(8,128)S(1)}, f32[32,512]{1,0:T(8,128)S(1)}, u32[]{:S(2)}, u32[]{:S(2)}) collective-permute-start(f32[32,512]{1,0:T(8,128)S(1)} %get-tuple-element.13), channel_id=1, source_target_pairs={{0,2},{2,0},{4,6},{6,4},{8,10},{10,8},{12,14},{14,12},{16,18},{18,... | collective-permute-start | bytes 196616 | tf_op jit(solution)/shard_map/ppermute | solution.py:77
  27.9 2.6 %collective-permute-done.1 = f32[128,1024]{1,0:T(8,128)} collective-permute-done((f32[128,1024]{1,0:T(8,128)}, f32[128,1024]{1,0:T(8,128)}, u32[]{:S(2)}, u32[]{:S(2)}) %collective-permute-start.1) | collective-permute-done | bytes 524320 | tf_op jit(solution)/shard_map/ppermute | solution.py:55
  30.5 2.2 %constant_dynamic-update-slice_fusion.3 = (f32[384,512]{1,0:T(8,128)S(1)}, f32[128,512]{1,0:T(8,128)S(1)}) fusion(f32[384,512]{1,0:T(8,128)S(1)} %get-tuple-element.19, f32[128,1024]{1,0:T(8,128)} %collective-permute-done.1, f32[512,2048]{1,0:T(8,128)S(1)} %copy-done.1, s32[]{:T(128)S(6)} %select_n.70, f32[256,512]{1,0:T(8,128)S(1)} %fusion.4), kind=kOutput, calls=%fused_computation.76 | convolution fusion | flops 402718720 | bytes 3407876 | tf_op jit(solution)/shard_map/dot_general | solution.py:11
  33.9 3.5 %collective-permute-start.5 = (f32[64,512]{1,0:T(8,128)S(1)}, f32[64,512]{1,0:T(8,128)S(1)}, u32[]{:S(2)}, u32[]{:S(2)}) collective-permute-start(f32[64,512]{1,0:T(8,128)S(1)} %slice.140), channel_id=1, source_target_pairs={{0,16},{2,18},{4,20},{6,22},{8,24},{10,26},{12,28},{14,30},{16,0},... | collective-permute-start | bytes 393224 | tf_op jit(solution)/shard_map/ppermute | solution.py:75
  37.3 1.0 %collective-permute-start.7 = (f32[32,512]{1,0:T(8,128)S(1)}, f32[32,512]{1,0:T(8,128)S(1)}, u32[]{:S(2)}, u32[]{:S(2)}) collective-permute-start(f32[32,512]{1,0:T(8,128)S(1)} %get-tuple-element.11), channel_id=1, source_target_pairs={{0,2},{2,0},{4,6},{6,4},{8,10},{10,8},{12,14},{14,12},{16,18},{18,... | collective-permute-start | bytes 196616 | tf_op jit(solution)/shard_map/ppermute | solution.py:77
  38.6 3.7 %collective-permute-done.5 = f32[64,512]{1,0:T(8,128)S(1)} collective-permute-done((f32[64,512]{1,0:T(8,128)S(1)}, f32[64,512]{1,0:T(8,128)S(1)}, u32[]{:S(2)}, u32[]{:S(2)}) %collective-permute-start.5) | collective-permute-done | bytes 131104 | tf_op jit(solution)/shard_map/ppermute | solution.py:75
  42.3 1.5 %collective-permute-done.6 = f32[32,512]{1,0:T(8,128)S(1)} collective-permute-done((f32[32,512]{1,0:T(8,128)S(1)}, f32[32,512]{1,0:T(8,128)S(1)}, u32[]{:S(2)}, u32[]{:S(2)}) %collective-permute-start.6) | collective-permute-done | bytes 65568 | tf_op jit(solution)/shard_map/ppermute | solution.py:76
  44.5 2.6 %collective-permute-start.8 = (f32[64,512]{1,0:T(8,128)S(1)}, f32[64,512]{1,0:T(8,128)S(1)}, u32[]{:S(2)}, u32[]{:S(2)}) collective-permute-start(f32[64,512]{1,0:T(8,128)S(1)} %slice.146), channel_id=1, source_target_pairs={{0,16},{2,18},{4,20},{6,22},{8,24},{10,26},{12,28},{14,30},{16,0},... | collective-permute-start | bytes 393224 | tf_op jit(solution)/shard_map/ppermute | solution.py:75
  47.6 4.2 %collective-permute-done.8 = f32[64,512]{1,0:T(8,128)S(1)} collective-permute-done((f32[64,512]{1,0:T(8,128)S(1)}, f32[64,512]{1,0:T(8,128)S(1)}, u32[]{:S(2)}, u32[]{:S(2)}) %collective-permute-start.8) | collective-permute-done | bytes 131104 | tf_op jit(solution)/shard_map/ppermute | solution.py:75
  51.8 1.7 %collective-permute-done.9 = f32[32,512]{1,0:T(8,128)S(1)} collective-permute-done((f32[32,512]{1,0:T(8,128)S(1)}, f32[32,512]{1,0:T(8,128)S(1)}, u32[]{:S(2)}, u32[]{:S(2)}) %collective-permute-start.9) | collective-permute-done | bytes 65568 | tf_op jit(solution)/shard_map/ppermute | solution.py:76
  54.4 1.7 %collective-permute-start.12 = (f32[32,512]{1,0:T(8,128)S(1)}, f32[32,512]{1,0:T(8,128)S(1)}, u32[]{:S(2)}, u32[]{:S(2)}) collective-permute-start(f32[32,512]{1,0:T(8,128)S(1)} %get-tuple-element.7), channel_id=1, source_target_pairs={{0,30},{2,4},{4,2},{6,8},{8,6},{10,12},{12,10},{14,16},{16,14},{18... | collective-permute-start | bytes 196616 | tf_op jit(solution)/shard_map/ppermute | solution.py:76
  56.6 5.1 %collective-permute-done.12 = f32[32,512]{1,0:T(8,128)S(1)} collective-permute-done((f32[32,512]{1,0:T(8,128)S(1)}, f32[32,512]{1,0:T(8,128)S(1)}, u32[]{:S(2)}, u32[]{:S(2)}) %collective-permute-start.12) | collective-permute-done | bytes 65568 | tf_op jit(solution)/shard_map/ppermute | solution.py:76
  61.6 2.3 %collective-permute-done.11 = f32[64,512]{1,0:T(8,128)S(1)} collective-permute-done((f32[64,512]{1,0:T(8,128)S(1)}, f32[64,512]{1,0:T(8,128)S(1)}, u32[]{:S(2)}, u32[]{:S(2)}) %collective-permute-start.11) | collective-permute-done | bytes 131104 | tf_op jit(solution)/shard_map/ppermute | solution.py:75
  63.9 1.2 %convolution_add_fusion = f32[512,256]{1,0:T(8,128)} fusion(f32[512,256]{1,0:T(8,128)S(1)} %fusion.37, f32[32,512]{1,0:T(8,128)S(1)} %collective-permute-done.13, f32[32,512]{1,0:T(8,128)S(1)} %collective-permute-done.12, f32[64,512]{1,0:T(8,128)S(1)} %collective-permute-done.11, s32[128]{0:T(128)S(1)} %pad_add_fusion.1), kind=kOutput, calls=%fused_computation.17 | convolution fusion | flops 100990976 | bytes 1311232 | tf_op jit(solution)/shard_map/dot_general | solution.py:11
  (64 shorter events, 6.7 us)
Async XLA Ops:
  0.0 2.5 %copy-start = (f32[1024,256]{1,0:T(8,128)S(1)}, f32[1024,256]{1,0:T(8,128)}, u32[]{:S(2)}) copy-start(f32[1024,256]{1,0:T(8,128)} %param.5) | copy-start | bytes 3145732
  0.0 7.3 %copy-start.3 = (s32[16,125]{1,0:T(8,128)S(1)}, s32[16,125]{1,0:T(8,128)}, u32[]{:S(2)}) copy-start(s32[16,125]{1,0:T(8,128)} %param.8) | copy-start | bytes 24004
  0.0 7.4 %copy-start.2 = (f32[16,125,125]{2,0,1:T(8,128)S(1)}, f32[16,125,125]{2,0,1:T(8,128)}, u32[]{:S(2)}) copy-start(f32[16,125,125]{2,0,1:T(8,128)} %param.7) | copy-start | bytes 3000004
  4.0 16.4 %collective-permute-start = (f32[128,1024]{1,0:T(8,128)}, f32[128,1024]{1,0:T(8,128)}, u32[]{:S(2)}, u32[]{:S(2)}) collective-permute-start(f32[128,1024]{1,0:T(8,128)} %get-tuple-element.6), channel_id=1, source_target_pairs={{0,1},{1,0},{2,3},{3,2},{4,5},{5,4},{6,7},{7,6},{8,9},{9,8},{10,11... | collective-permute-start | bytes 1572872 | tf_op jit(solution)/shard_map/ppermute | solution.py:55
  7.0 23.5 %collective-permute-start.1 = (f32[128,1024]{1,0:T(8,128)}, f32[128,1024]{1,0:T(8,128)}, u32[]{:S(2)}, u32[]{:S(2)}) collective-permute-start(f32[128,1024]{1,0:T(8,128)} %get-tuple-element.5), channel_id=1, source_target_pairs={{0,1},{1,0},{2,3},{3,2},{4,5},{5,4},{6,7},{7,6},{8,9},{9,8},{10,11... | collective-permute-start | bytes 1572872 | tf_op jit(solution)/shard_map/ppermute | solution.py:55
  13.3 7.1 %copy-start.1 = (f32[512,2048]{1,0:T(8,128)S(1)}, f32[512,2048]{1,0:T(8,128)}, u32[]{:S(2)}) copy-start(f32[512,2048]{1,0:T(8,128)} %param.6) | copy-start | bytes 12582916
  23.0 9.7 %collective-permute-start.2 = (f32[64,512]{1,0:T(8,128)S(1)}, f32[64,512]{1,0:T(8,128)S(1)}, u32[]{:S(2)}, u32[]{:S(2)}) collective-permute-start(f32[64,512]{1,0:T(8,128)S(1)} %slice.135), channel_id=1, source_target_pairs={{0,16},{2,18},{4,20},{6,22},{8,24},{10,26},{12,28},{14,30},{16,0},... | collective-permute-start | bytes 393224 | tf_op jit(solution)/shard_map/ppermute | solution.py:75
  26.2 6.6 %collective-permute-start.3 = (f32[32,512]{1,0:T(8,128)S(1)}, f32[32,512]{1,0:T(8,128)S(1)}, u32[]{:S(2)}, u32[]{:S(2)}) collective-permute-start(f32[32,512]{1,0:T(8,128)S(1)} %get-tuple-element.14), channel_id=1, source_target_pairs={{0,30},{2,4},{4,2},{6,8},{8,6},{10,12},{12,10},{14,16},{16,14},{18... | collective-permute-start | bytes 196616 | tf_op jit(solution)/shard_map/ppermute | solution.py:76
  27.1 5.7 %collective-permute-start.4 = (f32[32,512]{1,0:T(8,128)S(1)}, f32[32,512]{1,0:T(8,128)S(1)}, u32[]{:S(2)}, u32[]{:S(2)}) collective-permute-start(f32[32,512]{1,0:T(8,128)S(1)} %get-tuple-element.13), channel_id=1, source_target_pairs={{0,2},{2,0},{4,6},{6,4},{8,10},{10,8},{12,14},{14,12},{16,18},{18,... | collective-permute-start | bytes 196616 | tf_op jit(solution)/shard_map/ppermute | solution.py:77
  33.9 8.5 %collective-permute-start.5 = (f32[64,512]{1,0:T(8,128)S(1)}, f32[64,512]{1,0:T(8,128)S(1)}, u32[]{:S(2)}, u32[]{:S(2)}) collective-permute-start(f32[64,512]{1,0:T(8,128)S(1)} %slice.140), channel_id=1, source_target_pairs={{0,16},{2,18},{4,20},{6,22},{8,24},{10,26},{12,28},{14,30},{16,0},... | collective-permute-start | bytes 393224 | tf_op jit(solution)/shard_map/ppermute | solution.py:75
  37.3 6.5 %collective-permute-start.6 = (f32[32,512]{1,0:T(8,128)S(1)}, f32[32,512]{1,0:T(8,128)S(1)}, u32[]{:S(2)}, u32[]{:S(2)}) collective-permute-start(f32[32,512]{1,0:T(8,128)S(1)} %get-tuple-element.12), channel_id=1, source_target_pairs={{0,30},{2,4},{4,2},{6,8},{8,6},{10,12},{12,10},{14,16},{16,14},{18... | collective-permute-start | bytes 196616 | tf_op jit(solution)/shard_map/ppermute | solution.py:76
  37.3 6.5 %collective-permute-start.7 = (f32[32,512]{1,0:T(8,128)S(1)}, f32[32,512]{1,0:T(8,128)S(1)}, u32[]{:S(2)}, u32[]{:S(2)}) collective-permute-start(f32[32,512]{1,0:T(8,128)S(1)} %get-tuple-element.11), channel_id=1, source_target_pairs={{0,2},{2,0},{4,6},{6,4},{8,10},{10,8},{12,14},{14,12},{16,18},{18,... | collective-permute-start | bytes 196616 | tf_op jit(solution)/shard_map/ppermute | solution.py:77
  44.5 7.3 %collective-permute-start.8 = (f32[64,512]{1,0:T(8,128)S(1)}, f32[64,512]{1,0:T(8,128)S(1)}, u32[]{:S(2)}, u32[]{:S(2)}) collective-permute-start(f32[64,512]{1,0:T(8,128)S(1)} %slice.146), channel_id=1, source_target_pairs={{0,16},{2,18},{4,20},{6,22},{8,24},{10,26},{12,28},{14,30},{16,0},... | collective-permute-start | bytes 393224 | tf_op jit(solution)/shard_map/ppermute | solution.py:75
  47.1 6.4 %collective-permute-start.9 = (f32[32,512]{1,0:T(8,128)S(1)}, f32[32,512]{1,0:T(8,128)S(1)}, u32[]{:S(2)}, u32[]{:S(2)}) collective-permute-start(f32[32,512]{1,0:T(8,128)S(1)} %get-tuple-element.10), channel_id=1, source_target_pairs={{0,30},{2,4},{4,2},{6,8},{8,6},{10,12},{12,10},{14,16},{16,14},{18... | collective-permute-start | bytes 196616 | tf_op jit(solution)/shard_map/ppermute | solution.py:76
  47.1 6.4 %collective-permute-start.10 = (f32[32,512]{1,0:T(8,128)S(1)}, f32[32,512]{1,0:T(8,128)S(1)}, u32[]{:S(2)}, u32[]{:S(2)}) collective-permute-start(f32[32,512]{1,0:T(8,128)S(1)} %get-tuple-element.9), channel_id=1, source_target_pairs={{0,2},{2,0},{4,6},{6,4},{8,10},{10,8},{12,14},{14,12},{16,18},{18,... | collective-permute-start | bytes 196616 | tf_op jit(solution)/shard_map/ppermute | solution.py:77
  54.3 2.2 %collective-permute-start.13 = (f32[32,512]{1,0:T(8,128)S(1)}, f32[32,512]{1,0:T(8,128)S(1)}, u32[]{:S(2)}, u32[]{:S(2)}) collective-permute-start(f32[32,512]{1,0:T(8,128)S(1)} %get-tuple-element.8), channel_id=1, source_target_pairs={{0,2},{2,0},{4,6},{6,4},{8,10},{10,8},{12,14},{14,12},{16,18},{18,... | collective-permute-start | bytes 196616 | tf_op jit(solution)/shard_map/ppermute | solution.py:77
  54.4 7.3 %collective-permute-start.12 = (f32[32,512]{1,0:T(8,128)S(1)}, f32[32,512]{1,0:T(8,128)S(1)}, u32[]{:S(2)}, u32[]{:S(2)}) collective-permute-start(f32[32,512]{1,0:T(8,128)S(1)} %get-tuple-element.7), channel_id=1, source_target_pairs={{0,30},{2,4},{4,2},{6,8},{8,6},{10,12},{12,10},{14,16},{16,14},{18... | collective-permute-start | bytes 196616 | tf_op jit(solution)/shard_map/ppermute | solution.py:76
  56.1 7.8 %collective-permute-start.11 = (f32[64,512]{1,0:T(8,128)S(1)}, f32[64,512]{1,0:T(8,128)S(1)}, u32[]{:S(2)}, u32[]{:S(2)}) collective-permute-start(f32[64,512]{1,0:T(8,128)S(1)} %slice.151), channel_id=1, source_target_pairs={{0,16},{2,18},{4,20},{6,22},{8,24},{10,26},{12,28},{14,30},{16,0},... | collective-permute-start | bytes 393224 | tf_op jit(solution)/shard_map/ppermute | solution.py:75

commit v2 on v1

--- a/solution.py
+++ b/solution.py
@@ -19,7 +19,7 @@
     groups = lax.axis_size("state")
     across = partitions // 2
     wide = slots * halo
-    half_nodes = wide
+    edge_nodes = wide
 
     odd = lax.axis_index("mesh") % 2
     group = lax.axis_index("state")
@@ -45,17 +45,17 @@
     ghost_ids = nodes + jnp.concatenate(
         [3 * halo + lane, 2 * halo + lane, (1 - odd) * halo + lane, odd * halo + lane]
     )
-    pick = (sent[:, None] == origin[None, :half_nodes]).astype(F32)
-
-    turned = mm(shuffle, subspace, ((1,), (1,)))
-    first_rows = turned[:half_nodes]
-    other_rows = turned[half_nodes:]
+    pick = (sent[:, None] == origin[None, :edge_nodes]).astype(F32)
 
     def from_group(rows, step):
         return lax.ppermute(rows, "state", [(i, (i + step) % groups) for i in range(groups)])
 
-    edge_in = [from_group(first_rows, step) for step in range(1, groups)]
-    rest_in = [from_group(other_rows, step) for step in range(1, groups)]
+    head = depth // 4
+    steps = range(1, groups)
+    head_in = [from_group(subspace[:head], step) for step in steps]
+    turned = mm(shuffle, subspace, ((1,), (1,)))
+    edge_in = [from_group(turned[:edge_nodes, head:], step) for step in steps]
+    rest_in = [from_group(turned[edge_nodes:, head:], step) for step in steps]
 
     def ritz_part(step):
         return lax.dynamic_slice_in_dim(ritz, ((group - step) % groups) * depth, depth, 1)
@@ -71,20 +71,36 @@
     )
     ham = mm(spread, blocks.reshape(elems * size, nodes + wide), ((0,), (0,)))
 
-    def exchange(packed):
-        far = lax.ppermute(packed[: 2 * halo], "mesh", pairs_far)
-        out = lax.ppermute(packed[2 * halo : 3 * halo], "mesh", pairs_out)
-        near = lax.ppermute(packed[3 * halo :], "mesh", pairs_in)
-        return jnp.concatenate([far, out, near], 0)
+    def far(rows):
+        return lax.ppermute(rows, "mesh", pairs_far)
+
+    def ring(rows):
+        out = lax.ppermute(rows[:halo], "mesh", pairs_out)
+        near = lax.ppermute(rows[halo:], "mesh", pairs_in)
+        return jnp.concatenate([out, near], 0)
+
+    duo = 2 * halo
+    pick_far, pick_ring = pick[:duo], pick[duo:]
+    far_rows = slice(nodes, nodes + duo)
+    ring_rows = slice(nodes + duo, nodes + wide)
 
     own_start = mm(turned, ritz_part(0), ((1,), (1,)))
-    start_edge = own_start[:half_nodes]
-    for step in range(1, groups):
-        start_edge = start_edge + mm(edge_in[step - 1], ritz_part(step), ((1,), (1,)))
-    ghosts = exchange(mm(pick, start_edge))
-    start_rest = own_start[half_nodes:]
-    for step in range(1, groups):
-        start_rest = start_rest + mm(rest_in[step - 1], ritz_part(step), ((1,), (1,)))
+    for step in steps:
+        turned_head = mm(shuffle, head_in[step - 1], ((1,), (1,)))
+        own_start = own_start + mm(turned_head, ritz_part(step)[:, :head], ((1,), (1,)))
+    start_edge = own_start[:edge_nodes]
+    for step in steps:
+        start_edge = start_edge + mm(edge_in[step - 1], ritz_part(step)[:, head:], ((1,), (1,)))
+    packed = mm(pick, start_edge)
+    overlap = mm(pick_far, pick_far, ((1,), (1,)))
+    message = far(jnp.concatenate([packed[:duo], overlap, ham[far_rows, far_rows]], 1))
+    block_rows = ritz.shape[0]
+    ghosts = jnp.concatenate([message[:, :block_rows], ring(packed[duo:])], 0)
+    overlap_in = message[:, block_rows : block_rows + duo]
+    couple_in = message[:, block_rows + duo :]
+    start_rest = own_start[edge_nodes:]
+    for step in steps:
+        start_rest = start_rest + mm(rest_in[step - 1], ritz_part(step)[:, head:], ((1,), (1,)))
 
     half = 1.5
     centre = 2.5
@@ -95,24 +111,38 @@
 
     extended = jnp.concatenate([start_edge, start_rest, ghosts], 0)
     start = extended[:nodes]
-    returned = exchange(mm(ham[nodes:], extended))
+    sent_back = mm(ham[nodes:], extended)
+    back_far = far(sent_back[:duo])
+    back_ring = ring(sent_back[duo:])
     base = scale_one * (mm(ham[:nodes], extended) - centre * start)
-    packed = mm(pick, base[:half_nodes]) + mm(scale_one * mm(pick, pick, ((1,), (1,))), returned)
-    ghosts = exchange(packed)
-    first = jnp.concatenate(
-        [
-            base[:half_nodes] + scale_one * mm(pick, returned, ((0,), (0,))),
-            base[half_nodes:],
-        ],
-        0,
+    base_edge = base[:edge_nodes]
+    fetched_far = far(
+        mm(pick_far, base_edge)
+        + mm(scale_one * mm(pick_far, pick_ring, ((1,), (1,))), back_ring)
     )
+    back = jnp.concatenate([back_far, back_ring], 0)
+    fetched_ring = ring(
+        mm(pick_ring, base_edge) + mm(scale_one * mm(pick_ring, pick, ((1,), (1,))), back)
+    )
+    first_edge = base_edge + scale_one * mm(pick, back, ((0,), (0,)))
+    first = jnp.concatenate([first_edge, base[edge_nodes:]], 0)
+
     own_part = mm(ham[:, :nodes], first)
-    returned = exchange(own_part[nodes:] + mm(ham[nodes:, nodes:], ghosts))
+    ring_part = mm(ham[:, ring_rows], fetched_ring)
+    returned_far = far(own_part[far_rows] + ring_part[far_rows])
+    ghosts_far = fetched_far + mm(scale_one * overlap_in, sent_back[:duo])
+    known = mm(couple_in, mm(pick_far, first_edge))
+    far_part = mm(ham[:, far_rows], ghosts_far)
+    returned_ring = ring(own_part[ring_rows] + ring_part[ring_rows] + far_part[ring_rows])
     second = (
-        scale_two * (own_part[:nodes] + mm(ham[:nodes, nodes:], ghosts) - centre * first)
+        scale_two * (own_part[:nodes] + ring_part[:nodes] + far_part[:nodes] - centre * first)
         - sigma_one * sigma_two * start
     )
-    return mm(second, shuffle, ((0,), (0,))) + mm(returned, scale_two * hits, ((0,), (0,)))
+    weights = scale_two * hits
+    result = mm(second, shuffle, ((0,), (0,))) + mm(
+        jnp.concatenate([known, returned_ring], 0), weights, ((0,), (0,))
+    )
+    return result + mm(returned_far, weights[:duo], ((0,), (0,)))
 
 
 def solution(mesh):

time: 65.4 us -> 78.8 us (1.20)
  starting transfers between devices: 16.7 us -> 23.4 us
  matrix products: 19.8 us -> 26 us
  waiting for transfers between devices: 21 us -> 19.2 us
  local copies, waits for them, and re-layouts: 4.53 us -> 6.02 us
    dot_general x17 -> x27, matrix products: 17.1 us -> 23.3 us  [mm(): lax.dot_general(a, b, (dims, ((), ())), precision=HIGH, preferred_element...]
    ppermute x12, starting transfers between devices: 13.7 us -> 18.4 us  [the longest x4 11.7 us: ring(): out = lax.ppermute(rows[:halo], 'mesh', pairs_out)]
    ppermute x2 -> x3, waiting for transfers between devices: 2.64 us -> 0.01 us  [from_group(): lax.ppermute(rows, 'state', [(i, (i + step) % groups) for i in range(grou...]
    ppermute x2 -> x3, starting transfers between devices: 3.02 us -> 5.06 us  [from_group(): lax.ppermute(rows, 'state', [(i, (i + step) % groups) for i in range(grou...]
    slice x11 -> x12, local copies, waits for them, and re-layouts: 1.14 us -> 2.61 us  [the longest x1 1.77 us: per_device(): head_in = [from_group(subspace[:head], step) for step in steps]]
    ppermute x12, waiting for transfers between devices: 18.4 us -> 19.2 us  [the longest x4 14 us: far(): return lax.ppermute(rows, 'mesh', pairs_far)]
  transfers between devices with their start and end apart: 14 -> 15, of which waited for: 7 -> 6; matrix products, arithmetic and copies ran while one was open for 30% -> 40% of each run, Pallas kernels for 0% -> 0%
where the time goes in v2:
time: 78.8 us; the launch traced here: 78.5 us
  matrix products  26 us (33%)
  starting transfers between devices  23.4 us (30%)
  waiting for transfers between devices  19.2 us (24%)
  local copies, waits for them, and re-layouts  6.02 us (8%)
  other arithmetic  3.33 us (4%)
    dot_general x27, matrix products, mm(): lax.dot_general(a, b, (dims, ((), ())), precision=HIGH, preferred_element...  23.3 us
    ppermute x4, waiting for transfers between devices, far(): return lax.ppermute(rows, 'mesh', pairs_far)  14 us
    ppermute x4, starting transfers between devices, ring(): out = lax.ppermute(rows[:halo], 'mesh', pairs_out)  11.7 us
    ppermute x4, starting transfers between devices, far(): return lax.ppermute(rows, 'mesh', pairs_far)  5.61 us
    ppermute x4, waiting for transfers between devices, ring(): out = lax.ppermute(rows[:halo], 'mesh', pairs_out)  5.18 us
    ppermute x3, starting transfers between devices, from_group(): lax.ppermute(rows, 'state', [(i, (i + step) % groups) for i in range(grou...  5.06 us
    reshape x1, local copies, waits for them, and re-layouts, per_device(): ham = mm(spread, blocks.reshape(elems * size, nodes + wide), ((0,), (0,)))  3.25 us
    dot_general x1, matrix products, per_device(): lax.dot_general(element_ham, spread.reshape(elems, size, nodes + wide), (...  2.72 us
  transfers between devices with their start and end apart: 15, of which 6 were waited for; matrix products, arithmetic and copies ran while one was open for 40% of the time, Pallas kernels for 0%

profile of v2, /device:TPU:0, one launch (start us, length us, event | category | flops | bytes accessed | tf_op | source)
XLA Modules:
  0.0 78.5 jit_solution(3130598043765928858)
XLA Ops:
  0.0 1.8 %slice.154 = f32[256,256]{1,0:T(8,128)} slice(f32[1024,256]{1,0:T(8,128)} %param.5), slice={[0:256], [0:256]} | slice | bytes 524288 | tf_op jit(solution)/shard_map/slice | solution.py:55
  1.8 3.0 %collective-permute-start = (f32[256,256]{1,0:T(8,128)}, f32[256,256]{1,0:T(8,128)}, u32[]{:S(2)}, u32[]{:S(2)}) collective-permute-start(f32[256,256]{1,0:T(8,128)} %slice.154), channel_id=1, source_target_pairs={{0,1},{1,0},{2,3},{3,2},{4,5},{5,4},{6,7},{7,6},{8,9},{9,8},{10,11... | collective-permute-start | bytes 786440 | tf_op jit(solution)/shard_map/ppermute | solution.py:51
  7.8 1.7 %fusion.51 = f32[256,1024]{1,0:T(8,128)S(1)} fusion(f32[1024,256]{1,0:T(8,128)} %param.5, s32[256]{0:T(256)S(1)} %compare_select_fusion), kind=kOutput, calls=%fused_computation.57 | convolution fusion | flops 402718720 | bytes 2098176 | tf_op jit(solution)/shard_map/dot_general | solution.py:11
  9.6 2.0 %collective-permute-start.2 = (f32[128,768]{1,0:T(8,128)S(1)}, f32[128,768]{1,0:T(8,128)}, u32[]{:S(2)}, u32[]{:S(2)}) collective-permute-start(f32[128,768]{1,0:T(8,128)S(1)} %get-tuple-element.7), channel_id=1, source_target_pairs={{0,1},{1,0},{2,3},{3,2},{4,5},{5,4},{6,7},{7,6},{8,9},{9,8},{10,11... | collective-permute-start | bytes 1179656 | tf_op jit(solution)/shard_map/ppermute | solution.py:51
  11.9 2.7 %fusion.6 = f32[16,125,384]{2,1,0:T(8,128)} fusion(s32[384]{0:T(512)S(1)} %pad_add_fusion, s32[16,125]{1,0:T(8,128)S(1)} %copy-done.4, f32[16,125,125]{2,0,1:T(8,128)S(1)} %copy-done), kind=kOutput, calls=%fused_computation.6 | convolution fusion | flops 576768000 | bytes 4081536 | tf_op jit(solution)/shard_map/dot_general | solution.py:65
  14.6 3.3 %reshape.45 = f32[2000,384]{1,0:T(8,128)} reshape(f32[16,125,384]{2,1,0:T(8,128)} %fusion.6) | data formatting | bytes 6144000 | tf_op jit(solution)/shard_map/reshape | solution.py:72
  18.8 4.2 %fusion.2 = f32[384,384]{0,1:T(8,128)S(1)} fusion(f32[2000,384]{1,0:T(8,128)} %reshape.45, s32[384]{0:T(512)S(1)} %pad_add_fusion, s32[2000]{0:T(1024)S(1)} %eq.76), kind=kOutput, calls=%fused_computation.2 | convolution fusion | flops 1770240000 | bytes 3671360 | tf_op jit(solution)/shard_map/dot_general | solution.py:11
  24.0 1.4 %fusion.50 = f32[256,256]{1,0:T(8,128)S(1)} fusion(f32[256,256]{1,0:T(8,128)} %collective-permute-done, s32[256]{0:T(256)S(1)} %compare_select_fusion), kind=kOutput, calls=%fused_computation.56 | convolution fusion | flops 100728832 | bytes 525312 | tf_op jit(solution)/shard_map/dot_general | solution.py:11
  25.4 1.5 %fusion.35 = f32[256,512]{1,0:T(8,128)S(1)} fusion(f32[256,256]{1,0:T(8,128)S(1)} %fusion.50, f32[512,2048]{1,0:T(8,128)} %param.6, s32[]{:T(128)S(6)} %select_n.73), kind=kOutput, calls=%fused_computation.37 | convolution fusion | flops 201326592 | bytes 1310724 | tf_op jit(solution)/shard_map/dot_general | solution.py:11
  26.8 2.6 %fusion.18 = f32[256,512]{1,0:T(8,128)S(1)} fusion(f32[256,512]{1,0:T(8,128)S(1)} %fusion.35, f32[256,1024]{1,0:T(8,128)S(1)} %fusion.51, f32[512,2048]{1,0:T(8,128)} %param.6, s32[]{:T(128)S(6)} %select_n.71), kind=kOutput, calls=%fused_computation.17 | convolution fusion | flops 805437440 | bytes 4194308 | tf_op jit(solution)/shard_map/dot_general | solution.py:11
  29.5 1.9 %constant_dynamic-update-slice_fusion.3 = (f32[384,512]{1,0:T(8,128)S(1)}, f32[128,512]{1,0:T(8,128)S(1)}) fusion(f32[128,768]{1,0:T(8,128)} %collective-permute-done.1, f32[512,2048]{1,0:T(8,128)S(1)} %copy-done.1, s32[]{:T(128)S(6)} %add.146, f32[256,512]{1,0:T(8,128)S(1)} %fusion.18), kind=kOutput, calls=%fused_computation.105 | convolution fusion | flops 302055424 | bytes 2752516 | tf_op jit(solution)/shard_map/dot_general | solution.py:11
  31.8 2.6 %collective-permute-start.3 = (f32[64,640]{1,0:T(8,128)S(1)}, f32[64,640]{1,0:T(8,128)S(1)}, u32[]{:S(2)}, u32[]{:S(2)}) collective-permute-start(f32[64,640]{1,0:T(8,128)S(1)} %pad_maximum_fusion.5), channel_id=1, source_target_pairs={{0,16},{2,18},{4,20},{6,22},{8,24},{10,26},{12,28},{14,30},{16,0},... | collective-permute-start | bytes 491528 | tf_op jit(solution)/shard_map/ppermute | solution.py:75
  35.1 1.0 %collective-permute-start.5 = (f32[32,512]{1,0:T(8,128)S(1)}, f32[32,512]{1,0:T(8,128)S(1)}, u32[]{:S(2)}, u32[]{:S(2)}) collective-permute-start(f32[32,512]{1,0:T(8,128)S(1)} %get-tuple-element.11), channel_id=1, source_target_pairs={{0,2},{2,0},{4,6},{6,4},{8,10},{10,8},{12,14},{14,12},{16,18},{18,... | collective-permute-start | bytes 196616 | tf_op jit(solution)/shard_map/ppermute | solution.py:79
  36.1 1.9 %constant_dynamic-update-slice_fusion.2 = (f32[384,512]{1,0:T(8,128)S(1)}, f32[128,512]{1,0:T(8,128)S(1)}) fusion(f32[384,512]{1,0:T(8,128)S(1)} %get-tuple-element.23, f32[128,768]{1,0:T(8,128)} %collective-permute-done.2, f32[512,2048]{1,0:T(8,128)S(1)} %copy-done.1, s32[]{:T(128)S(6)} %add.146, f32[256,512]{1,0:T(8,128)S(1)} %fusion.18), kind=kOutput, calls=%fused_computation.104 | convolution fusion | flops 302055424 | bytes 2752516 | tf_op jit(solution)/shard_map/dot_general | solution.py:11
  38.1 3.3 %collective-permute-done.3 = f32[64,640]{1,0:T(8,128)S(1)} collective-permute-done((f32[64,640]{1,0:T(8,128)S(1)}, f32[64,640]{1,0:T(8,128)S(1)}, u32[]{:S(2)}, u32[]{:S(2)}) %collective-permute-start.3) | collective-permute-done | bytes 163872 | tf_op jit(solution)/shard_map/ppermute | solution.py:75
  41.9 4.0 %collective-permute-start.7 = (f32[32,512]{1,0:T(8,128)S(1)}, f32[32,512]{1,0:T(8,128)S(1)}, u32[]{:S(2)}, u32[]{:S(2)}) collective-permute-start(f32[32,512]{1,0:T(8,128)S(1)} %get-tuple-element.9), channel_id=1, source_target_pairs={{0,30},{2,4},{4,2},{6,8},{8,6},{10,12},{12,10},{14,16},{16,14},{18... | collective-permute-start | bytes 196616 | tf_op jit(solution)/shard_map/ppermute | solution.py:78
  48.5 2.5 %collective-permute-start.11 = (f32[64,512]{1,0:T(8,128)S(1)}, f32[64,512]{1,0:T(8,128)S(1)}, u32[]{:S(2)}, u32[]{:S(2)}) collective-permute-start(f32[64,512]{1,0:T(8,128)S(1)} %convolution_add_fusion.3), channel_id=1, source_target_pairs={{0,16},{2,18},{4,20},{6,22},{8,24},{10,26},{12,28},{14,30},{16,0},... | collective-permute-start | bytes 393224 | tf_op jit(solution)/shard_map/ppermute | solution.py:75
  51.0 6.7 %collective-permute-done.6 = f32[64,512]{1,0:T(8,128)S(1)} collective-permute-done((f32[64,512]{1,0:T(8,128)S(1)}, f32[64,512]{1,0:T(8,128)S(1)}, u32[]{:S(2)}, u32[]{:S(2)}) %collective-permute-start.6) | collective-permute-done | bytes 131104 | tf_op jit(solution)/shard_map/ppermute | solution.py:75
  59.2 3.5 %collective-permute-start.9 = (f32[32,512]{1,0:T(8,128)S(1)}, f32[32,512]{1,0:T(8,128)S(1)}, u32[]{:S(2)}, u32[]{:S(2)}) collective-permute-start(f32[32,512]{1,0:T(8,128)S(1)} %get-tuple-element.15), channel_id=1, source_target_pairs={{0,30},{2,4},{4,2},{6,8},{8,6},{10,12},{12,10},{14,16},{16,14},{18... | collective-permute-start | bytes 196616 | tf_op jit(solution)/shard_map/ppermute | solution.py:78
  63.7 1.9 %collective-permute-done.9 = f32[32,512]{1,0:T(8,128)S(1)} collective-permute-done((f32[32,512]{1,0:T(8,128)S(1)}, f32[32,512]{1,0:T(8,128)S(1)}, u32[]{:S(2)}, u32[]{:S(2)}) %collective-permute-start.9) | collective-permute-done | bytes 65568 | tf_op jit(solution)/shard_map/ppermute | solution.py:78
  66.2 3.5 %collective-permute-start.12 = (f32[32,512]{1,0:T(8,128)S(1)}, f32[32,512]{1,0:T(8,128)S(1)}, u32[]{:S(2)}, u32[]{:S(2)}) collective-permute-start(f32[32,512]{1,0:T(8,128)S(1)} %get-tuple-element.13), channel_id=1, source_target_pairs={{0,30},{2,4},{4,2},{6,8},{8,6},{10,12},{12,10},{14,16},{16,14},{18... | collective-permute-start | bytes 196616 | tf_op jit(solution)/shard_map/ppermute | solution.py:78
  70.5 2.3 %collective-permute-done.12 = f32[32,512]{1,0:T(8,128)S(1)} collective-permute-done((f32[32,512]{1,0:T(8,128)S(1)}, f32[32,512]{1,0:T(8,128)S(1)}, u32[]{:S(2)}, u32[]{:S(2)}) %collective-permute-start.12) | collective-permute-done | bytes 65568 | tf_op jit(solution)/shard_map/ppermute | solution.py:78
  73.3 4.0 %collective-permute-done.14 = f32[64,512]{1,0:T(8,128)S(1)} collective-permute-done((f32[64,512]{1,0:T(8,128)S(1)}, f32[64,512]{1,0:T(8,128)S(1)}, u32[]{:S(2)}, u32[]{:S(2)}) %collective-permute-start.14) | collective-permute-done | bytes 131104 | tf_op jit(solution)/shard_map/ppermute | solution.py:75
  77.3 1.2 %convolution_add_fusion = f32[512,256]{1,0:T(8,128)} fusion(f32[512,256]{1,0:T(8,128)S(1)} %convolution_add_fusion.1, f32[64,512]{1,0:T(8,128)S(1)} %collective-permute-done.14, f32[128,256]{1,0:T(8,128)S(1)} %copy-done.2), kind=kOutput, calls=%fused_computation.18 | convolution fusion | flops 50462720 | bytes 1245184 | tf_op jit(solution)/shard_map/dot_general | solution.py:11
  (82 shorter events, 13.5 us)
Async XLA Ops:
  0.0 11.9 %copy-start = (f32[16,125,125]{2,0,1:T(8,128)S(1)}, f32[16,125,125]{2,0,1:T(8,128)}, u32[]{:S(2)}) copy-start(f32[16,125,125]{2,0,1:T(8,128)} %param.7) | copy-start | bytes 3000004
  0.0 11.8 %copy-start.4 = (s32[16,125]{1,0:T(8,128)S(1)}, s32[16,125]{1,0:T(8,128)}, u32[]{:S(2)}) copy-start(s32[16,125]{1,0:T(8,128)} %param.8) | copy-start | bytes 24004
  1.8 22.2 %collective-permute-start = (f32[256,256]{1,0:T(8,128)}, f32[256,256]{1,0:T(8,128)}, u32[]{:S(2)}, u32[]{:S(2)}) collective-permute-start(f32[256,256]{1,0:T(8,128)} %slice.154), channel_id=1, source_target_pairs={{0,1},{1,0},{2,3},{3,2},{4,5},{5,4},{6,7},{7,6},{8,9},{9,8},{10,11... | collective-permute-start | bytes 786440 | tf_op jit(solution)/shard_map/ppermute | solution.py:51
  9.5 19.9 %collective-permute-start.1 = (f32[128,768]{1,0:T(8,128)S(1)}, f32[128,768]{1,0:T(8,128)}, u32[]{:S(2)}, u32[]{:S(2)}) collective-permute-start(f32[128,768]{1,0:T(8,128)S(1)} %get-tuple-element.8), channel_id=1, source_target_pairs={{0,1},{1,0},{2,3},{3,2},{4,5},{5,4},{6,7},{7,6},{8,9},{9,8},{10,11... | collective-permute-start | bytes 1179656 | tf_op jit(solution)/shard_map/ppermute | solution.py:51
  9.6 26.5 %collective-permute-start.2 = (f32[128,768]{1,0:T(8,128)S(1)}, f32[128,768]{1,0:T(8,128)}, u32[]{:S(2)}, u32[]{:S(2)}) collective-permute-start(f32[128,768]{1,0:T(8,128)S(1)} %get-tuple-element.7), channel_id=1, source_target_pairs={{0,1},{1,0},{2,3},{3,2},{4,5},{5,4},{6,7},{7,6},{8,9},{9,8},{10,11... | collective-permute-start | bytes 1179656 | tf_op jit(solution)/shard_map/ppermute | solution.py:51
  23.8 5.7 %copy-start.1 = (f32[512,2048]{1,0:T(8,128)S(1)}, f32[512,2048]{1,0:T(8,128)}, u32[]{:S(2)}) copy-start(f32[512,2048]{1,0:T(8,128)} %param.6) | copy-start | bytes 12582916
  26.8 4.9 %copy-start.3 = (f32[64,64]{1,0:T(8,128)S(1)}, f32[64,64]{1,0:T(8,128)}, u32[]{:S(2)}) copy-start(f32[64,64]{1,0:T(8,128)} %copy.11) | copy-start | bytes 49156
  31.8 9.5 %collective-permute-start.3 = (f32[64,640]{1,0:T(8,128)S(1)}, f32[64,640]{1,0:T(8,128)S(1)}, u32[]{:S(2)}, u32[]{:S(2)}) collective-permute-start(f32[64,640]{1,0:T(8,128)S(1)} %pad_maximum_fusion.5), channel_id=1, source_target_pairs={{0,16},{2,18},{4,20},{6,22},{8,24},{10,26},{12,28},{14,30},{16,0},... | collective-permute-start | bytes 491528 | tf_op jit(solution)/shard_map/ppermute | solution.py:75
  34.4 6.9 %collective-permute-start.4 = (f32[32,512]{1,0:T(8,128)S(1)}, f32[32,512]{1,0:T(8,128)S(1)}, u32[]{:S(2)}, u32[]{:S(2)}) collective-permute-start(f32[32,512]{1,0:T(8,128)S(1)} %get-tuple-element.12), channel_id=1, source_target_pairs={{0,30},{2,4},{4,2},{6,8},{8,6},{10,12},{12,10},{14,16},{16,14},{18... | collective-permute-start | bytes 196616 | tf_op jit(solution)/shard_map/ppermute | solution.py:78
  35.1 6.3 %collective-permute-start.5 = (f32[32,512]{1,0:T(8,128)S(1)}, f32[32,512]{1,0:T(8,128)S(1)}, u32[]{:S(2)}, u32[]{:S(2)}) collective-permute-start(f32[32,512]{1,0:T(8,128)S(1)} %get-tuple-element.11), channel_id=1, source_target_pairs={{0,2},{2,0},{4,6},{6,4},{8,10},{10,8},{12,14},{14,12},{16,18},{18,... | collective-permute-start | bytes 196616 | tf_op jit(solution)/shard_map/ppermute | solution.py:79
  41.9 6.5 %collective-permute-start.7 = (f32[32,512]{1,0:T(8,128)S(1)}, f32[32,512]{1,0:T(8,128)S(1)}, u32[]{:S(2)}, u32[]{:S(2)}) collective-permute-start(f32[32,512]{1,0:T(8,128)S(1)} %get-tuple-element.9), channel_id=1, source_target_pairs={{0,30},{2,4},{4,2},{6,8},{8,6},{10,12},{12,10},{14,16},{16,14},{18... | collective-permute-start | bytes 196616 | tf_op jit(solution)/shard_map/ppermute | solution.py:78
  45.9 2.5 %collective-permute-start.8 = (f32[32,512]{1,0:T(8,128)S(1)}, f32[32,512]{1,0:T(8,128)S(1)}, u32[]{:S(2)}, u32[]{:S(2)}) collective-permute-start(f32[32,512]{1,0:T(8,128)S(1)} %get-tuple-element.10), channel_id=1, source_target_pairs={{0,2},{2,0},{4,6},{6,4},{8,10},{10,8},{12,14},{14,12},{16,18},{18,... | collective-permute-start | bytes 196616 | tf_op jit(solution)/shard_map/ppermute | solution.py:79
  46.5 12.3 %copy-start.5 = (f32[64,128]{1,0:T(8,128)S(1)}, f32[64,128]{1,0:T(8,128)}, u32[]{:S(2)}) copy-start(f32[64,128]{1,0:T(8,128)} %convolution_multiply_fusion.2) | copy-start | bytes 98308
  47.0 10.8 %collective-permute-start.6 = (f32[64,512]{1,0:T(8,128)S(1)}, f32[64,512]{1,0:T(8,128)S(1)}, u32[]{:S(2)}, u32[]{:S(2)}) collective-permute-start(f32[64,512]{1,0:T(8,128)S(1)} %slice.206), channel_id=1, source_target_pairs={{0,16},{2,18},{4,20},{6,22},{8,24},{10,26},{12,28},{14,30},{16,0},... | collective-permute-start | bytes 393224 | tf_op jit(solution)/shard_map/ppermute | solution.py:75
  48.5 14.4 %collective-permute-start.11 = (f32[64,512]{1,0:T(8,128)S(1)}, f32[64,512]{1,0:T(8,128)S(1)}, u32[]{:S(2)}, u32[]{:S(2)}) collective-permute-start(f32[64,512]{1,0:T(8,128)S(1)} %convolution_add_fusion.3), channel_id=1, source_target_pairs={{0,16},{2,18},{4,20},{6,22},{8,24},{10,26},{12,28},{14,30},{16,0},... | collective-permute-start | bytes 393224 | tf_op jit(solution)/shard_map/ppermute | solution.py:75
  59.1 4.6 %collective-permute-start.10 = (f32[32,512]{1,0:T(8,128)S(1)}, f32[32,512]{1,0:T(8,128)S(1)}, u32[]{:S(2)}, u32[]{:S(2)}) collective-permute-start(f32[32,512]{1,0:T(8,128)S(1)} %get-tuple-element.16), channel_id=1, source_target_pairs={{0,2},{2,0},{4,6},{6,4},{8,10},{10,8},{12,14},{14,12},{16,18},{18,... | collective-permute-start | bytes 196616 | tf_op jit(solution)/shard_map/ppermute | solution.py:79
  59.2 6.4 %collective-permute-start.9 = (f32[32,512]{1,0:T(8,128)S(1)}, f32[32,512]{1,0:T(8,128)S(1)}, u32[]{:S(2)}, u32[]{:S(2)}) collective-permute-start(f32[32,512]{1,0:T(8,128)S(1)} %get-tuple-element.15), channel_id=1, source_target_pairs={{0,30},{2,4},{4,2},{6,8},{8,6},{10,12},{12,10},{14,16},{16,14},{18... | collective-permute-start | bytes 196616 | tf_op jit(solution)/shard_map/ppermute | solution.py:78
  63.7 13.5 %copy-start.2 = (f32[128,256]{1,0:T(8,128)S(1)}, f32[128,256]{1,0:T(8,128)}, u32[]{:S(2)}) copy-start(f32[128,256]{1,0:T(8,128)} %get-tuple-element.21) | copy-start | bytes 393220
  66.2 6.6 %collective-permute-start.12 = (f32[32,512]{1,0:T(8,128)S(1)}, f32[32,512]{1,0:T(8,128)S(1)}, u32[]{:S(2)}, u32[]{:S(2)}) collective-permute-start(f32[32,512]{1,0:T(8,128)S(1)} %get-tuple-element.13), channel_id=1, source_target_pairs={{0,30},{2,4},{4,2},{6,8},{8,6},{10,12},{12,10},{14,16},{16,14},{18... | collective-permute-start | bytes 196616 | tf_op jit(solution)/shard_map/ppermute | solution.py:78
  69.8 3.0 %collective-permute-start.13 = (f32[32,512]{1,0:T(8,128)S(1)}, f32[32,512]{1,0:T(8,128)S(1)}, u32[]{:S(2)}, u32[]{:S(2)}) collective-permute-start(f32[32,512]{1,0:T(8,128)S(1)} %get-tuple-element.14), channel_id=1, source_target_pairs={{0,2},{2,0},{4,6},{6,4},{8,10},{10,8},{12,14},{14,12},{16,18},{18,... | collective-permute-start | bytes 196616 | tf_op jit(solution)/shard_map/ppermute | solution.py:79
  70.4 6.9 %collective-permute-start.14 = (f32[64,512]{1,0:T(8,128)S(1)}, f32[64,512]{1,0:T(8,128)S(1)}, u32[]{:S(2)}, u32[]{:S(2)}) collective-permute-start(f32[64,512]{1,0:T(8,128)S(1)} %get-tuple-element.5), channel_id=1, source_target_pairs={{0,16},{2,18},{4,20},{6,22},{8,24},{10,26},{12,28},{14,30},{16,0},... | collective-permute-start | bytes 393224 | tf_op jit(solution)/shard_map/ppermute | solution.py:75

commit v3 on v1

v3 whole, which is shorter than its diff:
```python
import jax
import jax.numpy as jnp
from jax import lax
from jax.experimental import pallas as pl
from jax.experimental.pallas import tpu as pltpu
from jax.sharding import PartitionSpec as P

F32 = jnp.float32
BF16 = jnp.bfloat16
I32 = jnp.int32
NN = ((1,), (0,))
NT = ((1,), (1,))

HALF = 1.5
CENTRE = 2.5
SIGMA_ONE = HALF / (-1.0 - CENTRE)
SIGMA_TWO = 1.0 / (2.0 / SIGMA_ONE - SIGMA_ONE)
SCALE_ONE = SIGMA_ONE / HALF
SCALE_TWO = 2.0 * SIGMA_TWO / HALF


def dot(a, b, dims=NN):
    return lax.dot_general(a, b, (dims, ((), ())), preferred_element_type=F32)


def split(x):
    top = x.astype(BF16)
    return top, (x - top.astype(F32)).astype(BF16)


def mul(a, b, dims=NN):
    return dot(a[0], b[0], dims) + (dot(a[0], b[1], dims) + dot(a[1], b[0], dims))


def sift(a, x):
    top, low = split(x)
    return dot(a, top) + dot(a, low)


def call(body, outs, *args, **rest):
    return pl.pallas_call(
        body,
        out_shape=[jax.ShapeDtypeStruct(*out) for out in outs],
        compiler_params=pltpu.CompilerParams(vmem_limit_bytes=16 << 20),
        cost_estimate=pl.CostEstimate(flops=1000, bytes_accessed=1000, transcendentals=0),
        **rest,
    )(*args)


def column(row, width):
    down = lax.broadcasted_iota(I32, (width, width), 0)
    along = lax.broadcasted_iota(I32, (width, width), 1)
    return jnp.sum(jnp.where(down == along, row, 0), axis=1, keepdims=True)


def renumber(lists, subspace, turned_edge, turned_rest, shuffle_out, origin_out):
    slots, halo = lists.shape[1:]
    nodes = subspace.shape[1]
    edge_nodes = slots * halo
    ids = lax.broadcasted_iota(I32, (halo, nodes), 1)
    seen = jnp.zeros((halo, nodes), F32)
    for slot in range(slots):
        sent = column(lists[0, slot : slot + 1, :], halo)
        seen = jnp.maximum(seen, jnp.where(sent == ids, 1.0, 0.0))
    edge = jnp.max(seen, axis=0, keepdims=True)
    down = lax.broadcasted_iota(I32, (nodes, nodes), 0)
    along = lax.broadcasted_iota(I32, (nodes, nodes), 1)
    upto = jnp.where(down <= along, 1.0, 0.0).astype(BF16)
    count = dot(jnp.broadcast_to(edge, (8, nodes)).astype(BF16), upto)[:1].astype(I32)
    total = jnp.sum(edge, axis=1, keepdims=True).astype(I32)
    place = jnp.where(edge > 0.5, count - 1, total + along[:1] - count)
    match = place == down
    shuffle = jnp.where(match, 1.0, 0.0).astype(BF16)
    shuffle_out[...] = shuffle
    origin_out[...] = jnp.sum(jnp.where(match, along, 0), axis=1, keepdims=True)
    top, low = split(subspace[...])
    turned = dot(shuffle, top, NT) + dot(shuffle, low, NT)
    turned_edge[...] = turned[:edge_nodes]
    turned_rest[...] = turned[edge_nodes:]


def assemble(
    odd, lists, connect, element_ham, shuffle, origin, top_out, low_out, pick_out, both_out, hits_out, pair_out
):
    elems, size = connect.shape
    slots, halo = lists.shape[1:]
    nodes = origin.shape[0]
    wide = slots * halo
    duo = 2 * halo
    swap = odd[0] == 1
    columns = [column(lists[0, slot : slot + 1, :], halo) for slot in range(slots)]
    outer = jnp.where(swap, columns[0], columns[1])
    inner = jnp.where(swap, columns[1], columns[0])
    sent = jnp.concatenate([columns[2], columns[3], outer, inner], 0)
    hits = jnp.where(sent == lax.broadcasted_iota(I32, (wide, nodes), 1), 1.0, 0.0).astype(BF16)
    hits_out[...] = hits
    pick = dot(hits, shuffle[:wide, :], NT).astype(BF16)
    pick_out[...] = pick
    both = dot(pick, pick, NT)
    both_out[...] = both.astype(BF16)

    lane = lax.broadcasted_iota(I32, (halo, 1), 0)
    flag = odd[0]
    ghost = jnp.concatenate(
        [3 * halo + lane, 2 * halo + lane, (1 - flag) * halo + lane, flag * halo + lane], 0
    )
    numbers = jnp.concatenate([origin[...], nodes + ghost], 0)
    ham = jnp.zeros((nodes + wide, nodes + wide), F32)
    for elem in range(elems):
        spread = jnp.where(numbers == connect[elem : elem + 1, :], 1.0, 0.0).astype(BF16)
        top, low = split(element_ham[elem])
        rows = dot(top, spread, NT) + dot(low, spread, NT)
        ham = ham + sift(spread, rows)
    top, low = split(ham)
    top_out[...] = top
    low_out[...] = low
    far = slice(nodes, nodes + duo)
    pair_out[...] = jnp.concatenate([both[:duo, :duo], ham[far, far]], 1)


def rotate_own(group, turned_edge, turned_rest, ritz, start_out, top_out, low_out):
    step = pl.program_id(0)
    top, low = split(ritz[...])

    @pl.when(step == 0)
    def _():
        edge_nodes = turned_edge.shape[0]
        start_out[:edge_nodes, :] = mul(split(turned_edge[...]), (top, low), NT)
        start_out[edge_nodes:, :] = mul(split(turned_rest[...]), (top, low), NT)

    @pl.when(step > 0)
    def _():
        top_out[...] = top.T
        low_out[...] = low.T


def rotate_edge(rows, start_own, top, low, pick, pair, start_out, far_out, out_out, near_out):
    edge_nodes = rows.shape[0]
    wide, block = pick.shape[0], start_own.shape[1]
    quarter = wide // 4
    start = start_own[:edge_nodes, :] + mul(split(rows[...]), (top[...], low[...]))
    start_out[...] = start
    packed = sift(pick[...], start)
    far_out[:, :block] = packed[: 2 * quarter]
    far_out[:, block:] = pair[...]
    out_out[...] = packed[2 * quarter : 3 * quarter]
    near_out[...] = packed[3 * quarter :]


def rotate_rest(
    rows, start_own, start_edge, top, low, far_in, out_in, near_in, ham_top, ham_low,
    ext_out, far_out, out_out, near_out,
):
    edge_nodes, block = start_edge.shape
    nodes = start_own.shape[0]
    halo = out_in.shape[0]
    rest = start_own[edge_nodes:, :] + mul(split(rows[...]), (top[...], low[...]))
    ext = jnp.concatenate(
        [start_edge[...], rest, far_in[:, :block], out_in[...], near_in[...]], 0
    )
    ext_out[...] = ext
    back = mul((ham_top[nodes:, :], ham_low[nodes:, :]), split(ext))
    far_out[...] = back[: 2 * halo]
    out_out[...] = back[2 * halo : 3 * halo]
    near_out[...] = back[3 * halo :]


def first_base(ext, ham_top, ham_low, pick, far_in, back_far, base_out, packed_out, adjust_out):
    nodes = ham_top.shape[0] - pick.shape[0]
    edge_nodes = pick.shape[1]
    block = ext.shape[1]
    duo = far_in.shape[0]
    own = (ham_top[:nodes, :], ham_low[:nodes, :])
    base = SCALE_ONE * (mul(own, split(ext[...])) - CENTRE * ext[:nodes, :])
    base_out[...] = base
    packed_out[...] = sift(pick[...], base[:edge_nodes])
    overlap = far_in[:, block : block + duo].astype(BF16)
    adjust_out[...] = SCALE_ONE * sift(overlap, back_far[...])


def fetch_far(packed, both, out_in, near_in, far_out):
    duo = 2 * out_in.shape[0]
    back = jnp.concatenate([out_in[...], near_in[...]], 0)
    far_out[...] = packed[:duo, :] + SCALE_ONE * sift(both[:duo, duo:], back)


def fetch_ring(packed, both, far_in, out_in, near_in, out_out, near_out):
    halo = out_in.shape[0]
    back = jnp.concatenate([far_in[...], out_in[...], near_in[...]], 0)
    rows = packed[2 * halo :, :] + SCALE_ONE * sift(both[2 * halo :, :], back)
    out_out[...] = rows[:halo]
    near_out[...] = rows[halo:]


def first_own(
    base, pick, far_in, out_in, near_in, ham_top, ham_low, pair_in, first_out, part_out, known_out
):
    edge_nodes = pick.shape[1]
    nodes = base.shape[0]
    block = base.shape[1]
    duo = far_in.shape[0]
    back = jnp.concatenate([far_in[...], out_in[...], near_in[...]], 0)
    edge = base[:edge_nodes, :] + SCALE_ONE * sift(pick[...].T, back)
    first = jnp.concatenate([edge, base[edge_nodes:, :]], 0)
    first_out[...] = first
    part_out[...] = mul((ham_top[:, :nodes], ham_low[:, :nodes]), split(first))
    couple = split(pair_in[:, block + duo :])
    known_out[...] = mul(couple, split(sift(pick[:duo, :], edge)))


def return_far(part, ham_top, ham_low, out_in, near_in, far_out):
    halo = out_in.shape[0]
    nodes = part.shape[0] - 4 * halo
    far = slice(nodes, nodes + 2 * halo)
    ring = slice(nodes + 2 * halo, nodes + 4 * halo)
    ghosts = split(jnp.concatenate([out_in[...], near_in[...]], 0))
    far_out[...] = part[far, :] + mul((ham_top[far, ring], ham_low[far, ring]), ghosts)


def return_ring(
    part, ham_top, ham_low, far_in, adjust, out_in, near_in, ghosts_out, out_out, near_out
):
    halo = out_in.shape[0]
    nodes = part.shape[0] - 4 * halo
    ring = slice(nodes + 2 * halo, nodes + 4 * halo)
    ghosts = jnp.concatenate([far_in[...] + adjust[...], out_in[...], near_in[...]], 0)
    ghosts_out[...] = ghosts
    rows = part[ring, :] + mul((ham_top[ring, nodes:], ham_low[ring, nodes:]), split(ghosts))
    out_out[...] = rows[:halo]
    near_out[...] = rows[halo:]


def second_base(part, ghosts, ham_top, ham_low, first, ext, known, shuffle, hits, result_out):
    nodes = first.shape[0]
    duo = known.shape[0]
    ham = (ham_top[:nodes, nodes:], ham_low[:nodes, nodes:])
    second = part[:nodes, :] + mul(ham, split(ghosts[...])) - CENTRE * first[...]
    second = SCALE_TWO * second - SIGMA_ONE * SIGMA_TWO * ext[:nodes, :]
    top, low = split(second.T)
    result = dot(top, shuffle[...]) + dot(low, shuffle[...])
    top, low = split(SCALE_TWO * known[...].T)
    result_out[...] = result + (dot(top, hits[:duo, :]) + dot(low, hits[:duo, :]))


def finish(result, hits, far_in, out_in, near_in, out):
    back = jnp.concatenate([far_in[...], out_in[...], near_in[...]], 0)
    top, low = split(SCALE_TWO * back.T)
    out[...] = result[...] + (dot(top, hits[...]) + dot(low, hits[...]))


def per_device(subspace, ritz, element_ham, connect, send_rows):
    depth, nodes = subspace.shape
    block = ritz.shape[0]
    slots, halo = send_rows.shape[1:]
    partitions = lax.axis_size("mesh")
    groups = lax.axis_size("state")
    across = partitions // 2
    wide = slots * halo
    duo = 2 * halo
    full = nodes + wide

    odd = (lax.axis_index("mesh") % 2).astype(I32).reshape(1)
    group = lax.axis_index("state").astype(I32).reshape(1)
    pairs_far = [(i, (i + across) % partitions) for i in range(partitions)]
    pairs_in = [(i, i ^ 1) for i in range(partitions)]
    pairs_out = [
        (i, (i + 1) % partitions if i % 2 else (i - 1) % partitions) for i in range(partitions)
    ]

    def far(rows):
        return lax.ppermute(rows, "mesh", pairs_far)

    def out(rows):
        return lax.ppermute(rows, "mesh", pairs_out)

    def near(rows):
        return lax.ppermute(rows, "mesh", pairs_in)

    def gather(rows):
        parts = [
            lax.ppermute(rows, "state", [(i, (i + step) % groups) for i in range(groups)])
            for step in range(1, groups)
        ]
        return parts[0] if len(parts) == 1 else jnp.concatenate(parts, 1)

    def rows_of(count):
        return ((count, block), F32)

    halo_out = [rows_of(duo), rows_of(halo), rows_of(halo)]
    smem = pl.BlockSpec(memory_space=pltpu.SMEM)
    vmem = pl.BlockSpec(memory_space=pltpu.VMEM)

    turned_edge, turned_rest, shuffle, origin = call(
        renumber,
        [((wide, depth), F32), ((nodes - wide, depth), F32), ((nodes, nodes), BF16), ((nodes, 1), I32)],
        send_rows,
        subspace,
    )
    edge_in = gather(turned_edge)
    rest_in = gather(turned_rest)
    ham_top, ham_low, pick, both, hits, pair = call(
        assemble,
        [
            ((full, full), BF16),
            ((full, full), BF16),
            ((wide, wide), BF16),
            ((wide, wide), BF16),
            ((wide, nodes), BF16),
            ((duo, 2 * duo), F32),
        ],
        odd,
        send_rows,
        connect,
        element_ham,
        shuffle,
        origin,
        in_specs=[smem] + [vmem] * 5,
    )
    others = groups - 1
    start_own, ritz_top, ritz_low = pl.pallas_call(
        rotate_own,
        out_shape=[
            jax.ShapeDtypeStruct((nodes, block), F32),
            jax.ShapeDtypeStruct((others * depth, block), BF16),
            jax.ShapeDtypeStruct((others * depth, block), BF16),
        ],
        grid_spec=pltpu.PrefetchScalarGridSpec(
            num_scalar_prefetch=1,
            grid=(groups,),
            in_specs=[
                pl.BlockSpec((wide, depth), lambda i, g: (0, 0)),
                pl.BlockSpec((nodes - wide, depth), lambda i, g: (0, 0)),
                pl.BlockSpec((block, depth), lambda i, g: (0, lax.rem(g[0] + groups - i, groups))),
            ],
            out_specs=[
                pl.BlockSpec((nodes, block), lambda i, g: (0, 0)),
                pl.BlockSpec((depth, block), lambda i, g: (jnp.maximum(i - 1, 0), 0)),
                pl.BlockSpec((depth, block), lambda i, g: (jnp.maximum(i - 1, 0), 0)),
            ],
        ),
        compiler_params=pltpu.CompilerParams(vmem_limit_bytes=32 << 20),
        cost_estimate=pl.CostEstimate(flops=1000, bytes_accessed=1000, transcendentals=0),
    )(group, turned_edge, turned_rest, ritz)

    start_edge, far_rows, out_rows, near_rows = call(
        rotate_edge,
        [rows_of(wide), ((duo, block + 2 * duo), F32), rows_of(halo), rows_of(halo)],
        edge_in, start_own, ritz_top, ritz_low, pick, pair,
    )
    pair_in, out_in, near_in = far(far_rows), out(out_rows), near(near_rows)

    ext, back_far, back_out, back_near = call(
        rotate_rest,
        [rows_of(full)] + halo_out,
        rest_in, start_own, start_edge, ritz_top, ritz_low, pair_in, out_in, near_in, ham_top, ham_low,
    )
    far_in, out_in, near_in = far(back_far), out(back_out), near(back_near)
    base, packed, adjust = call(
        first_base,
        [rows_of(nodes), rows_of(wide), rows_of(duo)],
        ext, ham_top, ham_low, pick, pair_in, back_far,
    )
    (far_rows,) = call(fetch_far, [rows_of(duo)], packed, both, out_in, near_in)
    fetched_far = far(far_rows)
    out_rows, near_rows = call(
        fetch_ring, halo_out[1:], packed, both, far_in, out_in, near_in
    )
    fetched_out, fetched_near = out(out_rows), near(near_rows)
    first, part, known = call(
        first_own,
        [rows_of(nodes), rows_of(full), rows_of(duo)],
        base, pick, far_in, out_in, near_in, ham_top, ham_low, pair_in,
    )

    (far_rows,) = call(
        return_far, [rows_of(duo)], part, ham_top, ham_low, fetched_out, fetched_near
    )
    returned_far = far(far_rows)
    ghosts, out_rows, near_rows = call(
        return_ring,
        [rows_of(wide)] + halo_out[1:],
        part, ham_top, ham_low, fetched_far, adjust, fetched_out, fetched_near,
    )
    returned_out, returned_near = out(out_rows), near(near_rows)
    (result,) = call(
        second_base,
        [((block, nodes), F32)],
        part, ghosts, ham_top, ham_low, first, ext, known, shuffle, hits,
    )
    (result,) = call(
        finish, [((block, nodes), F32)], result, hits, returned_far, returned_out, returned_near
    )
    return result


def solution(mesh):
    in_specs = (
        P("state", "mesh"),
        P("state", None),
        P("mesh", None, None),
        P("mesh", None),
        P("mesh", None, None),
    )
    out_specs = P("state", "mesh")
    return jax.shard_map(
        per_device, mesh=mesh, in_specs=in_specs, out_specs=out_specs, check_vma=False
    )
```

time: 65.4 us -> 65.3 us (level)
  Pallas kernels: 0 us -> 21 us
  matrix products: 19.8 us -> 0 us
  local copies, waits for them, and re-layouts: 4.53 us -> 7.48 us
  other arithmetic: 2.68 us -> 0 us
  waiting for transfers between devices: 21 us -> 18.6 us
  starting transfers between devices: 16.7 us -> 17.6 us
    pallas_call x0 -> x13, Pallas kernels: none -> 21 us  [the longest x12 16 us: call(): pl.pallas_call(body, out_shape=[jax.ShapeDtypeStruct(*out) for out in out...]
    dot_general x18 -> x0, matrix products: 19.8 us -> none  [the longest x17 17.1 us: mm(): lax.dot_general(a, b, (dims, ((), ())), precision=HIGH, preferred_element...]
    unnamed x14 -> x17, local copies, waits for them, and re-layouts: 0.06 us -> 7.48 us
    reshape x1 -> x0, local copies, waits for them, and re-layouts: 3.21 us -> none  [per_device(): ham = mm(spread, blocks.reshape(elems * size, nodes + wide), ((0,), (0,)))]
    ppermute x14, waiting for transfers between devices: 21 us -> 18.6 us  [the longest x4 17.7 us: out(): return lax.ppermute(rows, 'mesh', pairs_out)]
    slice x11 -> x0, local copies, waits for them, and re-layouts: 1.14 us -> none  [the longest x1 1.04 us: per_device(): other_rows = turned[half_nodes:]]
    squeeze x1 -> x0, other arithmetic: 0.88 us -> none  [per_device(): sent = jnp.concatenate([lists[2], lists[3], outer, inner])]
    ppermute x14, starting transfers between devices: 16.7 us -> 17.6 us  [the longest x4 9.27 us: far(): return lax.ppermute(rows, 'mesh', pairs_far)]
  transfers between devices with their start and end apart: 14 -> 14, of which waited for: 7 -> 6; matrix products, arithmetic and copies ran while one was open for 30% -> 2% of each run, Pallas kernels for 0% -> 25%
where the time goes in v3:
time: 65.3 us; the launch traced here: 64.9 us
  Pallas kernels  21 us (32%)
  waiting for transfers between devices  18.6 us (28%)
  starting transfers between devices  17.6 us (27%)
  local copies, waits for them, and re-layouts  7.48 us (11%)
    ppermute x4, waiting for transfers between devices, out(): return lax.ppermute(rows, 'mesh', pairs_out)  17.7 us
    pallas_call x12, Pallas kernels, call(): pl.pallas_call(body, out_shape=[jax.ShapeDtypeStruct(*out) for out in out...  16 us
    ppermute x4, starting transfers between devices, far(): return lax.ppermute(rows, 'mesh', pairs_far)  9.27 us
    unnamed x17, local copies, waits for them, and re-layouts  7.48 us
    pallas_call x1, Pallas kernels, per_device(): pl.pallas_call(rotate_own, out_shape=[jax.ShapeDtypeStruct((nodes, block)...  4.97 us
    ppermute x4, starting transfers between devices, out(): return lax.ppermute(rows, 'mesh', pairs_out)  4.51 us
    ppermute x2, starting transfers between devices, gather(): lax.ppermute(rows, 'state', [(i, (i + step) % groups) for i in range(grou...  3 us
  transfers between devices with their start and end apart: 14, of which 6 were waited for; matrix products, arithmetic and copies ran while one was open for 2% of the time, Pallas kernels for 25%

profile of v3, /device:TPU:0, one launch (start us, length us, event | category | flops | bytes accessed | tf_op | source)
XLA Modules:
  0.0 64.9 jit_solution(3682980378336660664)
XLA Ops:
  0.0 1.2 %copy-done.4 = f32[1024,256]{1,0:T(8,128)S(1)} copy-done((f32[1024,256]{1,0:T(8,128)S(1)}, f32[1024,256]{1,0:T(8,128)}, u32[]{:S(2)}) %copy-start.4) | copy-done | bytes 1048600
  1.9 1.7 %shard_map.55 = (f32[128,1024]{1,0:T(8,128)}, f32[128,1024]{1,0:T(8,128)}, bf16[256,256]{1,0:T(8,128)(2,1)S(1)}, s32[256,1]{1,0:T(8,128)S(1)}) custom-call(s32[1,4,32]{2,1,0:T(4,128)S(1)} %copy-done.6, f32[1024,256]{1,0:T(8,128)S(1)} %copy-done.4), custom_call_target="tpu_custom_call" | custom-call | flops 1000 | bytes 1000 | tf_op jit(solution)/shard_map/pallas_call | solution.py:41
  3.6 3.0 %collective-permute-start.1 = (f32[128,1024]{1,0:T(8,128)}, f32[128,1024]{1,0:T(8,128)}, u32[]{:S(2)}, u32[]{:S(2)}) collective-permute-start(f32[128,1024]{1,0:T(8,128)} %get-tuple-element.38.turned_edge), channel_id=1, source_target_pairs={{0,1},{1,0},{2,3},{3,2},{4,5},{5,4},{6,7},{7,6},{8,9},{9,8},{10,11... | collective-permute-start | bytes 1572872 | tf_op jit(solution)/shard_map/ppermute | solution.py:281
  6.6 2.2 %copy-done = f32[512,2048]{1,0:T(8,128)S(1)} copy-done((f32[512,2048]{1,0:T(8,128)S(1)}, f32[512,2048]{1,0:T(8,128)}, u32[]{:S(2)}) %copy-start) | copy-done | bytes 4194328
  8.8 5.0 %shard_map.56 = (f32[256,512]{1,0:T(8,128)S(1)}, bf16[1024,512]{1,0:T(8,128)(2,1)S(1)}, bf16[1024,512]{1,0:T(8,128)(2,1)S(1)}) custom-call(s32[1]{0:T(128)} %bitcast.group, f32[128,1024]{1,0:T(8,128)} %get-tuple-element.38.turned_edge, f32[128,1024]{1,0:T(8,128)} %get-tuple-element.37.turned_rest, f32[512,2048]{1,0:T(8,128)S(1)} %copy-done), custom_call_target="tpu_custom_call" | custom-call | flops 1000 | bytes 1000 | tf_op jit(solution)/shard_map/pallas_call | solution.py:320
  14.5 1.5 %copy.6.element_ham = f32[16,125,125]{2,1,0:T(8,128)S(1)} copy(f32[16,125,125]{2,0,1:T(8,128)} %param.7) | data formatting | bytes 2000000 | tf_op args[2]
  16.1 6.0 %shard_map.57 = (bf16[384,384]{1,0:T(8,128)(2,1)S(1)}, bf16[384,384]{1,0:T(8,128)(2,1)S(1)}, bf16[128,128]{1,0:T(8,128)(2,1)S(1)}, bf16[128,128]{1,0:T(8,128)(2,...) custom-call(s32[1]{0:T(128)} %bitcast.1.odd, s32[1,4,32]{2,1,0:T(4,128)S(1)} %copy-done.7, ...), custom_call_target="tpu_custom_call" | custom-call | flops 1000 | bytes 1000 | tf_op jit(solution)/shard_map/pallas_call | solution.py:41
  22.2 1.0 %copy-done.2 = f32[256,512]{1,0:T(8,128)S(1)} copy-done((f32[256,512]{1,0:T(8,128)S(1)}, f32[256,512]{1,0:T(8,128)}, u32[]{:S(2)}) %copy-start.2) | copy-done | bytes 524312
  23.2 1.8 %shard_map.58 = (f32[128,512]{1,0:T(8,128)S(1)}, f32[64,640]{1,0:T(8,128)S(1)}, f32[32,512]{1,0:T(8,128)S(1)}, f32[32,512]{1,0:T(8,128)S(1)}) custom-call(f32[128,1024]{1,0:T(8,128)} %collective-permute-done.1.rows, f32[256,512]{1,0:T(8,128)S(1)} %copy-done.2, bf16[1024,512]{1,0:T(8,128)(2,1)S(1)} %get-tuple-element.40.top, ...), custom_call_target="tpu_custom_call" | custom-call | flops 1000 | bytes 1000 | tf_op jit(solution)/shard_map/pallas_call | solution.py:41
  25.1 3.1 %collective-permute-start.2 = (f32[64,640]{1,0:T(8,128)S(1)}, f32[64,640]{1,0:T(8,128)S(1)}, u32[]{:S(2)}, u32[]{:S(2)}) collective-permute-start(f32[64,640]{1,0:T(8,128)S(1)} %get-tuple-element.47), channel_id=1, source_target_pairs={{0,16},{2,18},{4,20},{6,22},{8,24},{10,26},{12,28},{14,30},{16,0},... | collective-permute-start | bytes 491528 | tf_op jit(solution)/shard_map/ppermute | solution.py:271
  28.2 0.9 %collective-permute-start.3 = (f32[32,512]{1,0:T(8,128)S(1)}, f32[32,512]{1,0:T(8,128)S(1)}, u32[]{:S(2)}, u32[]{:S(2)}) collective-permute-start(f32[32,512]{1,0:T(8,128)S(1)} %get-tuple-element.48), channel_id=1, source_target_pairs={{0,30},{2,4},{4,2},{6,8},{8,6},{10,12},{12,10},{14,16},{16,14},{18... | collective-permute-start | bytes 196616 | tf_op jit(solution)/shard_map/ppermute | solution.py:274
  30.0 4.6 %collective-permute-done.3.out_in = f32[32,512]{1,0:T(8,128)S(1)} collective-permute-done((f32[32,512]{1,0:T(8,128)S(1)}, f32[32,512]{1,0:T(8,128)S(1)}, u32[]{:S(2)}, u32[]{:S(2)}) %collective-permute-start.3) | collective-permute-done | bytes 65568 | tf_op jit(solution)/shard_map/ppermute | solution.py:274
  35.3 2.0 %shard_map.59 = (f32[384,512]{1,0:T(8,128)S(1)}, f32[64,512]{1,0:T(8,128)S(1)}, f32[32,512]{1,0:T(8,128)S(1)}, f32[32,512]{1,0:T(8,128)S(1)}) custom-call(f32[128,1024]{1,0:T(8,128)} %collective-permute-done.rows, f32[256,512]{1,0:T(8,128)S(1)} %copy-done.3, f32[128,512]{1,0:T(8,128)S(1)} %get-tuple-element.46.start_edge, ...), custom_call_target="tpu_custom_call" | custom-call | flops 1000 | bytes 1000 | tf_op jit(solution)/shard_map/pallas_call | solution.py:41
  37.3 4.3 %collective-permute-start.5 = (f32[64,512]{1,0:T(8,128)S(1)}, f32[64,512]{1,0:T(8,128)S(1)}, u32[]{:S(2)}, u32[]{:S(2)}) collective-permute-start(f32[64,512]{1,0:T(8,128)S(1)} %get-tuple-element.53.back_far), channel_id=1, source_target_pairs={{0,16},{2,18},{4,20},{6,22},{8,24},{10,26},{12,28},{14,30},{16,0},... | collective-permute-start | bytes 393224 | tf_op jit(solution)/shard_map/ppermute | solution.py:271
  41.7 0.8 %shard_map.60 = (f32[256,512]{1,0:T(8,128)S(1)}, f32[128,512]{1,0:T(8,128)S(1)}, f32[64,512]{1,0:T(8,128)S(1)}) custom-call(f32[384,512]{1,0:T(8,128)S(1)} %get-tuple-element.52.ext, bf16[384,384]{1,0:T(8,128)(2,1)S(1)} %get-tuple-element.50.ham_top, bf16[384,384]{1,0:T(8,128)(2,1)S(1)} %get-tuple-element.51.ham_low, ...), custom_call_target="tpu_custom_call" | custom-call | flops 1000 | bytes 1000 | tf_op jit(solution)/shard_map/pallas_call | solution.py:41
  42.5 5.6 %collective-permute-done.6.out_in = f32[32,512]{1,0:T(8,128)S(1)} collective-permute-done((f32[32,512]{1,0:T(8,128)S(1)}, f32[32,512]{1,0:T(8,128)S(1)}, u32[]{:S(2)}, u32[]{:S(2)}) %collective-permute-start.6) | collective-permute-done | bytes 65568 | tf_op jit(solution)/shard_map/ppermute | solution.py:274
  49.1 2.4 %collective-permute-start.9 = (f32[32,512]{1,0:T(8,128)S(1)}, f32[32,512]{1,0:T(8,128)S(1)}, u32[]{:S(2)}, u32[]{:S(2)}) collective-permute-start(f32[32,512]{1,0:T(8,128)S(1)} %get-tuple-element.61), channel_id=1, source_target_pairs={{0,30},{2,4},{4,2},{6,8},{8,6},{10,12},{12,10},{14,16},{16,14},{18... | collective-permute-start | bytes 196616 | tf_op jit(solution)/shard_map/ppermute | solution.py:274
  51.5 0.9 %shard_map.61 = (f32[256,512]{1,0:T(8,128)S(1)}, f32[384,512]{1,0:T(8,128)S(1)}, f32[64,512]{1,0:T(8,128)S(1)}) custom-call(f32[256,512]{1,0:T(8,128)S(1)} %get-tuple-element.54.base, bf16[128,128]{1,0:T(8,128)(2,1)S(1)} %get-tuple-element.44.pick, f32[64,512]{1,0:T(8,128)S(1)} %collective-permute-done.5.far_in, ...), custom_call_target="tpu_custom_call" | custom-call | flops 1000 | bytes 1000 | tf_op jit(solution)/shard_map/pallas_call | solution.py:41
  52.4 3.1 %collective-permute-done.9.out_in = f32[32,512]{1,0:T(8,128)S(1)} collective-permute-done((f32[32,512]{1,0:T(8,128)S(1)}, f32[32,512]{1,0:T(8,128)S(1)}, u32[]{:S(2)}, u32[]{:S(2)}) %collective-permute-start.9) | collective-permute-done | bytes 65568 | tf_op jit(solution)/shard_map/ppermute | solution.py:274
  55.8 1.3 %collective-permute-start.11 = (f32[64,512]{1,0:T(8,128)S(1)}, f32[64,512]{1,0:T(8,128)S(1)}, u32[]{:S(2)}, u32[]{:S(2)}) collective-permute-start(f32[64,512]{1,0:T(8,128)S(1)} %shard_map.66), channel_id=1, source_target_pairs={{0,16},{2,18},{4,20},{6,22},{8,24},{10,26},{12,28},{14,30},{16,0},... | collective-permute-start | bytes 393224 | tf_op jit(solution)/shard_map/ppermute | solution.py:271
  57.3 1.2 %collective-permute-start.12 = (f32[32,512]{1,0:T(8,128)S(1)}, f32[32,512]{1,0:T(8,128)S(1)}, u32[]{:S(2)}, u32[]{:S(2)}) collective-permute-start(f32[32,512]{1,0:T(8,128)S(1)} %get-tuple-element.67), channel_id=1, source_target_pairs={{0,30},{2,4},{4,2},{6,8},{8,6},{10,12},{12,10},{14,16},{16,14},{18... | collective-permute-start | bytes 196616 | tf_op jit(solution)/shard_map/ppermute | solution.py:274
  58.5 0.8 %shard_map.65.result = f32[512,256]{1,0:T(8,128)S(1)} custom-call(f32[384,512]{1,0:T(8,128)S(1)} %get-tuple-element.57.part, f32[128,512]{1,0:T(8,128)S(1)} %get-tuple-element.63.ghosts, bf16[384,384]{1,0:T(8,128)(2,1)S(1)} %get-tuple-element.50.ham_top, bf16[384,384]{1,0:T(8,128)(2,1)S(1)} %get-tuple-element.51.ham_low, ...), custom_call_target="tpu_custom_call" | custom-call | flops 1000 | bytes 1000 | tf_op jit(solution)/shard_map/pallas_call | solution.py:41
  59.3 4.4 %collective-permute-done.12.out_in = f32[32,512]{1,0:T(8,128)S(1)} collective-permute-done((f32[32,512]{1,0:T(8,128)S(1)}, f32[32,512]{1,0:T(8,128)S(1)}, u32[]{:S(2)}, u32[]{:S(2)}) %collective-permute-start.12) | collective-permute-done | bytes 65568 | tf_op jit(solution)/shard_map/ppermute | solution.py:274
  63.8 1.1 %shard_map.67 = f32[512,256]{1,0:T(8,128)} custom-call(f32[512,256]{1,0:T(8,128)S(1)} %shard_map.65.result, bf16[128,256]{1,0:T(8,128)(2,1)S(1)} %get-tuple-element.66.hits, f32[64,512]{1,0:T(8,128)S(1)} %collective-permute-done.11.far_in, f32[32,512]{1,0:T(8,128)S(1)} %collective-permute-done.12.out_in, f32[32,512]{1,0:T(8,128)S(1)} %collective-permute-done.13.near_in), custom_call_target="tpu_custom_call" | custom-call | flops 1000 | bytes 1000 | tf_op jit(solution)/shard_map/pallas_call | solution.py:41
  (34 shorter events, 4.7 us)
Async XLA Ops:
  0.0 1.2 %copy-start.4 = (f32[1024,256]{1,0:T(8,128)S(1)}, f32[1024,256]{1,0:T(8,128)}, u32[]{:S(2)}) copy-start(f32[1024,256]{1,0:T(8,128)} %subspace.1) | copy-start | bytes 3145732
  1.2 0.7 %copy-start.6 = (s32[1,4,32]{2,1,0:T(4,128)S(1)}, s32[1,4,32]{2,1,0:T(4,128)}, u32[]{:S(2)}) copy-start(s32[1,4,32]{2,1,0:T(4,128)} %lists.3) | copy-start | bytes 1540
  1.9 14.2 %copy-start.5 = (s32[16,125]{1,0:T(8,128)S(1)}, s32[16,125]{1,0:T(8,128)}, u32[]{:S(2)}) copy-start(s32[16,125]{1,0:T(8,128)} %connect.1) | copy-start | bytes 24004
  1.9 14.2 %copy-start.7 = (s32[1,4,32]{2,1,0:T(4,128)S(1)}, s32[1,4,32]{2,1,0:T(4,128)}, u32[]{:S(2)}) copy-start(s32[1,4,32]{2,1,0:T(4,128)} %lists.3) | copy-start | bytes 1540
  3.6 18.6 %collective-permute-start.1 = (f32[128,1024]{1,0:T(8,128)}, f32[128,1024]{1,0:T(8,128)}, u32[]{:S(2)}, u32[]{:S(2)}) collective-permute-start(f32[128,1024]{1,0:T(8,128)} %get-tuple-element.38.turned_edge), channel_id=1, source_target_pairs={{0,1},{1,0},{2,3},{3,2},{4,5},{5,4},{6,7},{7,6},{8,9},{9,8},{10,11... | collective-permute-start | bytes 1572872 | tf_op jit(solution)/shard_map/ppermute | solution.py:281
  6.5 23.5 %collective-permute-start = (f32[128,1024]{1,0:T(8,128)}, f32[128,1024]{1,0:T(8,128)}, u32[]{:S(2)}, u32[]{:S(2)}) collective-permute-start(f32[128,1024]{1,0:T(8,128)} %get-tuple-element.37.turned_rest), channel_id=1, source_target_pairs={{0,1},{1,0},{2,3},{3,2},{4,5},{5,4},{6,7},{7,6},{8,9},{9,8},{10,11... | collective-permute-start | bytes 1572872 | tf_op jit(solution)/shard_map/ppermute | solution.py:281
  6.6 2.2 %copy-start = (f32[512,2048]{1,0:T(8,128)S(1)}, f32[512,2048]{1,0:T(8,128)}, u32[]{:S(2)}) copy-start(f32[512,2048]{1,0:T(8,128)} %ritz.1) | copy-start | bytes 12582916
  13.7 0.8 %copy-start.1 = (f32[256,512]{1,0:T(8,128)}, f32[256,512]{1,0:T(8,128)S(1)}, u32[]{:S(2)}) copy-start(f32[256,512]{1,0:T(8,128)S(1)} %get-tuple-element.39.start_own) | copy-start | bytes 1572868
  16.1 19.2 %copy-start.3 = (f32[256,512]{1,0:T(8,128)S(1)}, f32[256,512]{1,0:T(8,128)}, u32[]{:S(2)}) copy-start(f32[256,512]{1,0:T(8,128)} %copy-done.1) | copy-start | bytes 1572868
  22.2 1.0 %copy-start.2 = (f32[256,512]{1,0:T(8,128)S(1)}, f32[256,512]{1,0:T(8,128)}, u32[]{:S(2)}) copy-start(f32[256,512]{1,0:T(8,128)} %copy-done.1) | copy-start | bytes 1572868
  25.1 10.3 %collective-permute-start.2 = (f32[64,640]{1,0:T(8,128)S(1)}, f32[64,640]{1,0:T(8,128)S(1)}, u32[]{:S(2)}, u32[]{:S(2)}) collective-permute-start(f32[64,640]{1,0:T(8,128)S(1)} %get-tuple-element.47), channel_id=1, source_target_pairs={{0,16},{2,18},{4,20},{6,22},{8,24},{10,26},{12,28},{14,30},{16,0},... | collective-permute-start | bytes 491528 | tf_op jit(solution)/shard_map/ppermute | solution.py:271
  28.2 6.4 %collective-permute-start.3 = (f32[32,512]{1,0:T(8,128)S(1)}, f32[32,512]{1,0:T(8,128)S(1)}, u32[]{:S(2)}, u32[]{:S(2)}) collective-permute-start(f32[32,512]{1,0:T(8,128)S(1)} %get-tuple-element.48), channel_id=1, source_target_pairs={{0,30},{2,4},{4,2},{6,8},{8,6},{10,12},{12,10},{14,16},{16,14},{18... | collective-permute-start | bytes 196616 | tf_op jit(solution)/shard_map/ppermute | solution.py:274
  29.1 5.5 %collective-permute-start.4 = (f32[32,512]{1,0:T(8,128)S(1)}, f32[32,512]{1,0:T(8,128)S(1)}, u32[]{:S(2)}, u32[]{:S(2)}) collective-permute-start(f32[32,512]{1,0:T(8,128)S(1)} %get-tuple-element.49), channel_id=1, source_target_pairs={{0,2},{2,0},{4,6},{6,4},{8,10},{10,8},{12,14},{14,12},{16,18},{18,... | collective-permute-start | bytes 196616 | tf_op jit(solution)/shard_map/ppermute | solution.py:277
  37.3 11.5 %collective-permute-start.5 = (f32[64,512]{1,0:T(8,128)S(1)}, f32[64,512]{1,0:T(8,128)S(1)}, u32[]{:S(2)}, u32[]{:S(2)}) collective-permute-start(f32[64,512]{1,0:T(8,128)S(1)} %get-tuple-element.53.back_far), channel_id=1, source_target_pairs={{0,16},{2,18},{4,20},{6,22},{8,24},{10,26},{12,28},{14,30},{16,0},... | collective-permute-start | bytes 393224 | tf_op jit(solution)/shard_map/ppermute | solution.py:271
  41.7 6.4 %collective-permute-start.6 = (f32[32,512]{1,0:T(8,128)S(1)}, f32[32,512]{1,0:T(8,128)S(1)}, u32[]{:S(2)}, u32[]{:S(2)}) collective-permute-start(f32[32,512]{1,0:T(8,128)S(1)} %get-tuple-element.55), channel_id=1, source_target_pairs={{0,30},{2,4},{4,2},{6,8},{8,6},{10,12},{12,10},{14,16},{16,14},{18... | collective-permute-start | bytes 196616 | tf_op jit(solution)/shard_map/ppermute | solution.py:274
  41.7 6.4 %collective-permute-start.7 = (f32[32,512]{1,0:T(8,128)S(1)}, f32[32,512]{1,0:T(8,128)S(1)}, u32[]{:S(2)}, u32[]{:S(2)}) collective-permute-start(f32[32,512]{1,0:T(8,128)S(1)} %get-tuple-element.56), channel_id=1, source_target_pairs={{0,2},{2,0},{4,6},{6,4},{8,10},{10,8},{12,14},{14,12},{16,18},{18,... | collective-permute-start | bytes 196616 | tf_op jit(solution)/shard_map/ppermute | solution.py:277
  48.3 8.8 %collective-permute-start.8 = (f32[64,512]{1,0:T(8,128)S(1)}, f32[64,512]{1,0:T(8,128)S(1)}, u32[]{:S(2)}, u32[]{:S(2)}) collective-permute-start(f32[64,512]{1,0:T(8,128)S(1)} %shard_map.62), channel_id=1, source_target_pairs={{0,16},{2,18},{4,20},{6,22},{8,24},{10,26},{12,28},{14,30},{16,0},... | collective-permute-start | bytes 393224 | tf_op jit(solution)/shard_map/ppermute | solution.py:271
  49.0 3.4 %collective-permute-start.10 = (f32[32,512]{1,0:T(8,128)S(1)}, f32[32,512]{1,0:T(8,128)S(1)}, u32[]{:S(2)}, u32[]{:S(2)}) collective-permute-start(f32[32,512]{1,0:T(8,128)S(1)} %get-tuple-element.62), channel_id=1, source_target_pairs={{0,2},{2,0},{4,6},{6,4},{8,10},{10,8},{12,14},{14,12},{16,18},{18,... | collective-permute-start | bytes 196616 | tf_op jit(solution)/shard_map/ppermute | solution.py:277
  49.1 6.5 %collective-permute-start.9 = (f32[32,512]{1,0:T(8,128)S(1)}, f32[32,512]{1,0:T(8,128)S(1)}, u32[]{:S(2)}, u32[]{:S(2)}) collective-permute-start(f32[32,512]{1,0:T(8,128)S(1)} %get-tuple-element.61), channel_id=1, source_target_pairs={{0,30},{2,4},{4,2},{6,8},{8,6},{10,12},{12,10},{14,16},{16,14},{18... | collective-permute-start | bytes 196616 | tf_op jit(solution)/shard_map/ppermute | solution.py:274
  55.8 8.0 %collective-permute-start.11 = (f32[64,512]{1,0:T(8,128)S(1)}, f32[64,512]{1,0:T(8,128)S(1)}, u32[]{:S(2)}, u32[]{:S(2)}) collective-permute-start(f32[64,512]{1,0:T(8,128)S(1)} %shard_map.66), channel_id=1, source_target_pairs={{0,16},{2,18},{4,20},{6,22},{8,24},{10,26},{12,28},{14,30},{16,0},... | collective-permute-start | bytes 393224 | tf_op jit(solution)/shard_map/ppermute | solution.py:271
  57.3 6.5 %collective-permute-start.12 = (f32[32,512]{1,0:T(8,128)S(1)}, f32[32,512]{1,0:T(8,128)S(1)}, u32[]{:S(2)}, u32[]{:S(2)}) collective-permute-start(f32[32,512]{1,0:T(8,128)S(1)} %get-tuple-element.67), channel_id=1, source_target_pairs={{0,30},{2,4},{4,2},{6,8},{8,6},{10,12},{12,10},{14,16},{16,14},{18... | collective-permute-start | bytes 196616 | tf_op jit(solution)/shard_map/ppermute | solution.py:274
  58.5 5.3 %collective-permute-start.13 = (f32[32,512]{1,0:T(8,128)S(1)}, f32[32,512]{1,0:T(8,128)S(1)}, u32[]{:S(2)}, u32[]{:S(2)}) collective-permute-start(f32[32,512]{1,0:T(8,128)S(1)} %get-tuple-element.68), channel_id=1, source_target_pairs={{0,2},{2,0},{4,6},{6,4},{8,10},{10,8},{12,14},{14,12},{16,18},{18,... | collective-permute-start | bytes 196616 | tf_op jit(solution)/shard_map/ppermute | solution.py:277

commit v4 on v3

--- a/solution.py
+++ b/solution.py
@@ -37,11 +37,11 @@
     return dot(a, top) + dot(a, low)
 
 
-def call(body, outs, *args, **rest):
+def call(body, outs, *args, limit=16, **rest):
     return pl.pallas_call(
         body,
         out_shape=[jax.ShapeDtypeStruct(*out) for out in outs],
-        compiler_params=pltpu.CompilerParams(vmem_limit_bytes=16 << 20),
+        compiler_params=pltpu.CompilerParams(vmem_limit_bytes=limit << 20),
         cost_estimate=pl.CostEstimate(flops=1000, bytes_accessed=1000, transcendentals=0),
         **rest,
     )(*args)
@@ -53,10 +53,22 @@
     return jnp.sum(jnp.where(down == along, row, 0), axis=1, keepdims=True)
 
 
-def renumber(lists, subspace, turned_edge, turned_rest, shuffle_out, origin_out):
+def renumber(lists_in, subspace_in, edge_out, rest_out, shuffle_out, origin_out, lists, subspace, sems):
     slots, halo = lists.shape[1:]
-    nodes = subspace.shape[1]
-    edge_nodes = slots * halo
+    depth, nodes = subspace.shape
+    wide = slots * halo
+    parts = sems.shape[0] - 1
+    span = depth // parts
+    index_copy = pltpu.make_async_copy(lists_in, lists, sems.at[parts])
+    index_copy.start()
+    copies = []
+    for part in range(parts):
+        rows = pl.ds(part * span, span)
+        copies.append(
+            pltpu.make_async_copy(subspace_in.at[rows], subspace.at[rows], sems.at[part])
+        )
+        copies[-1].start()
+    index_copy.wait()
     ids = lax.broadcasted_iota(I32, (halo, nodes), 1)
     seen = jnp.zeros((halo, nodes), F32)
     for slot in range(slots):
@@ -73,14 +85,18 @@
     shuffle = jnp.where(match, 1.0, 0.0).astype(BF16)
     shuffle_out[...] = shuffle
     origin_out[...] = jnp.sum(jnp.where(match, along, 0), axis=1, keepdims=True)
-    top, low = split(subspace[...])
-    turned = dot(shuffle, top, NT) + dot(shuffle, low, NT)
-    turned_edge[...] = turned[:edge_nodes]
-    turned_rest[...] = turned[edge_nodes:]
+    for part in range(parts):
+        rows = slice(part * span, (part + 1) * span)
+        copies[part].wait()
+        top, low = split(subspace[rows, :])
+        turned = dot(top, shuffle, NT) + dot(low, shuffle, NT)
+        edge_out[rows, :] = turned[:, :wide]
+        rest_out[rows, :] = turned[:, wide:]
 
 
 def assemble(
-    odd, lists, connect, element_ham, shuffle, origin, top_out, low_out, pick_out, both_out, hits_out, pair_out
+    odd, lists, connect, blocks, shuffle, origin, top_out, low_out, pick_out, both_out, hits_out, pair_out,
+    spread, rows_top, rows_low,
 ):
     elems, size = connect.shape
     slots, halo = lists.shape[1:]
@@ -105,12 +121,18 @@
         [3 * halo + lane, 2 * halo + lane, (1 - flag) * halo + lane, flag * halo + lane], 0
     )
     numbers = jnp.concatenate([origin[...], nodes + ghost], 0)
-    ham = jnp.zeros((nodes + wide, nodes + wide), F32)
+    pitch = spread.shape[1] // elems
     for elem in range(elems):
-        spread = jnp.where(numbers == connect[elem : elem + 1, :], 1.0, 0.0).astype(BF16)
-        top, low = split(element_ham[elem])
-        rows = dot(top, spread, NT) + dot(low, spread, NT)
-        ham = ham + sift(spread, rows)
+        cols = slice(elem * pitch, (elem + 1) * pitch)
+        wanted = jnp.pad(connect[elem : elem + 1, :], ((0, 0), (0, pitch - size)), constant_values=-1)
+        chosen = jnp.where(numbers == wanted, 1.0, 0.0).astype(BF16)
+        spread[:, cols] = chosen
+        block = blocks[pl.ds(elem, size, stride=elems), :]
+        top, low = split(jnp.pad(block, ((0, pitch - size), (0, pitch - size))))
+        top, low = split(dot(top, chosen, NT) + dot(low, chosen, NT))
+        rows_top[cols, :] = top
+        rows_low[cols, :] = low
+    ham = dot(spread[...], rows_top[...]) + dot(spread[...], rows_low[...])
     top, low = split(ham)
     top_out[...] = top
     low_out[...] = low
@@ -118,27 +140,49 @@
     pair_out[...] = jnp.concatenate([both[:duo, :duo], ham[far, far]], 1)
 
 
-def rotate_own(group, turned_edge, turned_rest, ritz, start_out, top_out, low_out):
-    step = pl.program_id(0)
-    top, low = split(ritz[...])
-
-    @pl.when(step == 0)
-    def _():
-        edge_nodes = turned_edge.shape[0]
-        start_out[:edge_nodes, :] = mul(split(turned_edge[...]), (top, low), NT)
-        start_out[edge_nodes:, :] = mul(split(turned_rest[...]), (top, low), NT)
-
-    @pl.when(step > 0)
-    def _():
-        top_out[...] = top.T
-        low_out[...] = low.T
-
-
-def rotate_edge(rows, start_own, top, low, pick, pair, start_out, far_out, out_out, near_out):
-    edge_nodes = rows.shape[0]
-    wide, block = pick.shape[0], start_own.shape[1]
+def rotate_own(group, edge, rest, ritz_in, start_out, top_out, low_out, ritz, sems):
+    block, depth = ritz.shape[1:]
+    groups = ritz.shape[0]
+    parts = sems.shape[1]
+    span = block // parts
+    copies = []
+    for step in range(groups):
+        first = lax.rem(group[0] + groups - step, groups) * depth
+        cols = pl.ds(pl.multiple_of(first, depth), depth)
+        for part in range(parts):
+            rows = pl.ds(part * span, span)
+            copies.append(
+                pltpu.make_async_copy(
+                    ritz_in.at[rows, cols], ritz.at[step, rows], sems.at[step, part]
+                )
+            )
+            copies[-1].start()
+    own = split(jnp.concatenate([edge[...], rest[...]], 1))
+    for step in range(groups):
+        for part in range(parts):
+            rows = slice(part * span, (part + 1) * span)
+            copies[step * parts + part].wait()
+            top, low = split(ritz[step, rows, :])
+            if step == 0:
+                start_out[rows, :] = mul((top, low), own)
+            else:
+                cols = slice((step - 1) * depth, step * depth)
+                top_out[rows, cols] = top
+                low_out[rows, cols] = low
+
+
+def rotate(top, low, columns):
+    width = columns.shape[1]
+    high, rest = split(columns)
+    wide = dot(top, jnp.concatenate([high, rest], 1))
+    return wide[:, :width] + (wide[:, width:] + dot(low, high))
+
+
+def rotate_edge(columns, start_own, top, low, pick, pair, start_out, far_out, out_out, near_out):
+    edge_nodes = columns.shape[1]
+    wide, block = pick.shape[0], start_own.shape[0]
     quarter = wide // 4
-    start = start_own[:edge_nodes, :] + mul(split(rows[...]), (top[...], low[...]))
+    start = (start_own[:, :edge_nodes] + rotate(top[...], low[...], columns[...])).T
     start_out[...] = start
     packed = sift(pick[...], start)
     far_out[:, :block] = packed[: 2 * quarter]
@@ -147,31 +191,44 @@
     near_out[...] = packed[3 * quarter :]
 
 
+def first_part(start_edge, far_in, out_in, near_in, ham_top, ham_low, part_out):
+    edge_nodes, block = start_edge.shape
+    nodes = ham_top.shape[0] - 4 * out_in.shape[0]
+    ghosts = jnp.concatenate([far_in[:, :block], out_in[...], near_in[...]], 0)
+    part_out[...] = mul(
+        (ham_top[:, :edge_nodes], ham_low[:, :edge_nodes]), split(start_edge[...])
+    ) + mul((ham_top[:, nodes:], ham_low[:, nodes:]), split(ghosts))
+
+
 def rotate_rest(
-    rows, start_own, start_edge, top, low, far_in, out_in, near_in, ham_top, ham_low,
-    ext_out, far_out, out_out, near_out,
+    columns, start_own, top, low, part, ham_top, ham_low, rest_out, far_out, out_out, near_out
 ):
-    edge_nodes, block = start_edge.shape
-    nodes = start_own.shape[0]
-    halo = out_in.shape[0]
-    rest = start_own[edge_nodes:, :] + mul(split(rows[...]), (top[...], low[...]))
-    ext = jnp.concatenate(
-        [start_edge[...], rest, far_in[:, :block], out_in[...], near_in[...]], 0
-    )
-    ext_out[...] = ext
-    back = mul((ham_top[nodes:, :], ham_low[nodes:, :]), split(ext))
+    nodes = start_own.shape[1]
+    edge_nodes = nodes - columns.shape[1]
+    halo = out_out.shape[0]
+    rest = (start_own[:, edge_nodes:] + rotate(top[...], low[...], columns[...])).T
+    rest_out[...] = rest
+    cols = slice(edge_nodes, nodes)
+    back = part[nodes:, :] + mul((ham_top[nodes:, cols], ham_low[nodes:, cols]), split(rest))
     far_out[...] = back[: 2 * halo]
     out_out[...] = back[2 * halo : 3 * halo]
     near_out[...] = back[3 * halo :]
 
 
-def first_base(ext, ham_top, ham_low, pick, far_in, back_far, base_out, packed_out, adjust_out):
+def first_base(
+    start_edge, start_rest, part, ham_top, ham_low, pick, far_in, back_far,
+    start_out, base_out, packed_out, adjust_out,
+):
     nodes = ham_top.shape[0] - pick.shape[0]
-    edge_nodes = pick.shape[1]
-    block = ext.shape[1]
+    edge_nodes, block = start_edge.shape
     duo = far_in.shape[0]
-    own = (ham_top[:nodes, :], ham_low[:nodes, :])
-    base = SCALE_ONE * (mul(own, split(ext[...])) - CENTRE * ext[:nodes, :])
+    cols = slice(edge_nodes, nodes)
+    start = jnp.concatenate([start_edge[...], start_rest[...]], 0)
+    start_out[...] = start
+    own = part[:nodes, :] + mul(
+        (ham_top[:nodes, cols], ham_low[:nodes, cols]), split(start_rest[...])
+    )
+    base = SCALE_ONE * (own - CENTRE * start)
     base_out[...] = base
     packed_out[...] = sift(pick[...], base[:edge_nodes])
     overlap = far_in[:, block : block + duo].astype(BF16)
@@ -230,12 +287,12 @@
     near_out[...] = rows[halo:]
 
 
-def second_base(part, ghosts, ham_top, ham_low, first, ext, known, shuffle, hits, result_out):
+def second_base(part, ghosts, ham_top, ham_low, first, start, known, shuffle, hits, result_out):
     nodes = first.shape[0]
     duo = known.shape[0]
     ham = (ham_top[:nodes, nodes:], ham_low[:nodes, nodes:])
     second = part[:nodes, :] + mul(ham, split(ghosts[...])) - CENTRE * first[...]
-    second = SCALE_TWO * second - SIGMA_ONE * SIGMA_TWO * ext[:nodes, :]
+    second = SCALE_TWO * second - SIGMA_ONE * SIGMA_TWO * start[...]
     top, low = split(second.T)
     result = dot(top, shuffle[...]) + dot(low, shuffle[...])
     top, low = split(SCALE_TWO * known[...].T)
@@ -281,7 +338,7 @@
             lax.ppermute(rows, "state", [(i, (i + step) % groups) for i in range(groups)])
             for step in range(1, groups)
         ]
-        return parts[0] if len(parts) == 1 else jnp.concatenate(parts, 1)
+        return parts[0] if len(parts) == 1 else jnp.concatenate(parts, 0)
 
     def rows_of(count):
         return ((count, block), F32)
@@ -289,15 +346,24 @@
     halo_out = [rows_of(duo), rows_of(halo), rows_of(halo)]
     smem = pl.BlockSpec(memory_space=pltpu.SMEM)
     vmem = pl.BlockSpec(memory_space=pltpu.VMEM)
-
-    turned_edge, turned_rest, shuffle, origin = call(
+    hbm = pl.BlockSpec(memory_space=pltpu.HBM)
+
+    edge, rest, shuffle, origin = call(
         renumber,
-        [((wide, depth), F32), ((nodes - wide, depth), F32), ((nodes, nodes), BF16), ((nodes, 1), I32)],
-        send_rows,
-        subspace,
-    )
-    edge_in = gather(turned_edge)
-    rest_in = gather(turned_rest)
+        [((depth, wide), F32), ((depth, nodes - wide), F32), ((nodes, nodes), BF16), ((nodes, 1), I32)],
+        send_rows, subspace,
+        in_specs=[hbm, hbm],
+        scratch_shapes=[
+            pltpu.VMEM(send_rows.shape, I32),
+            pltpu.VMEM(subspace.shape, F32),
+            pltpu.SemaphoreType.DMA((5,)),
+        ],
+    )
+    edge_in = gather(edge)
+    rest_in = gather(rest)
+    elems, size = connect.shape
+    pitch = -(-size // 128) * 128
+    blocks = jnp.transpose(element_ham, (1, 0, 2)).reshape(size * elems, size)
     ham_top, ham_low, pick, both, hits, pair = call(
         assemble,
         [
@@ -308,39 +374,30 @@
             ((wide, nodes), BF16),
             ((duo, 2 * duo), F32),
         ],
-        odd,
-        send_rows,
-        connect,
-        element_ham,
-        shuffle,
-        origin,
+        odd, send_rows, connect, blocks, shuffle, origin,
         in_specs=[smem] + [vmem] * 5,
+        scratch_shapes=[
+            pltpu.VMEM((full, elems * pitch), BF16),
+            pltpu.VMEM((elems * pitch, full), BF16),
+            pltpu.VMEM((elems * pitch, full), BF16),
+        ],
     )
     others = groups - 1
-    start_own, ritz_top, ritz_low = pl.pallas_call(
+    start_own, ritz_top, ritz_low = call(
         rotate_own,
-        out_shape=[
-            jax.ShapeDtypeStruct((nodes, block), F32),
-            jax.ShapeDtypeStruct((others * depth, block), BF16),
-            jax.ShapeDtypeStruct((others * depth, block), BF16),
+        [
+            ((block, nodes), F32),
+            ((block, others * depth), BF16),
+            ((block, others * depth), BF16),
         ],
-        grid_spec=pltpu.PrefetchScalarGridSpec(
-            num_scalar_prefetch=1,
-            grid=(groups,),
-            in_specs=[
-                pl.BlockSpec((wide, depth), lambda i, g: (0, 0)),
-                pl.BlockSpec((nodes - wide, depth), lambda i, g: (0, 0)),
-                pl.BlockSpec((block, depth), lambda i, g: (0, lax.rem(g[0] + groups - i, groups))),
-            ],
-            out_specs=[
-                pl.BlockSpec((nodes, block), lambda i, g: (0, 0)),
-                pl.BlockSpec((depth, block), lambda i, g: (jnp.maximum(i - 1, 0), 0)),
-                pl.BlockSpec((depth, block), lambda i, g: (jnp.maximum(i - 1, 0), 0)),
-            ],
-        ),
-        compiler_params=pltpu.CompilerParams(vmem_limit_bytes=32 << 20),
-        cost_estimate=pl.CostEstimate(flops=1000, bytes_accessed=1000, transcendentals=0),
-    )(group, turned_edge, turned_rest, ritz)
+        group, edge, rest, ritz,
+        limit=24,
+        in_specs=[smem, vmem, vmem, hbm],
+        scratch_shapes=[
+            pltpu.VMEM((groups, block, depth), F32),
+            pltpu.SemaphoreType.DMA((groups, 2)),
+        ],
+    )
 
     start_edge, far_rows, out_rows, near_rows = call(
         rotate_edge,
@@ -348,17 +405,20 @@
         edge_in, start_own, ritz_top, ritz_low, pick, pair,
     )
     pair_in, out_in, near_in = far(far_rows), out(out_rows), near(near_rows)
-
-    ext, back_far, back_out, back_near = call(
+    (part,) = call(
+        first_part, [rows_of(full)], start_edge, pair_in, out_in, near_in, ham_top, ham_low
+    )
+
+    start_rest, back_far, back_out, back_near = call(
         rotate_rest,
-        [rows_of(full)] + halo_out,
-        rest_in, start_own, start_edge, ritz_top, ritz_low, pair_in, out_in, near_in, ham_top, ham_low,
+        [rows_of(nodes - wide)] + halo_out,
+        rest_in, start_own, ritz_top, ritz_low, part, ham_top, ham_low,
     )
     far_in, out_in, near_in = far(back_far), out(back_out), near(back_near)
-    base, packed, adjust = call(
+    start, base, packed, adjust = call(
         first_base,
-        [rows_of(nodes), rows_of(wide), rows_of(duo)],
-        ext, ham_top, ham_low, pick, pair_in, back_far,
+        [rows_of(nodes), rows_of(nodes), rows_of(wide), rows_of(duo)],
+        start_edge, start_rest, part, ham_top, ham_low, pick, pair_in, back_far,
     )
     (far_rows,) = call(fetch_far, [rows_of(duo)], packed, both, out_in, near_in)
     fetched_far = far(far_rows)
@@ -385,7 +445,7 @@
     (result,) = call(
         second_base,
         [((block, nodes), F32)],
-        part, ghosts, ham_top, ham_low, first, ext, known, shuffle, hits,
+        part, ghosts, ham_top, ham_low, first, start, known, shuffle, hits,
     )
     (result,) = call(
         finish, [((block, nodes), F32)], result, hits, returned_far, returned_out, returned_near

time: 65.3 us -> 61.4 us (0.940)
  Pallas kernels: 21 us -> 18.7 us
  local copies, waits for them, and re-layouts: 7.48 us -> 5.31 us
  waiting for transfers between devices: 18.6 us -> 19.5 us
    pallas_call x1 -> x0, Pallas kernels: 4.97 us -> none  [per_device(): pl.pallas_call(rotate_own, out_shape=[jax.ShapeDtypeStruct((nodes, block)...]
    pallas_call x12 -> x14, Pallas kernels: 16 us -> 18.7 us  [call(): pl.pallas_call(body, out_shape=[jax.ShapeDtypeStruct(*out) for out in out...]
    unnamed x17 -> x12, local copies, waits for them, and re-layouts: 7.48 us -> 5.31 us
    ppermute x2, waiting for transfers between devices: 0.23 us -> 1.82 us  [gather(): lax.ppermute(rows, 'state', [(i, (i + step) % groups) for i in range(grou...]
    ppermute x4, starting transfers between devices: 0.79 us -> 1.61 us  [near(): return lax.ppermute(rows, 'mesh', pairs_in)]
    ppermute x4, waiting for transfers between devices: 0.72 us -> 0.01 us  [far(): return lax.ppermute(rows, 'mesh', pairs_far)]
    ppermute x4, starting transfers between devices: 9.27 us -> 8.58 us  [far(): return lax.ppermute(rows, 'mesh', pairs_far)]
  transfers between devices with their start and end apart: 14 -> 14, of which waited for: 6 -> 5; matrix products, arithmetic and copies ran while one was open for 2% -> 0% of each run, Pallas kernels for 25% -> 22%
where the time goes in v4:
time: 61.4 us; the launch traced here: 61.1 us
  waiting for transfers between devices  19.5 us (32%)
  Pallas kernels  18.7 us (30%)
  starting transfers between devices  17.4 us (28%)
  local copies, waits for them, and re-layouts  5.31 us (9%)
    pallas_call x14, Pallas kernels, call(): pl.pallas_call(body, out_shape=[jax.ShapeDtypeStruct(*out) for out in out...  18.7 us
    ppermute x4, waiting for transfers between devices, out(): return lax.ppermute(rows, 'mesh', pairs_out)  17.6 us
    ppermute x4, starting transfers between devices, far(): return lax.ppermute(rows, 'mesh', pairs_far)  8.58 us
    unnamed x12, local copies, waits for them, and re-layouts  5.31 us
    ppermute x4, starting transfers between devices, out(): return lax.ppermute(rows, 'mesh', pairs_out)  4.15 us
    ppermute x2, starting transfers between devices, gather(): lax.ppermute(rows, 'state', [(i, (i + step) % groups) for i in range(grou...  3.11 us
    ppermute x2, waiting for transfers between devices, gather(): lax.ppermute(rows, 'state', [(i, (i + step) % groups) for i in range(grou...  1.82 us
    ppermute x4, starting transfers between devices, near(): return lax.ppermute(rows, 'mesh', pairs_in)  1.61 us
  transfers between devices with their start and end apart: 14, of which 5 were waited for; matrix products, arithmetic and copies ran while one was open for 0% of the time, Pallas kernels for 22%

profile of v4, /device:TPU:0, one launch (start us, length us, event | category | flops | bytes accessed | tf_op | source)
XLA Modules:
  0.0 61.1 jit_solution(8916929931611561335)
XLA Ops:
  0.0 1.2 %copy-done.1 = f32[1024,256]{1,0:T(8,128)S(1)} copy-done((f32[1024,256]{1,0:T(8,128)S(1)}, f32[1024,256]{1,0:T(8,128)}, u32[]{:S(2)}) %copy-start.1) | copy-done | bytes 1048600
  1.9 2.8 %shard_map.55 = (f32[1024,128]{1,0:T(8,128)}, f32[1024,128]{1,0:T(8,128)}, bf16[256,256]{1,0:T(8,128)(2,1)S(1)}, s32[256,1]{1,0:T(8,128)S(1)}) custom-call(s32[1,4,32]{2,1,0:T(4,128)S(1)} %copy-done.4, f32[1024,256]{1,0:T(8,128)S(1)} %copy-done.1), custom_call_target="tpu_custom_call" | custom-call | flops 1000 | bytes 1000 | tf_op jit(solution)/shard_map/pallas_call | solution.py:41
  4.7 3.0 %collective-permute-start = (f32[1024,128]{1,0:T(8,128)}, f32[1024,128]{1,0:T(8,128)}, u32[]{:S(2)}, u32[]{:S(2)}) collective-permute-start(f32[1024,128]{1,0:T(8,128)} %get-tuple-element.38.edge), channel_id=1, source_target_pairs={{0,1},{1,0},{2,3},{3,2},{4,5},{5,4},{6,7},{7,6},{8,9},{9,8},{10,11... | collective-permute-start | bytes 1572872 | tf_op jit(solution)/shard_map/ppermute | solution.py:338
  7.8 2.2 %copy-done = f32[512,2048]{1,0:T(8,128)S(1)} copy-done((f32[512,2048]{1,0:T(8,128)S(1)}, f32[512,2048]{1,0:T(8,128)}, u32[]{:S(2)}) %copy-start) | copy-done | bytes 4194328
  10.0 4.1 %shard_map.56 = (f32[512,256]{1,0:T(8,128)S(1)}, bf16[512,1024]{1,0:T(8,128)(2,1)S(1)}, bf16[512,1024]{1,0:T(8,128)(2,1)S(1)}) custom-call(s32[1]{0:T(128)} %bitcast.group, f32[1024,128]{1,0:T(8,128)} %get-tuple-element.38.edge, f32[1024,128]{1,0:T(8,128)} %get-tuple-element.39.rest, f32[512,2048]{1,0:T(8,128)S(1)} %copy-done), custom_call_target="tpu_custom_call" | custom-call | flops 1000 | bytes 1000 | tf_op jit(solution)/shard_map/pallas_call | solution.py:41
  14.1 1.2 %copy-done.2 = f32[16,125,125]{2,0,1:T(8,128)S(1)} copy-done((f32[16,125,125]{2,0,1:T(8,128)S(1)}, f32[16,125,125]{2,0,1:T(8,128)}, u32[]{:S(2)}) %copy-start.2) | copy-done | bytes 1000024
  15.3 3.6 %shard_map.57 = (bf16[384,384]{1,0:T(8,128)(2,1)S(1)}, bf16[384,384]{1,0:T(8,128)(2,1)S(1)}, bf16[128,128]{1,0:T(8,128)(2,1)S(1)}, bf16[128,128]{1,0:T(8,128)(2,...) custom-call(s32[1]{0:T(128)} %bitcast.1.odd, s32[1,4,32]{2,1,0:T(4,128)S(1)} %copy-done.5, ...), custom_call_target="tpu_custom_call" | custom-call | flops 1000 | bytes 1000 | tf_op jit(solution)/shard_map/pallas_call | solution.py:41
  19.0 1.8 %collective-permute-done.columns = f32[1024,128]{1,0:T(8,128)} collective-permute-done((f32[1024,128]{1,0:T(8,128)}, f32[1024,128]{1,0:T(8,128)}, u32[]{:S(2)}, u32[]{:S(2)}) %collective-permute-start) | collective-permute-done | bytes 524320 | tf_op jit(solution)/shard_map/ppermute | solution.py:338
  20.8 2.0 %shard_map.58 = (f32[128,512]{1,0:T(8,128)S(1)}, f32[64,640]{1,0:T(8,128)S(1)}, f32[32,512]{1,0:T(8,128)S(1)}, f32[32,512]{1,0:T(8,128)S(1)}) custom-call(f32[1024,128]{1,0:T(8,128)} %collective-permute-done.columns, f32[512,256]{1,0:T(8,128)S(1)} %get-tuple-element.40.start_own, bf16[512,1024]{1,0:T(8,128)(2,1)S(1)} %get-tuple-element.41.top, ...), custom_call_target="tpu_custom_call" | custom-call | flops 1000 | bytes 1000 | tf_op jit(solution)/shard_map/pallas_call | solution.py:41
  22.8 3.2 %collective-permute-start.2 = (f32[64,640]{1,0:T(8,128)S(1)}, f32[64,640]{1,0:T(8,128)S(1)}, u32[]{:S(2)}, u32[]{:S(2)}) collective-permute-start(f32[64,640]{1,0:T(8,128)S(1)} %get-tuple-element.48), channel_id=1, source_target_pairs={{0,16},{2,18},{4,20},{6,22},{8,24},{10,26},{12,28},{14,30},{16,0},... | collective-permute-start | bytes 491528 | tf_op jit(solution)/shard_map/ppermute | solution.py:328
  26.0 1.6 %collective-permute-start.4 = (f32[32,512]{1,0:T(8,128)S(1)}, f32[32,512]{1,0:T(8,128)S(1)}, u32[]{:S(2)}, u32[]{:S(2)}) collective-permute-start(f32[32,512]{1,0:T(8,128)S(1)} %get-tuple-element.50), channel_id=1, source_target_pairs={{0,2},{2,0},{4,6},{6,4},{8,10},{10,8},{12,14},{14,12},{16,18},{18,... | collective-permute-start | bytes 196616 | tf_op jit(solution)/shard_map/ppermute | solution.py:334
  27.6 4.8 %collective-permute-done.3.out_in = f32[32,512]{1,0:T(8,128)S(1)} collective-permute-done((f32[32,512]{1,0:T(8,128)S(1)}, f32[32,512]{1,0:T(8,128)S(1)}, u32[]{:S(2)}, u32[]{:S(2)}) %collective-permute-start.3) | collective-permute-done | bytes 65568 | tf_op jit(solution)/shard_map/ppermute | solution.py:331
  33.2 1.0 %shard_map.60 = (f32[128,512]{1,0:T(8,128)S(1)}, f32[64,512]{1,0:T(8,128)S(1)}, f32[32,512]{1,0:T(8,128)S(1)}, f32[32,512]{1,0:T(8,128)S(1)}) custom-call(f32[1024,128]{1,0:T(8,128)S(1)} %collective-permute-done.1.columns, f32[512,256]{1,0:T(8,128)S(1)} %get-tuple-element.40.start_own, bf16[512,1024]{1,0:T(8,128)(2,1)S(1)} %get-tuple-element.41.top, ...), custom_call_target="tpu_custom_call" | custom-call | flops 1000 | bytes 1000 | tf_op jit(solution)/shard_map/pallas_call | solution.py:41
  34.2 2.8 %collective-permute-start.5 = (f32[64,512]{1,0:T(8,128)S(1)}, f32[64,512]{1,0:T(8,128)S(1)}, u32[]{:S(2)}, u32[]{:S(2)}) collective-permute-start(f32[64,512]{1,0:T(8,128)S(1)} %get-tuple-element.54.back_far), channel_id=1, source_target_pairs={{0,16},{2,18},{4,20},{6,22},{8,24},{10,26},{12,28},{14,30},{16,0},... | collective-permute-start | bytes 393224 | tf_op jit(solution)/shard_map/ppermute | solution.py:328
  38.1 5.4 %collective-permute-done.6.out_in = f32[32,512]{1,0:T(8,128)S(1)} collective-permute-done((f32[32,512]{1,0:T(8,128)S(1)}, f32[32,512]{1,0:T(8,128)S(1)}, u32[]{:S(2)}, u32[]{:S(2)}) %collective-permute-start.6) | collective-permute-done | bytes 65568 | tf_op jit(solution)/shard_map/ppermute | solution.py:331
  43.7 0.8 %collective-permute-start.8 = (f32[64,512]{1,0:T(8,128)S(1)}, f32[64,512]{1,0:T(8,128)S(1)}, u32[]{:S(2)}, u32[]{:S(2)}) collective-permute-start(f32[64,512]{1,0:T(8,128)S(1)} %shard_map.63), channel_id=1, source_target_pairs={{0,16},{2,18},{4,20},{6,22},{8,24},{10,26},{12,28},{14,30},{16,0},... | collective-permute-start | bytes 393224 | tf_op jit(solution)/shard_map/ppermute | solution.py:328
  44.7 1.4 %collective-permute-start.9 = (f32[32,512]{1,0:T(8,128)S(1)}, f32[32,512]{1,0:T(8,128)S(1)}, u32[]{:S(2)}, u32[]{:S(2)}) collective-permute-start(f32[32,512]{1,0:T(8,128)S(1)} %get-tuple-element.62), channel_id=1, source_target_pairs={{0,30},{2,4},{4,2},{6,8},{8,6},{10,12},{12,10},{14,16},{16,14},{18... | collective-permute-start | bytes 196616 | tf_op jit(solution)/shard_map/ppermute | solution.py:331
  46.1 0.9 %shard_map.62 = (f32[256,512]{1,0:T(8,128)S(1)}, f32[384,512]{1,0:T(8,128)S(1)}, f32[64,512]{1,0:T(8,128)S(1)}) custom-call(f32[256,512]{1,0:T(8,128)S(1)} %get-tuple-element.55.base, bf16[128,128]{1,0:T(8,128)(2,1)S(1)} %get-tuple-element.45.pick, f32[64,512]{1,0:T(8,128)S(1)} %collective-permute-done.5.far_in, ...), custom_call_target="tpu_custom_call" | custom-call | flops 1000 | bytes 1000 | tf_op jit(solution)/shard_map/pallas_call | solution.py:41
  47.0 4.1 %collective-permute-done.9.out_in = f32[32,512]{1,0:T(8,128)S(1)} collective-permute-done((f32[32,512]{1,0:T(8,128)S(1)}, f32[32,512]{1,0:T(8,128)S(1)}, u32[]{:S(2)}, u32[]{:S(2)}) %collective-permute-start.9) | collective-permute-done | bytes 65568 | tf_op jit(solution)/shard_map/ppermute | solution.py:331
  51.4 1.8 %collective-permute-start.11 = (f32[64,512]{1,0:T(8,128)S(1)}, f32[64,512]{1,0:T(8,128)S(1)}, u32[]{:S(2)}, u32[]{:S(2)}) collective-permute-start(f32[64,512]{1,0:T(8,128)S(1)} %shard_map.67), channel_id=1, source_target_pairs={{0,16},{2,18},{4,20},{6,22},{8,24},{10,26},{12,28},{14,30},{16,0},... | collective-permute-start | bytes 393224 | tf_op jit(solution)/shard_map/ppermute | solution.py:328
  53.5 2.3 %collective-permute-start.12 = (f32[32,512]{1,0:T(8,128)S(1)}, f32[32,512]{1,0:T(8,128)S(1)}, u32[]{:S(2)}, u32[]{:S(2)}) collective-permute-start(f32[32,512]{1,0:T(8,128)S(1)} %get-tuple-element.69), channel_id=1, source_target_pairs={{0,30},{2,4},{4,2},{6,8},{8,6},{10,12},{12,10},{14,16},{16,14},{18... | collective-permute-start | bytes 196616 | tf_op jit(solution)/shard_map/ppermute | solution.py:331
  55.8 0.8 %shard_map.66.result = f32[512,256]{1,0:T(8,128)S(1)} custom-call(f32[384,512]{1,0:T(8,128)S(1)} %get-tuple-element.58.part, f32[128,512]{1,0:T(8,128)S(1)} %get-tuple-element.64.ghosts, bf16[384,384]{1,0:T(8,128)(2,1)S(1)} %get-tuple-element.51.ham_top, bf16[384,384]{1,0:T(8,128)(2,1)S(1)} %get-tuple-element.52.ham_low, ...), custom_call_target="tpu_custom_call" | custom-call | flops 1000 | bytes 1000 | tf_op jit(solution)/shard_map/pallas_call | solution.py:41
  56.6 3.3 %collective-permute-done.12.out_in = f32[32,512]{1,0:T(8,128)S(1)} collective-permute-done((f32[32,512]{1,0:T(8,128)S(1)}, f32[32,512]{1,0:T(8,128)S(1)}, u32[]{:S(2)}, u32[]{:S(2)}) %collective-permute-start.12) | collective-permute-done | bytes 65568 | tf_op jit(solution)/shard_map/ppermute | solution.py:331
  59.9 1.1 %shard_map.68 = f32[512,256]{1,0:T(8,128)} custom-call(f32[512,256]{1,0:T(8,128)S(1)} %shard_map.66.result, bf16[128,256]{1,0:T(8,128)(2,1)S(1)} %get-tuple-element.68.hits, f32[64,512]{1,0:T(8,128)S(1)} %collective-permute-done.11.far_in, f32[32,512]{1,0:T(8,128)S(1)} %collective-permute-done.12.out_in, f32[32,512]{1,0:T(8,128)S(1)} %collective-permute-done.13.near_in), custom_call_target="tpu_custom_call" | custom-call | flops 1000 | bytes 1000 | tf_op jit(solution)/shard_map/pallas_call | solution.py:41
  (30 shorter events, 3.5 us)
Async XLA Ops:
  0.0 1.2 %copy-start.1 = (f32[1024,256]{1,0:T(8,128)S(1)}, f32[1024,256]{1,0:T(8,128)}, u32[]{:S(2)}) copy-start(f32[1024,256]{1,0:T(8,128)} %subspace_in.1) | copy-start | bytes 3145732
  1.2 0.7 %copy-start.4 = (s32[1,4,32]{2,1,0:T(4,128)S(1)}, s32[1,4,32]{2,1,0:T(4,128)}, u32[]{:S(2)}) copy-start(s32[1,4,32]{2,1,0:T(4,128)} %lists.1) | copy-start | bytes 1540
  1.9 12.2 %copy-start.3 = (s32[16,125]{1,0:T(8,128)S(1)}, s32[16,125]{1,0:T(8,128)}, u32[]{:S(2)}) copy-start(s32[16,125]{1,0:T(8,128)} %connect.1) | copy-start | bytes 24004
  1.9 12.2 %copy-start.5 = (s32[1,4,32]{2,1,0:T(4,128)S(1)}, s32[1,4,32]{2,1,0:T(4,128)}, u32[]{:S(2)}) copy-start(s32[1,4,32]{2,1,0:T(4,128)} %lists.1) | copy-start | bytes 1540
  4.7 16.1 %collective-permute-start = (f32[1024,128]{1,0:T(8,128)}, f32[1024,128]{1,0:T(8,128)}, u32[]{:S(2)}, u32[]{:S(2)}) collective-permute-start(f32[1024,128]{1,0:T(8,128)} %get-tuple-element.38.edge), channel_id=1, source_target_pairs={{0,1},{1,0},{2,3},{3,2},{4,5},{5,4},{6,7},{7,6},{8,9},{9,8},{10,11... | collective-permute-start | bytes 1572872 | tf_op jit(solution)/shard_map/ppermute | solution.py:338
  7.7 25.5 %collective-permute-start.1 = (f32[1024,128]{1,0:T(8,128)}, f32[1024,128]{1,0:T(8,128)S(1)}, u32[]{:S(2)}, u32[]{:S(2)}) collective-permute-start(f32[1024,128]{1,0:T(8,128)} %get-tuple-element.39.rest), channel_id=1, source_target_pairs={{0,1},{1,0},{2,3},{3,2},{4,5},{5,4},{6,7},{7,6},{8,9},{9,8},{10,11... | collective-permute-start | bytes 1572872 | tf_op jit(solution)/shard_map/ppermute | solution.py:338
  7.8 2.2 %copy-start = (f32[512,2048]{1,0:T(8,128)S(1)}, f32[512,2048]{1,0:T(8,128)}, u32[]{:S(2)}) copy-start(f32[512,2048]{1,0:T(8,128)} %ritz_in.1) | copy-start | bytes 12582916
  14.1 1.2 %copy-start.2 = (f32[16,125,125]{2,0,1:T(8,128)S(1)}, f32[16,125,125]{2,0,1:T(8,128)}, u32[]{:S(2)}) copy-start(f32[16,125,125]{2,0,1:T(8,128)} %param.7) | copy-start | bytes 3000004
  22.8 9.6 %collective-permute-start.2 = (f32[64,640]{1,0:T(8,128)S(1)}, f32[64,640]{1,0:T(8,128)S(1)}, u32[]{:S(2)}, u32[]{:S(2)}) collective-permute-start(f32[64,640]{1,0:T(8,128)S(1)} %get-tuple-element.48), channel_id=1, source_target_pairs={{0,16},{2,18},{4,20},{6,22},{8,24},{10,26},{12,28},{14,30},{16,0},... | collective-permute-start | bytes 491528 | tf_op jit(solution)/shard_map/ppermute | solution.py:328
  26.0 6.4 %collective-permute-start.3 = (f32[32,512]{1,0:T(8,128)S(1)}, f32[32,512]{1,0:T(8,128)S(1)}, u32[]{:S(2)}, u32[]{:S(2)}) collective-permute-start(f32[32,512]{1,0:T(8,128)S(1)} %get-tuple-element.49), channel_id=1, source_target_pairs={{0,30},{2,4},{4,2},{6,8},{8,6},{10,12},{12,10},{14,16},{16,14},{18... | collective-permute-start | bytes 196616 | tf_op jit(solution)/shard_map/ppermute | solution.py:331
  26.0 6.4 %collective-permute-start.4 = (f32[32,512]{1,0:T(8,128)S(1)}, f32[32,512]{1,0:T(8,128)S(1)}, u32[]{:S(2)}, u32[]{:S(2)}) collective-permute-start(f32[32,512]{1,0:T(8,128)S(1)} %get-tuple-element.50), channel_id=1, source_target_pairs={{0,2},{2,0},{4,6},{6,4},{8,10},{10,8},{12,14},{14,12},{16,18},{18,... | collective-permute-start | bytes 196616 | tf_op jit(solution)/shard_map/ppermute | solution.py:334
  34.2 10.3 %collective-permute-start.5 = (f32[64,512]{1,0:T(8,128)S(1)}, f32[64,512]{1,0:T(8,128)S(1)}, u32[]{:S(2)}, u32[]{:S(2)}) collective-permute-start(f32[64,512]{1,0:T(8,128)S(1)} %get-tuple-element.54.back_far), channel_id=1, source_target_pairs={{0,16},{2,18},{4,20},{6,22},{8,24},{10,26},{12,28},{14,30},{16,0},... | collective-permute-start | bytes 393224 | tf_op jit(solution)/shard_map/ppermute | solution.py:328
  37.0 6.5 %collective-permute-start.6 = (f32[32,512]{1,0:T(8,128)S(1)}, f32[32,512]{1,0:T(8,128)S(1)}, u32[]{:S(2)}, u32[]{:S(2)}) collective-permute-start(f32[32,512]{1,0:T(8,128)S(1)} %get-tuple-element.56), channel_id=1, source_target_pairs={{0,30},{2,4},{4,2},{6,8},{8,6},{10,12},{12,10},{14,16},{16,14},{18... | collective-permute-start | bytes 196616 | tf_op jit(solution)/shard_map/ppermute | solution.py:331
  37.4 6.1 %collective-permute-start.7 = (f32[32,512]{1,0:T(8,128)S(1)}, f32[32,512]{1,0:T(8,128)S(1)}, u32[]{:S(2)}, u32[]{:S(2)}) collective-permute-start(f32[32,512]{1,0:T(8,128)S(1)} %get-tuple-element.57), channel_id=1, source_target_pairs={{0,2},{2,0},{4,6},{6,4},{8,10},{10,8},{12,14},{14,12},{16,18},{18,... | collective-permute-start | bytes 196616 | tf_op jit(solution)/shard_map/ppermute | solution.py:334
  43.7 9.5 %collective-permute-start.8 = (f32[64,512]{1,0:T(8,128)S(1)}, f32[64,512]{1,0:T(8,128)S(1)}, u32[]{:S(2)}, u32[]{:S(2)}) collective-permute-start(f32[64,512]{1,0:T(8,128)S(1)} %shard_map.63), channel_id=1, source_target_pairs={{0,16},{2,18},{4,20},{6,22},{8,24},{10,26},{12,28},{14,30},{16,0},... | collective-permute-start | bytes 393224 | tf_op jit(solution)/shard_map/ppermute | solution.py:328
  44.7 6.5 %collective-permute-start.9 = (f32[32,512]{1,0:T(8,128)S(1)}, f32[32,512]{1,0:T(8,128)S(1)}, u32[]{:S(2)}, u32[]{:S(2)}) collective-permute-start(f32[32,512]{1,0:T(8,128)S(1)} %get-tuple-element.62), channel_id=1, source_target_pairs={{0,30},{2,4},{4,2},{6,8},{8,6},{10,12},{12,10},{14,16},{16,14},{18... | collective-permute-start | bytes 196616 | tf_op jit(solution)/shard_map/ppermute | solution.py:331
  46.1 5.0 %collective-permute-start.10 = (f32[32,512]{1,0:T(8,128)S(1)}, f32[32,512]{1,0:T(8,128)S(1)}, u32[]{:S(2)}, u32[]{:S(2)}) collective-permute-start(f32[32,512]{1,0:T(8,128)S(1)} %get-tuple-element.63), channel_id=1, source_target_pairs={{0,2},{2,0},{4,6},{6,4},{8,10},{10,8},{12,14},{14,12},{16,18},{18,... | collective-permute-start | bytes 196616 | tf_op jit(solution)/shard_map/ppermute | solution.py:334
  51.4 8.5 %collective-permute-start.11 = (f32[64,512]{1,0:T(8,128)S(1)}, f32[64,512]{1,0:T(8,128)S(1)}, u32[]{:S(2)}, u32[]{:S(2)}) collective-permute-start(f32[64,512]{1,0:T(8,128)S(1)} %shard_map.67), channel_id=1, source_target_pairs={{0,16},{2,18},{4,20},{6,22},{8,24},{10,26},{12,28},{14,30},{16,0},... | collective-permute-start | bytes 393224 | tf_op jit(solution)/shard_map/ppermute | solution.py:328
  53.5 6.5 %collective-permute-start.12 = (f32[32,512]{1,0:T(8,128)S(1)}, f32[32,512]{1,0:T(8,128)S(1)}, u32[]{:S(2)}, u32[]{:S(2)}) collective-permute-start(f32[32,512]{1,0:T(8,128)S(1)} %get-tuple-element.69), channel_id=1, source_target_pairs={{0,30},{2,4},{4,2},{6,8},{8,6},{10,12},{12,10},{14,16},{16,14},{18... | collective-permute-start | bytes 196616 | tf_op jit(solution)/shard_map/ppermute | solution.py:331
  55.8 4.1 %collective-permute-start.13 = (f32[32,512]{1,0:T(8,128)S(1)}, f32[32,512]{1,0:T(8,128)S(1)}, u32[]{:S(2)}, u32[]{:S(2)}) collective-permute-start(f32[32,512]{1,0:T(8,128)S(1)} %get-tuple-element.70), channel_id=1, source_target_pairs={{0,2},{2,0},{4,6},{6,4},{8,10},{10,8},{12,14},{14,12},{16,18},{18,... | collective-permute-start | bytes 196616 | tf_op jit(solution)/shard_map/ppermute | solution.py:334

commit v5 on v4

--- a/solution.py
+++ b/solution.py
@@ -37,7 +37,7 @@
     return dot(a, top) + dot(a, low)
 
 
-def call(body, outs, *args, limit=16, **rest):
+def call(body, outs, *args, limit=8, **rest):
     return pl.pallas_call(
         body,
         out_shape=[jax.ShapeDtypeStruct(*out) for out in outs],
@@ -45,6 +45,10 @@
         cost_estimate=pl.CostEstimate(flops=1000, bytes_accessed=1000, transcendentals=0),
         **rest,
     )(*args)
+
+
+def in_hbm(x):
+    return pltpu.with_memory_space_constraint(x, pltpu.HBM)
 
 
 def column(row, width):
@@ -95,9 +99,11 @@
 
 
 def assemble(
-    odd, lists, connect, blocks, shuffle, origin, top_out, low_out, pick_out, both_out, hits_out, pair_out,
-    spread, rows_top, rows_low,
+    odd, lists, connect, blocks_in, shuffle, origin, top_out, low_out, pick_out, both_out, hits_out, pair_out,
+    blocks, sem, spread, rows_top, rows_low,
 ):
+    copy = pltpu.make_async_copy(blocks_in, blocks, sem)
+    copy.start()
     elems, size = connect.shape
     slots, halo = lists.shape[1:]
     nodes = origin.shape[0]
@@ -122,6 +128,7 @@
     )
     numbers = jnp.concatenate([origin[...], nodes + ghost], 0)
     pitch = spread.shape[1] // elems
+    copy.wait()
     for elem in range(elems):
         cols = slice(elem * pitch, (elem + 1) * pitch)
         wanted = jnp.pad(connect[elem : elem + 1, :], ((0, 0), (0, pitch - size)), constant_values=-1)
@@ -351,7 +358,7 @@
     edge, rest, shuffle, origin = call(
         renumber,
         [((depth, wide), F32), ((depth, nodes - wide), F32), ((nodes, nodes), BF16), ((nodes, 1), I32)],
-        send_rows, subspace,
+        in_hbm(send_rows), in_hbm(subspace),
         in_specs=[hbm, hbm],
         scratch_shapes=[
             pltpu.VMEM(send_rows.shape, I32),
@@ -374,9 +381,12 @@
             ((wide, nodes), BF16),
             ((duo, 2 * duo), F32),
         ],
-        odd, send_rows, connect, blocks, shuffle, origin,
-        in_specs=[smem] + [vmem] * 5,
+        odd, send_rows, connect, in_hbm(blocks), shuffle, origin,
+        limit=12,
+        in_specs=[smem, vmem, vmem, hbm, vmem, vmem],
         scratch_shapes=[
+            pltpu.VMEM(blocks.shape, F32),
+            pltpu.SemaphoreType.DMA,
             pltpu.VMEM((full, elems * pitch), BF16),
             pltpu.VMEM((elems * pitch, full), BF16),
             pltpu.VMEM((elems * pitch, full), BF16),
@@ -390,8 +400,8 @@
             ((block, others * depth), BF16),
             ((block, others * depth), BF16),
         ],
-        group, edge, rest, ritz,
-        limit=24,
+        group, edge, rest, in_hbm(ritz),
+        limit=12,
         in_specs=[smem, vmem, vmem, hbm],
         scratch_shapes=[
             pltpu.VMEM((groups, block, depth), F32),

time: 61.4 us -> 60.1 us (0.979)
  local copies, waits for them, and re-layouts: 5.31 us -> 0.01 us
  Pallas kernels: 18.7 us -> 20.9 us
  waiting for transfers between devices: 19.5 us -> 21.4 us
    unnamed x12 -> x4, local copies, waits for them, and re-layouts: 5.31 us -> 0.01 us
    pallas_call x14, Pallas kernels: 18.7 us -> 20.9 us  [call(): pl.pallas_call(body, out_shape=[jax.ShapeDtypeStruct(*out) for out in out...]
    ppermute x2, waiting for transfers between devices: 1.82 us -> 3.72 us  [gather(): lax.ppermute(rows, 'state', [(i, (i + step) % groups) for i in range(grou...]
  transfers between devices with their start and end apart: 14 -> 14, of which waited for: 5 -> 5; matrix products, arithmetic and copies ran while one was open for 0% -> 0% of each run, Pallas kernels for 22% -> 25%
where the time goes in v5:
time: 60.1 us; the launch traced here: 59.8 us
  waiting for transfers between devices  21.4 us (36%)
  Pallas kernels  20.9 us (35%)
  starting transfers between devices  17.4 us (29%)
    pallas_call x14, Pallas kernels, call(): pl.pallas_call(body, out_shape=[jax.ShapeDtypeStruct(*out) for out in out...  20.9 us
    ppermute x4, waiting for transfers between devices, out(): return lax.ppermute(rows, 'mesh', pairs_out)  17.6 us
    ppermute x4, starting transfers between devices, far(): return lax.ppermute(rows, 'mesh', pairs_far)  8.56 us
    ppermute x4, starting transfers between devices, out(): return lax.ppermute(rows, 'mesh', pairs_out)  4.16 us
    ppermute x2, waiting for transfers between devices, gather(): lax.ppermute(rows, 'state', [(i, (i + step) % groups) for i in range(grou...  3.72 us
    ppermute x2, starting transfers between devices, gather(): lax.ppermute(rows, 'state', [(i, (i + step) % groups) for i in range(grou...  3.11 us
    ppermute x4, starting transfers between devices, near(): return lax.ppermute(rows, 'mesh', pairs_in)  1.61 us
  transfers between devices with their start and end apart: 14, of which 5 were waited for; matrix products, arithmetic and copies ran while one was open for 0% of the time, Pallas kernels for 25%

profile of v5, /device:TPU:0, one launch (start us, length us, event | category | flops | bytes accessed | tf_op | source)
XLA Modules:
  0.0 59.8 jit_solution(13980272157240986916)
XLA Ops:
  0.0 3.4 %shard_map.55 = (f32[1024,128]{1,0:T(8,128)}, f32[1024,128]{1,0:T(8,128)}, bf16[256,256]{1,0:T(8,128)(2,1)S(1)}, s32[256,1]{1,0:T(8,128)S(1)}) custom-call(s32[1,4,32]{2,1,0:T(4,128)} %lists.1, f32[1024,256]{1,0:T(8,128)} %subspace_in.1), custom_call_target="tpu_custom_call" | custom-call | flops 1000 | bytes 1000 | tf_op jit(solution)/shard_map/pallas_call | solution.py:41
  3.4 3.0 %collective-permute-start = (f32[1024,128]{1,0:T(8,128)}, f32[1024,128]{1,0:T(8,128)}, u32[]{:S(2)}, u32[]{:S(2)}) collective-permute-start(f32[1024,128]{1,0:T(8,128)} %get-tuple-element.38.edge), channel_id=1, source_target_pairs={{0,1},{1,0},{2,3},{3,2},{4,5},{5,4},{6,7},{7,6},{8,9},{9,8},{10,11... | collective-permute-start | bytes 1572872 | tf_op jit(solution)/shard_map/ppermute | solution.py:345
  6.6 4.7 %shard_map.56 = (f32[512,256]{1,0:T(8,128)S(1)}, bf16[512,1024]{1,0:T(8,128)(2,1)S(1)}, bf16[512,1024]{1,0:T(8,128)(2,1)S(1)}) custom-call(s32[1]{0:T(128)} %bitcast.group, f32[1024,128]{1,0:T(8,128)} %get-tuple-element.38.edge, f32[1024,128]{1,0:T(8,128)} %get-tuple-element.39.rest, f32[512,2048]{1,0:T(8,128)} %ritz_in.1), custom_call_target="tpu_custom_call" | custom-call | flops 1000 | bytes 1000 | tf_op jit(solution)/shard_map/pallas_call | solution.py:41
  11.3 4.6 %shard_map.57 = (bf16[384,384]{1,0:T(8,128)(2,1)S(1)}, bf16[384,384]{1,0:T(8,128)(2,1)S(1)}, bf16[128,128]{1,0:T(8,128)(2,1)S(1)}, bf16[128,128]{1,0:T(8,128)(2,...) custom-call(s32[1]{0:T(128)} %bitcast.1.odd, s32[1,4,32]{2,1,0:T(4,128)S(1)} %copy-done.1, ...), custom_call_target="tpu_custom_call" | custom-call | flops 1000 | bytes 1000 | tf_op jit(solution)/shard_map/pallas_call | solution.py:41
  15.8 3.7 %collective-permute-done.columns = f32[1024,128]{1,0:T(8,128)} collective-permute-done((f32[1024,128]{1,0:T(8,128)}, f32[1024,128]{1,0:T(8,128)}, u32[]{:S(2)}, u32[]{:S(2)}) %collective-permute-start) | collective-permute-done | bytes 524320 | tf_op jit(solution)/shard_map/ppermute | solution.py:345
  19.6 2.0 %shard_map.58 = (f32[128,512]{1,0:T(8,128)S(1)}, f32[64,640]{1,0:T(8,128)S(1)}, f32[32,512]{1,0:T(8,128)S(1)}, f32[32,512]{1,0:T(8,128)S(1)}) custom-call(f32[1024,128]{1,0:T(8,128)} %collective-permute-done.columns, f32[512,256]{1,0:T(8,128)S(1)} %get-tuple-element.40.start_own, bf16[512,1024]{1,0:T(8,128)(2,1)S(1)} %get-tuple-element.41.top, ...), custom_call_target="tpu_custom_call" | custom-call | flops 1000 | bytes 1000 | tf_op jit(solution)/shard_map/pallas_call | solution.py:41
  21.6 3.2 %collective-permute-start.2 = (f32[64,640]{1,0:T(8,128)S(1)}, f32[64,640]{1,0:T(8,128)S(1)}, u32[]{:S(2)}, u32[]{:S(2)}) collective-permute-start(f32[64,640]{1,0:T(8,128)S(1)} %get-tuple-element.48), channel_id=1, source_target_pairs={{0,16},{2,18},{4,20},{6,22},{8,24},{10,26},{12,28},{14,30},{16,0},... | collective-permute-start | bytes 491528 | tf_op jit(solution)/shard_map/ppermute | solution.py:335
  24.8 1.6 %collective-permute-start.4 = (f32[32,512]{1,0:T(8,128)S(1)}, f32[32,512]{1,0:T(8,128)S(1)}, u32[]{:S(2)}, u32[]{:S(2)}) collective-permute-start(f32[32,512]{1,0:T(8,128)S(1)} %get-tuple-element.50), channel_id=1, source_target_pairs={{0,2},{2,0},{4,6},{6,4},{8,10},{10,8},{12,14},{14,12},{16,18},{18,... | collective-permute-start | bytes 196616 | tf_op jit(solution)/shard_map/ppermute | solution.py:341
  26.4 4.8 %collective-permute-done.3.out_in = f32[32,512]{1,0:T(8,128)S(1)} collective-permute-done((f32[32,512]{1,0:T(8,128)S(1)}, f32[32,512]{1,0:T(8,128)S(1)}, u32[]{:S(2)}, u32[]{:S(2)}) %collective-permute-start.3) | collective-permute-done | bytes 65568 | tf_op jit(solution)/shard_map/ppermute | solution.py:338
  31.2 0.8 %shard_map.59.part = f32[384,512]{1,0:T(8,128)S(1)} custom-call(f32[128,512]{1,0:T(8,128)S(1)} %get-tuple-element.47.start_edge, f32[64,640]{1,0:T(8,128)S(1)} %collective-permute-done.2.far_in.pair_in, f32[32,512]{1,0:T(8,128)S(1)} %collective-permute-done.3.out_in, f32[32,512]{1,0:T(8,128)S(1)} %collective-permute-done.4.near_in, ...), custom_call_target="tpu_custom_call" | custom-call | flops 1000 | bytes 1000 | tf_op jit(solution)/shard_map/pallas_call | solution.py:41
  32.0 1.0 %shard_map.60 = (f32[128,512]{1,0:T(8,128)S(1)}, f32[64,512]{1,0:T(8,128)S(1)}, f32[32,512]{1,0:T(8,128)S(1)}, f32[32,512]{1,0:T(8,128)S(1)}) custom-call(f32[1024,128]{1,0:T(8,128)S(1)} %collective-permute-done.1.columns, f32[512,256]{1,0:T(8,128)S(1)} %get-tuple-element.40.start_own, bf16[512,1024]{1,0:T(8,128)(2,1)S(1)} %get-tuple-element.41.top, ...), custom_call_target="tpu_custom_call" | custom-call | flops 1000 | bytes 1000 | tf_op jit(solution)/shard_map/pallas_call | solution.py:41
  33.0 2.8 %collective-permute-start.5 = (f32[64,512]{1,0:T(8,128)S(1)}, f32[64,512]{1,0:T(8,128)S(1)}, u32[]{:S(2)}, u32[]{:S(2)}) collective-permute-start(f32[64,512]{1,0:T(8,128)S(1)} %get-tuple-element.54.back_far), channel_id=1, source_target_pairs={{0,16},{2,18},{4,20},{6,22},{8,24},{10,26},{12,28},{14,30},{16,0},... | collective-permute-start | bytes 393224 | tf_op jit(solution)/shard_map/ppermute | solution.py:335
  35.8 0.4 collective-permute-start.6
  36.2 0.6 %shard_map.61 = (f32[256,512]{1,0:T(8,128)S(1)}, f32[256,512]{1,0:T(8,128)S(1)}, f32[128,512]{1,0:T(8,128)S(1)}, f32[64,512]{1,0:T(8,128)S(1)}) custom-call(f32[128,512]{1,0:T(8,128)S(1)} %get-tuple-element.47.start_edge, f32[128,512]{1,0:T(8,128)S(1)} %get-tuple-element.53.start_rest, f32[384,512]{1,0:T(8,128)S(1)} %shard_map.59.part, ...), custom_call_target="tpu_custom_call" | custom-call | flops 1000 | bytes 1000 | tf_op jit(solution)/shard_map/pallas_call | solution.py:41
  36.8 5.4 %collective-permute-done.6.out_in = f32[32,512]{1,0:T(8,128)S(1)} collective-permute-done((f32[32,512]{1,0:T(8,128)S(1)}, f32[32,512]{1,0:T(8,128)S(1)}, u32[]{:S(2)}, u32[]{:S(2)}) %collective-permute-start.6) | collective-permute-done | bytes 65568 | tf_op jit(solution)/shard_map/ppermute | solution.py:338
  42.5 0.8 %collective-permute-start.8 = (f32[64,512]{1,0:T(8,128)S(1)}, f32[64,512]{1,0:T(8,128)S(1)}, u32[]{:S(2)}, u32[]{:S(2)}) collective-permute-start(f32[64,512]{1,0:T(8,128)S(1)} %shard_map.63), channel_id=1, source_target_pairs={{0,16},{2,18},{4,20},{6,22},{8,24},{10,26},{12,28},{14,30},{16,0},... | collective-permute-start | bytes 393224 | tf_op jit(solution)/shard_map/ppermute | solution.py:335
  43.5 1.4 %collective-permute-start.9 = (f32[32,512]{1,0:T(8,128)S(1)}, f32[32,512]{1,0:T(8,128)S(1)}, u32[]{:S(2)}, u32[]{:S(2)}) collective-permute-start(f32[32,512]{1,0:T(8,128)S(1)} %get-tuple-element.62), channel_id=1, source_target_pairs={{0,30},{2,4},{4,2},{6,8},{8,6},{10,12},{12,10},{14,16},{16,14},{18... | collective-permute-start | bytes 196616 | tf_op jit(solution)/shard_map/ppermute | solution.py:338
  44.9 0.9 %shard_map.62 = (f32[256,512]{1,0:T(8,128)S(1)}, f32[384,512]{1,0:T(8,128)S(1)}, f32[64,512]{1,0:T(8,128)S(1)}) custom-call(f32[256,512]{1,0:T(8,128)S(1)} %get-tuple-element.55.base, bf16[128,128]{1,0:T(8,128)(2,1)S(1)} %get-tuple-element.45.pick, f32[64,512]{1,0:T(8,128)S(1)} %collective-permute-done.5.far_in, ...), custom_call_target="tpu_custom_call" | custom-call | flops 1000 | bytes 1000 | tf_op jit(solution)/shard_map/pallas_call | solution.py:41
  45.8 4.1 %collective-permute-done.9.out_in = f32[32,512]{1,0:T(8,128)S(1)} collective-permute-done((f32[32,512]{1,0:T(8,128)S(1)}, f32[32,512]{1,0:T(8,128)S(1)}, u32[]{:S(2)}, u32[]{:S(2)}) %collective-permute-start.9) | collective-permute-done | bytes 65568 | tf_op jit(solution)/shard_map/ppermute | solution.py:338
  50.2 1.8 %collective-permute-start.11 = (f32[64,512]{1,0:T(8,128)S(1)}, f32[64,512]{1,0:T(8,128)S(1)}, u32[]{:S(2)}, u32[]{:S(2)}) collective-permute-start(f32[64,512]{1,0:T(8,128)S(1)} %shard_map.67), channel_id=1, source_target_pairs={{0,16},{2,18},{4,20},{6,22},{8,24},{10,26},{12,28},{14,30},{16,0},... | collective-permute-start | bytes 393224 | tf_op jit(solution)/shard_map/ppermute | solution.py:335
  52.2 2.3 %collective-permute-start.12 = (f32[32,512]{1,0:T(8,128)S(1)}, f32[32,512]{1,0:T(8,128)S(1)}, u32[]{:S(2)}, u32[]{:S(2)}) collective-permute-start(f32[32,512]{1,0:T(8,128)S(1)} %get-tuple-element.69), channel_id=1, source_target_pairs={{0,30},{2,4},{4,2},{6,8},{8,6},{10,12},{12,10},{14,16},{16,14},{18... | collective-permute-start | bytes 196616 | tf_op jit(solution)/shard_map/ppermute | solution.py:338
  54.6 0.8 %shard_map.66.result = f32[512,256]{1,0:T(8,128)S(1)} custom-call(f32[384,512]{1,0:T(8,128)S(1)} %get-tuple-element.58.part, f32[128,512]{1,0:T(8,128)S(1)} %get-tuple-element.64.ghosts, bf16[384,384]{1,0:T(8,128)(2,1)S(1)} %get-tuple-element.51.ham_top, bf16[384,384]{1,0:T(8,128)(2,1)S(1)} %get-tuple-element.52.ham_low, ...), custom_call_target="tpu_custom_call" | custom-call | flops 1000 | bytes 1000 | tf_op jit(solution)/shard_map/pallas_call | solution.py:41
  55.4 3.3 %collective-permute-done.12.out_in = f32[32,512]{1,0:T(8,128)S(1)} collective-permute-done((f32[32,512]{1,0:T(8,128)S(1)}, f32[32,512]{1,0:T(8,128)S(1)}, u32[]{:S(2)}, u32[]{:S(2)}) %collective-permute-start.12) | collective-permute-done | bytes 65568 | tf_op jit(solution)/shard_map/ppermute | solution.py:338
  58.7 1.1 %shard_map.68 = f32[512,256]{1,0:T(8,128)} custom-call(f32[512,256]{1,0:T(8,128)S(1)} %shard_map.66.result, bf16[128,256]{1,0:T(8,128)(2,1)S(1)} %get-tuple-element.68.hits, f32[64,512]{1,0:T(8,128)S(1)} %collective-permute-done.11.far_in, f32[32,512]{1,0:T(8,128)S(1)} %collective-permute-done.12.out_in, f32[32,512]{1,0:T(8,128)S(1)} %collective-permute-done.13.near_in), custom_call_target="tpu_custom_call" | custom-call | flops 1000 | bytes 1000 | tf_op jit(solution)/shard_map/pallas_call | solution.py:41
  (22 shorter events, 1.0 us)
Async XLA Ops:
  0.0 11.2 %copy-start.1 = (s32[1,4,32]{2,1,0:T(4,128)S(1)}, s32[1,4,32]{2,1,0:T(4,128)}, u32[]{:S(2)}) copy-start(s32[1,4,32]{2,1,0:T(4,128)} %lists.1) | copy-start | bytes 1540
  0.0 11.2 %copy-start = (s32[16,125]{1,0:T(8,128)S(1)}, s32[16,125]{1,0:T(8,128)}, u32[]{:S(2)}) copy-start(s32[16,125]{1,0:T(8,128)} %connect.1) | copy-start | bytes 24004
  3.4 16.1 %collective-permute-start = (f32[1024,128]{1,0:T(8,128)}, f32[1024,128]{1,0:T(8,128)}, u32[]{:S(2)}, u32[]{:S(2)}) collective-permute-start(f32[1024,128]{1,0:T(8,128)} %get-tuple-element.38.edge), channel_id=1, source_target_pairs={{0,1},{1,0},{2,3},{3,2},{4,5},{5,4},{6,7},{7,6},{8,9},{9,8},{10,11... | collective-permute-start | bytes 1572872 | tf_op jit(solution)/shard_map/ppermute | solution.py:345
  6.5 25.5 %collective-permute-start.1 = (f32[1024,128]{1,0:T(8,128)}, f32[1024,128]{1,0:T(8,128)S(1)}, u32[]{:S(2)}, u32[]{:S(2)}) collective-permute-start(f32[1024,128]{1,0:T(8,128)} %get-tuple-element.39.rest), channel_id=1, source_target_pairs={{0,1},{1,0},{2,3},{3,2},{4,5},{5,4},{6,7},{7,6},{8,9},{9,8},{10,11... | collective-permute-start | bytes 1572872 | tf_op jit(solution)/shard_map/ppermute | solution.py:345
  21.6 9.6 %collective-permute-start.2 = (f32[64,640]{1,0:T(8,128)S(1)}, f32[64,640]{1,0:T(8,128)S(1)}, u32[]{:S(2)}, u32[]{:S(2)}) collective-permute-start(f32[64,640]{1,0:T(8,128)S(1)} %get-tuple-element.48), channel_id=1, source_target_pairs={{0,16},{2,18},{4,20},{6,22},{8,24},{10,26},{12,28},{14,30},{16,0},... | collective-permute-start | bytes 491528 | tf_op jit(solution)/shard_map/ppermute | solution.py:335
  24.8 6.4 %collective-permute-start.3 = (f32[32,512]{1,0:T(8,128)S(1)}, f32[32,512]{1,0:T(8,128)S(1)}, u32[]{:S(2)}, u32[]{:S(2)}) collective-permute-start(f32[32,512]{1,0:T(8,128)S(1)} %get-tuple-element.49), channel_id=1, source_target_pairs={{0,30},{2,4},{4,2},{6,8},{8,6},{10,12},{12,10},{14,16},{16,14},{18... | collective-permute-start | bytes 196616 | tf_op jit(solution)/shard_map/ppermute | solution.py:338
  24.8 6.4 %collective-permute-start.4 = (f32[32,512]{1,0:T(8,128)S(1)}, f32[32,512]{1,0:T(8,128)S(1)}, u32[]{:S(2)}, u32[]{:S(2)}) collective-permute-start(f32[32,512]{1,0:T(8,128)S(1)} %get-tuple-element.50), channel_id=1, source_target_pairs={{0,2},{2,0},{4,6},{6,4},{8,10},{10,8},{12,14},{14,12},{16,18},{18,... | collective-permute-start | bytes 196616 | tf_op jit(solution)/shard_map/ppermute | solution.py:341
  33.0 10.3 %collective-permute-start.5 = (f32[64,512]{1,0:T(8,128)S(1)}, f32[64,512]{1,0:T(8,128)S(1)}, u32[]{:S(2)}, u32[]{:S(2)}) collective-permute-start(f32[64,512]{1,0:T(8,128)S(1)} %get-tuple-element.54.back_far), channel_id=1, source_target_pairs={{0,16},{2,18},{4,20},{6,22},{8,24},{10,26},{12,28},{14,30},{16,0},... | collective-permute-start | bytes 393224 | tf_op jit(solution)/shard_map/ppermute | solution.py:335
  35.8 6.5 %collective-permute-start.6 = (f32[32,512]{1,0:T(8,128)S(1)}, f32[32,512]{1,0:T(8,128)S(1)}, u32[]{:S(2)}, u32[]{:S(2)}) collective-permute-start(f32[32,512]{1,0:T(8,128)S(1)} %get-tuple-element.56), channel_id=1, source_target_pairs={{0,30},{2,4},{4,2},{6,8},{8,6},{10,12},{12,10},{14,16},{16,14},{18... | collective-permute-start | bytes 196616 | tf_op jit(solution)/shard_map/ppermute | solution.py:338
  36.2 6.1 %collective-permute-start.7 = (f32[32,512]{1,0:T(8,128)S(1)}, f32[32,512]{1,0:T(8,128)S(1)}, u32[]{:S(2)}, u32[]{:S(2)}) collective-permute-start(f32[32,512]{1,0:T(8,128)S(1)} %get-tuple-element.57), channel_id=1, source_target_pairs={{0,2},{2,0},{4,6},{6,4},{8,10},{10,8},{12,14},{14,12},{16,18},{18,... | collective-permute-start | bytes 196616 | tf_op jit(solution)/shard_map/ppermute | solution.py:341
  42.5 9.5 %collective-permute-start.8 = (f32[64,512]{1,0:T(8,128)S(1)}, f32[64,512]{1,0:T(8,128)S(1)}, u32[]{:S(2)}, u32[]{:S(2)}) collective-permute-start(f32[64,512]{1,0:T(8,128)S(1)} %shard_map.63), channel_id=1, source_target_pairs={{0,16},{2,18},{4,20},{6,22},{8,24},{10,26},{12,28},{14,30},{16,0},... | collective-permute-start | bytes 393224 | tf_op jit(solution)/shard_map/ppermute | solution.py:335
  43.5 6.5 %collective-permute-start.9 = (f32[32,512]{1,0:T(8,128)S(1)}, f32[32,512]{1,0:T(8,128)S(1)}, u32[]{:S(2)}, u32[]{:S(2)}) collective-permute-start(f32[32,512]{1,0:T(8,128)S(1)} %get-tuple-element.62), channel_id=1, source_target_pairs={{0,30},{2,4},{4,2},{6,8},{8,6},{10,12},{12,10},{14,16},{16,14},{18... | collective-permute-start | bytes 196616 | tf_op jit(solution)/shard_map/ppermute | solution.py:338
  44.9 5.0 %collective-permute-start.10 = (f32[32,512]{1,0:T(8,128)S(1)}, f32[32,512]{1,0:T(8,128)S(1)}, u32[]{:S(2)}, u32[]{:S(2)}) collective-permute-start(f32[32,512]{1,0:T(8,128)S(1)} %get-tuple-element.63), channel_id=1, source_target_pairs={{0,2},{2,0},{4,6},{6,4},{8,10},{10,8},{12,14},{14,12},{16,18},{18,... | collective-permute-start | bytes 196616 | tf_op jit(solution)/shard_map/ppermute | solution.py:341
  50.2 8.5 %collective-permute-start.11 = (f32[64,512]{1,0:T(8,128)S(1)}, f32[64,512]{1,0:T(8,128)S(1)}, u32[]{:S(2)}, u32[]{:S(2)}) collective-permute-start(f32[64,512]{1,0:T(8,128)S(1)} %shard_map.67), channel_id=1, source_target_pairs={{0,16},{2,18},{4,20},{6,22},{8,24},{10,26},{12,28},{14,30},{16,0},... | collective-permute-start | bytes 393224 | tf_op jit(solution)/shard_map/ppermute | solution.py:335
  52.2 6.5 %collective-permute-start.12 = (f32[32,512]{1,0:T(8,128)S(1)}, f32[32,512]{1,0:T(8,128)S(1)}, u32[]{:S(2)}, u32[]{:S(2)}) collective-permute-start(f32[32,512]{1,0:T(8,128)S(1)} %get-tuple-element.69), channel_id=1, source_target_pairs={{0,30},{2,4},{4,2},{6,8},{8,6},{10,12},{12,10},{14,16},{16,14},{18... | collective-permute-start | bytes 196616 | tf_op jit(solution)/shard_map/ppermute | solution.py:338
  54.5 4.1 %collective-permute-start.13 = (f32[32,512]{1,0:T(8,128)S(1)}, f32[32,512]{1,0:T(8,128)S(1)}, u32[]{:S(2)}, u32[]{:S(2)}) collective-permute-start(f32[32,512]{1,0:T(8,128)S(1)} %get-tuple-element.70), channel_id=1, source_target_pairs={{0,2},{2,0},{4,6},{6,4},{8,10},{10,8},{12,14},{14,12},{16,18},{18,... | collective-permute-start | bytes 196616 | tf_op jit(solution)/shard_map/ppermute | solution.py:341

commit v6 on v5

--- a/solution.py
+++ b/solution.py
@@ -1,3 +1,5 @@
+import functools
+
 import jax
 import jax.numpy as jnp
 from jax import lax
@@ -37,10 +39,10 @@
     return dot(a, top) + dot(a, low)
 
 
-def call(body, outs, *args, limit=8, **rest):
+def call(body, outs, *args, limit=8, kept=False, **rest):
     return pl.pallas_call(
         body,
-        out_shape=[jax.ShapeDtypeStruct(*out) for out in outs],
+        out_shape=[pltpu.VMEM(*out) if kept else jax.ShapeDtypeStruct(*out) for out in outs],
         compiler_params=pltpu.CompilerParams(vmem_limit_bytes=limit << 20),
         cost_estimate=pl.CostEstimate(flops=1000, bytes_accessed=1000, transcendentals=0),
         **rest,
@@ -51,51 +53,65 @@
     return pltpu.with_memory_space_constraint(x, pltpu.HBM)
 
 
+def in_vmem(x):
+    return pltpu.with_memory_space_constraint(x, pltpu.VMEM)
+
+
 def column(row, width):
     down = lax.broadcasted_iota(I32, (width, width), 0)
     along = lax.broadcasted_iota(I32, (width, width), 1)
     return jnp.sum(jnp.where(down == along, row, 0), axis=1, keepdims=True)
 
 
-def renumber(lists_in, subspace_in, edge_out, rest_out, shuffle_out, origin_out, lists, subspace, sems):
+def renumber(
+    lists_in, subspace_in, far_out, ring_out, low_out, high_out, shuffle_out, origin_out, lists, subspace, sems
+):
     slots, halo = lists.shape[1:]
     depth, nodes = subspace.shape
-    wide = slots * halo
-    parts = sems.shape[0] - 1
-    span = depth // parts
-    index_copy = pltpu.make_async_copy(lists_in, lists, sems.at[parts])
+    duo = 2 * halo
+    span = depth // 2
+    index_copy = pltpu.make_async_copy(lists_in, lists, sems.at[0])
     index_copy.start()
-    copies = []
-    for part in range(parts):
-        rows = pl.ds(part * span, span)
-        copies.append(
-            pltpu.make_async_copy(subspace_in.at[rows], subspace.at[rows], sems.at[part])
-        )
-        copies[-1].start()
+    copy = pltpu.make_async_copy(subspace_in, subspace, sems.at[1])
+    copy.start()
     index_copy.wait()
     ids = lax.broadcasted_iota(I32, (halo, nodes), 1)
-    seen = jnp.zeros((halo, nodes), F32)
+    seen = []
     for slot in range(slots):
         sent = column(lists[0, slot : slot + 1, :], halo)
-        seen = jnp.maximum(seen, jnp.where(sent == ids, 1.0, 0.0))
-    edge = jnp.max(seen, axis=0, keepdims=True)
+        seen.append(jnp.where(sent == ids, 1.0, 0.0))
+    far = jnp.max(jnp.maximum(seen[2], seen[3]), axis=0, keepdims=True)
+    ring = jnp.max(jnp.maximum(seen[0], seen[1]), axis=0, keepdims=True) * (1.0 - far)
     down = lax.broadcasted_iota(I32, (nodes, nodes), 0)
     along = lax.broadcasted_iota(I32, (nodes, nodes), 1)
     upto = jnp.where(down <= along, 1.0, 0.0).astype(BF16)
-    count = dot(jnp.broadcast_to(edge, (8, nodes)).astype(BF16), upto)[:1].astype(I32)
-    total = jnp.sum(edge, axis=1, keepdims=True).astype(I32)
-    place = jnp.where(edge > 0.5, count - 1, total + along[:1] - count)
+    flags = jnp.concatenate([far, ring, jnp.zeros((6, nodes), F32)], 0)
+    counts = dot(flags.astype(BF16), upto).astype(I32)
+    far_count, ring_count = counts[0:1], counts[1:2]
+    totals = jnp.sum(flags, axis=1, keepdims=True).astype(I32)
+    far_total, ring_total = totals[0:1], totals[1:2]
+    place = jnp.where(
+        far > 0.5,
+        far_count - 1,
+        jnp.where(
+            ring > 0.5,
+            far_total + ring_count - 1,
+            far_total + ring_total + along[:1] - far_count - ring_count,
+        ),
+    )
     match = place == down
     shuffle = jnp.where(match, 1.0, 0.0).astype(BF16)
     shuffle_out[...] = shuffle
     origin_out[...] = jnp.sum(jnp.where(match, along, 0), axis=1, keepdims=True)
-    for part in range(parts):
-        rows = slice(part * span, (part + 1) * span)
-        copies[part].wait()
-        top, low = split(subspace[rows, :])
+    copy.wait()
+    halves = []
+    for part, rest_out in enumerate((low_out, high_out)):
+        top, low = split(subspace[part * span : (part + 1) * span, :])
         turned = dot(top, shuffle, NT) + dot(low, shuffle, NT)
-        edge_out[rows, :] = turned[:, :wide]
-        rest_out[rows, :] = turned[:, wide:]
+        rest_out[...] = turned[:, 2 * duo :]
+        halves.append(turned)
+    far_out[...] = jnp.concatenate([half[:, :duo] for half in halves], 1)
+    ring_out[...] = jnp.concatenate([half[:, duo : 2 * duo] for half in halves], 1)
 
 
 def assemble(
@@ -147,7 +163,7 @@
     pair_out[...] = jnp.concatenate([both[:duo, :duo], ham[far, far]], 1)
 
 
-def rotate_own(group, edge, rest, ritz_in, start_out, top_out, low_out, ritz, sems):
+def rotate_own(group, far, ring, low_rest, high_rest, ritz_in, start_out, top_out, low_out, ritz, sems):
     block, depth = ritz.shape[1:]
     groups = ritz.shape[0]
     parts = sems.shape[1]
@@ -164,7 +180,10 @@
                 )
             )
             copies[-1].start()
-    own = split(jnp.concatenate([edge[...], rest[...]], 1))
+    width = far.shape[1] // 2
+    columns = [jnp.concatenate([x[:, :width], x[:, width:]], 0) for x in (far, ring)]
+    rest = jnp.concatenate([low_rest[...], high_rest[...]], 0)
+    own = split(jnp.concatenate(columns + [rest], 1))
     for step in range(groups):
         for part in range(parts):
             rows = slice(part * span, (part + 1) * span)
@@ -185,36 +204,79 @@
     return wide[:, :width] + (wide[:, width:] + dot(low, high))
 
 
-def rotate_edge(columns, start_own, top, low, pick, pair, start_out, far_out, out_out, near_out):
-    edge_nodes = columns.shape[1]
-    wide, block = pick.shape[0], start_own.shape[0]
-    quarter = wide // 4
-    start = (start_own[:, :edge_nodes] + rotate(top[...], low[...], columns[...])).T
+def pieces(x, groups, part, axis):
+    span = x.shape[axis] // (2 * (groups - 1))
+    starts = [(2 * step + part) * span for step in range(groups - 1)]
+    if axis == 0:
+        return [x[start : start + span, :] for start in starts]
+    return [x[:, start : start + span] for start in starts]
+
+
+def rotate_sides(columns, top, low, groups):
+    width = columns.shape[1] // 2
+    span = columns.shape[0] // (groups - 1)
+    whole = jnp.concatenate(
+        [
+            columns[step * span : (step + 1) * span, part * width : (part + 1) * width]
+            for step in range(groups - 1)
+            for part in range(2)
+        ],
+        0,
+    )
+    return rotate(top[...], low[...], whole)
+
+
+def rotate_half(columns, top, low, groups, part):
+    return rotate(
+        jnp.concatenate(pieces(top, groups, part, 1), 1),
+        jnp.concatenate(pieces(low, groups, part, 1), 1),
+        columns[...],
+    )
+
+
+def rotate_far(groups, columns, start_own, top, low, pick, start_out, far_out):
+    duo = far_out.shape[0]
+    start = (start_own[:, :duo] + rotate_sides(columns, top, low, groups)).T
     start_out[...] = start
-    packed = sift(pick[...], start)
-    far_out[:, :block] = packed[: 2 * quarter]
-    far_out[:, block:] = pair[...]
-    out_out[...] = packed[2 * quarter : 3 * quarter]
-    near_out[...] = packed[3 * quarter :]
-
-
-def first_part(start_edge, far_in, out_in, near_in, ham_top, ham_low, part_out):
-    edge_nodes, block = start_edge.shape
+    far_out[...] = sift(pick[:duo, :duo], start)
+
+
+def rotate_ring(groups, columns, start_own, start_far, top, low, pick, start_out, out_out, near_out):
+    halo = out_out.shape[0]
+    duo = 2 * halo
+    start = (start_own[:, duo : 2 * duo] + rotate_sides(columns, top, low, groups)).T
+    start = jnp.concatenate([start_far[...], start], 0)
+    start_out[...] = start
+    packed = sift(pick[duo:, :], start)
+    out_out[...] = packed[:halo]
+    near_out[...] = packed[halo:]
+
+
+def rotate_low(groups, columns, start_own, top, low, rest_out):
+    edge_nodes = start_own.shape[1] - columns.shape[1]
+    rest_out[...] = start_own[:, edge_nodes:] + rotate_half(columns, top, low, groups, 0)
+
+
+def first_part(start_edge, far_in, out_in, near_in, ham_top, ham_low, pair_in, part_out, overlap_out, couple_out):
+    edge_nodes = start_edge.shape[0]
     nodes = ham_top.shape[0] - 4 * out_in.shape[0]
-    ghosts = jnp.concatenate([far_in[:, :block], out_in[...], near_in[...]], 0)
+    duo = far_in.shape[0]
+    ghosts = jnp.concatenate([far_in[...], out_in[...], near_in[...]], 0)
     part_out[...] = mul(
         (ham_top[:, :edge_nodes], ham_low[:, :edge_nodes]), split(start_edge[...])
     ) + mul((ham_top[:, nodes:], ham_low[:, nodes:]), split(ghosts))
+    overlap_out[...] = SCALE_ONE * pair_in[:, :duo]
+    couple_out[...] = pair_in[:, duo:]
 
 
 def rotate_rest(
-    columns, start_own, top, low, part, ham_top, ham_low, rest_out, far_out, out_out, near_out
+    groups, columns, rest_low, top, low, part, ham_top, ham_low, rest_out, far_out, out_out, near_out
 ):
-    nodes = start_own.shape[1]
-    edge_nodes = nodes - columns.shape[1]
+    rest = (rest_low[...] + rotate_half(columns, top, low, groups, 1)).T
+    rest_out[...] = rest
     halo = out_out.shape[0]
-    rest = (start_own[:, edge_nodes:] + rotate(top[...], low[...], columns[...])).T
-    rest_out[...] = rest
+    edge_nodes, width = part.shape[0] - 4 * halo - rest.shape[0], rest.shape[0]
+    nodes = edge_nodes + width
     cols = slice(edge_nodes, nodes)
     back = part[nodes:, :] + mul((ham_top[nodes:, cols], ham_low[nodes:, cols]), split(rest))
     far_out[...] = back[: 2 * halo]
@@ -223,12 +285,11 @@
 
 
 def first_base(
-    start_edge, start_rest, part, ham_top, ham_low, pick, far_in, back_far,
+    start_edge, start_rest, part, ham_top, ham_low, pick, overlap, back_far,
     start_out, base_out, packed_out, adjust_out,
 ):
     nodes = ham_top.shape[0] - pick.shape[0]
-    edge_nodes, block = start_edge.shape
-    duo = far_in.shape[0]
+    edge_nodes = start_edge.shape[0]
     cols = slice(edge_nodes, nodes)
     start = jnp.concatenate([start_edge[...], start_rest[...]], 0)
     start_out[...] = start
@@ -238,8 +299,7 @@
     base = SCALE_ONE * (own - CENTRE * start)
     base_out[...] = base
     packed_out[...] = sift(pick[...], base[:edge_nodes])
-    overlap = far_in[:, block : block + duo].astype(BF16)
-    adjust_out[...] = SCALE_ONE * sift(overlap, back_far[...])
+    adjust_out[...] = mul(split(overlap[...]), split(back_far[...]))
 
 
 def fetch_far(packed, both, out_in, near_in, far_out):
@@ -257,19 +317,17 @@
 
 
 def first_own(
-    base, pick, far_in, out_in, near_in, ham_top, ham_low, pair_in, first_out, part_out, known_out
+    base, pick, far_in, out_in, near_in, ham_top, ham_low, couple, first_out, part_out, known_out
 ):
     edge_nodes = pick.shape[1]
     nodes = base.shape[0]
-    block = base.shape[1]
     duo = far_in.shape[0]
     back = jnp.concatenate([far_in[...], out_in[...], near_in[...]], 0)
     edge = base[:edge_nodes, :] + SCALE_ONE * sift(pick[...].T, back)
     first = jnp.concatenate([edge, base[edge_nodes:, :]], 0)
     first_out[...] = first
     part_out[...] = mul((ham_top[:, :nodes], ham_low[:, :nodes]), split(first))
-    couple = split(pair_in[:, block + duo :])
-    known_out[...] = mul(couple, split(sift(pick[:duo, :], edge)))
+    known_out[...] = mul(split(couple[...]), split(sift(pick[:duo, :], edge)))
 
 
 def return_far(part, ham_top, ham_low, out_in, near_in, far_out):
@@ -355,19 +413,29 @@
     vmem = pl.BlockSpec(memory_space=pltpu.VMEM)
     hbm = pl.BlockSpec(memory_space=pltpu.HBM)
 
-    edge, rest, shuffle, origin = call(
+    far_cols, ring_cols, low_cols, high_cols, shuffle, origin = call(
         renumber,
-        [((depth, wide), F32), ((depth, nodes - wide), F32), ((nodes, nodes), BF16), ((nodes, 1), I32)],
+        [
+            ((depth // 2, 2 * duo), F32),
+            ((depth // 2, 2 * duo), F32),
+            ((depth // 2, nodes - wide), F32),
+            ((depth // 2, nodes - wide), F32),
+            ((nodes, nodes), BF16),
+            ((nodes, 1), I32),
+        ],
         in_hbm(send_rows), in_hbm(subspace),
+        kept=True,
         in_specs=[hbm, hbm],
         scratch_shapes=[
             pltpu.VMEM(send_rows.shape, I32),
             pltpu.VMEM(subspace.shape, F32),
-            pltpu.SemaphoreType.DMA((5,)),
-        ],
-    )
-    edge_in = gather(edge)
-    rest_in = gather(rest)
+            pltpu.SemaphoreType.DMA((2,)),
+        ],
+    )
+    far_cols_in = gather(far_cols)
+    ring_cols_in = gather(ring_cols)
+    low_cols_in = gather(low_cols)
+    high_cols_in = gather(high_cols)
     elems, size = connect.shape
     pitch = -(-size // 128) * 128
     blocks = jnp.transpose(element_ham, (1, 0, 2)).reshape(size * elems, size)
@@ -392,6 +460,7 @@
             pltpu.VMEM((elems * pitch, full), BF16),
         ],
     )
+    pair_in = far(pair)
     others = groups - 1
     start_own, ritz_top, ritz_low = call(
         rotate_own,
@@ -400,35 +469,48 @@
             ((block, others * depth), BF16),
             ((block, others * depth), BF16),
         ],
-        group, edge, rest, in_hbm(ritz),
+        group, far_cols, ring_cols, low_cols, high_cols, in_hbm(ritz),
         limit=12,
-        in_specs=[smem, vmem, vmem, hbm],
+        in_specs=[smem, vmem, vmem, vmem, vmem, hbm],
         scratch_shapes=[
             pltpu.VMEM((groups, block, depth), F32),
             pltpu.SemaphoreType.DMA((groups, 2)),
         ],
     )
 
-    start_edge, far_rows, out_rows, near_rows = call(
-        rotate_edge,
-        [rows_of(wide), ((duo, block + 2 * duo), F32), rows_of(halo), rows_of(halo)],
-        edge_in, start_own, ritz_top, ritz_low, pick, pair,
-    )
-    pair_in, out_in, near_in = far(far_rows), out(out_rows), near(near_rows)
-    (part,) = call(
-        first_part, [rows_of(full)], start_edge, pair_in, out_in, near_in, ham_top, ham_low
+    start_far, far_rows = call(
+        functools.partial(rotate_far, groups),
+        [rows_of(duo), rows_of(duo)],
+        in_vmem(far_cols_in), start_own, ritz_top, ritz_low, pick,
+    )
+    far_in = far(far_rows)
+    start_edge, out_rows, near_rows = call(
+        functools.partial(rotate_ring, groups),
+        [rows_of(wide), rows_of(halo), rows_of(halo)],
+        in_vmem(ring_cols_in), start_own, start_far, ritz_top, ritz_low, pick,
+    )
+    out_in, near_in = out(out_rows), near(near_rows)
+    part, overlap, couple = call(
+        first_part,
+        [rows_of(full), ((duo, duo), F32), ((duo, duo), F32)],
+        start_edge, far_in, out_in, near_in, ham_top, ham_low, pair_in,
+    )
+    (rest_low,) = call(
+        functools.partial(rotate_low, groups),
+        [((block, nodes - wide), F32)],
+        in_vmem(low_cols_in), start_own, ritz_top, ritz_low,
     )
 
     start_rest, back_far, back_out, back_near = call(
-        rotate_rest,
+        functools.partial(rotate_rest, groups),
         [rows_of(nodes - wide)] + halo_out,
-        rest_in, start_own, ritz_top, ritz_low, part, ham_top, ham_low,
+        in_vmem(high_cols_in), rest_low, ritz_top, ritz_low, part, ham_top, ham_low,
     )
     far_in, out_in, near_in = far(back_far), out(back_out), near(back_near)
     start, base, packed, adjust = call(
         first_base,
         [rows_of(nodes), rows_of(nodes), rows_of(wide), rows_of(duo)],
-        start_edge, start_rest, part, ham_top, ham_low, pick, pair_in, back_far,
+        start_edge, start_rest, part, ham_top, ham_low, pick, overlap, back_far,
     )
     (far_rows,) = call(fetch_far, [rows_of(duo)], packed, both, out_in, near_in)
     fetched_far = far(far_rows)
@@ -439,7 +521,7 @@
     first, part, known = call(
         first_own,
         [rows_of(nodes), rows_of(full), rows_of(duo)],
-        base, pick, far_in, out_in, near_in, ham_top, ham_low, pair_in,
+        base, pick, far_in, out_in, near_in, ham_top, ham_low, couple,
     )
 
     (far_rows,) = call(

time: 60.1 us -> 60.1 us (level)
  waiting for transfers between devices: 21.4 us -> 14.8 us
  starting transfers between devices: 17.4 us -> 21.8 us
  local copies, waits for them, and re-layouts: 0.01 us -> 1.54 us
    ppermute x4, waiting for transfers between devices: 17.6 us -> 12.4 us  [out(): return lax.ppermute(rows, 'mesh', pairs_out)]
    ppermute x2 -> x4, waiting for transfers between devices: 3.72 us -> 0.01 us  [gather(): lax.ppermute(rows, 'state', [(i, (i + step) % groups) for i in range(grou...]
    ppermute x4 -> x5, waiting for transfers between devices: 0.01 us -> 2.35 us  [far(): return lax.ppermute(rows, 'mesh', pairs_far)]
    ppermute x2 -> x4, starting transfers between devices: 3.11 us -> 5.04 us  [gather(): lax.ppermute(rows, 'state', [(i, (i + step) % groups) for i in range(grou...]
    ppermute x4 -> x5, starting transfers between devices: 8.56 us -> 10.5 us  [far(): return lax.ppermute(rows, 'mesh', pairs_far)]
    unnamed x4 -> x8, local copies, waits for them, and re-layouts: 0.01 us -> 1.54 us
    pallas_call x14 -> x16, Pallas kernels: 20.9 us -> 21.5 us  [call(): pl.pallas_call(body, out_shape=[pltpu.VMEM(*out) if kept else jax.ShapeDt...]
    ppermute x4, starting transfers between devices: 1.61 us -> 2.21 us  [near(): return lax.ppermute(rows, 'mesh', pairs_in)]
  transfers between devices with their start and end apart: 14 -> 17, of which waited for: 5 -> 4; matrix products, arithmetic and copies ran while one was open for 0% -> 0% of each run, Pallas kernels for 25% -> 27%
where the time goes in v6:
time: 60.1 us; the launch traced here: 59.8 us
  starting transfers between devices  21.8 us (36%)
  Pallas kernels  21.5 us (36%)
  waiting for transfers between devices  14.8 us (25%)
  local copies, waits for them, and re-layouts  1.54 us (3%)
    pallas_call x16, Pallas kernels, call(): pl.pallas_call(body, out_shape=[pltpu.VMEM(*out) if kept else jax.ShapeDt...  21.5 us
    ppermute x4, waiting for transfers between devices, out(): return lax.ppermute(rows, 'mesh', pairs_out)  12.4 us
    ppermute x5, starting transfers between devices, far(): return lax.ppermute(rows, 'mesh', pairs_far)  10.5 us
    ppermute x4, starting transfers between devices, gather(): lax.ppermute(rows, 'state', [(i, (i + step) % groups) for i in range(grou...  5.04 us
    ppermute x4, starting transfers between devices, out(): return lax.ppermute(rows, 'mesh', pairs_out)  4.08 us
    ppermute x5, waiting for transfers between devices, far(): return lax.ppermute(rows, 'mesh', pairs_far)  2.35 us
    ppermute x4, starting transfers between devices, near(): return lax.ppermute(rows, 'mesh', pairs_in)  2.21 us
    unnamed x8, local copies, waits for them, and re-layouts  1.54 us
  transfers between devices with their start and end apart: 17, of which 4 were waited for; matrix products, arithmetic and copies ran while one was open for 0% of the time, Pallas kernels for 27%

profile of v6, /device:TPU:0, one launch (start us, length us, event | category | flops | bytes accessed | tf_op | source)
XLA Modules:
  0.0 59.8 jit_solution(13199200230506636488)
XLA Ops:
  0.0 2.7 %shard_map.55 = (f32[512,128]{1,0:T(8,128)}, f32[512,128]{1,0:T(8,128)}, f32[512,128]{1,0:T(8,128)}, f32[512,128]{1,0:T(8,128)}, bf16[256,256]{1,0:T(8,128)(2,1)S(1)}, /*index=5*/s32[256,1]{1,0:T(8,128)S(1)}) custom-call(s32[1,4,32]{2,1,0:T(4,128)} %lists.1, f32[1024,256]{1,0:T(8,128)} %subspace_in.1), custom_call_target="tpu_custom_call" | custom-call | flops 1000 | bytes 1000 | tf_op jit(solution)/shard_map/pallas_call | solution.py:43
  3.4 3.0 %collective-permute-start.1 = (f32[512,128]{1,0:T(8,128)}, f32[512,128]{1,0:T(8,128)S(1)}, u32[]{:S(2)}, u32[]{:S(2)}) collective-permute-start(f32[512,128]{1,0:T(8,128)} %get-tuple-element.45.far), channel_id=1, source_target_pairs={{0,1},{1,0},{2,3},{3,2},{4,5},{5,4},{6,7},{7,6},{8,9},{9,8},{10,11... | collective-permute-start | bytes 786440 | tf_op jit(solution)/shard_map/ppermute | solution.py:403
  6.4 2.0 %collective-permute-start.3 = (f32[512,128]{1,0:T(8,128)}, f32[512,128]{1,0:T(8,128)S(1)}, u32[]{:S(2)}, u32[]{:S(2)}) collective-permute-start(f32[512,128]{1,0:T(8,128)} %get-tuple-element.46.low_rest), channel_id=1, source_target_pairs={{0,1},{1,0},{2,3},{3,2},{4,5},{5,4},{6,7},{7,6},{8,9},{9,8},{10,11... | collective-permute-start | bytes 786440 | tf_op jit(solution)/shard_map/ppermute | solution.py:403
  8.4 4.6 %shard_map.56 = (f32[512,256]{1,0:T(8,128)S(1)}, bf16[512,1024]{1,0:T(8,128)(2,1)S(1)}, bf16[512,1024]{1,0:T(8,128)(2,1)S(1)}) custom-call(s32[1]{0:T(128)} %bitcast.group, f32[512,128]{1,0:T(8,128)} %get-tuple-element.45.far, f32[512,128]{1,0:T(8,128)} %get-tuple-element.44.ring, f32[512,128]{1,0:T(8,128)} %get-tuple-element.46.low_rest, ...), custom_call_target="tpu_custom_call" | custom-call | flops 1000 | bytes 1000 | tf_op jit(solution)/shard_map/pallas_call | solution.py:43
  13.1 0.9 %copy-done.1 = s32[256,1]{1,0:T(8,128)S(1)} copy-done((s32[256,1]{1,0:T(8,128)S(1)}, s32[256,1]{1,0:T(8,128)}, u32[]{:S(2)}) %copy-start.1) | copy-done | bytes 1048
  14.0 4.6 %shard_map.57 = (bf16[384,384]{1,0:T(8,128)(2,1)S(1)}, bf16[384,384]{1,0:T(8,128)(2,1)S(1)}, bf16[128,128]{1,0:T(8,128)(2,1)S(1)}, bf16[128,128]{1,0:T(8,128)(2,...) custom-call(s32[1]{0:T(128)} %bitcast.1.odd, s32[1,4,32]{2,1,0:T(4,128)S(1)} %copy-done.3, ...), custom_call_target="tpu_custom_call" | custom-call | flops 1000 | bytes 1000 | tf_op jit(solution)/shard_map/pallas_call | solution.py:43
  18.6 1.1 %shard_map.58 = (f32[64,512]{1,0:T(8,128)S(1)}, f32[64,512]{1,0:T(8,128)S(1)}) custom-call(f32[512,128]{1,0:T(8,128)S(1)} %collective-permute-done.1.columns, f32[512,256]{1,0:T(8,128)S(1)} %get-tuple-element.48.start_own, bf16[512,1024]{1,0:T(8,128)(2,1)S(1)} %get-tuple-element.49.top, bf16[512,1024]{1,0:T(8,128)(2,1)S(1)} %get-tuple-element.50.low, ...), custom_call_target="tpu_custom_call" | custom-call | flops 1000 | bytes 1000 | tf_op jit(solution)/shard_map/pallas_call | solution.py:43
  19.7 3.1 %collective-permute-start.4 = (f32[64,512]{1,0:T(8,128)S(1)}, f32[64,512]{1,0:T(8,128)S(1)}, u32[]{:S(2)}, u32[]{:S(2)}) collective-permute-start(f32[64,512]{1,0:T(8,128)S(1)} %get-tuple-element.56), channel_id=1, source_target_pairs={{0,16},{2,18},{4,20},{6,22},{8,24},{10,26},{12,28},{14,30},{16,0},... | collective-permute-start | bytes 393224 | tf_op jit(solution)/shard_map/ppermute | solution.py:393
  22.8 1.2 %shard_map.59 = (f32[128,512]{1,0:T(8,128)S(1)}, f32[32,512]{1,0:T(8,128)S(1)}, f32[32,512]{1,0:T(8,128)S(1)}) custom-call(f32[512,128]{1,0:T(8,128)S(1)} %collective-permute-done.columns, f32[512,256]{1,0:T(8,128)S(1)} %get-tuple-element.48.start_own, f32[64,512]{1,0:T(8,128)S(1)} %get-tuple-element.54.start_far, ...), custom_call_target="tpu_custom_call" | custom-call | flops 1000 | bytes 1000 | tf_op jit(solution)/shard_map/pallas_call | solution.py:43
  24.4 1.3 %collective-permute-start.6 = (f32[32,512]{1,0:T(8,128)S(1)}, f32[32,512]{1,0:T(8,128)S(1)}, u32[]{:S(2)}, u32[]{:S(2)}) collective-permute-start(f32[32,512]{1,0:T(8,128)S(1)} %get-tuple-element.58), channel_id=1, source_target_pairs={{0,2},{2,0},{4,6},{6,4},{8,10},{10,8},{12,14},{14,12},{16,18},{18,... | collective-permute-start | bytes 196616 | tf_op jit(solution)/shard_map/ppermute | solution.py:399
  25.7 2.4 %collective-permute-start.7 = (f32[64,128]{1,0:T(8,128)S(1)}, f32[64,128]{1,0:T(8,128)S(1)}, u32[]{:S(2)}, u32[]{:S(2)}) collective-permute-start(f32[64,128]{1,0:T(8,128)S(1)} %get-tuple-element.61), channel_id=1, source_target_pairs={{0,16},{2,18},{4,20},{6,22},{8,24},{10,26},{12,28},{14,30},{16,0},... | collective-permute-start | bytes 98312 | tf_op jit(solution)/shard_map/ppermute | solution.py:393
  28.5 2.3 %collective-permute-done.7.pair_in = f32[64,128]{1,0:T(8,128)S(1)} collective-permute-done((f32[64,128]{1,0:T(8,128)S(1)}, f32[64,128]{1,0:T(8,128)S(1)}, u32[]{:S(2)}, u32[]{:S(2)}) %collective-permute-start.7) | collective-permute-done | bytes 32800 | tf_op jit(solution)/shard_map/ppermute | solution.py:393
  31.7 1.7 %shard_map.62 = (f32[128,512]{1,0:T(8,128)S(1)}, f32[64,512]{1,0:T(8,128)S(1)}, f32[32,512]{1,0:T(8,128)S(1)}, f32[32,512]{1,0:T(8,128)S(1)}) custom-call(f32[512,128]{1,0:T(8,128)} %collective-permute-done.2.columns, f32[512,128]{1,0:T(8,128)S(1)} %shard_map.60.rest_low, bf16[512,1024]{1,0:T(8,128)(2,1)S(1)} %get-tuple-element.49.top, ...), custom_call_target="tpu_custom_call" | custom-call | flops 1000 | bytes 1000 | tf_op jit(solution)/shard_map/pallas_call | solution.py:43
  33.4 2.1 %collective-permute-start.8 = (f32[64,512]{1,0:T(8,128)S(1)}, f32[64,512]{1,0:T(8,128)S(1)}, u32[]{:S(2)}, u32[]{:S(2)}) collective-permute-start(f32[64,512]{1,0:T(8,128)S(1)} %get-tuple-element.65.back_far), channel_id=1, source_target_pairs={{0,16},{2,18},{4,20},{6,22},{8,24},{10,26},{12,28},{14,30},{16,0},... | collective-permute-start | bytes 393224 | tf_op jit(solution)/shard_map/ppermute | solution.py:393
  36.2 0.9 %collective-permute-start.10 = (f32[32,512]{1,0:T(8,128)S(1)}, f32[32,512]{1,0:T(8,128)S(1)}, u32[]{:S(2)}, u32[]{:S(2)}) collective-permute-start(f32[32,512]{1,0:T(8,128)S(1)} %get-tuple-element.68), channel_id=1, source_target_pairs={{0,2},{2,0},{4,6},{6,4},{8,10},{10,8},{12,14},{14,12},{16,18},{18,... | collective-permute-start | bytes 196616 | tf_op jit(solution)/shard_map/ppermute | solution.py:399
  37.7 4.2 %collective-permute-done.9.out_in = f32[32,512]{1,0:T(8,128)S(1)} collective-permute-done((f32[32,512]{1,0:T(8,128)S(1)}, f32[32,512]{1,0:T(8,128)S(1)}, u32[]{:S(2)}, u32[]{:S(2)}) %collective-permute-start.9) | collective-permute-done | bytes 65568 | tf_op jit(solution)/shard_map/ppermute | solution.py:396
  42.2 1.1 %collective-permute-start.11 = (f32[64,512]{1,0:T(8,128)S(1)}, f32[64,512]{1,0:T(8,128)S(1)}, u32[]{:S(2)}, u32[]{:S(2)}) collective-permute-start(f32[64,512]{1,0:T(8,128)S(1)} %shard_map.65), channel_id=1, source_target_pairs={{0,16},{2,18},{4,20},{6,22},{8,24},{10,26},{12,28},{14,30},{16,0},... | collective-permute-start | bytes 393224 | tf_op jit(solution)/shard_map/ppermute | solution.py:393
  43.5 1.8 %collective-permute-start.12 = (f32[32,512]{1,0:T(8,128)S(1)}, f32[32,512]{1,0:T(8,128)S(1)}, u32[]{:S(2)}, u32[]{:S(2)}) collective-permute-start(f32[32,512]{1,0:T(8,128)S(1)} %get-tuple-element.74), channel_id=1, source_target_pairs={{0,30},{2,4},{4,2},{6,8},{8,6},{10,12},{12,10},{14,16},{16,14},{18... | collective-permute-start | bytes 196616 | tf_op jit(solution)/shard_map/ppermute | solution.py:396
  45.3 0.9 %shard_map.64 = (f32[256,512]{1,0:T(8,128)S(1)}, f32[384,512]{1,0:T(8,128)S(1)}, f32[64,512]{1,0:T(8,128)S(1)}) custom-call(f32[256,512]{1,0:T(8,128)S(1)} %get-tuple-element.66.base, bf16[128,128]{1,0:T(8,128)(2,1)S(1)} %get-tuple-element.53.pick, f32[64,512]{1,0:T(8,128)S(1)} %collective-permute-done.8.far_in, ...), custom_call_target="tpu_custom_call" | custom-call | flops 1000 | bytes 1000 | tf_op jit(solution)/shard_map/pallas_call | solution.py:43
  46.2 3.7 %collective-permute-done.12.out_in = f32[32,512]{1,0:T(8,128)S(1)} collective-permute-done((f32[32,512]{1,0:T(8,128)S(1)}, f32[32,512]{1,0:T(8,128)S(1)}, u32[]{:S(2)}, u32[]{:S(2)}) %collective-permute-start.12) | collective-permute-done | bytes 65568 | tf_op jit(solution)/shard_map/ppermute | solution.py:396
  50.2 1.8 %collective-permute-start.14 = (f32[64,512]{1,0:T(8,128)S(1)}, f32[64,512]{1,0:T(8,128)S(1)}, u32[]{:S(2)}, u32[]{:S(2)}) collective-permute-start(f32[64,512]{1,0:T(8,128)S(1)} %shard_map.69), channel_id=1, source_target_pairs={{0,16},{2,18},{4,20},{6,22},{8,24},{10,26},{12,28},{14,30},{16,0},... | collective-permute-start | bytes 393224 | tf_op jit(solution)/shard_map/ppermute | solution.py:393
  52.2 1.2 %collective-permute-start.15 = (f32[32,512]{1,0:T(8,128)S(1)}, f32[32,512]{1,0:T(8,128)S(1)}, u32[]{:S(2)}, u32[]{:S(2)}) collective-permute-start(f32[32,512]{1,0:T(8,128)S(1)} %get-tuple-element.81), channel_id=1, source_target_pairs={{0,30},{2,4},{4,2},{6,8},{8,6},{10,12},{12,10},{14,16},{16,14},{18... | collective-permute-start | bytes 196616 | tf_op jit(solution)/shard_map/ppermute | solution.py:396
  54.3 4.4 %collective-permute-done.15.out_in = f32[32,512]{1,0:T(8,128)S(1)} collective-permute-done((f32[32,512]{1,0:T(8,128)S(1)}, f32[32,512]{1,0:T(8,128)S(1)}, u32[]{:S(2)}, u32[]{:S(2)}) %collective-permute-start.15) | collective-permute-done | bytes 65568 | tf_op jit(solution)/shard_map/ppermute | solution.py:396
  58.7 1.1 %shard_map.70 = f32[512,256]{1,0:T(8,128)} custom-call(f32[512,256]{1,0:T(8,128)S(1)} %shard_map.68.result, bf16[128,256]{1,0:T(8,128)(2,1)S(1)} %get-tuple-element.80.hits, f32[64,512]{1,0:T(8,128)S(1)} %collective-permute-done.14.far_in, f32[32,512]{1,0:T(8,128)S(1)} %collective-permute-done.15.out_in, f32[32,512]{1,0:T(8,128)S(1)} %collective-permute-done.16.near_in), custom_call_target="tpu_custom_call" | custom-call | flops 1000 | bytes 1000 | tf_op jit(solution)/shard_map/pallas_call | solution.py:43
  (34 shorter events, 5.4 us)
Async XLA Ops:
  0.0 13.1 %copy-start.3 = (s32[1,4,32]{2,1,0:T(4,128)S(1)}, s32[1,4,32]{2,1,0:T(4,128)}, u32[]{:S(2)}) copy-start(s32[1,4,32]{2,1,0:T(4,128)} %lists.1) | copy-start | bytes 1540
  0.0 13.1 %copy-start.2 = (s32[16,125]{1,0:T(8,128)S(1)}, s32[16,125]{1,0:T(8,128)}, u32[]{:S(2)}) copy-start(s32[16,125]{1,0:T(8,128)} %connect.1) | copy-start | bytes 24004
  2.8 0.6 %copy-start = (s32[256,1]{1,0:T(8,128)}, s32[256,1]{1,0:T(8,128)S(1)}, u32[]{:S(2)}) copy-start(s32[256,1]{1,0:T(8,128)S(1)} %get-tuple-element.52.origin) | copy-start | bytes 3076
  3.4 15.2 %collective-permute-start.1 = (f32[512,128]{1,0:T(8,128)}, f32[512,128]{1,0:T(8,128)S(1)}, u32[]{:S(2)}, u32[]{:S(2)}) collective-permute-start(f32[512,128]{1,0:T(8,128)} %get-tuple-element.45.far), channel_id=1, source_target_pairs={{0,1},{1,0},{2,3},{3,2},{4,5},{5,4},{6,7},{7,6},{8,9},{9,8},{10,11... | collective-permute-start | bytes 786440 | tf_op jit(solution)/shard_map/ppermute | solution.py:403
  6.4 16.4 %collective-permute-start = (f32[512,128]{1,0:T(8,128)}, f32[512,128]{1,0:T(8,128)S(1)}, u32[]{:S(2)}, u32[]{:S(2)}) collective-permute-start(f32[512,128]{1,0:T(8,128)} %get-tuple-element.44.ring), channel_id=1, source_target_pairs={{0,1},{1,0},{2,3},{3,2},{4,5},{5,4},{6,7},{7,6},{8,9},{9,8},{10,11... | collective-permute-start | bytes 786440 | tf_op jit(solution)/shard_map/ppermute | solution.py:403
  6.4 19.3 %collective-permute-start.3 = (f32[512,128]{1,0:T(8,128)}, f32[512,128]{1,0:T(8,128)S(1)}, u32[]{:S(2)}, u32[]{:S(2)}) collective-permute-start(f32[512,128]{1,0:T(8,128)} %get-tuple-element.46.low_rest), channel_id=1, source_target_pairs={{0,1},{1,0},{2,3},{3,2},{4,5},{5,4},{6,7},{7,6},{8,9},{9,8},{10,11... | collective-permute-start | bytes 786440 | tf_op jit(solution)/shard_map/ppermute | solution.py:403
  8.4 23.2 %collective-permute-start.2 = (f32[512,128]{1,0:T(8,128)}, f32[512,128]{1,0:T(8,128)}, u32[]{:S(2)}, u32[]{:S(2)}) collective-permute-start(f32[512,128]{1,0:T(8,128)} %get-tuple-element.47.high_rest), channel_id=1, source_target_pairs={{0,1},{1,0},{2,3},{3,2},{4,5},{5,4},{6,7},{7,6},{8,9},{9,8},{10,11... | collective-permute-start | bytes 786440 | tf_op jit(solution)/shard_map/ppermute | solution.py:403
  13.1 0.9 %copy-start.1 = (s32[256,1]{1,0:T(8,128)S(1)}, s32[256,1]{1,0:T(8,128)}, u32[]{:S(2)}) copy-start(s32[256,1]{1,0:T(8,128)} %copy-done) | copy-start | bytes 3076
  19.7 11.2 %collective-permute-start.4 = (f32[64,512]{1,0:T(8,128)S(1)}, f32[64,512]{1,0:T(8,128)S(1)}, u32[]{:S(2)}, u32[]{:S(2)}) collective-permute-start(f32[64,512]{1,0:T(8,128)S(1)} %get-tuple-element.56), channel_id=1, source_target_pairs={{0,16},{2,18},{4,20},{6,22},{8,24},{10,26},{12,28},{14,30},{16,0},... | collective-permute-start | bytes 393224 | tf_op jit(solution)/shard_map/ppermute | solution.py:393
  24.0 6.8 %collective-permute-start.5 = (f32[32,512]{1,0:T(8,128)S(1)}, f32[32,512]{1,0:T(8,128)S(1)}, u32[]{:S(2)}, u32[]{:S(2)}) collective-permute-start(f32[32,512]{1,0:T(8,128)S(1)} %get-tuple-element.57), channel_id=1, source_target_pairs={{0,30},{2,4},{4,2},{6,8},{8,6},{10,12},{12,10},{14,16},{16,14},{18... | collective-permute-start | bytes 196616 | tf_op jit(solution)/shard_map/ppermute | solution.py:396
  24.4 6.5 %collective-permute-start.6 = (f32[32,512]{1,0:T(8,128)S(1)}, f32[32,512]{1,0:T(8,128)S(1)}, u32[]{:S(2)}, u32[]{:S(2)}) collective-permute-start(f32[32,512]{1,0:T(8,128)S(1)} %get-tuple-element.58), channel_id=1, source_target_pairs={{0,2},{2,0},{4,6},{6,4},{8,10},{10,8},{12,14},{14,12},{16,18},{18,... | collective-permute-start | bytes 196616 | tf_op jit(solution)/shard_map/ppermute | solution.py:399
  25.7 5.2 %collective-permute-start.7 = (f32[64,128]{1,0:T(8,128)S(1)}, f32[64,128]{1,0:T(8,128)S(1)}, u32[]{:S(2)}, u32[]{:S(2)}) collective-permute-start(f32[64,128]{1,0:T(8,128)S(1)} %get-tuple-element.61), channel_id=1, source_target_pairs={{0,16},{2,18},{4,20},{6,22},{8,24},{10,26},{12,28},{14,30},{16,0},... | collective-permute-start | bytes 98312 | tf_op jit(solution)/shard_map/ppermute | solution.py:393
  33.4 9.9 %collective-permute-start.8 = (f32[64,512]{1,0:T(8,128)S(1)}, f32[64,512]{1,0:T(8,128)S(1)}, u32[]{:S(2)}, u32[]{:S(2)}) collective-permute-start(f32[64,512]{1,0:T(8,128)S(1)} %get-tuple-element.65.back_far), channel_id=1, source_target_pairs={{0,16},{2,18},{4,20},{6,22},{8,24},{10,26},{12,28},{14,30},{16,0},... | collective-permute-start | bytes 393224 | tf_op jit(solution)/shard_map/ppermute | solution.py:393
  35.5 6.5 %collective-permute-start.9 = (f32[32,512]{1,0:T(8,128)S(1)}, f32[32,512]{1,0:T(8,128)S(1)}, u32[]{:S(2)}, u32[]{:S(2)}) collective-permute-start(f32[32,512]{1,0:T(8,128)S(1)} %get-tuple-element.67), channel_id=1, source_target_pairs={{0,30},{2,4},{4,2},{6,8},{8,6},{10,12},{12,10},{14,16},{16,14},{18... | collective-permute-start | bytes 196616 | tf_op jit(solution)/shard_map/ppermute | solution.py:396
  36.2 5.8 %collective-permute-start.10 = (f32[32,512]{1,0:T(8,128)S(1)}, f32[32,512]{1,0:T(8,128)S(1)}, u32[]{:S(2)}, u32[]{:S(2)}) collective-permute-start(f32[32,512]{1,0:T(8,128)S(1)} %get-tuple-element.68), channel_id=1, source_target_pairs={{0,2},{2,0},{4,6},{6,4},{8,10},{10,8},{12,14},{14,12},{16,18},{18,... | collective-permute-start | bytes 196616 | tf_op jit(solution)/shard_map/ppermute | solution.py:399
  42.2 9.8 %collective-permute-start.11 = (f32[64,512]{1,0:T(8,128)S(1)}, f32[64,512]{1,0:T(8,128)S(1)}, u32[]{:S(2)}, u32[]{:S(2)}) collective-permute-start(f32[64,512]{1,0:T(8,128)S(1)} %shard_map.65), channel_id=1, source_target_pairs={{0,16},{2,18},{4,20},{6,22},{8,24},{10,26},{12,28},{14,30},{16,0},... | collective-permute-start | bytes 393224 | tf_op jit(solution)/shard_map/ppermute | solution.py:393
  43.5 6.5 %collective-permute-start.12 = (f32[32,512]{1,0:T(8,128)S(1)}, f32[32,512]{1,0:T(8,128)S(1)}, u32[]{:S(2)}, u32[]{:S(2)}) collective-permute-start(f32[32,512]{1,0:T(8,128)S(1)} %get-tuple-element.74), channel_id=1, source_target_pairs={{0,30},{2,4},{4,2},{6,8},{8,6},{10,12},{12,10},{14,16},{16,14},{18... | collective-permute-start | bytes 196616 | tf_op jit(solution)/shard_map/ppermute | solution.py:396
  45.3 4.7 %collective-permute-start.13 = (f32[32,512]{1,0:T(8,128)S(1)}, f32[32,512]{1,0:T(8,128)S(1)}, u32[]{:S(2)}, u32[]{:S(2)}) collective-permute-start(f32[32,512]{1,0:T(8,128)S(1)} %get-tuple-element.75), channel_id=1, source_target_pairs={{0,2},{2,0},{4,6},{6,4},{8,10},{10,8},{12,14},{14,12},{16,18},{18,... | collective-permute-start | bytes 196616 | tf_op jit(solution)/shard_map/ppermute | solution.py:399
  50.2 8.5 %collective-permute-start.14 = (f32[64,512]{1,0:T(8,128)S(1)}, f32[64,512]{1,0:T(8,128)S(1)}, u32[]{:S(2)}, u32[]{:S(2)}) collective-permute-start(f32[64,512]{1,0:T(8,128)S(1)} %shard_map.69), channel_id=1, source_target_pairs={{0,16},{2,18},{4,20},{6,22},{8,24},{10,26},{12,28},{14,30},{16,0},... | collective-permute-start | bytes 393224 | tf_op jit(solution)/shard_map/ppermute | solution.py:393
  52.2 6.5 %collective-permute-start.15 = (f32[32,512]{1,0:T(8,128)S(1)}, f32[32,512]{1,0:T(8,128)S(1)}, u32[]{:S(2)}, u32[]{:S(2)}) collective-permute-start(f32[32,512]{1,0:T(8,128)S(1)} %get-tuple-element.81), channel_id=1, source_target_pairs={{0,30},{2,4},{4,2},{6,8},{8,6},{10,12},{12,10},{14,16},{16,14},{18... | collective-permute-start | bytes 196616 | tf_op jit(solution)/shard_map/ppermute | solution.py:396
  53.4 5.2 %collective-permute-start.16 = (f32[32,512]{1,0:T(8,128)S(1)}, f32[32,512]{1,0:T(8,128)S(1)}, u32[]{:S(2)}, u32[]{:S(2)}) collective-permute-start(f32[32,512]{1,0:T(8,128)S(1)} %get-tuple-element.82), channel_id=1, source_target_pairs={{0,2},{2,0},{4,6},{6,4},{8,10},{10,8},{12,14},{14,12},{16,18},{18,... | collective-permute-start | bytes 196616 | tf_op jit(solution)/shard_map/ppermute | solution.py:399

commit v7 on v6

--- a/solution.py
+++ b/solution.py
@@ -64,7 +64,7 @@
 
 
 def renumber(
-    lists_in, subspace_in, far_out, ring_out, low_out, high_out, shuffle_out, origin_out, lists, subspace, sems
+    lists_in, subspace_in, far_out, ring_out, low_out, high_out, shuffle_out, lists, subspace, sems
 ):
     slots, halo = lists.shape[1:]
     depth, nodes = subspace.shape
@@ -102,11 +102,11 @@
     match = place == down
     shuffle = jnp.where(match, 1.0, 0.0).astype(BF16)
     shuffle_out[...] = shuffle
-    origin_out[...] = jnp.sum(jnp.where(match, along, 0), axis=1, keepdims=True)
     copy.wait()
     halves = []
     for part, rest_out in enumerate((low_out, high_out)):
-        top, low = split(subspace[part * span : (part + 1) * span, :])
+        rows = slice(part * span, (part + 1) * span)
+        top, low = split(subspace[rows, :])
         turned = dot(top, shuffle, NT) + dot(low, shuffle, NT)
         rest_out[...] = turned[:, 2 * duo :]
         halves.append(turned)
@@ -114,15 +114,20 @@
     ring_out[...] = jnp.concatenate([half[:, duo : 2 * duo] for half in halves], 1)
 
 
+def list_hits(sent, nodes):
+    ids = lax.broadcasted_iota(I32, (sent.shape[0], nodes), 1)
+    return jnp.where(sent == ids, 1.0, 0.0).astype(BF16)
+
+
 def assemble(
-    odd, lists, connect, blocks_in, shuffle, origin, top_out, low_out, pick_out, both_out, hits_out, pair_out,
+    odd, lists, connect, blocks_in, shuffle, _, top_out, low_out, pick_out, both_out, hits_out, pair_out,
     blocks, sem, spread, rows_top, rows_low,
 ):
     copy = pltpu.make_async_copy(blocks_in, blocks, sem)
     copy.start()
     elems, size = connect.shape
     slots, halo = lists.shape[1:]
-    nodes = origin.shape[0]
+    nodes = shuffle.shape[0]
     wide = slots * halo
     duo = 2 * halo
     swap = odd[0] == 1
@@ -130,7 +135,7 @@
     outer = jnp.where(swap, columns[0], columns[1])
     inner = jnp.where(swap, columns[1], columns[0])
     sent = jnp.concatenate([columns[2], columns[3], outer, inner], 0)
-    hits = jnp.where(sent == lax.broadcasted_iota(I32, (wide, nodes), 1), 1.0, 0.0).astype(BF16)
+    hits = list_hits(sent, nodes)
     hits_out[...] = hits
     pick = dot(hits, shuffle[:wide, :], NT).astype(BF16)
     pick_out[...] = pick
@@ -142,7 +147,9 @@
     ghost = jnp.concatenate(
         [3 * halo + lane, 2 * halo + lane, (1 - flag) * halo + lane, flag * halo + lane], 0
     )
-    numbers = jnp.concatenate([origin[...], nodes + ghost], 0)
+    along = lax.broadcasted_iota(I32, (nodes, nodes), 1).astype(F32)
+    origin = jnp.sum(along * shuffle[...].astype(F32), axis=1, keepdims=True).astype(I32)
+    numbers = jnp.concatenate([origin, nodes + ghost], 0)
     pitch = spread.shape[1] // elems
     copy.wait()
     for elem in range(elems):
@@ -234,11 +241,15 @@
     )
 
 
-def rotate_far(groups, columns, start_own, top, low, pick, start_out, far_out):
+def rotate_far(groups, columns, start_own, top, low, lists, shuffle, start_out, far_out):
     duo = far_out.shape[0]
+    halo = duo // 2
+    sent = [column(lists[0, slot : slot + 1, :], halo) for slot in (2, 3)]
+    hits = list_hits(jnp.concatenate(sent, 0), shuffle.shape[0])
+    pick = dot(hits, shuffle[:duo, :], NT).astype(BF16)
     start = (start_own[:, :duo] + rotate_sides(columns, top, low, groups)).T
     start_out[...] = start
-    far_out[...] = sift(pick[:duo, :duo], start)
+    far_out[...] = sift(pick, start)
 
 
 def rotate_ring(groups, columns, start_own, start_far, top, low, pick, start_out, out_out, near_out):
@@ -413,7 +424,7 @@
     vmem = pl.BlockSpec(memory_space=pltpu.VMEM)
     hbm = pl.BlockSpec(memory_space=pltpu.HBM)
 
-    far_cols, ring_cols, low_cols, high_cols, shuffle, origin = call(
+    far_cols, ring_cols, low_cols, high_cols, shuffle = call(
         renumber,
         [
             ((depth // 2, 2 * duo), F32),
@@ -421,7 +432,6 @@
             ((depth // 2, nodes - wide), F32),
             ((depth // 2, nodes - wide), F32),
             ((nodes, nodes), BF16),
-            ((nodes, 1), I32),
         ],
         in_hbm(send_rows), in_hbm(subspace),
         kept=True,
@@ -436,6 +446,29 @@
     ring_cols_in = gather(ring_cols)
     low_cols_in = gather(low_cols)
     high_cols_in = gather(high_cols)
+    others = groups - 1
+    start_own, ritz_top, ritz_low = call(
+        rotate_own,
+        [
+            ((block, nodes), F32),
+            ((block, others * depth), BF16),
+            ((block, others * depth), BF16),
+        ],
+        group, far_cols, ring_cols, low_cols, high_cols, in_hbm(ritz),
+        limit=12,
+        in_specs=[smem, vmem, vmem, vmem, vmem, hbm],
+        scratch_shapes=[
+            pltpu.VMEM((groups, block, depth), F32),
+            pltpu.SemaphoreType.DMA((groups, 2)),
+        ],
+    )
+
+    start_far, far_rows = call(
+        functools.partial(rotate_far, groups),
+        [rows_of(duo), rows_of(duo)],
+        in_vmem(far_cols_in), start_own, ritz_top, ritz_low, send_rows, shuffle,
+    )
+    far_in = far(far_rows)
     elems, size = connect.shape
     pitch = -(-size // 128) * 128
     blocks = jnp.transpose(element_ham, (1, 0, 2)).reshape(size * elems, size)
@@ -449,7 +482,7 @@
             ((wide, nodes), BF16),
             ((duo, 2 * duo), F32),
         ],
-        odd, send_rows, connect, in_hbm(blocks), shuffle, origin,
+        odd, send_rows, connect, in_hbm(blocks), shuffle, start_far,
         limit=12,
         in_specs=[smem, vmem, vmem, hbm, vmem, vmem],
         scratch_shapes=[
@@ -461,29 +494,6 @@
         ],
     )
     pair_in = far(pair)
-    others = groups - 1
-    start_own, ritz_top, ritz_low = call(
-        rotate_own,
-        [
-            ((block, nodes), F32),
-            ((block, others * depth), BF16),
-            ((block, others * depth), BF16),
-        ],
-        group, far_cols, ring_cols, low_cols, high_cols, in_hbm(ritz),
-        limit=12,
-        in_specs=[smem, vmem, vmem, vmem, vmem, hbm],
-        scratch_shapes=[
-            pltpu.VMEM((groups, block, depth), F32),
-            pltpu.SemaphoreType.DMA((groups, 2)),
-        ],
-    )
-
-    start_far, far_rows = call(
-        functools.partial(rotate_far, groups),
-        [rows_of(duo), rows_of(duo)],
-        in_vmem(far_cols_in), start_own, ritz_top, ritz_low, pick,
-    )
-    far_in = far(far_rows)
     start_edge, out_rows, near_rows = call(
         functools.partial(rotate_ring, groups),
         [rows_of(wide), rows_of(halo), rows_of(halo)],

time: 60.1 us -> 61.3 us (1.020)
  waiting for transfers between devices: 14.8 us -> 18.4 us
  starting transfers between devices: 21.8 us -> 18.9 us
  Pallas kernels: 21.5 us -> 23.6 us
  local copies, waits for them, and re-layouts: 1.54 us -> 0.01 us
    ppermute x5, starting transfers between devices: 10.5 us -> 7.67 us  [far(): return lax.ppermute(rows, 'mesh', pairs_far)]
    pallas_call x16, Pallas kernels: 21.5 us -> 23.6 us  [call(): pl.pallas_call(body, out_shape=[pltpu.VMEM(*out) if kept else jax.ShapeDt...]
    ppermute x5, waiting for transfers between devices: 2.35 us -> 4.26 us  [far(): return lax.ppermute(rows, 'mesh', pairs_far)]
    unnamed x8 -> x4, local copies, waits for them, and re-layouts: 1.54 us -> 0.01 us
    ppermute x4, waiting for transfers between devices: 12.4 us -> 13.4 us  [out(): return lax.ppermute(rows, 'mesh', pairs_out)]
    ppermute x4, waiting for transfers between devices: 0.01 us -> 0.7 us  [gather(): lax.ppermute(rows, 'state', [(i, (i + step) % groups) for i in range(grou...]
    ppermute x4, starting transfers between devices: 2.21 us -> 1.6 us  [near(): return lax.ppermute(rows, 'mesh', pairs_in)]
  transfers between devices with their start and end apart: 17 -> 17, of which waited for: 4 -> 5; matrix products, arithmetic and copies ran while one was open for 0% -> 0% of each run, Pallas kernels for 27% -> 30%
where the time goes in v7:
time: 61.3 us; the launch traced here: 61 us
  Pallas kernels  23.6 us (38%)
  starting transfers between devices  18.9 us (31%)
  waiting for transfers between devices  18.4 us (30%)
    pallas_call x16, Pallas kernels, call(): pl.pallas_call(body, out_shape=[pltpu.VMEM(*out) if kept else jax.ShapeDt...  23.6 us
    ppermute x4, waiting for transfers between devices, out(): return lax.ppermute(rows, 'mesh', pairs_out)  13.4 us
    ppermute x5, starting transfers between devices, far(): return lax.ppermute(rows, 'mesh', pairs_far)  7.67 us
    ppermute x4, starting transfers between devices, gather(): lax.ppermute(rows, 'state', [(i, (i + step) % groups) for i in range(grou...  5.14 us
    ppermute x4, starting transfers between devices, out(): return lax.ppermute(rows, 'mesh', pairs_out)  4.45 us
    ppermute x5, waiting for transfers between devices, far(): return lax.ppermute(rows, 'mesh', pairs_far)  4.26 us
    ppermute x4, starting transfers between devices, near(): return lax.ppermute(rows, 'mesh', pairs_in)  1.6 us
  transfers between devices with their start and end apart: 17, of which 5 were waited for; matrix products, arithmetic and copies ran while one was open for 0% of the time, Pallas kernels for 30%

profile of v7, /device:TPU:0, one launch (start us, length us, event | category | flops | bytes accessed | tf_op | source)
XLA Modules:
  0.0 61.0 jit_solution(17248830191648207048)
XLA Ops:
  0.0 2.7 %shard_map.55 = (f32[512,128]{1,0:T(8,128)}, f32[512,128]{1,0:T(8,128)}, f32[512,128]{1,0:T(8,128)}, f32[512,128]{1,0:T(8,128)}, bf16[256,256]{1,0:T(8,128)(2,1)S(1)}) custom-call(s32[1,4,32]{2,1,0:T(4,128)} %lists.3, f32[1024,256]{1,0:T(8,128)} %subspace_in.1), custom_call_target="tpu_custom_call" | custom-call | flops 1000 | bytes 1000 | tf_op jit(solution)/shard_map/pallas_call | solution.py:43
  2.7 3.0 %collective-permute-start.1 = (f32[512,128]{1,0:T(8,128)}, f32[512,128]{1,0:T(8,128)}, u32[]{:S(2)}, u32[]{:S(2)}) collective-permute-start(f32[512,128]{1,0:T(8,128)} %get-tuple-element.44.far), channel_id=1, source_target_pairs={{0,1},{1,0},{2,3},{3,2},{4,5},{5,4},{6,7},{7,6},{8,9},{9,8},{10,11... | collective-permute-start | bytes 786440 | tf_op jit(solution)/shard_map/ppermute | solution.py:414
  5.9 1.9 %collective-permute-start.3 = (f32[512,128]{1,0:T(8,128)}, f32[512,128]{1,0:T(8,128)S(1)}, u32[]{:S(2)}, u32[]{:S(2)}) collective-permute-start(f32[512,128]{1,0:T(8,128)} %get-tuple-element.45.low_rest), channel_id=1, source_target_pairs={{0,1},{1,0},{2,3},{3,2},{4,5},{5,4},{6,7},{7,6},{8,9},{9,8},{10,11... | collective-permute-start | bytes 786440 | tf_op jit(solution)/shard_map/ppermute | solution.py:414
  7.9 4.6 %shard_map.56 = (f32[512,256]{1,0:T(8,128)S(1)}, bf16[512,1024]{1,0:T(8,128)(2,1)S(1)}, bf16[512,1024]{1,0:T(8,128)(2,1)S(1)}) custom-call(s32[1]{0:T(128)} %bitcast.group, f32[512,128]{1,0:T(8,128)} %get-tuple-element.44.far, f32[512,128]{1,0:T(8,128)} %get-tuple-element.43.ring, f32[512,128]{1,0:T(8,128)} %get-tuple-element.45.low_rest, ...), custom_call_target="tpu_custom_call" | custom-call | flops 1000 | bytes 1000 | tf_op jit(solution)/shard_map/pallas_call | solution.py:43
  12.5 0.7 %collective-permute-done.1.columns = f32[512,128]{1,0:T(8,128)} collective-permute-done((f32[512,128]{1,0:T(8,128)}, f32[512,128]{1,0:T(8,128)}, u32[]{:S(2)}, u32[]{:S(2)}) %collective-permute-start.1) | collective-permute-done | bytes 262176 | tf_op jit(solution)/shard_map/ppermute | solution.py:414
  13.2 2.8 %shard_map.57 = (f32[64,512]{1,0:T(8,128)S(1)}, f32[64,512]{1,0:T(8,128)}) custom-call(f32[512,128]{1,0:T(8,128)} %collective-permute-done.1.columns, f32[512,256]{1,0:T(8,128)S(1)} %get-tuple-element.47.start_own, bf16[512,1024]{1,0:T(8,128)(2,1)S(1)} %get-tuple-element.48.top, bf16[512,1024]{1,0:T(8,128)(2,1)S(1)} %get-tuple-element.49.low, ...), custom_call_target="tpu_custom_call" | custom-call | flops 1000 | bytes 1000 | tf_op jit(solution)/shard_map/pallas_call | solution.py:43
  16.1 3.1 %collective-permute-start.4 = (f32[64,512]{1,0:T(8,128)}, f32[64,512]{1,0:T(8,128)S(1)}, u32[]{:S(2)}, u32[]{:S(2)}) collective-permute-start(f32[64,512]{1,0:T(8,128)} %get-tuple-element.54), channel_id=1, source_target_pairs={{0,16},{2,18},{4,20},{6,22},{8,24},{10,26},{12,28},{14,30},{16,0},... | collective-permute-start | bytes 393224 | tf_op jit(solution)/shard_map/ppermute | solution.py:404
  19.2 4.9 %shard_map.58 = (bf16[384,384]{1,0:T(8,128)(2,1)S(1)}, bf16[384,384]{1,0:T(8,128)(2,1)S(1)}, bf16[128,128]{1,0:T(8,128)(2,1)S(1)}, bf16[128,128]{1,0:T(8,128)(2,...) custom-call(s32[1]{0:T(128)} %bitcast.1.odd, s32[1,4,32]{2,1,0:T(4,128)S(1)} %copy-done, ...), custom_call_target="tpu_custom_call" | custom-call | flops 1000 | bytes 1000 | tf_op jit(solution)/shard_map/pallas_call | solution.py:43
  24.1 1.2 %shard_map.59 = (f32[128,512]{1,0:T(8,128)S(1)}, f32[32,512]{1,0:T(8,128)S(1)}, f32[32,512]{1,0:T(8,128)S(1)}) custom-call(f32[512,128]{1,0:T(8,128)S(1)} %collective-permute-done.columns, f32[512,256]{1,0:T(8,128)S(1)} %get-tuple-element.47.start_own, f32[64,512]{1,0:T(8,128)S(1)} %get-tuple-element.51._.start_far, ...), custom_call_target="tpu_custom_call" | custom-call | flops 1000 | bytes 1000 | tf_op jit(solution)/shard_map/pallas_call | solution.py:43
  25.4 1.6 %collective-permute-start.6 = (f32[32,512]{1,0:T(8,128)S(1)}, f32[32,512]{1,0:T(8,128)S(1)}, u32[]{:S(2)}, u32[]{:S(2)}) collective-permute-start(f32[32,512]{1,0:T(8,128)S(1)} %get-tuple-element.56), channel_id=1, source_target_pairs={{0,2},{2,0},{4,6},{6,4},{8,10},{10,8},{12,14},{14,12},{16,18},{18,... | collective-permute-start | bytes 196616 | tf_op jit(solution)/shard_map/ppermute | solution.py:410
  27.9 4.2 %collective-permute-done.7.pair_in = f32[64,128]{1,0:T(8,128)S(1)} collective-permute-done((f32[64,128]{1,0:T(8,128)S(1)}, f32[64,128]{1,0:T(8,128)S(1)}, u32[]{:S(2)}, u32[]{:S(2)}) %collective-permute-start.7) | collective-permute-done | bytes 32800 | tf_op jit(solution)/shard_map/ppermute | solution.py:404
  32.2 0.8 %shard_map.61 = (f32[384,512]{1,0:T(8,128)S(1)}, f32[64,64]{1,0:T(8,128)S(1)}, f32[64,64]{1,0:T(8,128)S(1)}) custom-call(f32[128,512]{1,0:T(8,128)S(1)} %get-tuple-element.53.start_edge, f32[64,512]{1,0:T(8,128)S(1)} %collective-permute-done.4.far_in, f32[32,512]{1,0:T(8,128)S(1)} %collective-permute-done.5.out_in, ...), custom_call_target="tpu_custom_call" | custom-call | flops 1000 | bytes 1000 | tf_op jit(solution)/shard_map/pallas_call | solution.py:43
  33.0 1.7 %shard_map.62 = (f32[128,512]{1,0:T(8,128)S(1)}, f32[64,512]{1,0:T(8,128)S(1)}, f32[32,512]{1,0:T(8,128)S(1)}, f32[32,512]{1,0:T(8,128)S(1)}) custom-call(f32[512,128]{1,0:T(8,128)} %collective-permute-done.2.columns, f32[512,128]{1,0:T(8,128)S(1)} %shard_map.60.rest_low, bf16[512,1024]{1,0:T(8,128)(2,1)S(1)} %get-tuple-element.48.top, ...), custom_call_target="tpu_custom_call" | custom-call | flops 1000 | bytes 1000 | tf_op jit(solution)/shard_map/pallas_call | solution.py:43
  34.9 2.4 %collective-permute-start.9 = (f32[32,512]{1,0:T(8,128)S(1)}, f32[32,512]{1,0:T(8,128)S(1)}, u32[]{:S(2)}, u32[]{:S(2)}) collective-permute-start(f32[32,512]{1,0:T(8,128)S(1)} %get-tuple-element.65), channel_id=1, source_target_pairs={{0,30},{2,4},{4,2},{6,8},{8,6},{10,12},{12,10},{14,16},{16,14},{18... | collective-permute-start | bytes 196616 | tf_op jit(solution)/shard_map/ppermute | solution.py:407
  37.3 0.6 %shard_map.63 = (f32[256,512]{1,0:T(8,128)S(1)}, f32[256,512]{1,0:T(8,128)S(1)}, f32[128,512]{1,0:T(8,128)S(1)}, f32[64,512]{1,0:T(8,128)S(1)}) custom-call(f32[128,512]{1,0:T(8,128)S(1)} %get-tuple-element.53.start_edge, f32[128,512]{1,0:T(8,128)S(1)} %get-tuple-element.61.start_rest, f32[384,512]{1,0:T(8,128)S(1)} %get-tuple-element.60.part, ...), custom_call_target="tpu_custom_call" | custom-call | flops 1000 | bytes 1000 | tf_op jit(solution)/shard_map/pallas_call | solution.py:43
  37.9 4.2 %collective-permute-done.9.out_in = f32[32,512]{1,0:T(8,128)S(1)} collective-permute-done((f32[32,512]{1,0:T(8,128)S(1)}, f32[32,512]{1,0:T(8,128)S(1)}, u32[]{:S(2)}, u32[]{:S(2)}) %collective-permute-start.9) | collective-permute-done | bytes 65568 | tf_op jit(solution)/shard_map/ppermute | solution.py:407
  42.3 3.8 %collective-permute-start.11 = (f32[64,512]{1,0:T(8,128)S(1)}, f32[64,512]{1,0:T(8,128)S(1)}, u32[]{:S(2)}, u32[]{:S(2)}) collective-permute-start(f32[64,512]{1,0:T(8,128)S(1)} %shard_map.65), channel_id=1, source_target_pairs={{0,16},{2,18},{4,20},{6,22},{8,24},{10,26},{12,28},{14,30},{16,0},... | collective-permute-start | bytes 393224 | tf_op jit(solution)/shard_map/ppermute | solution.py:404
  46.3 0.8 %collective-permute-start.12 = (f32[32,512]{1,0:T(8,128)S(1)}, f32[32,512]{1,0:T(8,128)S(1)}, u32[]{:S(2)}, u32[]{:S(2)}) collective-permute-start(f32[32,512]{1,0:T(8,128)S(1)} %get-tuple-element.72), channel_id=1, source_target_pairs={{0,30},{2,4},{4,2},{6,8},{8,6},{10,12},{12,10},{14,16},{16,14},{18... | collective-permute-start | bytes 196616 | tf_op jit(solution)/shard_map/ppermute | solution.py:407
  47.1 0.9 %shard_map.64 = (f32[256,512]{1,0:T(8,128)S(1)}, f32[384,512]{1,0:T(8,128)S(1)}, f32[64,512]{1,0:T(8,128)S(1)}) custom-call(f32[256,512]{1,0:T(8,128)S(1)} %get-tuple-element.64.base, bf16[128,128]{1,0:T(8,128)(2,1)S(1)} %get-tuple-element.52.pick, f32[64,512]{1,0:T(8,128)S(1)} %collective-permute-done.8.far_in, ...), custom_call_target="tpu_custom_call" | custom-call | flops 1000 | bytes 1000 | tf_op jit(solution)/shard_map/pallas_call | solution.py:43
  48.1 4.7 %collective-permute-done.12.out_in = f32[32,512]{1,0:T(8,128)S(1)} collective-permute-done((f32[32,512]{1,0:T(8,128)S(1)}, f32[32,512]{1,0:T(8,128)S(1)}, u32[]{:S(2)}, u32[]{:S(2)}) %collective-permute-start.12) | collective-permute-done | bytes 65568 | tf_op jit(solution)/shard_map/ppermute | solution.py:407
  53.3 1.2 %collective-permute-start.15 = (f32[32,512]{1,0:T(8,128)S(1)}, f32[32,512]{1,0:T(8,128)S(1)}, u32[]{:S(2)}, u32[]{:S(2)}) collective-permute-start(f32[32,512]{1,0:T(8,128)S(1)} %get-tuple-element.79), channel_id=1, source_target_pairs={{0,30},{2,4},{4,2},{6,8},{8,6},{10,12},{12,10},{14,16},{16,14},{18... | collective-permute-start | bytes 196616 | tf_op jit(solution)/shard_map/ppermute | solution.py:407
  54.5 0.8 %shard_map.68.result = f32[512,256]{1,0:T(8,128)S(1)} custom-call(f32[384,512]{1,0:T(8,128)S(1)} %get-tuple-element.68.part, f32[128,512]{1,0:T(8,128)S(1)} %get-tuple-element.74.ghosts, bf16[384,384]{1,0:T(8,128)(2,1)S(1)} %get-tuple-element.57.ham_top, bf16[384,384]{1,0:T(8,128)(2,1)S(1)} %get-tuple-element.58.ham_low, ...), custom_call_target="tpu_custom_call" | custom-call | flops 1000 | bytes 1000 | tf_op jit(solution)/shard_map/pallas_call | solution.py:43
  55.4 4.5 %collective-permute-done.15.out_in = f32[32,512]{1,0:T(8,128)S(1)} collective-permute-done((f32[32,512]{1,0:T(8,128)S(1)}, f32[32,512]{1,0:T(8,128)S(1)}, u32[]{:S(2)}, u32[]{:S(2)}) %collective-permute-start.15) | collective-permute-done | bytes 65568 | tf_op jit(solution)/shard_map/ppermute | solution.py:407
  59.9 1.1 %shard_map.70 = f32[512,256]{1,0:T(8,128)} custom-call(f32[512,256]{1,0:T(8,128)S(1)} %shard_map.68.result, bf16[128,256]{1,0:T(8,128)(2,1)S(1)} %get-tuple-element.78.hits, f32[64,512]{1,0:T(8,128)S(1)} %collective-permute-done.14.far_in, f32[32,512]{1,0:T(8,128)S(1)} %collective-permute-done.15.out_in, f32[32,512]{1,0:T(8,128)S(1)} %collective-permute-done.16.near_in), custom_call_target="tpu_custom_call" | custom-call | flops 1000 | bytes 1000 | tf_op jit(solution)/shard_map/pallas_call | solution.py:43
  (30 shorter events, 2.3 us)
Async XLA Ops:
  0.0 13.2 %copy-start = (s32[1,4,32]{2,1,0:T(4,128)S(1)}, s32[1,4,32]{2,1,0:T(4,128)}, u32[]{:S(2)}) copy-start(s32[1,4,32]{2,1,0:T(4,128)} %lists.3) | copy-start | bytes 1540
  2.7 16.5 %copy-start.1 = (s32[16,125]{1,0:T(8,128)S(1)}, s32[16,125]{1,0:T(8,128)}, u32[]{:S(2)}) copy-start(s32[16,125]{1,0:T(8,128)} %connect.1) | copy-start | bytes 24004
  2.7 10.5 %collective-permute-start.1 = (f32[512,128]{1,0:T(8,128)}, f32[512,128]{1,0:T(8,128)}, u32[]{:S(2)}, u32[]{:S(2)}) collective-permute-start(f32[512,128]{1,0:T(8,128)} %get-tuple-element.44.far), channel_id=1, source_target_pairs={{0,1},{1,0},{2,3},{3,2},{4,5},{5,4},{6,7},{7,6},{8,9},{9,8},{10,11... | collective-permute-start | bytes 786440 | tf_op jit(solution)/shard_map/ppermute | solution.py:414
  5.8 18.3 %collective-permute-start = (f32[512,128]{1,0:T(8,128)}, f32[512,128]{1,0:T(8,128)S(1)}, u32[]{:S(2)}, u32[]{:S(2)}) collective-permute-start(f32[512,128]{1,0:T(8,128)} %get-tuple-element.43.ring), channel_id=1, source_target_pairs={{0,1},{1,0},{2,3},{3,2},{4,5},{5,4},{6,7},{7,6},{8,9},{9,8},{10,11... | collective-permute-start | bytes 786440 | tf_op jit(solution)/shard_map/ppermute | solution.py:414
  5.9 21.2 %collective-permute-start.3 = (f32[512,128]{1,0:T(8,128)}, f32[512,128]{1,0:T(8,128)S(1)}, u32[]{:S(2)}, u32[]{:S(2)}) collective-permute-start(f32[512,128]{1,0:T(8,128)} %get-tuple-element.45.low_rest), channel_id=1, source_target_pairs={{0,1},{1,0},{2,3},{3,2},{4,5},{5,4},{6,7},{7,6},{8,9},{9,8},{10,11... | collective-permute-start | bytes 786440 | tf_op jit(solution)/shard_map/ppermute | solution.py:414
  7.8 25.2 %collective-permute-start.2 = (f32[512,128]{1,0:T(8,128)}, f32[512,128]{1,0:T(8,128)}, u32[]{:S(2)}, u32[]{:S(2)}) collective-permute-start(f32[512,128]{1,0:T(8,128)} %get-tuple-element.46.high_rest), channel_id=1, source_target_pairs={{0,1},{1,0},{2,3},{3,2},{4,5},{5,4},{6,7},{7,6},{8,9},{9,8},{10,11... | collective-permute-start | bytes 786440 | tf_op jit(solution)/shard_map/ppermute | solution.py:414
  16.1 16.1 %collective-permute-start.4 = (f32[64,512]{1,0:T(8,128)}, f32[64,512]{1,0:T(8,128)S(1)}, u32[]{:S(2)}, u32[]{:S(2)}) collective-permute-start(f32[64,512]{1,0:T(8,128)} %get-tuple-element.54), channel_id=1, source_target_pairs={{0,16},{2,18},{4,20},{6,22},{8,24},{10,26},{12,28},{14,30},{16,0},... | collective-permute-start | bytes 393224 | tf_op jit(solution)/shard_map/ppermute | solution.py:404
  25.4 6.8 %collective-permute-start.5 = (f32[32,512]{1,0:T(8,128)S(1)}, f32[32,512]{1,0:T(8,128)S(1)}, u32[]{:S(2)}, u32[]{:S(2)}) collective-permute-start(f32[32,512]{1,0:T(8,128)S(1)} %get-tuple-element.55), channel_id=1, source_target_pairs={{0,30},{2,4},{4,2},{6,8},{8,6},{10,12},{12,10},{14,16},{16,14},{18... | collective-permute-start | bytes 196616 | tf_op jit(solution)/shard_map/ppermute | solution.py:407
  25.4 6.8 %collective-permute-start.6 = (f32[32,512]{1,0:T(8,128)S(1)}, f32[32,512]{1,0:T(8,128)S(1)}, u32[]{:S(2)}, u32[]{:S(2)}) collective-permute-start(f32[32,512]{1,0:T(8,128)S(1)} %get-tuple-element.56), channel_id=1, source_target_pairs={{0,2},{2,0},{4,6},{6,4},{8,10},{10,8},{12,14},{14,12},{16,18},{18,... | collective-permute-start | bytes 196616 | tf_op jit(solution)/shard_map/ppermute | solution.py:410
  27.0 5.2 %collective-permute-start.7 = (f32[64,128]{1,0:T(8,128)S(1)}, f32[64,128]{1,0:T(8,128)S(1)}, u32[]{:S(2)}, u32[]{:S(2)}) collective-permute-start(f32[64,128]{1,0:T(8,128)S(1)} %get-tuple-element.59), channel_id=1, source_target_pairs={{0,16},{2,18},{4,20},{6,22},{8,24},{10,26},{12,28},{14,30},{16,0},... | collective-permute-start | bytes 98312 | tf_op jit(solution)/shard_map/ppermute | solution.py:404
  34.7 11.4 %collective-permute-start.8 = (f32[64,512]{1,0:T(8,128)S(1)}, f32[64,512]{1,0:T(8,128)S(1)}, u32[]{:S(2)}, u32[]{:S(2)}) collective-permute-start(f32[64,512]{1,0:T(8,128)S(1)} %get-tuple-element.63.back_far), channel_id=1, source_target_pairs={{0,16},{2,18},{4,20},{6,22},{8,24},{10,26},{12,28},{14,30},{16,0},... | collective-permute-start | bytes 393224 | tf_op jit(solution)/shard_map/ppermute | solution.py:404
  34.9 7.2 %collective-permute-start.9 = (f32[32,512]{1,0:T(8,128)S(1)}, f32[32,512]{1,0:T(8,128)S(1)}, u32[]{:S(2)}, u32[]{:S(2)}) collective-permute-start(f32[32,512]{1,0:T(8,128)S(1)} %get-tuple-element.65), channel_id=1, source_target_pairs={{0,30},{2,4},{4,2},{6,8},{8,6},{10,12},{12,10},{14,16},{16,14},{18... | collective-permute-start | bytes 196616 | tf_op jit(solution)/shard_map/ppermute | solution.py:407
  37.3 4.8 %collective-permute-start.10 = (f32[32,512]{1,0:T(8,128)S(1)}, f32[32,512]{1,0:T(8,128)S(1)}, u32[]{:S(2)}, u32[]{:S(2)}) collective-permute-start(f32[32,512]{1,0:T(8,128)S(1)} %get-tuple-element.66), channel_id=1, source_target_pairs={{0,2},{2,0},{4,6},{6,4},{8,10},{10,8},{12,14},{14,12},{16,18},{18,... | collective-permute-start | bytes 196616 | tf_op jit(solution)/shard_map/ppermute | solution.py:410
  42.3 10.8 %collective-permute-start.11 = (f32[64,512]{1,0:T(8,128)S(1)}, f32[64,512]{1,0:T(8,128)S(1)}, u32[]{:S(2)}, u32[]{:S(2)}) collective-permute-start(f32[64,512]{1,0:T(8,128)S(1)} %shard_map.65), channel_id=1, source_target_pairs={{0,16},{2,18},{4,20},{6,22},{8,24},{10,26},{12,28},{14,30},{16,0},... | collective-permute-start | bytes 393224 | tf_op jit(solution)/shard_map/ppermute | solution.py:404
  46.3 6.5 %collective-permute-start.12 = (f32[32,512]{1,0:T(8,128)S(1)}, f32[32,512]{1,0:T(8,128)S(1)}, u32[]{:S(2)}, u32[]{:S(2)}) collective-permute-start(f32[32,512]{1,0:T(8,128)S(1)} %get-tuple-element.72), channel_id=1, source_target_pairs={{0,30},{2,4},{4,2},{6,8},{8,6},{10,12},{12,10},{14,16},{16,14},{18... | collective-permute-start | bytes 196616 | tf_op jit(solution)/shard_map/ppermute | solution.py:407
  47.1 5.7 %collective-permute-start.13 = (f32[32,512]{1,0:T(8,128)S(1)}, f32[32,512]{1,0:T(8,128)S(1)}, u32[]{:S(2)}, u32[]{:S(2)}) collective-permute-start(f32[32,512]{1,0:T(8,128)S(1)} %get-tuple-element.73), channel_id=1, source_target_pairs={{0,2},{2,0},{4,6},{6,4},{8,10},{10,8},{12,14},{14,12},{16,18},{18,... | collective-permute-start | bytes 196616 | tf_op jit(solution)/shard_map/ppermute | solution.py:410
  53.0 6.9 %collective-permute-start.14 = (f32[64,512]{1,0:T(8,128)S(1)}, f32[64,512]{1,0:T(8,128)S(1)}, u32[]{:S(2)}, u32[]{:S(2)}) collective-permute-start(f32[64,512]{1,0:T(8,128)S(1)} %shard_map.69), channel_id=1, source_target_pairs={{0,16},{2,18},{4,20},{6,22},{8,24},{10,26},{12,28},{14,30},{16,0},... | collective-permute-start | bytes 393224 | tf_op jit(solution)/shard_map/ppermute | solution.py:404
  53.3 6.5 %collective-permute-start.15 = (f32[32,512]{1,0:T(8,128)S(1)}, f32[32,512]{1,0:T(8,128)S(1)}, u32[]{:S(2)}, u32[]{:S(2)}) collective-permute-start(f32[32,512]{1,0:T(8,128)S(1)} %get-tuple-element.79), channel_id=1, source_target_pairs={{0,30},{2,4},{4,2},{6,8},{8,6},{10,12},{12,10},{14,16},{16,14},{18... | collective-permute-start | bytes 196616 | tf_op jit(solution)/shard_map/ppermute | solution.py:407
  54.5 5.4 %collective-permute-start.16 = (f32[32,512]{1,0:T(8,128)S(1)}, f32[32,512]{1,0:T(8,128)S(1)}, u32[]{:S(2)}, u32[]{:S(2)}) collective-permute-start(f32[32,512]{1,0:T(8,128)S(1)} %get-tuple-element.80), channel_id=1, source_target_pairs={{0,2},{2,0},{4,6},{6,4},{8,10},{10,8},{12,14},{14,12},{16,18},{18,... | collective-permute-start | bytes 196616 | tf_op jit(solution)/shard_map/ppermute | solution.py:410

commit v8 on v7

--- a/solution.py
+++ b/solution.py
@@ -268,16 +268,13 @@
     rest_out[...] = start_own[:, edge_nodes:] + rotate_half(columns, top, low, groups, 0)
 
 
-def first_part(start_edge, far_in, out_in, near_in, ham_top, ham_low, pair_in, part_out, overlap_out, couple_out):
+def first_part(start_edge, far_in, out_in, near_in, ham_top, ham_low, part_out):
     edge_nodes = start_edge.shape[0]
     nodes = ham_top.shape[0] - 4 * out_in.shape[0]
-    duo = far_in.shape[0]
     ghosts = jnp.concatenate([far_in[...], out_in[...], near_in[...]], 0)
     part_out[...] = mul(
         (ham_top[:, :edge_nodes], ham_low[:, :edge_nodes]), split(start_edge[...])
     ) + mul((ham_top[:, nodes:], ham_low[:, nodes:]), split(ghosts))
-    overlap_out[...] = SCALE_ONE * pair_in[:, :duo]
-    couple_out[...] = pair_in[:, duo:]
 
 
 def rotate_rest(
@@ -296,8 +293,7 @@
 
 
 def first_base(
-    start_edge, start_rest, part, ham_top, ham_low, pick, overlap, back_far,
-    start_out, base_out, packed_out, adjust_out,
+    start_edge, start_rest, part, ham_top, ham_low, pick, start_out, base_out, packed_out
 ):
     nodes = ham_top.shape[0] - pick.shape[0]
     edge_nodes = start_edge.shape[0]
@@ -310,13 +306,14 @@
     base = SCALE_ONE * (own - CENTRE * start)
     base_out[...] = base
     packed_out[...] = sift(pick[...], base[:edge_nodes])
-    adjust_out[...] = mul(split(overlap[...]), split(back_far[...]))
-
-
-def fetch_far(packed, both, out_in, near_in, far_out):
+
+
+def fetch_far(packed, both, pair, out_in, near_in, far_out):
     duo = 2 * out_in.shape[0]
+    block = packed.shape[1]
     back = jnp.concatenate([out_in[...], near_in[...]], 0)
-    far_out[...] = packed[:duo, :] + SCALE_ONE * sift(both[:duo, duo:], back)
+    far_out[:, block:] = pair[...]
+    far_out[:, :block] = packed[:duo, :] + SCALE_ONE * sift(both[:duo, duo:], back)
 
 
 def fetch_ring(packed, both, far_in, out_in, near_in, out_out, near_out):
@@ -328,7 +325,7 @@
 
 
 def first_own(
-    base, pick, far_in, out_in, near_in, ham_top, ham_low, couple, first_out, part_out, known_out
+    base, pick, far_in, out_in, near_in, ham_top, ham_low, first_out, part_out, picked_out
 ):
     edge_nodes = pick.shape[1]
     nodes = base.shape[0]
@@ -338,7 +335,7 @@
     first = jnp.concatenate([edge, base[edge_nodes:, :]], 0)
     first_out[...] = first
     part_out[...] = mul((ham_top[:, :nodes], ham_low[:, :nodes]), split(first))
-    known_out[...] = mul(split(couple[...]), split(sift(pick[:duo, :], edge)))
+    picked_out[...] = sift(pick[:duo, :], edge)
 
 
 def return_far(part, ham_top, ham_low, out_in, near_in, far_out):
@@ -351,27 +348,33 @@
 
 
 def return_ring(
-    part, ham_top, ham_low, far_in, adjust, out_in, near_in, ghosts_out, out_out, near_out
+    part, ham_top, ham_low, far_in, back_far, out_in, near_in, ghosts_out, out_out, near_out
 ):
     halo = out_in.shape[0]
     nodes = part.shape[0] - 4 * halo
     ring = slice(nodes + 2 * halo, nodes + 4 * halo)
-    ghosts = jnp.concatenate([far_in[...] + adjust[...], out_in[...], near_in[...]], 0)
+    duo, block = back_far.shape
+    overlap = far_in[:, block : block + duo].astype(BF16)
+    far = far_in[:, :block] + SCALE_ONE * sift(overlap, back_far[...])
+    ghosts = jnp.concatenate([far, out_in[...], near_in[...]], 0)
     ghosts_out[...] = ghosts
     rows = part[ring, :] + mul((ham_top[ring, nodes:], ham_low[ring, nodes:]), split(ghosts))
     out_out[...] = rows[:halo]
     near_out[...] = rows[halo:]
 
 
-def second_base(part, ghosts, ham_top, ham_low, first, start, known, shuffle, hits, result_out):
+def second_base(
+    part, ghosts, ham_top, ham_low, first, start, picked, far_in, shuffle, hits, result_out
+):
     nodes = first.shape[0]
-    duo = known.shape[0]
+    duo, block = picked.shape
+    known = mul(split(far_in[:, block + duo :]), split(picked[...]))
     ham = (ham_top[:nodes, nodes:], ham_low[:nodes, nodes:])
     second = part[:nodes, :] + mul(ham, split(ghosts[...])) - CENTRE * first[...]
     second = SCALE_TWO * second - SIGMA_ONE * SIGMA_TWO * start[...]
     top, low = split(second.T)
     result = dot(top, shuffle[...]) + dot(low, shuffle[...])
-    top, low = split(SCALE_TWO * known[...].T)
+    top, low = split(SCALE_TWO * known.T)
     result_out[...] = result + (dot(top, hits[:duo, :]) + dot(low, hits[:duo, :]))
 
 
@@ -493,17 +496,14 @@
             pltpu.VMEM((elems * pitch, full), BF16),
         ],
     )
-    pair_in = far(pair)
     start_edge, out_rows, near_rows = call(
         functools.partial(rotate_ring, groups),
         [rows_of(wide), rows_of(halo), rows_of(halo)],
         in_vmem(ring_cols_in), start_own, start_far, ritz_top, ritz_low, pick,
     )
     out_in, near_in = out(out_rows), near(near_rows)
-    part, overlap, couple = call(
-        first_part,
-        [rows_of(full), ((duo, duo), F32), ((duo, duo), F32)],
-        start_edge, far_in, out_in, near_in, ham_top, ham_low, pair_in,
+    (part,) = call(
+        first_part, [rows_of(full)], start_edge, far_in, out_in, near_in, ham_top, ham_low
     )
     (rest_low,) = call(
         functools.partial(rotate_low, groups),
@@ -517,21 +517,23 @@
         in_vmem(high_cols_in), rest_low, ritz_top, ritz_low, part, ham_top, ham_low,
     )
     far_in, out_in, near_in = far(back_far), out(back_out), near(back_near)
-    start, base, packed, adjust = call(
+    start, base, packed = call(
         first_base,
-        [rows_of(nodes), rows_of(nodes), rows_of(wide), rows_of(duo)],
-        start_edge, start_rest, part, ham_top, ham_low, pick, overlap, back_far,
-    )
-    (far_rows,) = call(fetch_far, [rows_of(duo)], packed, both, out_in, near_in)
+        [rows_of(nodes), rows_of(nodes), rows_of(wide)],
+        start_edge, start_rest, part, ham_top, ham_low, pick,
+    )
+    (far_rows,) = call(
+        fetch_far, [((duo, block + 2 * duo), F32)], packed, both, pair, out_in, near_in
+    )
     fetched_far = far(far_rows)
     out_rows, near_rows = call(
         fetch_ring, halo_out[1:], packed, both, far_in, out_in, near_in
     )
     fetched_out, fetched_near = out(out_rows), near(near_rows)
-    first, part, known = call(
+    first, part, picked = call(
         first_own,
         [rows_of(nodes), rows_of(full), rows_of(duo)],
-        base, pick, far_in, out_in, near_in, ham_top, ham_low, couple,
+        base, pick, far_in, out_in, near_in, ham_top, ham_low,
     )
 
     (far_rows,) = call(
@@ -541,13 +543,13 @@
     ghosts, out_rows, near_rows = call(
         return_ring,
         [rows_of(wide)] + halo_out[1:],
-        part, ham_top, ham_low, fetched_far, adjust, fetched_out, fetched_near,
+        part, ham_top, ham_low, fetched_far, back_far, fetched_out, fetched_near,
     )
     returned_out, returned_near = out(out_rows), near(near_rows)
     (result,) = call(
         second_base,
         [((block, nodes), F32)],
-        part, ghosts, ham_top, ham_low, first, start, known, shuffle, hits,
+        part, ghosts, ham_top, ham_low, first, start, picked, fetched_far, shuffle, hits,
     )
     (result,) = call(
         finish, [((block, nodes), F32)], result, hits, returned_far, returned_out, returned_near

time: 61.3 us -> 63.4 us (1.034)
  starting transfers between devices: 18.9 us -> 20.1 us
  waiting for transfers between devices: 18.4 us -> 19.2 us
    ppermute x4, waiting for transfers between devices: 13.4 us -> 18.5 us  [out(): return lax.ppermute(rows, 'mesh', pairs_out)]
    ppermute x5 -> x4, waiting for transfers between devices: 4.26 us -> 0.01 us  [far(): return lax.ppermute(rows, 'mesh', pairs_far)]
    ppermute x5 -> x4, starting transfers between devices: 7.67 us -> 10.3 us  [far(): return lax.ppermute(rows, 'mesh', pairs_far)]
    ppermute x4, starting transfers between devices: 4.45 us -> 1.99 us  [out(): return lax.ppermute(rows, 'mesh', pairs_out)]
    ppermute x4, starting transfers between devices: 1.6 us -> 2.66 us  [near(): return lax.ppermute(rows, 'mesh', pairs_in)]
  transfers between devices with their start and end apart: 17 -> 16, of which waited for: 5 -> 5; matrix products, arithmetic and copies ran while one was open for 0% -> 0% of each run, Pallas kernels for 30% -> 29%
where the time goes in v8:
time: 63.4 us; the launch traced here: 63.2 us
  Pallas kernels  23.7 us (37%)
  starting transfers between devices  20.1 us (32%)
  waiting for transfers between devices  19.2 us (30%)
    pallas_call x16, Pallas kernels, call(): pl.pallas_call(body, out_shape=[pltpu.VMEM(*out) if kept else jax.ShapeDt...  23.7 us
    ppermute x4, waiting for transfers between devices, out(): return lax.ppermute(rows, 'mesh', pairs_out)  18.5 us
    ppermute x4, starting transfers between devices, far(): return lax.ppermute(rows, 'mesh', pairs_far)  10.3 us
    ppermute x4, starting transfers between devices, gather(): lax.ppermute(rows, 'state', [(i, (i + step) % groups) for i in range(grou...  5.14 us
    ppermute x4, starting transfers between devices, near(): return lax.ppermute(rows, 'mesh', pairs_in)  2.66 us
    ppermute x4, starting transfers between devices, out(): return lax.ppermute(rows, 'mesh', pairs_out)  1.99 us
  transfers between devices with their start and end apart: 16, of which 5 were waited for; matrix products, arithmetic and copies ran while one was open for 0% of the time, Pallas kernels for 29%

profile of v8, /device:TPU:0, one launch (start us, length us, event | category | flops | bytes accessed | tf_op | source)
XLA Modules:
  0.0 63.2 jit_solution(15153765588723810888)
XLA Ops:
  0.0 2.7 %shard_map.55 = (f32[512,128]{1,0:T(8,128)}, f32[512,128]{1,0:T(8,128)}, f32[512,128]{1,0:T(8,128)}, f32[512,128]{1,0:T(8,128)}, bf16[256,256]{1,0:T(8,128)(2,1)S(1)}) custom-call(s32[1,4,32]{2,1,0:T(4,128)} %lists.3, f32[1024,256]{1,0:T(8,128)} %subspace_in.1), custom_call_target="tpu_custom_call" | custom-call | flops 1000 | bytes 1000 | tf_op jit(solution)/shard_map/pallas_call | solution.py:43
  2.7 3.0 %collective-permute-start.1 = (f32[512,128]{1,0:T(8,128)}, f32[512,128]{1,0:T(8,128)}, u32[]{:S(2)}, u32[]{:S(2)}) collective-permute-start(f32[512,128]{1,0:T(8,128)} %get-tuple-element.40.far), channel_id=1, source_target_pairs={{0,1},{1,0},{2,3},{3,2},{4,5},{5,4},{6,7},{7,6},{8,9},{9,8},{10,11... | collective-permute-start | bytes 786440 | tf_op jit(solution)/shard_map/ppermute | solution.py:417
  5.9 1.9 %collective-permute-start.3 = (f32[512,128]{1,0:T(8,128)}, f32[512,128]{1,0:T(8,128)S(1)}, u32[]{:S(2)}, u32[]{:S(2)}) collective-permute-start(f32[512,128]{1,0:T(8,128)} %get-tuple-element.41.low_rest), channel_id=1, source_target_pairs={{0,1},{1,0},{2,3},{3,2},{4,5},{5,4},{6,7},{7,6},{8,9},{9,8},{10,11... | collective-permute-start | bytes 786440 | tf_op jit(solution)/shard_map/ppermute | solution.py:417
  7.9 4.6 %shard_map.56 = (f32[512,256]{1,0:T(8,128)S(1)}, bf16[512,1024]{1,0:T(8,128)(2,1)S(1)}, bf16[512,1024]{1,0:T(8,128)(2,1)S(1)}) custom-call(s32[1]{0:T(128)} %bitcast.group, f32[512,128]{1,0:T(8,128)} %get-tuple-element.40.far, f32[512,128]{1,0:T(8,128)} %get-tuple-element.39.ring, f32[512,128]{1,0:T(8,128)} %get-tuple-element.41.low_rest, ...), custom_call_target="tpu_custom_call" | custom-call | flops 1000 | bytes 1000 | tf_op jit(solution)/shard_map/pallas_call | solution.py:43
  12.5 0.7 %collective-permute-done.1.columns = f32[512,128]{1,0:T(8,128)} collective-permute-done((f32[512,128]{1,0:T(8,128)}, f32[512,128]{1,0:T(8,128)}, u32[]{:S(2)}, u32[]{:S(2)}) %collective-permute-start.1) | collective-permute-done | bytes 262176 | tf_op jit(solution)/shard_map/ppermute | solution.py:417
  13.2 2.8 %shard_map.57 = (f32[64,512]{1,0:T(8,128)S(1)}, f32[64,512]{1,0:T(8,128)}) custom-call(f32[512,128]{1,0:T(8,128)} %collective-permute-done.1.columns, f32[512,256]{1,0:T(8,128)S(1)} %get-tuple-element.43.start_own, bf16[512,1024]{1,0:T(8,128)(2,1)S(1)} %get-tuple-element.44.top, bf16[512,1024]{1,0:T(8,128)(2,1)S(1)} %get-tuple-element.45.low, ...), custom_call_target="tpu_custom_call" | custom-call | flops 1000 | bytes 1000 | tf_op jit(solution)/shard_map/pallas_call | solution.py:43
  16.1 3.1 %collective-permute-start.4 = (f32[64,512]{1,0:T(8,128)}, f32[64,512]{1,0:T(8,128)S(1)}, u32[]{:S(2)}, u32[]{:S(2)}) collective-permute-start(f32[64,512]{1,0:T(8,128)} %get-tuple-element.50), channel_id=1, source_target_pairs={{0,16},{2,18},{4,20},{6,22},{8,24},{10,26},{12,28},{14,30},{16,0},... | collective-permute-start | bytes 393224 | tf_op jit(solution)/shard_map/ppermute | solution.py:407
  19.2 4.9 %shard_map.58 = (bf16[384,384]{1,0:T(8,128)(2,1)S(1)}, bf16[384,384]{1,0:T(8,128)(2,1)S(1)}, bf16[128,128]{1,0:T(8,128)(2,1)S(1)}, bf16[128,128]{1,0:T(8,128)(2,...) custom-call(s32[1]{0:T(128)} %bitcast.1.odd, s32[1,4,32]{2,1,0:T(4,128)S(1)} %copy-done, ...), custom_call_target="tpu_custom_call" | custom-call | flops 1000 | bytes 1000 | tf_op jit(solution)/shard_map/pallas_call | solution.py:43
  24.1 1.2 %shard_map.59 = (f32[128,512]{1,0:T(8,128)S(1)}, f32[32,512]{1,0:T(8,128)S(1)}, f32[32,512]{1,0:T(8,128)S(1)}) custom-call(f32[512,128]{1,0:T(8,128)S(1)} %collective-permute-done.columns, f32[512,256]{1,0:T(8,128)S(1)} %get-tuple-element.43.start_own, f32[64,512]{1,0:T(8,128)S(1)} %get-tuple-element.47._.start_far, ...), custom_call_target="tpu_custom_call" | custom-call | flops 1000 | bytes 1000 | tf_op jit(solution)/shard_map/pallas_call | solution.py:43
  25.4 1.6 %collective-permute-start.6 = (f32[32,512]{1,0:T(8,128)S(1)}, f32[32,512]{1,0:T(8,128)S(1)}, u32[]{:S(2)}, u32[]{:S(2)}) collective-permute-start(f32[32,512]{1,0:T(8,128)S(1)} %get-tuple-element.52), channel_id=1, source_target_pairs={{0,2},{2,0},{4,6},{6,4},{8,10},{10,8},{12,14},{14,12},{16,18},{18,... | collective-permute-start | bytes 196616 | tf_op jit(solution)/shard_map/ppermute | solution.py:413
  27.5 4.3 %collective-permute-done.5.out_in = f32[32,512]{1,0:T(8,128)S(1)} collective-permute-done((f32[32,512]{1,0:T(8,128)S(1)}, f32[32,512]{1,0:T(8,128)S(1)}, u32[]{:S(2)}, u32[]{:S(2)}) %collective-permute-start.5) | collective-permute-done | bytes 65568 | tf_op jit(solution)/shard_map/ppermute | solution.py:410
  31.8 0.8 %shard_map.61.part = f32[384,512]{1,0:T(8,128)S(1)} custom-call(f32[128,512]{1,0:T(8,128)S(1)} %get-tuple-element.49.start_edge, f32[64,512]{1,0:T(8,128)S(1)} %collective-permute-done.4.far_in, f32[32,512]{1,0:T(8,128)S(1)} %collective-permute-done.5.out_in, f32[32,512]{1,0:T(8,128)S(1)} %collective-permute-done.6.near_in, ...), custom_call_target="tpu_custom_call" | custom-call | flops 1000 | bytes 1000 | tf_op jit(solution)/shard_map/pallas_call | solution.py:43
  32.6 1.7 %shard_map.62 = (f32[128,512]{1,0:T(8,128)S(1)}, f32[64,512]{1,0:T(8,128)S(1)}, f32[32,512]{1,0:T(8,128)S(1)}, f32[32,512]{1,0:T(8,128)S(1)}) custom-call(f32[512,128]{1,0:T(8,128)} %collective-permute-done.2.columns, f32[512,128]{1,0:T(8,128)S(1)} %shard_map.60.rest_low, bf16[512,1024]{1,0:T(8,128)(2,1)S(1)} %get-tuple-element.44.top, ...), custom_call_target="tpu_custom_call" | custom-call | flops 1000 | bytes 1000 | tf_op jit(solution)/shard_map/pallas_call | solution.py:43
  34.5 1.0 %collective-permute-start.9 = (f32[32,512]{1,0:T(8,128)S(1)}, f32[32,512]{1,0:T(8,128)S(1)}, u32[]{:S(2)}, u32[]{:S(2)}) collective-permute-start(f32[32,512]{1,0:T(8,128)S(1)} %get-tuple-element.59), channel_id=1, source_target_pairs={{0,2},{2,0},{4,6},{6,4},{8,10},{10,8},{12,14},{14,12},{16,18},{18,... | collective-permute-start | bytes 196616 | tf_op jit(solution)/shard_map/ppermute | solution.py:413
  35.5 0.6 shard_map.63
  36.0 4.9 %collective-permute-done.8.out_in = f32[32,512]{1,0:T(8,128)S(1)} collective-permute-done((f32[32,512]{1,0:T(8,128)S(1)}, f32[32,512]{1,0:T(8,128)S(1)}, u32[]{:S(2)}, u32[]{:S(2)}) %collective-permute-start.8) | collective-permute-done | bytes 65568 | tf_op jit(solution)/shard_map/ppermute | solution.py:410
  41.2 2.6 %collective-permute-start.10 = (f32[64,640]{1,0:T(8,128)S(1)}, f32[64,640]{1,0:T(8,128)S(1)}, u32[]{:S(2)}, u32[]{:S(2)}) collective-permute-start(f32[64,640]{1,0:T(8,128)S(1)} %shard_map.65), channel_id=1, source_target_pairs={{0,16},{2,18},{4,20},{6,22},{8,24},{10,26},{12,28},{14,30},{16,0},... | collective-permute-start | bytes 491528 | tf_op jit(solution)/shard_map/ppermute | solution.py:407
  44.0 1.8 %collective-permute-start.11 = (f32[32,512]{1,0:T(8,128)S(1)}, f32[32,512]{1,0:T(8,128)S(1)}, u32[]{:S(2)}, u32[]{:S(2)}) collective-permute-start(f32[32,512]{1,0:T(8,128)S(1)} %get-tuple-element.64), channel_id=1, source_target_pairs={{0,30},{2,4},{4,2},{6,8},{8,6},{10,12},{12,10},{14,16},{16,14},{18... | collective-permute-start | bytes 196616 | tf_op jit(solution)/shard_map/ppermute | solution.py:410
  45.8 0.7 %shard_map.64 = (f32[256,512]{1,0:T(8,128)S(1)}, f32[384,512]{1,0:T(8,128)S(1)}, f32[64,512]{1,0:T(8,128)S(1)}) custom-call(f32[256,512]{1,0:T(8,128)S(1)} %get-tuple-element.56.base, bf16[128,128]{1,0:T(8,128)(2,1)S(1)} %get-tuple-element.48.pick, f32[64,512]{1,0:T(8,128)S(1)} %collective-permute-done.7.far_in, ...), custom_call_target="tpu_custom_call" | custom-call | flops 1000 | bytes 1000 | tf_op jit(solution)/shard_map/pallas_call | solution.py:43
  46.5 3.9 %collective-permute-done.11.out_in = f32[32,512]{1,0:T(8,128)S(1)} collective-permute-done((f32[32,512]{1,0:T(8,128)S(1)}, f32[32,512]{1,0:T(8,128)S(1)}, u32[]{:S(2)}, u32[]{:S(2)}) %collective-permute-start.11) | collective-permute-done | bytes 65568 | tf_op jit(solution)/shard_map/ppermute | solution.py:410
  50.7 4.5 %collective-permute-start.13 = (f32[64,512]{1,0:T(8,128)S(1)}, f32[64,512]{1,0:T(8,128)S(1)}, u32[]{:S(2)}, u32[]{:S(2)}) collective-permute-start(f32[64,512]{1,0:T(8,128)S(1)} %shard_map.69), channel_id=1, source_target_pairs={{0,16},{2,18},{4,20},{6,22},{8,24},{10,26},{12,28},{14,30},{16,0},... | collective-permute-start | bytes 393224 | tf_op jit(solution)/shard_map/ppermute | solution.py:407
  55.7 0.9 %shard_map.68.result = f32[512,256]{1,0:T(8,128)S(1)} custom-call(f32[384,512]{1,0:T(8,128)S(1)} %get-tuple-element.60.part, f32[128,512]{1,0:T(8,128)S(1)} %get-tuple-element.66.ghosts, bf16[384,384]{1,0:T(8,128)(2,1)S(1)} %get-tuple-element.53.ham_top, bf16[384,384]{1,0:T(8,128)(2,1)S(1)} %get-tuple-element.54.ham_low, ...), custom_call_target="tpu_custom_call" | custom-call | flops 1000 | bytes 1000 | tf_op jit(solution)/shard_map/pallas_call | solution.py:43
  56.7 5.4 %collective-permute-done.14.out_in = f32[32,512]{1,0:T(8,128)S(1)} collective-permute-done((f32[32,512]{1,0:T(8,128)S(1)}, f32[32,512]{1,0:T(8,128)S(1)}, u32[]{:S(2)}, u32[]{:S(2)}) %collective-permute-start.14) | collective-permute-done | bytes 65568 | tf_op jit(solution)/shard_map/ppermute | solution.py:410
  62.0 1.1 %shard_map.70 = f32[512,256]{1,0:T(8,128)} custom-call(f32[512,256]{1,0:T(8,128)S(1)} %shard_map.68.result, bf16[128,256]{1,0:T(8,128)(2,1)S(1)} %get-tuple-element.70.hits, f32[64,512]{1,0:T(8,128)S(1)} %collective-permute-done.13.far_in, f32[32,512]{1,0:T(8,128)S(1)} %collective-permute-done.14.out_in, f32[32,512]{1,0:T(8,128)S(1)} %collective-permute-done.15.near_in), custom_call_target="tpu_custom_call" | custom-call | flops 1000 | bytes 1000 | tf_op jit(solution)/shard_map/pallas_call | solution.py:43
  (28 shorter events, 2.0 us)
Async XLA Ops:
  0.0 13.2 %copy-start = (s32[1,4,32]{2,1,0:T(4,128)S(1)}, s32[1,4,32]{2,1,0:T(4,128)}, u32[]{:S(2)}) copy-start(s32[1,4,32]{2,1,0:T(4,128)} %lists.3) | copy-start | bytes 1540
  2.7 16.5 %copy-start.1 = (s32[16,125]{1,0:T(8,128)S(1)}, s32[16,125]{1,0:T(8,128)}, u32[]{:S(2)}) copy-start(s32[16,125]{1,0:T(8,128)} %connect.1) | copy-start | bytes 24004
  2.7 10.5 %collective-permute-start.1 = (f32[512,128]{1,0:T(8,128)}, f32[512,128]{1,0:T(8,128)}, u32[]{:S(2)}, u32[]{:S(2)}) collective-permute-start(f32[512,128]{1,0:T(8,128)} %get-tuple-element.40.far), channel_id=1, source_target_pairs={{0,1},{1,0},{2,3},{3,2},{4,5},{5,4},{6,7},{7,6},{8,9},{9,8},{10,11... | collective-permute-start | bytes 786440 | tf_op jit(solution)/shard_map/ppermute | solution.py:417
  5.8 18.3 %collective-permute-start = (f32[512,128]{1,0:T(8,128)}, f32[512,128]{1,0:T(8,128)S(1)}, u32[]{:S(2)}, u32[]{:S(2)}) collective-permute-start(f32[512,128]{1,0:T(8,128)} %get-tuple-element.39.ring), channel_id=1, source_target_pairs={{0,1},{1,0},{2,3},{3,2},{4,5},{5,4},{6,7},{7,6},{8,9},{9,8},{10,11... | collective-permute-start | bytes 786440 | tf_op jit(solution)/shard_map/ppermute | solution.py:417
  5.9 21.2 %collective-permute-start.3 = (f32[512,128]{1,0:T(8,128)}, f32[512,128]{1,0:T(8,128)S(1)}, u32[]{:S(2)}, u32[]{:S(2)}) collective-permute-start(f32[512,128]{1,0:T(8,128)} %get-tuple-element.41.low_rest), channel_id=1, source_target_pairs={{0,1},{1,0},{2,3},{3,2},{4,5},{5,4},{6,7},{7,6},{8,9},{9,8},{10,11... | collective-permute-start | bytes 786440 | tf_op jit(solution)/shard_map/ppermute | solution.py:417
  7.8 24.8 %collective-permute-start.2 = (f32[512,128]{1,0:T(8,128)}, f32[512,128]{1,0:T(8,128)}, u32[]{:S(2)}, u32[]{:S(2)}) collective-permute-start(f32[512,128]{1,0:T(8,128)} %get-tuple-element.42.high_rest), channel_id=1, source_target_pairs={{0,1},{1,0},{2,3},{3,2},{4,5},{5,4},{6,7},{7,6},{8,9},{9,8},{10,11... | collective-permute-start | bytes 786440 | tf_op jit(solution)/shard_map/ppermute | solution.py:417
  16.1 15.7 %collective-permute-start.4 = (f32[64,512]{1,0:T(8,128)}, f32[64,512]{1,0:T(8,128)S(1)}, u32[]{:S(2)}, u32[]{:S(2)}) collective-permute-start(f32[64,512]{1,0:T(8,128)} %get-tuple-element.50), channel_id=1, source_target_pairs={{0,16},{2,18},{4,20},{6,22},{8,24},{10,26},{12,28},{14,30},{16,0},... | collective-permute-start | bytes 393224 | tf_op jit(solution)/shard_map/ppermute | solution.py:407
  25.4 6.5 %collective-permute-start.5 = (f32[32,512]{1,0:T(8,128)S(1)}, f32[32,512]{1,0:T(8,128)S(1)}, u32[]{:S(2)}, u32[]{:S(2)}) collective-permute-start(f32[32,512]{1,0:T(8,128)S(1)} %get-tuple-element.51), channel_id=1, source_target_pairs={{0,30},{2,4},{4,2},{6,8},{8,6},{10,12},{12,10},{14,16},{16,14},{18... | collective-permute-start | bytes 196616 | tf_op jit(solution)/shard_map/ppermute | solution.py:410
  25.4 6.4 %collective-permute-start.6 = (f32[32,512]{1,0:T(8,128)S(1)}, f32[32,512]{1,0:T(8,128)S(1)}, u32[]{:S(2)}, u32[]{:S(2)}) collective-permute-start(f32[32,512]{1,0:T(8,128)S(1)} %get-tuple-element.52), channel_id=1, source_target_pairs={{0,2},{2,0},{4,6},{6,4},{8,10},{10,8},{12,14},{14,12},{16,18},{18,... | collective-permute-start | bytes 196616 | tf_op jit(solution)/shard_map/ppermute | solution.py:413
  34.3 9.5 %collective-permute-start.7 = (f32[64,512]{1,0:T(8,128)S(1)}, f32[64,512]{1,0:T(8,128)S(1)}, u32[]{:S(2)}, u32[]{:S(2)}) collective-permute-start(f32[64,512]{1,0:T(8,128)S(1)} %get-tuple-element.57.back_far), channel_id=1, source_target_pairs={{0,16},{2,18},{4,20},{6,22},{8,24},{10,26},{12,28},{14,30},{16,0},... | collective-permute-start | bytes 393224 | tf_op jit(solution)/shard_map/ppermute | solution.py:407
  34.4 6.6 %collective-permute-start.8 = (f32[32,512]{1,0:T(8,128)S(1)}, f32[32,512]{1,0:T(8,128)S(1)}, u32[]{:S(2)}, u32[]{:S(2)}) collective-permute-start(f32[32,512]{1,0:T(8,128)S(1)} %get-tuple-element.58), channel_id=1, source_target_pairs={{0,30},{2,4},{4,2},{6,8},{8,6},{10,12},{12,10},{14,16},{16,14},{18... | collective-permute-start | bytes 196616 | tf_op jit(solution)/shard_map/ppermute | solution.py:410
  34.5 6.5 %collective-permute-start.9 = (f32[32,512]{1,0:T(8,128)S(1)}, f32[32,512]{1,0:T(8,128)S(1)}, u32[]{:S(2)}, u32[]{:S(2)}) collective-permute-start(f32[32,512]{1,0:T(8,128)S(1)} %get-tuple-element.59), channel_id=1, source_target_pairs={{0,2},{2,0},{4,6},{6,4},{8,10},{10,8},{12,14},{14,12},{16,18},{18,... | collective-permute-start | bytes 196616 | tf_op jit(solution)/shard_map/ppermute | solution.py:413
  41.2 14.0 %collective-permute-start.10 = (f32[64,640]{1,0:T(8,128)S(1)}, f32[64,640]{1,0:T(8,128)S(1)}, u32[]{:S(2)}, u32[]{:S(2)}) collective-permute-start(f32[64,640]{1,0:T(8,128)S(1)} %shard_map.65), channel_id=1, source_target_pairs={{0,16},{2,18},{4,20},{6,22},{8,24},{10,26},{12,28},{14,30},{16,0},... | collective-permute-start | bytes 491528 | tf_op jit(solution)/shard_map/ppermute | solution.py:407
  44.0 6.5 %collective-permute-start.11 = (f32[32,512]{1,0:T(8,128)S(1)}, f32[32,512]{1,0:T(8,128)S(1)}, u32[]{:S(2)}, u32[]{:S(2)}) collective-permute-start(f32[32,512]{1,0:T(8,128)S(1)} %get-tuple-element.64), channel_id=1, source_target_pairs={{0,30},{2,4},{4,2},{6,8},{8,6},{10,12},{12,10},{14,16},{16,14},{18... | collective-permute-start | bytes 196616 | tf_op jit(solution)/shard_map/ppermute | solution.py:410
  45.8 4.7 %collective-permute-start.12 = (f32[32,512]{1,0:T(8,128)S(1)}, f32[32,512]{1,0:T(8,128)S(1)}, u32[]{:S(2)}, u32[]{:S(2)}) collective-permute-start(f32[32,512]{1,0:T(8,128)S(1)} %get-tuple-element.65), channel_id=1, source_target_pairs={{0,2},{2,0},{4,6},{6,4},{8,10},{10,8},{12,14},{14,12},{16,18},{18,... | collective-permute-start | bytes 196616 | tf_op jit(solution)/shard_map/ppermute | solution.py:413
  50.7 11.3 %collective-permute-start.13 = (f32[64,512]{1,0:T(8,128)S(1)}, f32[64,512]{1,0:T(8,128)S(1)}, u32[]{:S(2)}, u32[]{:S(2)}) collective-permute-start(f32[64,512]{1,0:T(8,128)S(1)} %shard_map.69), channel_id=1, source_target_pairs={{0,16},{2,18},{4,20},{6,22},{8,24},{10,26},{12,28},{14,30},{16,0},... | collective-permute-start | bytes 393224 | tf_op jit(solution)/shard_map/ppermute | solution.py:407
  55.6 6.5 %collective-permute-start.14 = (f32[32,512]{1,0:T(8,128)S(1)}, f32[32,512]{1,0:T(8,128)S(1)}, u32[]{:S(2)}, u32[]{:S(2)}) collective-permute-start(f32[32,512]{1,0:T(8,128)S(1)} %get-tuple-element.71), channel_id=1, source_target_pairs={{0,30},{2,4},{4,2},{6,8},{8,6},{10,12},{12,10},{14,16},{16,14},{18... | collective-permute-start | bytes 196616 | tf_op jit(solution)/shard_map/ppermute | solution.py:410
  55.6 6.4 %collective-permute-start.15 = (f32[32,512]{1,0:T(8,128)S(1)}, f32[32,512]{1,0:T(8,128)S(1)}, u32[]{:S(2)}, u32[]{:S(2)}) collective-permute-start(f32[32,512]{1,0:T(8,128)S(1)} %get-tuple-element.72), channel_id=1, source_target_pairs={{0,2},{2,0},{4,6},{6,4},{8,10},{10,8},{12,14},{14,12},{16,18},{18,... | collective-permute-start | bytes 196616 | tf_op jit(solution)/shard_map/ppermute | solution.py:413

commit v9 on v6

--- a/solution.py
+++ b/solution.py
@@ -64,7 +64,7 @@
 
 
 def renumber(
-    lists_in, subspace_in, far_out, ring_out, low_out, high_out, shuffle_out, origin_out, lists, subspace, sems
+    lists_in, subspace_in, far_out, ring_out, low_out, high_out, shuffle_out, lists, subspace, sems
 ):
     slots, halo = lists.shape[1:]
     depth, nodes = subspace.shape
@@ -102,7 +102,6 @@
     match = place == down
     shuffle = jnp.where(match, 1.0, 0.0).astype(BF16)
     shuffle_out[...] = shuffle
-    origin_out[...] = jnp.sum(jnp.where(match, along, 0), axis=1, keepdims=True)
     copy.wait()
     halves = []
     for part, rest_out in enumerate((low_out, high_out)):
@@ -115,14 +114,14 @@
 
 
 def assemble(
-    odd, lists, connect, blocks_in, shuffle, origin, top_out, low_out, pick_out, both_out, hits_out, pair_out,
-    blocks, sem, spread, rows_top, rows_low,
+    odd, lists, connect, blocks_in, shuffle, top_out, low_out, pick_out, both_out, hits_out, pair_out,
+    blocks, sem, spread, rows_both,
 ):
     copy = pltpu.make_async_copy(blocks_in, blocks, sem)
     copy.start()
     elems, size = connect.shape
     slots, halo = lists.shape[1:]
-    nodes = origin.shape[0]
+    nodes = shuffle.shape[0]
     wide = slots * halo
     duo = 2 * halo
     swap = odd[0] == 1
@@ -142,8 +141,11 @@
     ghost = jnp.concatenate(
         [3 * halo + lane, 2 * halo + lane, (1 - flag) * halo + lane, flag * halo + lane], 0
     )
-    numbers = jnp.concatenate([origin[...], nodes + ghost], 0)
+    along = lax.broadcasted_iota(I32, (nodes, nodes), 1).astype(F32)
+    origin = jnp.sum(along * shuffle[...].astype(F32), axis=1, keepdims=True).astype(I32)
     pitch = spread.shape[1] // elems
+    full = nodes + wide
+    numbers = jnp.broadcast_to(jnp.concatenate([origin, nodes + ghost], 0), (full, pitch))
     copy.wait()
     for elem in range(elems):
         cols = slice(elem * pitch, (elem + 1) * pitch)
@@ -152,10 +154,12 @@
         spread[:, cols] = chosen
         block = blocks[pl.ds(elem, size, stride=elems), :]
         top, low = split(jnp.pad(block, ((0, pitch - size), (0, pitch - size))))
-        top, low = split(dot(top, chosen, NT) + dot(low, chosen, NT))
-        rows_top[cols, :] = top
-        rows_low[cols, :] = low
-    ham = dot(spread[...], rows_top[...]) + dot(spread[...], rows_low[...])
+        rows = dot(jnp.concatenate([top, low], 0), chosen, NT)
+        top, low = split(rows[:pitch] + rows[pitch:])
+        rows_both[cols, :full] = top
+        rows_both[cols, full:] = low
+    ham = dot(spread[...], rows_both[...])
+    ham = ham[:, :full] + ham[:, full:]
     top, low = split(ham)
     top_out[...] = top
     low_out[...] = low
@@ -234,11 +238,12 @@
     )
 
 
-def rotate_far(groups, columns, start_own, top, low, pick, start_out, far_out):
-    duo = far_out.shape[0]
+def rotate_far(groups, columns, start_own, top, low, pick, pair, start_out, far_out):
+    duo, block = start_out.shape
     start = (start_own[:, :duo] + rotate_sides(columns, top, low, groups)).T
     start_out[...] = start
-    far_out[...] = sift(pick[:duo, :duo], start)
+    far_out[:, :block] = sift(pick[:duo, :duo], start)
+    far_out[:, block:] = pair[...]
 
 
 def rotate_ring(groups, columns, start_own, start_far, top, low, pick, start_out, out_out, near_out):
@@ -257,16 +262,17 @@
     rest_out[...] = start_own[:, edge_nodes:] + rotate_half(columns, top, low, groups, 0)
 
 
-def first_part(start_edge, far_in, out_in, near_in, ham_top, ham_low, pair_in, part_out, overlap_out, couple_out):
+def first_part(start_edge, far_in, out_in, near_in, ham_top, ham_low, part_out, overlap_out, couple_out):
     edge_nodes = start_edge.shape[0]
     nodes = ham_top.shape[0] - 4 * out_in.shape[0]
     duo = far_in.shape[0]
-    ghosts = jnp.concatenate([far_in[...], out_in[...], near_in[...]], 0)
+    block = start_edge.shape[1]
+    ghosts = jnp.concatenate([far_in[:, :block], out_in[...], near_in[...]], 0)
     part_out[...] = mul(
         (ham_top[:, :edge_nodes], ham_low[:, :edge_nodes]), split(start_edge[...])
     ) + mul((ham_top[:, nodes:], ham_low[:, nodes:]), split(ghosts))
-    overlap_out[...] = SCALE_ONE * pair_in[:, :duo]
-    couple_out[...] = pair_in[:, duo:]
+    overlap_out[...] = SCALE_ONE * far_in[:, block : block + duo]
+    couple_out[...] = far_in[:, block + duo :]
 
 
 def rotate_rest(
@@ -413,7 +419,7 @@
     vmem = pl.BlockSpec(memory_space=pltpu.VMEM)
     hbm = pl.BlockSpec(memory_space=pltpu.HBM)
 
-    far_cols, ring_cols, low_cols, high_cols, shuffle, origin = call(
+    far_cols, ring_cols, low_cols, high_cols, shuffle = call(
         renumber,
         [
             ((depth // 2, 2 * duo), F32),
@@ -421,7 +427,6 @@
             ((depth // 2, nodes - wide), F32),
             ((depth // 2, nodes - wide), F32),
             ((nodes, nodes), BF16),
-            ((nodes, 1), I32),
         ],
         in_hbm(send_rows), in_hbm(subspace),
         kept=True,
@@ -449,18 +454,16 @@
             ((wide, nodes), BF16),
             ((duo, 2 * duo), F32),
         ],
-        odd, send_rows, connect, in_hbm(blocks), shuffle, origin,
+        odd, send_rows, connect, in_hbm(blocks), shuffle,
         limit=12,
-        in_specs=[smem, vmem, vmem, hbm, vmem, vmem],
+        in_specs=[smem, vmem, vmem, hbm, vmem],
         scratch_shapes=[
             pltpu.VMEM(blocks.shape, F32),
             pltpu.SemaphoreType.DMA,
             pltpu.VMEM((full, elems * pitch), BF16),
-            pltpu.VMEM((elems * pitch, full), BF16),
-            pltpu.VMEM((elems * pitch, full), BF16),
-        ],
-    )
-    pair_in = far(pair)
+            pltpu.VMEM((elems * pitch, 2 * full), BF16),
+        ],
+    )
     others = groups - 1
     start_own, ritz_top, ritz_low = call(
         rotate_own,
@@ -480,8 +483,8 @@
 
     start_far, far_rows = call(
         functools.partial(rotate_far, groups),
-        [rows_of(duo), rows_of(duo)],
-        in_vmem(far_cols_in), start_own, ritz_top, ritz_low, pick,
+        [rows_of(duo), ((duo, block + 2 * duo), F32)],
+        in_vmem(far_cols_in), start_own, ritz_top, ritz_low, pick, pair,
     )
     far_in = far(far_rows)
     start_edge, out_rows, near_rows = call(
@@ -493,7 +496,7 @@
     part, overlap, couple = call(
         first_part,
         [rows_of(full), ((duo, duo), F32), ((duo, duo), F32)],
-        start_edge, far_in, out_in, near_in, ham_top, ham_low, pair_in,
+        start_edge, far_in, out_in, near_in, ham_top, ham_low,
     )
     (rest_low,) = call(
         functools.partial(rotate_low, groups),

time: 60.1 us -> 58.8 us (0.978)
  waiting for transfers between devices: 14.8 us -> 18.3 us
  starting transfers between devices: 21.8 us -> 19 us
  local copies, waits for them, and re-layouts: 1.54 us -> 0.01 us
    ppermute x4, waiting for transfers between devices: 12.4 us -> 17.7 us  [out(): return lax.ppermute(rows, 'mesh', pairs_out)]
    ppermute x5 -> x4, waiting for transfers between devices: 2.35 us -> 0.01 us  [far(): return lax.ppermute(rows, 'mesh', pairs_far)]
    ppermute x4, starting transfers between devices: 4.08 us -> 2.49 us  [out(): return lax.ppermute(rows, 'mesh', pairs_out)]
    unnamed x8 -> x4, local copies, waits for them, and re-layouts: 1.54 us -> 0.01 us
    ppermute x5 -> x4, starting transfers between devices: 10.5 us -> 9.08 us  [far(): return lax.ppermute(rows, 'mesh', pairs_far)]
    ppermute x4, waiting for transfers between devices: 0.01 us -> 0.63 us  [gather(): lax.ppermute(rows, 'state', [(i, (i + step) % groups) for i in range(grou...]
  transfers between devices with their start and end apart: 17 -> 16, of which waited for: 4 -> 5; matrix products, arithmetic and copies ran while one was open for 0% -> 0% of each run, Pallas kernels for 27% -> 26%
where the time goes in v9:
time: 58.8 us; the launch traced here: 58.6 us
  Pallas kernels  21 us (36%)
  starting transfers between devices  19 us (32%)
  waiting for transfers between devices  18.3 us (31%)
    pallas_call x16, Pallas kernels, call(): pl.pallas_call(body, out_shape=[pltpu.VMEM(*out) if kept else jax.ShapeDt...  21 us
    ppermute x4, waiting for transfers between devices, out(): return lax.ppermute(rows, 'mesh', pairs_out)  17.7 us
    ppermute x4, starting transfers between devices, far(): return lax.ppermute(rows, 'mesh', pairs_far)  9.08 us
    ppermute x4, starting transfers between devices, gather(): lax.ppermute(rows, 'state', [(i, (i + step) % groups) for i in range(grou...  5.14 us
    ppermute x4, starting transfers between devices, out(): return lax.ppermute(rows, 'mesh', pairs_out)  2.49 us
    ppermute x4, starting transfers between devices, near(): return lax.ppermute(rows, 'mesh', pairs_in)  2.32 us
  transfers between devices with their start and end apart: 16, of which 5 were waited for; matrix products, arithmetic and copies ran while one was open for 0% of the time, Pallas kernels for 26%

profile of v9, /device:TPU:0, one launch (start us, length us, event | category | flops | bytes accessed | tf_op | source)
XLA Modules:
  0.0 58.6 jit_solution(4629726032665381485)
XLA Ops:
  0.0 2.7 %shard_map.55 = (f32[512,128]{1,0:T(8,128)}, f32[512,128]{1,0:T(8,128)}, f32[512,128]{1,0:T(8,128)}, f32[512,128]{1,0:T(8,128)}, bf16[256,256]{1,0:T(8,128)(2,1)S(1)}) custom-call(s32[1,4,32]{2,1,0:T(4,128)} %lists.1, f32[1024,256]{1,0:T(8,128)} %subspace_in.1), custom_call_target="tpu_custom_call" | custom-call | flops 1000 | bytes 1000 | tf_op jit(solution)/shard_map/pallas_call | solution.py:43
  2.7 3.0 %collective-permute-start.1 = (f32[512,128]{1,0:T(8,128)}, f32[512,128]{1,0:T(8,128)S(1)}, u32[]{:S(2)}, u32[]{:S(2)}) collective-permute-start(f32[512,128]{1,0:T(8,128)} %get-tuple-element.44.far), channel_id=1, source_target_pairs={{0,1},{1,0},{2,3},{3,2},{4,5},{5,4},{6,7},{7,6},{8,9},{9,8},{10,11... | collective-permute-start | bytes 786440 | tf_op jit(solution)/shard_map/ppermute | solution.py:409
  5.8 1.9 %collective-permute-start.3 = (f32[512,128]{1,0:T(8,128)}, f32[512,128]{1,0:T(8,128)S(1)}, u32[]{:S(2)}, u32[]{:S(2)}) collective-permute-start(f32[512,128]{1,0:T(8,128)} %get-tuple-element.45.low_rest), channel_id=1, source_target_pairs={{0,1},{1,0},{2,3},{3,2},{4,5},{5,4},{6,7},{7,6},{8,9},{9,8},{10,11... | collective-permute-start | bytes 786440 | tf_op jit(solution)/shard_map/ppermute | solution.py:409
  7.9 4.6 %shard_map.56 = (f32[512,256]{1,0:T(8,128)S(1)}, bf16[512,1024]{1,0:T(8,128)(2,1)S(1)}, bf16[512,1024]{1,0:T(8,128)(2,1)S(1)}) custom-call(s32[1]{0:T(128)} %bitcast.group, f32[512,128]{1,0:T(8,128)} %get-tuple-element.44.far, f32[512,128]{1,0:T(8,128)} %get-tuple-element.43.ring, f32[512,128]{1,0:T(8,128)} %get-tuple-element.45.low_rest, ...), custom_call_target="tpu_custom_call" | custom-call | flops 1000 | bytes 1000 | tf_op jit(solution)/shard_map/pallas_call | solution.py:43
  12.6 4.1 %shard_map.57 = (bf16[384,384]{1,0:T(8,128)(2,1)S(1)}, bf16[384,384]{1,0:T(8,128)(2,1)S(1)}, bf16[128,128]{1,0:T(8,128)(2,1)S(1)}, bf16[128,128]{1,0:T(8,128)(2,...) custom-call(s32[1]{0:T(128)} %bitcast.1.odd, s32[1,4,32]{2,1,0:T(4,128)S(1)} %copy-done.1, ...), custom_call_target="tpu_custom_call" | custom-call | flops 1000 | bytes 1000 | tf_op jit(solution)/shard_map/pallas_call | solution.py:43
  16.7 1.1 %shard_map.58 = (f32[64,512]{1,0:T(8,128)S(1)}, f32[64,640]{1,0:T(8,128)S(1)}) custom-call(f32[512,128]{1,0:T(8,128)S(1)} %collective-permute-done.1.columns, f32[512,256]{1,0:T(8,128)S(1)} %get-tuple-element.47.start_own, bf16[512,1024]{1,0:T(8,128)(2,1)S(1)} %get-tuple-element.48.top, bf16[512,1024]{1,0:T(8,128)(2,1)S(1)} %get-tuple-element.49.low, ...), custom_call_target="tpu_custom_call" | custom-call | flops 1000 | bytes 1000 | tf_op jit(solution)/shard_map/pallas_call | solution.py:43
  17.7 3.1 %collective-permute-start.4 = (f32[64,640]{1,0:T(8,128)S(1)}, f32[64,640]{1,0:T(8,128)S(1)}, u32[]{:S(2)}, u32[]{:S(2)}) collective-permute-start(f32[64,640]{1,0:T(8,128)S(1)} %get-tuple-element.55), channel_id=1, source_target_pairs={{0,16},{2,18},{4,20},{6,22},{8,24},{10,26},{12,28},{14,30},{16,0},... | collective-permute-start | bytes 491528 | tf_op jit(solution)/shard_map/ppermute | solution.py:399
  20.8 1.2 %shard_map.59 = (f32[128,512]{1,0:T(8,128)S(1)}, f32[32,512]{1,0:T(8,128)S(1)}, f32[32,512]{1,0:T(8,128)S(1)}) custom-call(f32[512,128]{1,0:T(8,128)S(1)} %collective-permute-done.columns, f32[512,256]{1,0:T(8,128)S(1)} %get-tuple-element.47.start_own, f32[64,512]{1,0:T(8,128)S(1)} %get-tuple-element.53.start_far, ...), custom_call_target="tpu_custom_call" | custom-call | flops 1000 | bytes 1000 | tf_op jit(solution)/shard_map/pallas_call | solution.py:43
  22.5 1.2 %collective-permute-start.6 = (f32[32,512]{1,0:T(8,128)S(1)}, f32[32,512]{1,0:T(8,128)S(1)}, u32[]{:S(2)}, u32[]{:S(2)}) collective-permute-start(f32[32,512]{1,0:T(8,128)S(1)} %get-tuple-element.57), channel_id=1, source_target_pairs={{0,2},{2,0},{4,6},{6,4},{8,10},{10,8},{12,14},{14,12},{16,18},{18,... | collective-permute-start | bytes 196616 | tf_op jit(solution)/shard_map/ppermute | solution.py:405
  23.7 0.6 %collective-permute-done.3.columns = f32[512,128]{1,0:T(8,128)S(1)} collective-permute-done((f32[512,128]{1,0:T(8,128)}, f32[512,128]{1,0:T(8,128)S(1)}, u32[]{:S(2)}, u32[]{:S(2)}) %collective-permute-start.3) | collective-permute-done | bytes 262176 | tf_op jit(solution)/shard_map/ppermute | solution.py:409
  24.8 3.8 %collective-permute-done.5.out_in = f32[32,512]{1,0:T(8,128)S(1)} collective-permute-done((f32[32,512]{1,0:T(8,128)S(1)}, f32[32,512]{1,0:T(8,128)S(1)}, u32[]{:S(2)}, u32[]{:S(2)}) %collective-permute-start.5) | collective-permute-done | bytes 65568 | tf_op jit(solution)/shard_map/ppermute | solution.py:402
  28.6 0.8 %shard_map.61 = (f32[384,512]{1,0:T(8,128)S(1)}, f32[64,64]{1,0:T(8,128)S(1)}, f32[64,64]{1,0:T(8,128)S(1)}) custom-call(f32[128,512]{1,0:T(8,128)S(1)} %get-tuple-element.54.start_edge, f32[64,640]{1,0:T(8,128)S(1)} %collective-permute-done.4.far_in, f32[32,512]{1,0:T(8,128)S(1)} %collective-permute-done.5.out_in, ...), custom_call_target="tpu_custom_call" | custom-call | flops 1000 | bytes 1000 | tf_op jit(solution)/shard_map/pallas_call | solution.py:43
  29.4 1.7 %shard_map.62 = (f32[128,512]{1,0:T(8,128)S(1)}, f32[64,512]{1,0:T(8,128)S(1)}, f32[32,512]{1,0:T(8,128)S(1)}, f32[32,512]{1,0:T(8,128)S(1)}) custom-call(f32[512,128]{1,0:T(8,128)} %collective-permute-done.2.columns, f32[512,128]{1,0:T(8,128)S(1)} %shard_map.60.rest_low, bf16[512,1024]{1,0:T(8,128)(2,1)S(1)} %get-tuple-element.48.top, ...), custom_call_target="tpu_custom_call" | custom-call | flops 1000 | bytes 1000 | tf_op jit(solution)/shard_map/pallas_call | solution.py:43
  31.1 3.1 %collective-permute-start.7 = (f32[64,512]{1,0:T(8,128)S(1)}, f32[64,512]{1,0:T(8,128)S(1)}, u32[]{:S(2)}, u32[]{:S(2)}) collective-permute-start(f32[64,512]{1,0:T(8,128)S(1)} %get-tuple-element.63.back_far), channel_id=1, source_target_pairs={{0,16},{2,18},{4,20},{6,22},{8,24},{10,26},{12,28},{14,30},{16,0},... | collective-permute-start | bytes 393224 | tf_op jit(solution)/shard_map/ppermute | solution.py:399
  34.4 1.0 %collective-permute-start.9 = (f32[32,512]{1,0:T(8,128)S(1)}, f32[32,512]{1,0:T(8,128)S(1)}, u32[]{:S(2)}, u32[]{:S(2)}) collective-permute-start(f32[32,512]{1,0:T(8,128)S(1)} %get-tuple-element.66), channel_id=1, source_target_pairs={{0,2},{2,0},{4,6},{6,4},{8,10},{10,8},{12,14},{14,12},{16,18},{18,... | collective-permute-start | bytes 196616 | tf_op jit(solution)/shard_map/ppermute | solution.py:405
  35.5 0.6 %shard_map.63 = (f32[256,512]{1,0:T(8,128)S(1)}, f32[256,512]{1,0:T(8,128)S(1)}, f32[128,512]{1,0:T(8,128)S(1)}, f32[64,512]{1,0:T(8,128)S(1)}) custom-call(f32[128,512]{1,0:T(8,128)S(1)} %get-tuple-element.54.start_edge, f32[128,512]{1,0:T(8,128)S(1)} %get-tuple-element.61.start_rest, f32[384,512]{1,0:T(8,128)S(1)} %get-tuple-element.60.part, ...), custom_call_target="tpu_custom_call" | custom-call | flops 1000 | bytes 1000 | tf_op jit(solution)/shard_map/pallas_call | solution.py:43
  36.1 4.7 %collective-permute-done.8.out_in = f32[32,512]{1,0:T(8,128)S(1)} collective-permute-done((f32[32,512]{1,0:T(8,128)S(1)}, f32[32,512]{1,0:T(8,128)S(1)}, u32[]{:S(2)}, u32[]{:S(2)}) %collective-permute-start.8) | collective-permute-done | bytes 65568 | tf_op jit(solution)/shard_map/ppermute | solution.py:402
  41.0 2.8 %collective-permute-start.10 = (f32[64,512]{1,0:T(8,128)S(1)}, f32[64,512]{1,0:T(8,128)S(1)}, u32[]{:S(2)}, u32[]{:S(2)}) collective-permute-start(f32[64,512]{1,0:T(8,128)S(1)} %shard_map.65), channel_id=1, source_target_pairs={{0,16},{2,18},{4,20},{6,22},{8,24},{10,26},{12,28},{14,30},{16,0},... | collective-permute-start | bytes 393224 | tf_op jit(solution)/shard_map/ppermute | solution.py:399
  44.1 0.9 %shard_map.64 = (f32[256,512]{1,0:T(8,128)S(1)}, f32[384,512]{1,0:T(8,128)S(1)}, f32[64,512]{1,0:T(8,128)S(1)}) custom-call(f32[256,512]{1,0:T(8,128)S(1)} %get-tuple-element.64.base, bf16[128,128]{1,0:T(8,128)(2,1)S(1)} %get-tuple-element.51.pick, f32[64,512]{1,0:T(8,128)S(1)} %collective-permute-done.7.far_in, ...), custom_call_target="tpu_custom_call" | custom-call | flops 1000 | bytes 1000 | tf_op jit(solution)/shard_map/pallas_call | solution.py:43
  45.0 5.4 %collective-permute-done.11.out_in = f32[32,512]{1,0:T(8,128)S(1)} collective-permute-done((f32[32,512]{1,0:T(8,128)S(1)}, f32[32,512]{1,0:T(8,128)S(1)}, u32[]{:S(2)}, u32[]{:S(2)}) %collective-permute-start.11) | collective-permute-done | bytes 65568 | tf_op jit(solution)/shard_map/ppermute | solution.py:402
  51.0 1.8 %collective-permute-start.14 = (f32[32,512]{1,0:T(8,128)S(1)}, f32[32,512]{1,0:T(8,128)S(1)}, u32[]{:S(2)}, u32[]{:S(2)}) collective-permute-start(f32[32,512]{1,0:T(8,128)S(1)} %get-tuple-element.79), channel_id=1, source_target_pairs={{0,30},{2,4},{4,2},{6,8},{8,6},{10,12},{12,10},{14,16},{16,14},{18... | collective-permute-start | bytes 196616 | tf_op jit(solution)/shard_map/ppermute | solution.py:402
  52.8 0.8 %shard_map.68.result = f32[512,256]{1,0:T(8,128)S(1)} custom-call(f32[384,512]{1,0:T(8,128)S(1)} %get-tuple-element.68.part, f32[128,512]{1,0:T(8,128)S(1)} %get-tuple-element.74.ghosts, bf16[384,384]{1,0:T(8,128)(2,1)S(1)} %get-tuple-element.58.ham_top, bf16[384,384]{1,0:T(8,128)(2,1)S(1)} %get-tuple-element.59.ham_low, ...), custom_call_target="tpu_custom_call" | custom-call | flops 1000 | bytes 1000 | tf_op jit(solution)/shard_map/pallas_call | solution.py:43
  53.6 3.8 %collective-permute-done.14.out_in = f32[32,512]{1,0:T(8,128)S(1)} collective-permute-done((f32[32,512]{1,0:T(8,128)S(1)}, f32[32,512]{1,0:T(8,128)S(1)}, u32[]{:S(2)}, u32[]{:S(2)}) %collective-permute-start.14) | collective-permute-done | bytes 65568 | tf_op jit(solution)/shard_map/ppermute | solution.py:402
  57.4 1.1 %shard_map.70 = f32[512,256]{1,0:T(8,128)} custom-call(f32[512,256]{1,0:T(8,128)S(1)} %shard_map.68.result, bf16[128,256]{1,0:T(8,128)(2,1)S(1)} %get-tuple-element.78.hits, f32[64,512]{1,0:T(8,128)S(1)} %collective-permute-done.13.far_in, f32[32,512]{1,0:T(8,128)S(1)} %collective-permute-done.14.out_in, f32[32,512]{1,0:T(8,128)S(1)} %collective-permute-done.15.near_in), custom_call_target="tpu_custom_call" | custom-call | flops 1000 | bytes 1000 | tf_op jit(solution)/shard_map/pallas_call | solution.py:43
  (28 shorter events, 2.3 us)
Async XLA Ops:
  0.0 12.5 %copy-start.1 = (s32[1,4,32]{2,1,0:T(4,128)S(1)}, s32[1,4,32]{2,1,0:T(4,128)}, u32[]{:S(2)}) copy-start(s32[1,4,32]{2,1,0:T(4,128)} %lists.1) | copy-start | bytes 1540
  0.0 12.6 %copy-start = (s32[16,125]{1,0:T(8,128)S(1)}, s32[16,125]{1,0:T(8,128)}, u32[]{:S(2)}) copy-start(s32[16,125]{1,0:T(8,128)} %connect.1) | copy-start | bytes 24004
  2.7 13.9 %collective-permute-start.1 = (f32[512,128]{1,0:T(8,128)}, f32[512,128]{1,0:T(8,128)S(1)}, u32[]{:S(2)}, u32[]{:S(2)}) collective-permute-start(f32[512,128]{1,0:T(8,128)} %get-tuple-element.44.far), channel_id=1, source_target_pairs={{0,1},{1,0},{2,3},{3,2},{4,5},{5,4},{6,7},{7,6},{8,9},{9,8},{10,11... | collective-permute-start | bytes 786440 | tf_op jit(solution)/shard_map/ppermute | solution.py:409
  5.8 15.1 %collective-permute-start = (f32[512,128]{1,0:T(8,128)}, f32[512,128]{1,0:T(8,128)S(1)}, u32[]{:S(2)}, u32[]{:S(2)}) collective-permute-start(f32[512,128]{1,0:T(8,128)} %get-tuple-element.43.ring), channel_id=1, source_target_pairs={{0,1},{1,0},{2,3},{3,2},{4,5},{5,4},{6,7},{7,6},{8,9},{9,8},{10,11... | collective-permute-start | bytes 786440 | tf_op jit(solution)/shard_map/ppermute | solution.py:409
  5.8 18.5 %collective-permute-start.3 = (f32[512,128]{1,0:T(8,128)}, f32[512,128]{1,0:T(8,128)S(1)}, u32[]{:S(2)}, u32[]{:S(2)}) collective-permute-start(f32[512,128]{1,0:T(8,128)} %get-tuple-element.45.low_rest), channel_id=1, source_target_pairs={{0,1},{1,0},{2,3},{3,2},{4,5},{5,4},{6,7},{7,6},{8,9},{9,8},{10,11... | collective-permute-start | bytes 786440 | tf_op jit(solution)/shard_map/ppermute | solution.py:409
  7.8 21.6 %collective-permute-start.2 = (f32[512,128]{1,0:T(8,128)}, f32[512,128]{1,0:T(8,128)}, u32[]{:S(2)}, u32[]{:S(2)}) collective-permute-start(f32[512,128]{1,0:T(8,128)} %get-tuple-element.46.high_rest), channel_id=1, source_target_pairs={{0,1},{1,0},{2,3},{3,2},{4,5},{5,4},{6,7},{7,6},{8,9},{9,8},{10,11... | collective-permute-start | bytes 786440 | tf_op jit(solution)/shard_map/ppermute | solution.py:409
  17.7 10.9 %collective-permute-start.4 = (f32[64,640]{1,0:T(8,128)S(1)}, f32[64,640]{1,0:T(8,128)S(1)}, u32[]{:S(2)}, u32[]{:S(2)}) collective-permute-start(f32[64,640]{1,0:T(8,128)S(1)} %get-tuple-element.55), channel_id=1, source_target_pairs={{0,16},{2,18},{4,20},{6,22},{8,24},{10,26},{12,28},{14,30},{16,0},... | collective-permute-start | bytes 491528 | tf_op jit(solution)/shard_map/ppermute | solution.py:399
  22.1 6.6 %collective-permute-start.5 = (f32[32,512]{1,0:T(8,128)S(1)}, f32[32,512]{1,0:T(8,128)S(1)}, u32[]{:S(2)}, u32[]{:S(2)}) collective-permute-start(f32[32,512]{1,0:T(8,128)S(1)} %get-tuple-element.56), channel_id=1, source_target_pairs={{0,30},{2,4},{4,2},{6,8},{8,6},{10,12},{12,10},{14,16},{16,14},{18... | collective-permute-start | bytes 196616 | tf_op jit(solution)/shard_map/ppermute | solution.py:402
  22.5 6.1 %collective-permute-start.6 = (f32[32,512]{1,0:T(8,128)S(1)}, f32[32,512]{1,0:T(8,128)S(1)}, u32[]{:S(2)}, u32[]{:S(2)}) collective-permute-start(f32[32,512]{1,0:T(8,128)S(1)} %get-tuple-element.57), channel_id=1, source_target_pairs={{0,2},{2,0},{4,6},{6,4},{8,10},{10,8},{12,14},{14,12},{16,18},{18,... | collective-permute-start | bytes 196616 | tf_op jit(solution)/shard_map/ppermute | solution.py:405
  31.1 12.7 %collective-permute-start.7 = (f32[64,512]{1,0:T(8,128)S(1)}, f32[64,512]{1,0:T(8,128)S(1)}, u32[]{:S(2)}, u32[]{:S(2)}) collective-permute-start(f32[64,512]{1,0:T(8,128)S(1)} %get-tuple-element.63.back_far), channel_id=1, source_target_pairs={{0,16},{2,18},{4,20},{6,22},{8,24},{10,26},{12,28},{14,30},{16,0},... | collective-permute-start | bytes 393224 | tf_op jit(solution)/shard_map/ppermute | solution.py:399
  34.3 6.5 %collective-permute-start.8 = (f32[32,512]{1,0:T(8,128)S(1)}, f32[32,512]{1,0:T(8,128)S(1)}, u32[]{:S(2)}, u32[]{:S(2)}) collective-permute-start(f32[32,512]{1,0:T(8,128)S(1)} %get-tuple-element.65), channel_id=1, source_target_pairs={{0,30},{2,4},{4,2},{6,8},{8,6},{10,12},{12,10},{14,16},{16,14},{18... | collective-permute-start | bytes 196616 | tf_op jit(solution)/shard_map/ppermute | solution.py:402
  34.4 6.3 %collective-permute-start.9 = (f32[32,512]{1,0:T(8,128)S(1)}, f32[32,512]{1,0:T(8,128)S(1)}, u32[]{:S(2)}, u32[]{:S(2)}) collective-permute-start(f32[32,512]{1,0:T(8,128)S(1)} %get-tuple-element.66), channel_id=1, source_target_pairs={{0,2},{2,0},{4,6},{6,4},{8,10},{10,8},{12,14},{14,12},{16,18},{18,... | collective-permute-start | bytes 196616 | tf_op jit(solution)/shard_map/ppermute | solution.py:405
  41.0 9.8 %collective-permute-start.10 = (f32[64,512]{1,0:T(8,128)S(1)}, f32[64,512]{1,0:T(8,128)S(1)}, u32[]{:S(2)}, u32[]{:S(2)}) collective-permute-start(f32[64,512]{1,0:T(8,128)S(1)} %shard_map.65), channel_id=1, source_target_pairs={{0,16},{2,18},{4,20},{6,22},{8,24},{10,26},{12,28},{14,30},{16,0},... | collective-permute-start | bytes 393224 | tf_op jit(solution)/shard_map/ppermute | solution.py:399
  44.0 6.5 %collective-permute-start.11 = (f32[32,512]{1,0:T(8,128)S(1)}, f32[32,512]{1,0:T(8,128)S(1)}, u32[]{:S(2)}, u32[]{:S(2)}) collective-permute-start(f32[32,512]{1,0:T(8,128)S(1)} %get-tuple-element.72), channel_id=1, source_target_pairs={{0,30},{2,4},{4,2},{6,8},{8,6},{10,12},{12,10},{14,16},{16,14},{18... | collective-permute-start | bytes 196616 | tf_op jit(solution)/shard_map/ppermute | solution.py:402
  44.0 6.4 %collective-permute-start.12 = (f32[32,512]{1,0:T(8,128)S(1)}, f32[32,512]{1,0:T(8,128)S(1)}, u32[]{:S(2)}, u32[]{:S(2)}) collective-permute-start(f32[32,512]{1,0:T(8,128)S(1)} %get-tuple-element.73), channel_id=1, source_target_pairs={{0,2},{2,0},{4,6},{6,4},{8,10},{10,8},{12,14},{14,12},{16,18},{18,... | collective-permute-start | bytes 196616 | tf_op jit(solution)/shard_map/ppermute | solution.py:405
  50.7 6.8 %collective-permute-start.13 = (f32[64,512]{1,0:T(8,128)S(1)}, f32[64,512]{1,0:T(8,128)S(1)}, u32[]{:S(2)}, u32[]{:S(2)}) collective-permute-start(f32[64,512]{1,0:T(8,128)S(1)} %shard_map.69), channel_id=1, source_target_pairs={{0,16},{2,18},{4,20},{6,22},{8,24},{10,26},{12,28},{14,30},{16,0},... | collective-permute-start | bytes 393224 | tf_op jit(solution)/shard_map/ppermute | solution.py:399
  51.0 6.5 %collective-permute-start.14 = (f32[32,512]{1,0:T(8,128)S(1)}, f32[32,512]{1,0:T(8,128)S(1)}, u32[]{:S(2)}, u32[]{:S(2)}) collective-permute-start(f32[32,512]{1,0:T(8,128)S(1)} %get-tuple-element.79), channel_id=1, source_target_pairs={{0,30},{2,4},{4,2},{6,8},{8,6},{10,12},{12,10},{14,16},{16,14},{18... | collective-permute-start | bytes 196616 | tf_op jit(solution)/shard_map/ppermute | solution.py:402
  52.8 4.7 %collective-permute-start.15 = (f32[32,512]{1,0:T(8,128)S(1)}, f32[32,512]{1,0:T(8,128)S(1)}, u32[]{:S(2)}, u32[]{:S(2)}) collective-permute-start(f32[32,512]{1,0:T(8,128)S(1)} %get-tuple-element.80), channel_id=1, source_target_pairs={{0,2},{2,0},{4,6},{6,4},{8,10},{10,8},{12,14},{14,12},{16,18},{18,... | collective-permute-start | bytes 196616 | tf_op jit(solution)/shard_map/ppermute | solution.py:405

commit v10 on v9

--- a/solution.py
+++ b/solution.py
@@ -276,7 +276,7 @@
 
 
 def rotate_rest(
-    groups, columns, rest_low, top, low, part, ham_top, ham_low, rest_out, far_out, out_out, near_out
+    groups, columns, rest_low, top, low, part, ham_top, ham_low, rest_out, far_out, lower_out, upper_out, out_out, near_out
 ):
     rest = (rest_low[...] + rotate_half(columns, top, low, groups, 1)).T
     rest_out[...] = rest
@@ -286,6 +286,8 @@
     cols = slice(edge_nodes, nodes)
     back = part[nodes:, :] + mul((ham_top[nodes:, cols], ham_low[nodes:, cols]), split(rest))
     far_out[...] = back[: 2 * halo]
+    lower_out[...] = back[:halo]
+    upper_out[...] = back[halo : 2 * halo]
     out_out[...] = back[2 * halo : 3 * halo]
     near_out[...] = back[3 * halo :]
 
@@ -314,21 +316,23 @@
     far_out[...] = packed[:duo, :] + SCALE_ONE * sift(both[:duo, duo:], back)
 
 
-def fetch_ring(packed, both, far_in, out_in, near_in, out_out, near_out):
+def fetch_ring(packed, both, far_in, lower_in, upper_in, out_in, near_in, out_out, near_out):
     halo = out_in.shape[0]
-    back = jnp.concatenate([far_in[...], out_in[...], near_in[...]], 0)
+    far = far_in[...] + jnp.concatenate([lower_in[...], upper_in[...]], 0)
+    back = jnp.concatenate([far, out_in[...], near_in[...]], 0)
     rows = packed[2 * halo :, :] + SCALE_ONE * sift(both[2 * halo :, :], back)
     out_out[...] = rows[:halo]
     near_out[...] = rows[halo:]
 
 
 def first_own(
-    base, pick, far_in, out_in, near_in, ham_top, ham_low, couple, first_out, part_out, known_out
+    base, pick, far_in, lower_in, upper_in, out_in, near_in, ham_top, ham_low, couple, first_out, part_out, known_out
 ):
     edge_nodes = pick.shape[1]
     nodes = base.shape[0]
     duo = far_in.shape[0]
-    back = jnp.concatenate([far_in[...], out_in[...], near_in[...]], 0)
+    far = far_in[...] + jnp.concatenate([lower_in[...], upper_in[...]], 0)
+    back = jnp.concatenate([far, out_in[...], near_in[...]], 0)
     edge = base[:edge_nodes, :] + SCALE_ONE * sift(pick[...].T, back)
     first = jnp.concatenate([edge, base[edge_nodes:, :]], 0)
     first_out[...] = first
@@ -395,8 +399,19 @@
         (i, (i + 1) % partitions if i % 2 else (i - 1) % partitions) for i in range(partitions)
     ]
 
+    slow = {0, partitions - 1, across, (across + partitions - 1) % partitions}
+
     def far(rows):
         return lax.ppermute(rows, "mesh", pairs_far)
+
+    def far_apart(rows, lower, upper):
+        most = [pair for pair in pairs_far if pair[0] not in slow]
+        few = [pair for pair in pairs_far if pair[0] in slow]
+        return (
+            lax.ppermute(rows, "mesh", most),
+            lax.ppermute(lower, "mesh", few),
+            lax.ppermute(upper, "mesh", few),
+        )
 
     def out(rows):
         return lax.ppermute(rows, "mesh", pairs_out)
@@ -504,12 +519,13 @@
         in_vmem(low_cols_in), start_own, ritz_top, ritz_low,
     )
 
-    start_rest, back_far, back_out, back_near = call(
+    start_rest, back_far, lower, upper, back_out, back_near = call(
         functools.partial(rotate_rest, groups),
-        [rows_of(nodes - wide)] + halo_out,
+        [rows_of(nodes - wide), rows_of(duo)] + [rows_of(halo)] * 4,
         in_vmem(high_cols_in), rest_low, ritz_top, ritz_low, part, ham_top, ham_low,
     )
-    far_in, out_in, near_in = far(back_far), out(back_out), near(back_near)
+    out_in, near_in = out(back_out), near(back_near)
+    back_in = far_apart(back_far, lower, upper)
     start, base, packed, adjust = call(
         first_base,
         [rows_of(nodes), rows_of(nodes), rows_of(wide), rows_of(duo)],
@@ -518,13 +534,13 @@
     (far_rows,) = call(fetch_far, [rows_of(duo)], packed, both, out_in, near_in)
     fetched_far = far(far_rows)
     out_rows, near_rows = call(
-        fetch_ring, halo_out[1:], packed, both, far_in, out_in, near_in
+        fetch_ring, halo_out[1:], packed, both, *back_in, out_in, near_in
     )
     fetched_out, fetched_near = out(out_rows), near(near_rows)
     first, part, known = call(
         first_own,
         [rows_of(nodes), rows_of(full), rows_of(duo)],
-        base, pick, far_in, out_in, near_in, ham_top, ham_low, couple,
+        base, pick, *back_in, out_in, near_in, ham_top, ham_low, couple,
     )
 
     (far_rows,) = call(

time: 58.8 us -> 65 us (1.11)
  starting transfers between devices: 19 us -> 27.6 us
  waiting for transfers between devices: 18.3 us -> 15.8 us
    ppermute x0 -> x3, starting transfers between devices: none -> 7.4 us  [the longest x1 4.5 us: far_apart(): lax.ppermute(upper, 'mesh', few)]
    ppermute x4, waiting for transfers between devices: 17.7 us -> 11.8 us  [out(): return lax.ppermute(rows, 'mesh', pairs_out)]
    ppermute x4 -> x3, starting transfers between devices: 9.08 us -> 4.69 us  [far(): return lax.ppermute(rows, 'mesh', pairs_far)]
    ppermute x4, starting transfers between devices: 2.49 us -> 6.8 us  [out(): return lax.ppermute(rows, 'mesh', pairs_out)]
    ppermute x0 -> x3, waiting for transfers between devices: none -> 3.36 us  [the longest x1 2.24 us: far_apart(): lax.ppermute(upper, 'mesh', few)]
    ppermute x4, starting transfers between devices: 2.32 us -> 3.57 us  [near(): return lax.ppermute(rows, 'mesh', pairs_in)]
  transfers between devices with their start and end apart: 16 -> 18, of which waited for: 5 -> 6; matrix products, arithmetic and copies ran while one was open for 0% -> 0% of each run, Pallas kernels for 26% -> 24%
where the time goes in v10:
time: 65 us; the launch traced here: 64.7 us
  starting transfers between devices  27.6 us (42%)
  Pallas kernels  21.1 us (32%)
  waiting for transfers between devices  15.8 us (24%)
    pallas_call x16, Pallas kernels, call(): pl.pallas_call(body, out_shape=[pltpu.VMEM(*out) if kept else jax.ShapeDt...  21.1 us
    ppermute x4, waiting for transfers between devices, out(): return lax.ppermute(rows, 'mesh', pairs_out)  11.8 us
    ppermute x4, starting transfers between devices, out(): return lax.ppermute(rows, 'mesh', pairs_out)  6.8 us
    ppermute x4, starting transfers between devices, gather(): lax.ppermute(rows, 'state', [(i, (i + step) % groups) for i in range(grou...  5.14 us
    ppermute x3, starting transfers between devices, far(): return lax.ppermute(rows, 'mesh', pairs_far)  4.69 us
    ppermute x1, starting transfers between devices, far_apart(): lax.ppermute(upper, 'mesh', few)  4.5 us
    ppermute x4, starting transfers between devices, near(): return lax.ppermute(rows, 'mesh', pairs_in)  3.57 us
    ppermute x1, waiting for transfers between devices, far_apart(): lax.ppermute(upper, 'mesh', few)  2.24 us
  transfers between devices with their start and end apart: 18, of which 6 were waited for; matrix products, arithmetic and copies ran while one was open for 0% of the time, Pallas kernels for 24%

profile of v10, /device:TPU:0, one launch (start us, length us, event | category | flops | bytes accessed | tf_op | source)
XLA Modules:
  0.0 64.7 jit_solution(17637081132910483226)
XLA Ops:
  0.0 2.8 %shard_map.55 = (f32[512,128]{1,0:T(8,128)}, f32[512,128]{1,0:T(8,128)}, f32[512,128]{1,0:T(8,128)}, f32[512,128]{1,0:T(8,128)}, bf16[256,256]{1,0:T(8,128)(2,1)S(1)}) custom-call(s32[1,4,32]{2,1,0:T(4,128)} %lists.1, f32[1024,256]{1,0:T(8,128)} %subspace_in.1), custom_call_target="tpu_custom_call" | custom-call | flops 1000 | bytes 1000 | tf_op jit(solution)/shard_map/pallas_call | solution.py:43
  2.8 3.0 %collective-permute-start.1 = (f32[512,128]{1,0:T(8,128)}, f32[512,128]{1,0:T(8,128)S(1)}, u32[]{:S(2)}, u32[]{:S(2)}) collective-permute-start(f32[512,128]{1,0:T(8,128)} %get-tuple-element.46.far), channel_id=1, source_target_pairs={{0,1},{1,0},{2,3},{3,2},{4,5},{5,4},{6,7},{7,6},{8,9},{9,8},{10,11... | collective-permute-start | bytes 786440 | tf_op jit(solution)/shard_map/ppermute | solution.py:424
  5.9 1.9 %collective-permute-start.3 = (f32[512,128]{1,0:T(8,128)}, f32[512,128]{1,0:T(8,128)S(1)}, u32[]{:S(2)}, u32[]{:S(2)}) collective-permute-start(f32[512,128]{1,0:T(8,128)} %get-tuple-element.47.low_rest), channel_id=1, source_target_pairs={{0,1},{1,0},{2,3},{3,2},{4,5},{5,4},{6,7},{7,6},{8,9},{9,8},{10,11... | collective-permute-start | bytes 786440 | tf_op jit(solution)/shard_map/ppermute | solution.py:424
  7.9 4.6 %shard_map.56 = (f32[512,256]{1,0:T(8,128)S(1)}, bf16[512,1024]{1,0:T(8,128)(2,1)S(1)}, bf16[512,1024]{1,0:T(8,128)(2,1)S(1)}) custom-call(s32[1]{0:T(128)} %bitcast.group, f32[512,128]{1,0:T(8,128)} %get-tuple-element.46.far, f32[512,128]{1,0:T(8,128)} %get-tuple-element.45.ring, f32[512,128]{1,0:T(8,128)} %get-tuple-element.47.low_rest, ...), custom_call_target="tpu_custom_call" | custom-call | flops 1000 | bytes 1000 | tf_op jit(solution)/shard_map/pallas_call | solution.py:43
  12.6 4.1 %shard_map.57 = (bf16[384,384]{1,0:T(8,128)(2,1)S(1)}, bf16[384,384]{1,0:T(8,128)(2,1)S(1)}, bf16[128,128]{1,0:T(8,128)(2,1)S(1)}, bf16[128,128]{1,0:T(8,128)(2,...) custom-call(s32[1]{0:T(128)} %bitcast.1.odd, s32[1,4,32]{2,1,0:T(4,128)S(1)} %copy-done.1, ...), custom_call_target="tpu_custom_call" | custom-call | flops 1000 | bytes 1000 | tf_op jit(solution)/shard_map/pallas_call | solution.py:43
  16.7 1.1 %shard_map.58 = (f32[64,512]{1,0:T(8,128)S(1)}, f32[64,640]{1,0:T(8,128)S(1)}) custom-call(f32[512,128]{1,0:T(8,128)S(1)} %collective-permute-done.1.columns, f32[512,256]{1,0:T(8,128)S(1)} %get-tuple-element.49.start_own, bf16[512,1024]{1,0:T(8,128)(2,1)S(1)} %get-tuple-element.50.top, bf16[512,1024]{1,0:T(8,128)(2,1)S(1)} %get-tuple-element.51.low, ...), custom_call_target="tpu_custom_call" | custom-call | flops 1000 | bytes 1000 | tf_op jit(solution)/shard_map/pallas_call | solution.py:43
  17.8 3.1 %collective-permute-start.4 = (f32[64,640]{1,0:T(8,128)S(1)}, f32[64,640]{1,0:T(8,128)S(1)}, u32[]{:S(2)}, u32[]{:S(2)}) collective-permute-start(f32[64,640]{1,0:T(8,128)S(1)} %get-tuple-element.57), channel_id=1, source_target_pairs={{0,16},{2,18},{4,20},{6,22},{8,24},{10,26},{12,28},{14,30},{16,0},... | collective-permute-start | bytes 491528 | tf_op jit(solution)/shard_map/ppermute | solution.py:405
  20.9 1.2 %shard_map.59 = (f32[128,512]{1,0:T(8,128)S(1)}, f32[32,512]{1,0:T(8,128)S(1)}, f32[32,512]{1,0:T(8,128)S(1)}) custom-call(f32[512,128]{1,0:T(8,128)S(1)} %collective-permute-done.columns, f32[512,256]{1,0:T(8,128)S(1)} %get-tuple-element.49.start_own, f32[64,512]{1,0:T(8,128)S(1)} %get-tuple-element.55.start_far, ...), custom_call_target="tpu_custom_call" | custom-call | flops 1000 | bytes 1000 | tf_op jit(solution)/shard_map/pallas_call | solution.py:43
  22.5 1.2 %collective-permute-start.6 = (f32[32,512]{1,0:T(8,128)S(1)}, f32[32,512]{1,0:T(8,128)S(1)}, u32[]{:S(2)}, u32[]{:S(2)}) collective-permute-start(f32[32,512]{1,0:T(8,128)S(1)} %get-tuple-element.59), channel_id=1, source_target_pairs={{0,2},{2,0},{4,6},{6,4},{8,10},{10,8},{12,14},{14,12},{16,18},{18,... | collective-permute-start | bytes 196616 | tf_op jit(solution)/shard_map/ppermute | solution.py:420
  24.8 3.8 %collective-permute-done.5.out_in = f32[32,512]{1,0:T(8,128)S(1)} collective-permute-done((f32[32,512]{1,0:T(8,128)S(1)}, f32[32,512]{1,0:T(8,128)S(1)}, u32[]{:S(2)}, u32[]{:S(2)}) %collective-permute-start.5) | collective-permute-done | bytes 65568 | tf_op jit(solution)/shard_map/ppermute | solution.py:417
  29.4 1.7 %shard_map.62 = (f32[128,512]{1,0:T(8,128)S(1)}, f32[64,512]{1,0:T(8,128)S(1)}, f32[32,512]{1,0:T(8,128)S(1)}, f32[32,512]{1,0:T(8,128)S(1)}, f32[32,512]{1,0:T(8,128)S(1)}, /*index=5*/f32[32,512]{1,0:T(8,128)S(1)}) custom-call(f32[512,128]{1,0:T(8,128)} %collective-permute-done.2.columns, f32[512,128]{1,0:T(8,128)S(1)} %shard_map.60.rest_low, ...), custom_call_target="tpu_custom_call" | custom-call | flops 1000 | bytes 1000 | tf_op jit(solution)/shard_map/pallas_call | solution.py:43
  31.8 3.2 %collective-permute-start.10 = (f32[32,512]{1,0:T(8,128)S(1)}, f32[32,512]{1,0:T(8,128)S(1)}, u32[]{:S(2)}, u32[]{:S(2)}) collective-permute-start(f32[32,512]{1,0:T(8,128)S(1)} %get-tuple-element.69), channel_id=1, source_target_pairs={{0,30},{2,4},{4,2},{6,8},{8,6},{10,12},{12,10},{14,16},{16,14},{18... | collective-permute-start | bytes 196616 | tf_op jit(solution)/shard_map/ppermute | solution.py:417
  35.0 2.3 %collective-permute-start.11 = (f32[32,512]{1,0:T(8,128)S(1)}, f32[32,512]{1,0:T(8,128)S(1)}, u32[]{:S(2)}, u32[]{:S(2)}) collective-permute-start(f32[32,512]{1,0:T(8,128)S(1)} %get-tuple-element.70), channel_id=1, source_target_pairs={{0,2},{2,0},{4,6},{6,4},{8,10},{10,8},{12,14},{14,12},{16,18},{18,... | collective-permute-start | bytes 196616 | tf_op jit(solution)/shard_map/ppermute | solution.py:420
  37.4 2.2 %collective-permute-start.8 = (f32[32,512]{1,0:T(8,128)S(1)}, f32[32,512]{1,0:T(8,128)S(1)}, u32[]{:S(2)}, u32[]{:S(2)}) collective-permute-start(f32[32,512]{1,0:T(8,128)S(1)} %get-tuple-element.67), channel_id=1, source_target_pairs={{0,16},{14,30},{16,0},{30,14},{1,17},{15,31},{17,1},{31,15}} | collective-permute-start | bytes 196616 | tf_op jit(solution)/shard_map/ppermute | solution.py:412
  39.6 4.5 %collective-permute-start.9 = (f32[32,512]{1,0:T(8,128)S(1)}, f32[32,512]{1,0:T(8,128)S(1)}, u32[]{:S(2)}, u32[]{:S(2)}) collective-permute-start(f32[32,512]{1,0:T(8,128)S(1)} %get-tuple-element.68), channel_id=1, source_target_pairs={{0,16},{14,30},{16,0},{30,14},{1,17},{15,31},{17,1},{31,15}} | collective-permute-start | bytes 196616 | tf_op jit(solution)/shard_map/ppermute | solution.py:413
  45.4 1.1 %collective-permute-done.8.lower_in = f32[32,512]{1,0:T(8,128)S(1)} collective-permute-done((f32[32,512]{1,0:T(8,128)S(1)}, f32[32,512]{1,0:T(8,128)S(1)}, u32[]{:S(2)}, u32[]{:S(2)}) %collective-permute-start.8) | collective-permute-done | bytes 65568 | tf_op jit(solution)/shard_map/ppermute | solution.py:412
  46.6 2.2 %collective-permute-done.9.upper_in = f32[32,512]{1,0:T(8,128)S(1)} collective-permute-done((f32[32,512]{1,0:T(8,128)S(1)}, f32[32,512]{1,0:T(8,128)S(1)}, u32[]{:S(2)}, u32[]{:S(2)}) %collective-permute-start.9) | collective-permute-done | bytes 65568 | tf_op jit(solution)/shard_map/ppermute | solution.py:413
  49.0 2.1 %collective-permute-start.13 = (f32[32,512]{1,0:T(8,128)S(1)}, f32[32,512]{1,0:T(8,128)S(1)}, u32[]{:S(2)}, u32[]{:S(2)}) collective-permute-start(f32[32,512]{1,0:T(8,128)S(1)} %get-tuple-element.76), channel_id=1, source_target_pairs={{0,30},{2,4},{4,2},{6,8},{8,6},{10,12},{12,10},{14,16},{16,14},{18... | collective-permute-start | bytes 196616 | tf_op jit(solution)/shard_map/ppermute | solution.py:417
  51.1 0.9 %shard_map.64 = (f32[256,512]{1,0:T(8,128)S(1)}, f32[384,512]{1,0:T(8,128)S(1)}, f32[64,512]{1,0:T(8,128)S(1)}) custom-call(f32[256,512]{1,0:T(8,128)S(1)} %get-tuple-element.66.base, bf16[128,128]{1,0:T(8,128)(2,1)S(1)} %get-tuple-element.53.pick, f32[64,512]{1,0:T(8,128)S(1)} %collective-permute-done.7.far_in, ...), custom_call_target="tpu_custom_call" | custom-call | flops 1000 | bytes 1000 | tf_op jit(solution)/shard_map/pallas_call | solution.py:43
  52.0 3.4 %collective-permute-done.13.out_in = f32[32,512]{1,0:T(8,128)S(1)} collective-permute-done((f32[32,512]{1,0:T(8,128)S(1)}, f32[32,512]{1,0:T(8,128)S(1)}, u32[]{:S(2)}, u32[]{:S(2)}) %collective-permute-start.13) | collective-permute-done | bytes 65568 | tf_op jit(solution)/shard_map/ppermute | solution.py:417
  55.7 1.2 %collective-permute-start.15 = (f32[64,512]{1,0:T(8,128)S(1)}, f32[64,512]{1,0:T(8,128)S(1)}, u32[]{:S(2)}, u32[]{:S(2)}) collective-permute-start(f32[64,512]{1,0:T(8,128)S(1)} %shard_map.69), channel_id=1, source_target_pairs={{0,16},{2,18},{4,20},{6,22},{8,24},{10,26},{12,28},{14,30},{16,0},... | collective-permute-start | bytes 393224 | tf_op jit(solution)/shard_map/ppermute | solution.py:405
  57.1 1.0 %collective-permute-start.16 = (f32[32,512]{1,0:T(8,128)S(1)}, f32[32,512]{1,0:T(8,128)S(1)}, u32[]{:S(2)}, u32[]{:S(2)}) collective-permute-start(f32[32,512]{1,0:T(8,128)S(1)} %get-tuple-element.83), channel_id=1, source_target_pairs={{0,30},{2,4},{4,2},{6,8},{8,6},{10,12},{12,10},{14,16},{16,14},{18... | collective-permute-start | bytes 196616 | tf_op jit(solution)/shard_map/ppermute | solution.py:417
  59.0 4.6 %collective-permute-done.16.out_in = f32[32,512]{1,0:T(8,128)S(1)} collective-permute-done((f32[32,512]{1,0:T(8,128)S(1)}, f32[32,512]{1,0:T(8,128)S(1)}, u32[]{:S(2)}, u32[]{:S(2)}) %collective-permute-start.16) | collective-permute-done | bytes 65568 | tf_op jit(solution)/shard_map/ppermute | solution.py:417
  63.6 1.1 %shard_map.70 = f32[512,256]{1,0:T(8,128)} custom-call(f32[512,256]{1,0:T(8,128)S(1)} %shard_map.68.result, bf16[128,256]{1,0:T(8,128)(2,1)S(1)} %get-tuple-element.82.hits, f32[64,512]{1,0:T(8,128)S(1)} %collective-permute-done.15.far_in, f32[32,512]{1,0:T(8,128)S(1)} %collective-permute-done.16.out_in, f32[32,512]{1,0:T(8,128)S(1)} %collective-permute-done.17.near_in), custom_call_target="tpu_custom_call" | custom-call | flops 1000 | bytes 1000 | tf_op jit(solution)/shard_map/pallas_call | solution.py:43
  (32 shorter events, 5.9 us)
Async XLA Ops:
  0.0 12.6 %copy-start.1 = (s32[1,4,32]{2,1,0:T(4,128)S(1)}, s32[1,4,32]{2,1,0:T(4,128)}, u32[]{:S(2)}) copy-start(s32[1,4,32]{2,1,0:T(4,128)} %lists.1) | copy-start | bytes 1540
  0.0 12.6 %copy-start = (s32[16,125]{1,0:T(8,128)S(1)}, s32[16,125]{1,0:T(8,128)}, u32[]{:S(2)}) copy-start(s32[16,125]{1,0:T(8,128)} %connect.1) | copy-start | bytes 24004
  2.8 13.9 %collective-permute-start.1 = (f32[512,128]{1,0:T(8,128)}, f32[512,128]{1,0:T(8,128)S(1)}, u32[]{:S(2)}, u32[]{:S(2)}) collective-permute-start(f32[512,128]{1,0:T(8,128)} %get-tuple-element.46.far), channel_id=1, source_target_pairs={{0,1},{1,0},{2,3},{3,2},{4,5},{5,4},{6,7},{7,6},{8,9},{9,8},{10,11... | collective-permute-start | bytes 786440 | tf_op jit(solution)/shard_map/ppermute | solution.py:424
  5.8 15.1 %collective-permute-start = (f32[512,128]{1,0:T(8,128)}, f32[512,128]{1,0:T(8,128)S(1)}, u32[]{:S(2)}, u32[]{:S(2)}) collective-permute-start(f32[512,128]{1,0:T(8,128)} %get-tuple-element.45.ring), channel_id=1, source_target_pairs={{0,1},{1,0},{2,3},{3,2},{4,5},{5,4},{6,7},{7,6},{8,9},{9,8},{10,11... | collective-permute-start | bytes 786440 | tf_op jit(solution)/shard_map/ppermute | solution.py:424
  5.9 18.5 %collective-permute-start.3 = (f32[512,128]{1,0:T(8,128)}, f32[512,128]{1,0:T(8,128)S(1)}, u32[]{:S(2)}, u32[]{:S(2)}) collective-permute-start(f32[512,128]{1,0:T(8,128)} %get-tuple-element.47.low_rest), channel_id=1, source_target_pairs={{0,1},{1,0},{2,3},{3,2},{4,5},{5,4},{6,7},{7,6},{8,9},{9,8},{10,11... | collective-permute-start | bytes 786440 | tf_op jit(solution)/shard_map/ppermute | solution.py:424
  7.8 21.6 %collective-permute-start.2 = (f32[512,128]{1,0:T(8,128)}, f32[512,128]{1,0:T(8,128)}, u32[]{:S(2)}, u32[]{:S(2)}) collective-permute-start(f32[512,128]{1,0:T(8,128)} %get-tuple-element.48.high_rest), channel_id=1, source_target_pairs={{0,1},{1,0},{2,3},{3,2},{4,5},{5,4},{6,7},{7,6},{8,9},{9,8},{10,11... | collective-permute-start | bytes 786440 | tf_op jit(solution)/shard_map/ppermute | solution.py:424
  17.8 10.9 %collective-permute-start.4 = (f32[64,640]{1,0:T(8,128)S(1)}, f32[64,640]{1,0:T(8,128)S(1)}, u32[]{:S(2)}, u32[]{:S(2)}) collective-permute-start(f32[64,640]{1,0:T(8,128)S(1)} %get-tuple-element.57), channel_id=1, source_target_pairs={{0,16},{2,18},{4,20},{6,22},{8,24},{10,26},{12,28},{14,30},{16,0},... | collective-permute-start | bytes 491528 | tf_op jit(solution)/shard_map/ppermute | solution.py:405
  22.1 6.6 %collective-permute-start.5 = (f32[32,512]{1,0:T(8,128)S(1)}, f32[32,512]{1,0:T(8,128)S(1)}, u32[]{:S(2)}, u32[]{:S(2)}) collective-permute-start(f32[32,512]{1,0:T(8,128)S(1)} %get-tuple-element.58), channel_id=1, source_target_pairs={{0,30},{2,4},{4,2},{6,8},{8,6},{10,12},{12,10},{14,16},{16,14},{18... | collective-permute-start | bytes 196616 | tf_op jit(solution)/shard_map/ppermute | solution.py:417
  22.5 6.1 %collective-permute-start.6 = (f32[32,512]{1,0:T(8,128)S(1)}, f32[32,512]{1,0:T(8,128)S(1)}, u32[]{:S(2)}, u32[]{:S(2)}) collective-permute-start(f32[32,512]{1,0:T(8,128)S(1)} %get-tuple-element.59), channel_id=1, source_target_pairs={{0,2},{2,0},{4,6},{6,4},{8,10},{10,8},{12,14},{14,12},{16,18},{18,... | collective-permute-start | bytes 196616 | tf_op jit(solution)/shard_map/ppermute | solution.py:420
  31.1 17.7 %collective-permute-start.7 = (f32[64,512]{1,0:T(8,128)S(1)}, f32[64,512]{1,0:T(8,128)S(1)}, u32[]{:S(2)}, u32[]{:S(2)}) collective-permute-start(f32[64,512]{1,0:T(8,128)S(1)} %get-tuple-element.65.back_far), channel_id=1, source_target_pairs={{2,18},{4,20},{6,22},{8,24},{10,26},{12,28},{18,2},{20,4},{22,6},{... | collective-permute-start | bytes 393224 | tf_op jit(solution)/shard_map/ppermute | solution.py:411
  31.8 13.0 %collective-permute-start.10 = (f32[32,512]{1,0:T(8,128)S(1)}, f32[32,512]{1,0:T(8,128)S(1)}, u32[]{:S(2)}, u32[]{:S(2)}) collective-permute-start(f32[32,512]{1,0:T(8,128)S(1)} %get-tuple-element.69), channel_id=1, source_target_pairs={{0,30},{2,4},{4,2},{6,8},{8,6},{10,12},{12,10},{14,16},{16,14},{18... | collective-permute-start | bytes 196616 | tf_op jit(solution)/shard_map/ppermute | solution.py:417
  35.0 9.7 %collective-permute-start.11 = (f32[32,512]{1,0:T(8,128)S(1)}, f32[32,512]{1,0:T(8,128)S(1)}, u32[]{:S(2)}, u32[]{:S(2)}) collective-permute-start(f32[32,512]{1,0:T(8,128)S(1)} %get-tuple-element.70), channel_id=1, source_target_pairs={{0,2},{2,0},{4,6},{6,4},{8,10},{10,8},{12,14},{14,12},{16,18},{18,... | collective-permute-start | bytes 196616 | tf_op jit(solution)/shard_map/ppermute | solution.py:420
  37.4 9.2 %collective-permute-start.8 = (f32[32,512]{1,0:T(8,128)S(1)}, f32[32,512]{1,0:T(8,128)S(1)}, u32[]{:S(2)}, u32[]{:S(2)}) collective-permute-start(f32[32,512]{1,0:T(8,128)S(1)} %get-tuple-element.67), channel_id=1, source_target_pairs={{0,16},{14,30},{16,0},{30,14},{1,17},{15,31},{17,1},{31,15}} | collective-permute-start | bytes 196616 | tf_op jit(solution)/shard_map/ppermute | solution.py:412
  39.6 9.2 %collective-permute-start.9 = (f32[32,512]{1,0:T(8,128)S(1)}, f32[32,512]{1,0:T(8,128)S(1)}, u32[]{:S(2)}, u32[]{:S(2)}) collective-permute-start(f32[32,512]{1,0:T(8,128)S(1)} %get-tuple-element.68), channel_id=1, source_target_pairs={{0,16},{14,30},{16,0},{30,14},{1,17},{15,31},{17,1},{31,15}} | collective-permute-start | bytes 196616 | tf_op jit(solution)/shard_map/ppermute | solution.py:413
  45.0 11.9 %collective-permute-start.12 = (f32[64,512]{1,0:T(8,128)S(1)}, f32[64,512]{1,0:T(8,128)S(1)}, u32[]{:S(2)}, u32[]{:S(2)}) collective-permute-start(f32[64,512]{1,0:T(8,128)S(1)} %shard_map.65), channel_id=1, source_target_pairs={{0,16},{2,18},{4,20},{6,22},{8,24},{10,26},{12,28},{14,30},{16,0},... | collective-permute-start | bytes 393224 | tf_op jit(solution)/shard_map/ppermute | solution.py:405
  49.0 6.5 %collective-permute-start.13 = (f32[32,512]{1,0:T(8,128)S(1)}, f32[32,512]{1,0:T(8,128)S(1)}, u32[]{:S(2)}, u32[]{:S(2)}) collective-permute-start(f32[32,512]{1,0:T(8,128)S(1)} %get-tuple-element.76), channel_id=1, source_target_pairs={{0,30},{2,4},{4,2},{6,8},{8,6},{10,12},{12,10},{14,16},{16,14},{18... | collective-permute-start | bytes 196616 | tf_op jit(solution)/shard_map/ppermute | solution.py:417
  51.1 4.3 %collective-permute-start.14 = (f32[32,512]{1,0:T(8,128)S(1)}, f32[32,512]{1,0:T(8,128)S(1)}, u32[]{:S(2)}, u32[]{:S(2)}) collective-permute-start(f32[32,512]{1,0:T(8,128)S(1)} %get-tuple-element.77), channel_id=1, source_target_pairs={{0,2},{2,0},{4,6},{6,4},{8,10},{10,8},{12,14},{14,12},{16,18},{18,... | collective-permute-start | bytes 196616 | tf_op jit(solution)/shard_map/ppermute | solution.py:420
  55.7 7.9 %collective-permute-start.15 = (f32[64,512]{1,0:T(8,128)S(1)}, f32[64,512]{1,0:T(8,128)S(1)}, u32[]{:S(2)}, u32[]{:S(2)}) collective-permute-start(f32[64,512]{1,0:T(8,128)S(1)} %shard_map.69), channel_id=1, source_target_pairs={{0,16},{2,18},{4,20},{6,22},{8,24},{10,26},{12,28},{14,30},{16,0},... | collective-permute-start | bytes 393224 | tf_op jit(solution)/shard_map/ppermute | solution.py:405
  57.1 6.5 %collective-permute-start.16 = (f32[32,512]{1,0:T(8,128)S(1)}, f32[32,512]{1,0:T(8,128)S(1)}, u32[]{:S(2)}, u32[]{:S(2)}) collective-permute-start(f32[32,512]{1,0:T(8,128)S(1)} %get-tuple-element.83), channel_id=1, source_target_pairs={{0,30},{2,4},{4,2},{6,8},{8,6},{10,12},{12,10},{14,16},{16,14},{18... | collective-permute-start | bytes 196616 | tf_op jit(solution)/shard_map/ppermute | solution.py:417
  58.1 5.5 %collective-permute-start.17 = (f32[32,512]{1,0:T(8,128)S(1)}, f32[32,512]{1,0:T(8,128)S(1)}, u32[]{:S(2)}, u32[]{:S(2)}) collective-permute-start(f32[32,512]{1,0:T(8,128)S(1)} %get-tuple-element.84), channel_id=1, source_target_pairs={{0,2},{2,0},{4,6},{6,4},{8,10},{10,8},{12,14},{14,12},{16,18},{18,... | collective-permute-start | bytes 196616 | tf_op jit(solution)/shard_map/ppermute | solution.py:420

commit v11 on v9

--- a/solution.py
+++ b/solution.py
@@ -39,10 +39,10 @@
     return dot(a, top) + dot(a, low)
 
 
-def call(body, outs, *args, limit=8, kept=False, **rest):
+def call(body, outs, *args, limit=8, **rest):
     return pl.pallas_call(
         body,
-        out_shape=[pltpu.VMEM(*out) if kept else jax.ShapeDtypeStruct(*out) for out in outs],
+        out_shape=[jax.ShapeDtypeStruct(*out) for out in outs],
         compiler_params=pltpu.CompilerParams(vmem_limit_bytes=limit << 20),
         cost_estimate=pl.CostEstimate(flops=1000, bytes_accessed=1000, transcendentals=0),
         **rest,
@@ -51,10 +51,6 @@
 
 def in_hbm(x):
     return pltpu.with_memory_space_constraint(x, pltpu.HBM)
-
-
-def in_vmem(x):
-    return pltpu.with_memory_space_constraint(x, pltpu.VMEM)
 
 
 def column(row, width):
@@ -167,11 +163,15 @@
     pair_out[...] = jnp.concatenate([both[:duo, :duo], ham[far, far]], 1)
 
 
-def rotate_own(group, far, ring, low_rest, high_rest, ritz_in, start_out, top_out, low_out, ritz, sems):
+def rotate_own(
+    group, shuffle, subspace_in, ritz_in, start_out, top_out, low_out, subspace, ritz, sem, sems
+):
     block, depth = ritz.shape[1:]
     groups = ritz.shape[0]
     parts = sems.shape[1]
     span = block // parts
+    own_copy = pltpu.make_async_copy(subspace_in, subspace, sem)
+    own_copy.start()
     copies = []
     for step in range(groups):
         first = lax.rem(group[0] + groups - step, groups) * depth
@@ -184,17 +184,16 @@
                 )
             )
             copies[-1].start()
-    width = far.shape[1] // 2
-    columns = [jnp.concatenate([x[:, :width], x[:, width:]], 0) for x in (far, ring)]
-    rest = jnp.concatenate([low_rest[...], high_rest[...]], 0)
-    own = split(jnp.concatenate(columns + [rest], 1))
+    own_copy.wait()
+    own = split(subspace[...])
     for step in range(groups):
         for part in range(parts):
             rows = slice(part * span, (part + 1) * span)
             copies[step * parts + part].wait()
             top, low = split(ritz[step, rows, :])
             if step == 0:
-                start_out[rows, :] = mul((top, low), own)
+                high, rest = split(mul((top, low), own))
+                start_out[rows, :] = dot(high, shuffle[...], NT) + dot(rest, shuffle[...], NT)
             else:
                 cols = slice((step - 1) * depth, step * depth)
                 top_out[rows, cols] = top
@@ -429,7 +428,6 @@
             ((nodes, nodes), BF16),
         ],
         in_hbm(send_rows), in_hbm(subspace),
-        kept=True,
         in_specs=[hbm, hbm],
         scratch_shapes=[
             pltpu.VMEM(send_rows.shape, I32),
@@ -472,11 +470,13 @@
             ((block, others * depth), BF16),
             ((block, others * depth), BF16),
         ],
-        group, far_cols, ring_cols, low_cols, high_cols, in_hbm(ritz),
+        group, shuffle, in_hbm(subspace), in_hbm(ritz),
         limit=12,
-        in_specs=[smem, vmem, vmem, vmem, vmem, hbm],
+        in_specs=[smem, vmem, hbm, hbm],
         scratch_shapes=[
+            pltpu.VMEM(subspace.shape, F32),
             pltpu.VMEM((groups, block, depth), F32),
+            pltpu.SemaphoreType.DMA,
             pltpu.SemaphoreType.DMA((groups, 2)),
         ],
     )
@@ -484,13 +484,13 @@
     start_far, far_rows = call(
         functools.partial(rotate_far, groups),
         [rows_of(duo), ((duo, block + 2 * duo), F32)],
-        in_vmem(far_cols_in), start_own, ritz_top, ritz_low, pick, pair,
+        far_cols_in, start_own, ritz_top, ritz_low, pick, pair,
     )
     far_in = far(far_rows)
     start_edge, out_rows, near_rows = call(
         functools.partial(rotate_ring, groups),
         [rows_of(wide), rows_of(halo), rows_of(halo)],
-        in_vmem(ring_cols_in), start_own, start_far, ritz_top, ritz_low, pick,
+        ring_cols_in, start_own, start_far, ritz_top, ritz_low, pick,
     )
     out_in, near_in = out(out_rows), near(near_rows)
     part, overlap, couple = call(
@@ -501,13 +501,13 @@
     (rest_low,) = call(
         functools.partial(rotate_low, groups),
         [((block, nodes - wide), F32)],
-        in_vmem(low_cols_in), start_own, ritz_top, ritz_low,
+        low_cols_in, start_own, ritz_top, ritz_low,
     )
 
     start_rest, back_far, back_out, back_near = call(
         functools.partial(rotate_rest, groups),
         [rows_of(nodes - wide)] + halo_out,
-        in_vmem(high_cols_in), rest_low, ritz_top, ritz_low, part, ham_top, ham_low,
+        high_cols_in, rest_low, ritz_top, ritz_low, part, ham_top, ham_low,
     )
     far_in, out_in, near_in = far(back_far), out(back_out), near(back_near)
     start, base, packed, adjust = call(

time: 58.8 us -> 58.8 us (level)
  starting transfers between devices: 19 us -> 18 us
  waiting for transfers between devices: 18.3 us -> 19 us
    ppermute x4, waiting for transfers between devices: 17.7 us -> 18.7 us  [out(): return lax.ppermute(rows, 'mesh', pairs_out)]
    ppermute x4, starting transfers between devices: 2.49 us -> 1.89 us  [out(): return lax.ppermute(rows, 'mesh', pairs_out)]
  transfers between devices with their start and end apart: 16 -> 16, of which waited for: 5 -> 5; matrix products, arithmetic and copies ran while one was open for 0% -> 0% of each run, Pallas kernels for 26% -> 27%
where the time goes in v11:
time: 58.8 us; the launch traced here: 58.6 us
  Pallas kernels  21.4 us (36%)
  waiting for transfers between devices  19 us (32%)
  starting transfers between devices  18 us (31%)
    pallas_call x16, Pallas kernels, call(): pl.pallas_call(body, out_shape=[jax.ShapeDtypeStruct(*out) for out in out...  21.4 us
    ppermute x4, waiting for transfers between devices, out(): return lax.ppermute(rows, 'mesh', pairs_out)  18.7 us
    ppermute x4, starting transfers between devices, far(): return lax.ppermute(rows, 'mesh', pairs_far)  8.75 us
    ppermute x4, starting transfers between devices, gather(): lax.ppermute(rows, 'state', [(i, (i + step) % groups) for i in range(grou...  5.14 us
    ppermute x4, starting transfers between devices, near(): return lax.ppermute(rows, 'mesh', pairs_in)  2.23 us
    ppermute x4, starting transfers between devices, out(): return lax.ppermute(rows, 'mesh', pairs_out)  1.89 us
  transfers between devices with their start and end apart: 16, of which 5 were waited for; matrix products, arithmetic and copies ran while one was open for 0% of the time, Pallas kernels for 27%

profile of v11, /device:TPU:0, one launch (start us, length us, event | category | flops | bytes accessed | tf_op | source)
XLA Modules:
  0.0 58.6 jit_solution(715146552648073126)
XLA Ops:
  0.0 2.7 %shard_map.55 = (f32[512,128]{1,0:T(8,128)}, f32[512,128]{1,0:T(8,128)}, f32[512,128]{1,0:T(8,128)}, f32[512,128]{1,0:T(8,128)}, bf16[256,256]{1,0:T(8,128)(2,1)S(1)}) custom-call(s32[1,4,32]{2,1,0:T(4,128)} %lists.1, f32[1024,256]{1,0:T(8,128)} %subspace_in.3), custom_call_target="tpu_custom_call" | custom-call | flops 1000 | bytes 1000 | tf_op jit(solution)/shard_map/pallas_call | solution.py:43
  2.7 3.0 %collective-permute-start.1 = (f32[512,128]{1,0:T(8,128)}, f32[512,128]{1,0:T(8,128)S(1)}, u32[]{:S(2)}, u32[]{:S(2)}) collective-permute-start(f32[512,128]{1,0:T(8,128)} %get-tuple-element.46), channel_id=1, source_target_pairs={{0,1},{1,0},{2,3},{3,2},{4,5},{5,4},{6,7},{7,6},{8,9},{9,8},{10,11... | collective-permute-start | bytes 786440 | tf_op jit(solution)/shard_map/ppermute | solution.py:408
  5.8 1.9 %collective-permute-start.3 = (f32[512,128]{1,0:T(8,128)}, f32[512,128]{1,0:T(8,128)S(1)}, u32[]{:S(2)}, u32[]{:S(2)}) collective-permute-start(f32[512,128]{1,0:T(8,128)} %get-tuple-element.54), channel_id=1, source_target_pairs={{0,1},{1,0},{2,3},{3,2},{4,5},{5,4},{6,7},{7,6},{8,9},{9,8},{10,11... | collective-permute-start | bytes 786440 | tf_op jit(solution)/shard_map/ppermute | solution.py:408
  7.9 5.0 %shard_map.56 = (f32[512,256]{1,0:T(8,128)S(1)}, bf16[512,1024]{1,0:T(8,128)(2,1)S(1)}, bf16[512,1024]{1,0:T(8,128)(2,1)S(1)}) custom-call(s32[1]{0:T(128)} %bitcast.group, bf16[256,256]{1,0:T(8,128)(2,1)S(1)} %get-tuple-element.44.shuffle, f32[1024,256]{1,0:T(8,128)} %subspace_in.3, f32[512,2048]{1,0:T(8,128)} %ritz_in.1), custom_call_target="tpu_custom_call" | custom-call | flops 1000 | bytes 1000 | tf_op jit(solution)/shard_map/pallas_call | solution.py:43
  12.9 4.1 %shard_map.57 = (bf16[384,384]{1,0:T(8,128)(2,1)S(1)}, bf16[384,384]{1,0:T(8,128)(2,1)S(1)}, bf16[128,128]{1,0:T(8,128)(2,1)S(1)}, bf16[128,128]{1,0:T(8,128)(2,...) custom-call(s32[1]{0:T(128)} %bitcast.1.odd, s32[1,4,32]{2,1,0:T(4,128)S(1)} %copy-done.1, ...), custom_call_target="tpu_custom_call" | custom-call | flops 1000 | bytes 1000 | tf_op jit(solution)/shard_map/pallas_call | solution.py:43
  17.0 1.1 %shard_map.58 = (f32[64,512]{1,0:T(8,128)S(1)}, f32[64,640]{1,0:T(8,128)S(1)}) custom-call(f32[512,128]{1,0:T(8,128)S(1)} %collective-permute-done.1.columns, f32[512,256]{1,0:T(8,128)S(1)} %get-tuple-element.45.start_own, bf16[512,1024]{1,0:T(8,128)(2,1)S(1)} %get-tuple-element.47.top, bf16[512,1024]{1,0:T(8,128)(2,1)S(1)} %get-tuple-element.48.low, ...), custom_call_target="tpu_custom_call" | custom-call | flops 1000 | bytes 1000 | tf_op jit(solution)/shard_map/pallas_call | solution.py:43
  18.1 3.1 %collective-permute-start.4 = (f32[64,640]{1,0:T(8,128)S(1)}, f32[64,640]{1,0:T(8,128)S(1)}, u32[]{:S(2)}, u32[]{:S(2)}) collective-permute-start(f32[64,640]{1,0:T(8,128)S(1)} %get-tuple-element.55), channel_id=1, source_target_pairs={{0,16},{2,18},{4,20},{6,22},{8,24},{10,26},{12,28},{14,30},{16,0},... | collective-permute-start | bytes 491528 | tf_op jit(solution)/shard_map/ppermute | solution.py:398
  21.2 1.2 %shard_map.59 = (f32[128,512]{1,0:T(8,128)S(1)}, f32[32,512]{1,0:T(8,128)S(1)}, f32[32,512]{1,0:T(8,128)S(1)}) custom-call(f32[512,128]{1,0:T(8,128)S(1)} %collective-permute-done.columns, f32[512,256]{1,0:T(8,128)S(1)} %get-tuple-element.45.start_own, f32[64,512]{1,0:T(8,128)S(1)} %get-tuple-element.51.start_far, ...), custom_call_target="tpu_custom_call" | custom-call | flops 1000 | bytes 1000 | tf_op jit(solution)/shard_map/pallas_call | solution.py:43
  22.8 1.3 %collective-permute-start.6 = (f32[32,512]{1,0:T(8,128)S(1)}, f32[32,512]{1,0:T(8,128)S(1)}, u32[]{:S(2)}, u32[]{:S(2)}) collective-permute-start(f32[32,512]{1,0:T(8,128)S(1)} %get-tuple-element.57), channel_id=1, source_target_pairs={{0,2},{2,0},{4,6},{6,4},{8,10},{10,8},{12,14},{14,12},{16,18},{18,... | collective-permute-start | bytes 196616 | tf_op jit(solution)/shard_map/ppermute | solution.py:404
  24.4 0.4 shard_map.60.rest_low
  24.8 4.1 %collective-permute-done.5.out_in = f32[32,512]{1,0:T(8,128)S(1)} collective-permute-done((f32[32,512]{1,0:T(8,128)S(1)}, f32[32,512]{1,0:T(8,128)S(1)}, u32[]{:S(2)}, u32[]{:S(2)}) %collective-permute-start.5) | collective-permute-done | bytes 65568 | tf_op jit(solution)/shard_map/ppermute | solution.py:401
  28.9 0.8 %shard_map.61 = (f32[384,512]{1,0:T(8,128)S(1)}, f32[64,64]{1,0:T(8,128)S(1)}, f32[64,64]{1,0:T(8,128)S(1)}) custom-call(f32[128,512]{1,0:T(8,128)S(1)} %get-tuple-element.52.start_edge, f32[64,640]{1,0:T(8,128)S(1)} %collective-permute-done.4.far_in, f32[32,512]{1,0:T(8,128)S(1)} %collective-permute-done.5.out_in, ...), custom_call_target="tpu_custom_call" | custom-call | flops 1000 | bytes 1000 | tf_op jit(solution)/shard_map/pallas_call | solution.py:43
  29.7 1.7 %shard_map.62 = (f32[128,512]{1,0:T(8,128)S(1)}, f32[64,512]{1,0:T(8,128)S(1)}, f32[32,512]{1,0:T(8,128)S(1)}, f32[32,512]{1,0:T(8,128)S(1)}) custom-call(f32[512,128]{1,0:T(8,128)} %collective-permute-done.2.columns, f32[512,128]{1,0:T(8,128)S(1)} %shard_map.60.rest_low, bf16[512,1024]{1,0:T(8,128)(2,1)S(1)} %get-tuple-element.47.top, ...), custom_call_target="tpu_custom_call" | custom-call | flops 1000 | bytes 1000 | tf_op jit(solution)/shard_map/pallas_call | solution.py:43
  31.4 3.1 %collective-permute-start.7 = (f32[64,512]{1,0:T(8,128)S(1)}, f32[64,512]{1,0:T(8,128)S(1)}, u32[]{:S(2)}, u32[]{:S(2)}) collective-permute-start(f32[64,512]{1,0:T(8,128)S(1)} %get-tuple-element.63.back_far), channel_id=1, source_target_pairs={{0,16},{2,18},{4,20},{6,22},{8,24},{10,26},{12,28},{14,30},{16,0},... | collective-permute-start | bytes 393224 | tf_op jit(solution)/shard_map/ppermute | solution.py:398
  34.6 0.9 %collective-permute-start.9 = (f32[32,512]{1,0:T(8,128)S(1)}, f32[32,512]{1,0:T(8,128)S(1)}, u32[]{:S(2)}, u32[]{:S(2)}) collective-permute-start(f32[32,512]{1,0:T(8,128)S(1)} %get-tuple-element.66), channel_id=1, source_target_pairs={{0,2},{2,0},{4,6},{6,4},{8,10},{10,8},{12,14},{14,12},{16,18},{18,... | collective-permute-start | bytes 196616 | tf_op jit(solution)/shard_map/ppermute | solution.py:404
  35.5 0.6 %shard_map.63 = (f32[256,512]{1,0:T(8,128)S(1)}, f32[256,512]{1,0:T(8,128)S(1)}, f32[128,512]{1,0:T(8,128)S(1)}, f32[64,512]{1,0:T(8,128)S(1)}) custom-call(f32[128,512]{1,0:T(8,128)S(1)} %get-tuple-element.52.start_edge, f32[128,512]{1,0:T(8,128)S(1)} %get-tuple-element.61.start_rest, f32[384,512]{1,0:T(8,128)S(1)} %get-tuple-element.60.part, ...), custom_call_target="tpu_custom_call" | custom-call | flops 1000 | bytes 1000 | tf_op jit(solution)/shard_map/pallas_call | solution.py:43
  36.1 5.0 %collective-permute-done.8.out_in = f32[32,512]{1,0:T(8,128)S(1)} collective-permute-done((f32[32,512]{1,0:T(8,128)S(1)}, f32[32,512]{1,0:T(8,128)S(1)}, u32[]{:S(2)}, u32[]{:S(2)}) %collective-permute-start.8) | collective-permute-done | bytes 65568 | tf_op jit(solution)/shard_map/ppermute | solution.py:401
  41.3 2.5 %collective-permute-start.10 = (f32[64,512]{1,0:T(8,128)S(1)}, f32[64,512]{1,0:T(8,128)S(1)}, u32[]{:S(2)}, u32[]{:S(2)}) collective-permute-start(f32[64,512]{1,0:T(8,128)S(1)} %shard_map.65), channel_id=1, source_target_pairs={{0,16},{2,18},{4,20},{6,22},{8,24},{10,26},{12,28},{14,30},{16,0},... | collective-permute-start | bytes 393224 | tf_op jit(solution)/shard_map/ppermute | solution.py:398
  44.1 0.9 %shard_map.64 = (f32[256,512]{1,0:T(8,128)S(1)}, f32[384,512]{1,0:T(8,128)S(1)}, f32[64,512]{1,0:T(8,128)S(1)}) custom-call(f32[256,512]{1,0:T(8,128)S(1)} %get-tuple-element.64.base, bf16[128,128]{1,0:T(8,128)(2,1)S(1)} %get-tuple-element.49.pick, f32[64,512]{1,0:T(8,128)S(1)} %collective-permute-done.7.far_in, ...), custom_call_target="tpu_custom_call" | custom-call | flops 1000 | bytes 1000 | tf_op jit(solution)/shard_map/pallas_call | solution.py:43
  45.0 5.4 %collective-permute-done.11.out_in = f32[32,512]{1,0:T(8,128)S(1)} collective-permute-done((f32[32,512]{1,0:T(8,128)S(1)}, f32[32,512]{1,0:T(8,128)S(1)}, u32[]{:S(2)}, u32[]{:S(2)}) %collective-permute-start.11) | collective-permute-done | bytes 65568 | tf_op jit(solution)/shard_map/ppermute | solution.py:401
  51.0 1.4 %collective-permute-start.14 = (f32[32,512]{1,0:T(8,128)S(1)}, f32[32,512]{1,0:T(8,128)S(1)}, u32[]{:S(2)}, u32[]{:S(2)}) collective-permute-start(f32[32,512]{1,0:T(8,128)S(1)} %get-tuple-element.79), channel_id=1, source_target_pairs={{0,30},{2,4},{4,2},{6,8},{8,6},{10,12},{12,10},{14,16},{16,14},{18... | collective-permute-start | bytes 196616 | tf_op jit(solution)/shard_map/ppermute | solution.py:401
  52.4 0.8 %shard_map.68.result = f32[512,256]{1,0:T(8,128)S(1)} custom-call(f32[384,512]{1,0:T(8,128)S(1)} %get-tuple-element.68.part, f32[128,512]{1,0:T(8,128)S(1)} %get-tuple-element.74.ghosts, bf16[384,384]{1,0:T(8,128)(2,1)S(1)} %get-tuple-element.58.ham_top, bf16[384,384]{1,0:T(8,128)(2,1)S(1)} %get-tuple-element.59.ham_low, ...), custom_call_target="tpu_custom_call" | custom-call | flops 1000 | bytes 1000 | tf_op jit(solution)/shard_map/pallas_call | solution.py:43
  53.2 4.2 %collective-permute-done.14.out_in = f32[32,512]{1,0:T(8,128)S(1)} collective-permute-done((f32[32,512]{1,0:T(8,128)S(1)}, f32[32,512]{1,0:T(8,128)S(1)}, u32[]{:S(2)}, u32[]{:S(2)}) %collective-permute-start.14) | collective-permute-done | bytes 65568 | tf_op jit(solution)/shard_map/ppermute | solution.py:401
  57.4 1.1 %shard_map.70 = f32[512,256]{1,0:T(8,128)} custom-call(f32[512,256]{1,0:T(8,128)S(1)} %shard_map.68.result, bf16[128,256]{1,0:T(8,128)(2,1)S(1)} %get-tuple-element.78.hits, f32[64,512]{1,0:T(8,128)S(1)} %collective-permute-done.13.far_in, f32[32,512]{1,0:T(8,128)S(1)} %collective-permute-done.14.out_in, f32[32,512]{1,0:T(8,128)S(1)} %collective-permute-done.15.near_in), custom_call_target="tpu_custom_call" | custom-call | flops 1000 | bytes 1000 | tf_op jit(solution)/shard_map/pallas_call | solution.py:43
  (28 shorter events, 2.0 us)
Async XLA Ops:
  0.0 12.9 %copy-start.1 = (s32[1,4,32]{2,1,0:T(4,128)S(1)}, s32[1,4,32]{2,1,0:T(4,128)}, u32[]{:S(2)}) copy-start(s32[1,4,32]{2,1,0:T(4,128)} %lists.1) | copy-start | bytes 1540
  0.0 12.9 %copy-start = (s32[16,125]{1,0:T(8,128)S(1)}, s32[16,125]{1,0:T(8,128)}, u32[]{:S(2)}) copy-start(s32[16,125]{1,0:T(8,128)} %connect.1) | copy-start | bytes 24004
  2.7 14.3 %collective-permute-start.1 = (f32[512,128]{1,0:T(8,128)}, f32[512,128]{1,0:T(8,128)S(1)}, u32[]{:S(2)}, u32[]{:S(2)}) collective-permute-start(f32[512,128]{1,0:T(8,128)} %get-tuple-element.46), channel_id=1, source_target_pairs={{0,1},{1,0},{2,3},{3,2},{4,5},{5,4},{6,7},{7,6},{8,9},{9,8},{10,11... | collective-permute-start | bytes 786440 | tf_op jit(solution)/shard_map/ppermute | solution.py:408
  5.8 15.4 %collective-permute-start = (f32[512,128]{1,0:T(8,128)}, f32[512,128]{1,0:T(8,128)S(1)}, u32[]{:S(2)}, u32[]{:S(2)}) collective-permute-start(f32[512,128]{1,0:T(8,128)} %get-tuple-element.43), channel_id=1, source_target_pairs={{0,1},{1,0},{2,3},{3,2},{4,5},{5,4},{6,7},{7,6},{8,9},{9,8},{10,11... | collective-permute-start | bytes 786440 | tf_op jit(solution)/shard_map/ppermute | solution.py:408
  5.8 18.5 %collective-permute-start.3 = (f32[512,128]{1,0:T(8,128)}, f32[512,128]{1,0:T(8,128)S(1)}, u32[]{:S(2)}, u32[]{:S(2)}) collective-permute-start(f32[512,128]{1,0:T(8,128)} %get-tuple-element.54), channel_id=1, source_target_pairs={{0,1},{1,0},{2,3},{3,2},{4,5},{5,4},{6,7},{7,6},{8,9},{9,8},{10,11... | collective-permute-start | bytes 786440 | tf_op jit(solution)/shard_map/ppermute | solution.py:408
  7.8 21.9 %collective-permute-start.2 = (f32[512,128]{1,0:T(8,128)}, f32[512,128]{1,0:T(8,128)}, u32[]{:S(2)}, u32[]{:S(2)}) collective-permute-start(f32[512,128]{1,0:T(8,128)} %get-tuple-element.53), channel_id=1, source_target_pairs={{0,1},{1,0},{2,3},{3,2},{4,5},{5,4},{6,7},{7,6},{8,9},{9,8},{10,11... | collective-permute-start | bytes 786440 | tf_op jit(solution)/shard_map/ppermute | solution.py:408
  18.1 10.9 %collective-permute-start.4 = (f32[64,640]{1,0:T(8,128)S(1)}, f32[64,640]{1,0:T(8,128)S(1)}, u32[]{:S(2)}, u32[]{:S(2)}) collective-permute-start(f32[64,640]{1,0:T(8,128)S(1)} %get-tuple-element.55), channel_id=1, source_target_pairs={{0,16},{2,18},{4,20},{6,22},{8,24},{10,26},{12,28},{14,30},{16,0},... | collective-permute-start | bytes 491528 | tf_op jit(solution)/shard_map/ppermute | solution.py:398
  22.4 6.6 %collective-permute-start.5 = (f32[32,512]{1,0:T(8,128)S(1)}, f32[32,512]{1,0:T(8,128)S(1)}, u32[]{:S(2)}, u32[]{:S(2)}) collective-permute-start(f32[32,512]{1,0:T(8,128)S(1)} %get-tuple-element.56), channel_id=1, source_target_pairs={{0,30},{2,4},{4,2},{6,8},{8,6},{10,12},{12,10},{14,16},{16,14},{18... | collective-permute-start | bytes 196616 | tf_op jit(solution)/shard_map/ppermute | solution.py:401
  22.8 6.2 %collective-permute-start.6 = (f32[32,512]{1,0:T(8,128)S(1)}, f32[32,512]{1,0:T(8,128)S(1)}, u32[]{:S(2)}, u32[]{:S(2)}) collective-permute-start(f32[32,512]{1,0:T(8,128)S(1)} %get-tuple-element.57), channel_id=1, source_target_pairs={{0,2},{2,0},{4,6},{6,4},{8,10},{10,8},{12,14},{14,12},{16,18},{18,... | collective-permute-start | bytes 196616 | tf_op jit(solution)/shard_map/ppermute | solution.py:404
  31.4 12.3 %collective-permute-start.7 = (f32[64,512]{1,0:T(8,128)S(1)}, f32[64,512]{1,0:T(8,128)S(1)}, u32[]{:S(2)}, u32[]{:S(2)}) collective-permute-start(f32[64,512]{1,0:T(8,128)S(1)} %get-tuple-element.63.back_far), channel_id=1, source_target_pairs={{0,16},{2,18},{4,20},{6,22},{8,24},{10,26},{12,28},{14,30},{16,0},... | collective-permute-start | bytes 393224 | tf_op jit(solution)/shard_map/ppermute | solution.py:398
  34.6 6.5 %collective-permute-start.8 = (f32[32,512]{1,0:T(8,128)S(1)}, f32[32,512]{1,0:T(8,128)S(1)}, u32[]{:S(2)}, u32[]{:S(2)}) collective-permute-start(f32[32,512]{1,0:T(8,128)S(1)} %get-tuple-element.65), channel_id=1, source_target_pairs={{0,30},{2,4},{4,2},{6,8},{8,6},{10,12},{12,10},{14,16},{16,14},{18... | collective-permute-start | bytes 196616 | tf_op jit(solution)/shard_map/ppermute | solution.py:401
  34.6 6.5 %collective-permute-start.9 = (f32[32,512]{1,0:T(8,128)S(1)}, f32[32,512]{1,0:T(8,128)S(1)}, u32[]{:S(2)}, u32[]{:S(2)}) collective-permute-start(f32[32,512]{1,0:T(8,128)S(1)} %get-tuple-element.66), channel_id=1, source_target_pairs={{0,2},{2,0},{4,6},{6,4},{8,10},{10,8},{12,14},{14,12},{16,18},{18,... | collective-permute-start | bytes 196616 | tf_op jit(solution)/shard_map/ppermute | solution.py:404
  41.3 9.4 %collective-permute-start.10 = (f32[64,512]{1,0:T(8,128)S(1)}, f32[64,512]{1,0:T(8,128)S(1)}, u32[]{:S(2)}, u32[]{:S(2)}) collective-permute-start(f32[64,512]{1,0:T(8,128)S(1)} %shard_map.65), channel_id=1, source_target_pairs={{0,16},{2,18},{4,20},{6,22},{8,24},{10,26},{12,28},{14,30},{16,0},... | collective-permute-start | bytes 393224 | tf_op jit(solution)/shard_map/ppermute | solution.py:398
  44.0 6.5 %collective-permute-start.11 = (f32[32,512]{1,0:T(8,128)S(1)}, f32[32,512]{1,0:T(8,128)S(1)}, u32[]{:S(2)}, u32[]{:S(2)}) collective-permute-start(f32[32,512]{1,0:T(8,128)S(1)} %get-tuple-element.72), channel_id=1, source_target_pairs={{0,30},{2,4},{4,2},{6,8},{8,6},{10,12},{12,10},{14,16},{16,14},{18... | collective-permute-start | bytes 196616 | tf_op jit(solution)/shard_map/ppermute | solution.py:401
  44.0 6.4 %collective-permute-start.12 = (f32[32,512]{1,0:T(8,128)S(1)}, f32[32,512]{1,0:T(8,128)S(1)}, u32[]{:S(2)}, u32[]{:S(2)}) collective-permute-start(f32[32,512]{1,0:T(8,128)S(1)} %get-tuple-element.73), channel_id=1, source_target_pairs={{0,2},{2,0},{4,6},{6,4},{8,10},{10,8},{12,14},{14,12},{16,18},{18,... | collective-permute-start | bytes 196616 | tf_op jit(solution)/shard_map/ppermute | solution.py:404
  50.7 6.8 %collective-permute-start.13 = (f32[64,512]{1,0:T(8,128)S(1)}, f32[64,512]{1,0:T(8,128)S(1)}, u32[]{:S(2)}, u32[]{:S(2)}) collective-permute-start(f32[64,512]{1,0:T(8,128)S(1)} %shard_map.69), channel_id=1, source_target_pairs={{0,16},{2,18},{4,20},{6,22},{8,24},{10,26},{12,28},{14,30},{16,0},... | collective-permute-start | bytes 393224 | tf_op jit(solution)/shard_map/ppermute | solution.py:398
  51.0 6.5 %collective-permute-start.14 = (f32[32,512]{1,0:T(8,128)S(1)}, f32[32,512]{1,0:T(8,128)S(1)}, u32[]{:S(2)}, u32[]{:S(2)}) collective-permute-start(f32[32,512]{1,0:T(8,128)S(1)} %get-tuple-element.79), channel_id=1, source_target_pairs={{0,30},{2,4},{4,2},{6,8},{8,6},{10,12},{12,10},{14,16},{16,14},{18... | collective-permute-start | bytes 196616 | tf_op jit(solution)/shard_map/ppermute | solution.py:401
  52.4 5.0 %collective-permute-start.15 = (f32[32,512]{1,0:T(8,128)S(1)}, f32[32,512]{1,0:T(8,128)S(1)}, u32[]{:S(2)}, u32[]{:S(2)}) collective-permute-start(f32[32,512]{1,0:T(8,128)S(1)} %get-tuple-element.80), channel_id=1, source_target_pairs={{0,2},{2,0},{4,6},{6,4},{8,10},{10,8},{12,14},{14,12},{16,18},{18,... | collective-permute-start | bytes 196616 | tf_op jit(solution)/shard_map/ppermute | solution.py:404

commit v12 on v11

--- a/solution.py
+++ b/solution.py
@@ -44,7 +44,6 @@
         body,
         out_shape=[jax.ShapeDtypeStruct(*out) for out in outs],
         compiler_params=pltpu.CompilerParams(vmem_limit_bytes=limit << 20),
-        cost_estimate=pl.CostEstimate(flops=1000, bytes_accessed=1000, transcendentals=0),
         **rest,
     )(*args)
 

time: 58.8 us -> 56.6 us (0.963)
  Pallas kernels: 21.4 us -> 19.6 us
  starting transfers between devices: 18 us -> 17.1 us
    pallas_call x16, Pallas kernels: 21.4 us -> 19.6 us  [call(): pl.pallas_call(body, out_shape=[jax.ShapeDtypeStruct(*out) for out in out...]
    ppermute x4, waiting for transfers between devices: 18.7 us -> 19.5 us  [out(): return lax.ppermute(rows, 'mesh', pairs_out)]
  transfers between devices with their start and end apart: 16 -> 16, of which waited for: 5 -> 5; matrix products, arithmetic and copies ran while one was open for 0% -> 0% of each run, Pallas kernels for 27% -> 28%
where the time goes in v12:
time: 56.6 us; the launch traced here: 56.5 us
  Pallas kernels  19.6 us (35%)
  waiting for transfers between devices  19.5 us (34%)
  starting transfers between devices  17.1 us (30%)
    pallas_call x16, Pallas kernels, call(): pl.pallas_call(body, out_shape=[jax.ShapeDtypeStruct(*out) for out in out...  19.6 us
    ppermute x4, waiting for transfers between devices, out(): return lax.ppermute(rows, 'mesh', pairs_out)  19.5 us
    ppermute x4, starting transfers between devices, far(): return lax.ppermute(rows, 'mesh', pairs_far)  8.42 us
    ppermute x4, starting transfers between devices, gather(): lax.ppermute(rows, 'state', [(i, (i + step) % groups) for i in range(grou...  5.14 us
    ppermute x4, starting transfers between devices, near(): return lax.ppermute(rows, 'mesh', pairs_in)  1.9 us
    ppermute x4, starting transfers between devices, out(): return lax.ppermute(rows, 'mesh', pairs_out)  1.66 us
  transfers between devices with their start and end apart: 16, of which 5 were waited for; matrix products, arithmetic and copies ran while one was open for 0% of the time, Pallas kernels for 28%

profile of v12, /device:TPU:0, one launch (start us, length us, event | category | flops | bytes accessed | tf_op | source)
XLA Modules:
  0.0 56.5 jit_solution(16622071378815610437)
XLA Ops:
  0.0 1.8 %shard_map.55 = (f32[512,128]{1,0:T(8,128)S(1)}, f32[512,128]{1,0:T(8,128)S(1)}, f32[512,128]{1,0:T(8,128)S(1)}, f32[512,128]{1,0:T(8,128)S(1)}, bf16[256,256]{1,0:T(8,128)(2,1)S(1)}) custom-call(s32[1,4,32]{2,1,0:T(4,128)} %lists.1, f32[1024,256]{1,0:T(8,128)} %subspace_in.3), custom_call_target="tpu_custom_call" | custom-call | tf_op jit(solution)/shard_map/pallas_call | solution.py:43
  1.9 3.0 %collective-permute-start.1 = (f32[512,128]{1,0:T(8,128)S(1)}, f32[512,128]{1,0:T(8,128)S(1)}, u32[]{:S(2)}, u32[]{:S(2)}) collective-permute-start(f32[512,128]{1,0:T(8,128)S(1)} %get-tuple-element.46), channel_id=1, source_target_pairs={{0,1},{1,0},{2,3},{3,2},{4,5},{5,4},{6,7},{7,6},{8,9},{9,8},{10,11... | collective-permute-start | bytes 786440 | tf_op jit(solution)/shard_map/ppermute | solution.py:407
  5.0 1.9 %collective-permute-start.3 = (f32[512,128]{1,0:T(8,128)S(1)}, f32[512,128]{1,0:T(8,128)S(1)}, u32[]{:S(2)}, u32[]{:S(2)}) collective-permute-start(f32[512,128]{1,0:T(8,128)S(1)} %get-tuple-element.54), channel_id=1, source_target_pairs={{0,1},{1,0},{2,3},{3,2},{4,5},{5,4},{6,7},{7,6},{8,9},{9,8},{10,11... | collective-permute-start | bytes 786440 | tf_op jit(solution)/shard_map/ppermute | solution.py:407
  7.0 5.0 %shard_map.56 = (f32[512,256]{1,0:T(8,128)S(1)}, bf16[512,1024]{1,0:T(8,128)(2,1)S(1)}, bf16[512,1024]{1,0:T(8,128)(2,1)S(1)}) custom-call(s32[1]{0:T(128)} %bitcast.group, bf16[256,256]{1,0:T(8,128)(2,1)S(1)} %get-tuple-element.44.shuffle, f32[1024,256]{1,0:T(8,128)} %subspace_in.3, f32[512,2048]{1,0:T(8,128)} %ritz_in.1), custom_call_target="tpu_custom_call" | custom-call | tf_op jit(solution)/shard_map/pallas_call | solution.py:43
  12.0 4.1 %shard_map.57 = (bf16[384,384]{1,0:T(8,128)(2,1)S(1)}, bf16[384,384]{1,0:T(8,128)(2,1)S(1)}, bf16[128,128]{1,0:T(8,128)(2,1)S(1)}, bf16[128,128]{1,0:T(8,128)(2,...) custom-call(s32[1]{0:T(128)} %bitcast.1.odd, s32[1,4,32]{2,1,0:T(4,128)S(1)} %copy-done.1, ...), custom_call_target="tpu_custom_call" | custom-call | tf_op jit(solution)/shard_map/pallas_call | solution.py:43
  16.1 1.1 %shard_map.58 = (f32[64,512]{1,0:T(8,128)S(1)}, f32[64,640]{1,0:T(8,128)S(1)}) custom-call(f32[512,128]{1,0:T(8,128)S(1)} %collective-permute-done.1.columns, f32[512,256]{1,0:T(8,128)S(1)} %get-tuple-element.45.start_own, bf16[512,1024]{1,0:T(8,128)(2,1)S(1)} %get-tuple-element.47.top, bf16[512,1024]{1,0:T(8,128)(2,1)S(1)} %get-tuple-element.48.low, ...), custom_call_target="tpu_custom_call" | custom-call | tf_op jit(solution)/shard_map/pallas_call | solution.py:43
  17.2 3.1 %collective-permute-start.4 = (f32[64,640]{1,0:T(8,128)S(1)}, f32[64,640]{1,0:T(8,128)S(1)}, u32[]{:S(2)}, u32[]{:S(2)}) collective-permute-start(f32[64,640]{1,0:T(8,128)S(1)} %get-tuple-element.55), channel_id=1, source_target_pairs={{0,16},{2,18},{4,20},{6,22},{8,24},{10,26},{12,28},{14,30},{16,0},... | collective-permute-start | bytes 491528 | tf_op jit(solution)/shard_map/ppermute | solution.py:397
  20.3 1.2 %shard_map.59 = (f32[128,512]{1,0:T(8,128)S(1)}, f32[32,512]{1,0:T(8,128)S(1)}, f32[32,512]{1,0:T(8,128)S(1)}) custom-call(f32[512,128]{1,0:T(8,128)S(1)} %collective-permute-done.columns, f32[512,256]{1,0:T(8,128)S(1)} %get-tuple-element.45.start_own, f32[64,512]{1,0:T(8,128)S(1)} %get-tuple-element.51.start_far, ...), custom_call_target="tpu_custom_call" | custom-call | tf_op jit(solution)/shard_map/pallas_call | solution.py:43
  21.9 1.3 %collective-permute-start.6 = (f32[32,512]{1,0:T(8,128)S(1)}, f32[32,512]{1,0:T(8,128)S(1)}, u32[]{:S(2)}, u32[]{:S(2)}) collective-permute-start(f32[32,512]{1,0:T(8,128)S(1)} %get-tuple-element.57), channel_id=1, source_target_pairs={{0,2},{2,0},{4,6},{6,4},{8,10},{10,8},{12,14},{14,12},{16,18},{18,... | collective-permute-start | bytes 196616 | tf_op jit(solution)/shard_map/ppermute | solution.py:403
  23.3 0.5 shard_map.60.rest_low
  23.7 4.4 %collective-permute-done.5.out_in = f32[32,512]{1,0:T(8,128)S(1)} collective-permute-done((f32[32,512]{1,0:T(8,128)S(1)}, f32[32,512]{1,0:T(8,128)S(1)}, u32[]{:S(2)}, u32[]{:S(2)}) %collective-permute-start.5) | collective-permute-done | bytes 65568 | tf_op jit(solution)/shard_map/ppermute | solution.py:400
  28.1 0.8 %shard_map.61 = (f32[384,512]{1,0:T(8,128)S(1)}, f32[64,64]{1,0:T(8,128)S(1)}, f32[64,64]{1,0:T(8,128)S(1)}) custom-call(f32[128,512]{1,0:T(8,128)S(1)} %get-tuple-element.52.start_edge, f32[64,640]{1,0:T(8,128)S(1)} %collective-permute-done.4.far_in, f32[32,512]{1,0:T(8,128)S(1)} %collective-permute-done.5.out_in, ...), custom_call_target="tpu_custom_call" | custom-call | tf_op jit(solution)/shard_map/pallas_call | solution.py:43
  28.9 0.8 %shard_map.62 = (f32[128,512]{1,0:T(8,128)S(1)}, f32[64,512]{1,0:T(8,128)S(1)}, f32[32,512]{1,0:T(8,128)S(1)}, f32[32,512]{1,0:T(8,128)S(1)}) custom-call(f32[512,128]{1,0:T(8,128)S(1)} %collective-permute-done.2.columns, f32[512,128]{1,0:T(8,128)S(1)} %shard_map.60.rest_low, bf16[512,1024]{1,0:T(8,128)(2,1)S(1)} %get-tuple-element.47.top, ...), custom_call_target="tpu_custom_call" | custom-call | tf_op jit(solution)/shard_map/pallas_call | solution.py:43
  29.6 3.1 %collective-permute-start.7 = (f32[64,512]{1,0:T(8,128)S(1)}, f32[64,512]{1,0:T(8,128)S(1)}, u32[]{:S(2)}, u32[]{:S(2)}) collective-permute-start(f32[64,512]{1,0:T(8,128)S(1)} %get-tuple-element.63.back_far), channel_id=1, source_target_pairs={{0,16},{2,18},{4,20},{6,22},{8,24},{10,26},{12,28},{14,30},{16,0},... | collective-permute-start | bytes 393224 | tf_op jit(solution)/shard_map/ppermute | solution.py:397
  32.8 0.5 collective-permute-start.9
  33.3 0.6 %shard_map.63 = (f32[256,512]{1,0:T(8,128)S(1)}, f32[256,512]{1,0:T(8,128)S(1)}, f32[128,512]{1,0:T(8,128)S(1)}, f32[64,512]{1,0:T(8,128)S(1)}) custom-call(f32[128,512]{1,0:T(8,128)S(1)} %get-tuple-element.52.start_edge, f32[128,512]{1,0:T(8,128)S(1)} %get-tuple-element.61.start_rest, f32[384,512]{1,0:T(8,128)S(1)} %get-tuple-element.60.part, ...), custom_call_target="tpu_custom_call" | custom-call | tf_op jit(solution)/shard_map/pallas_call | solution.py:43
  33.9 5.3 %collective-permute-done.8.out_in = f32[32,512]{1,0:T(8,128)S(1)} collective-permute-done((f32[32,512]{1,0:T(8,128)S(1)}, f32[32,512]{1,0:T(8,128)S(1)}, u32[]{:S(2)}, u32[]{:S(2)}) %collective-permute-start.8) | collective-permute-done | bytes 65568 | tf_op jit(solution)/shard_map/ppermute | solution.py:400
  39.5 2.1 %collective-permute-start.10 = (f32[64,512]{1,0:T(8,128)S(1)}, f32[64,512]{1,0:T(8,128)S(1)}, u32[]{:S(2)}, u32[]{:S(2)}) collective-permute-start(f32[64,512]{1,0:T(8,128)S(1)} %shard_map.65), channel_id=1, source_target_pairs={{0,16},{2,18},{4,20},{6,22},{8,24},{10,26},{12,28},{14,30},{16,0},... | collective-permute-start | bytes 393224 | tf_op jit(solution)/shard_map/ppermute | solution.py:397
  42.0 0.9 %shard_map.64 = (f32[256,512]{1,0:T(8,128)S(1)}, f32[384,512]{1,0:T(8,128)S(1)}, f32[64,512]{1,0:T(8,128)S(1)}) custom-call(f32[256,512]{1,0:T(8,128)S(1)} %get-tuple-element.64.base, bf16[128,128]{1,0:T(8,128)(2,1)S(1)} %get-tuple-element.49.pick, f32[64,512]{1,0:T(8,128)S(1)} %collective-permute-done.7.far_in, ...), custom_call_target="tpu_custom_call" | custom-call | tf_op jit(solution)/shard_map/pallas_call | solution.py:43
  42.9 5.4 %collective-permute-done.11.out_in = f32[32,512]{1,0:T(8,128)S(1)} collective-permute-done((f32[32,512]{1,0:T(8,128)S(1)}, f32[32,512]{1,0:T(8,128)S(1)}, u32[]{:S(2)}, u32[]{:S(2)}) %collective-permute-start.11) | collective-permute-done | bytes 65568 | tf_op jit(solution)/shard_map/ppermute | solution.py:400
  48.8 1.2 %collective-permute-start.14 = (f32[32,512]{1,0:T(8,128)S(1)}, f32[32,512]{1,0:T(8,128)S(1)}, u32[]{:S(2)}, u32[]{:S(2)}) collective-permute-start(f32[32,512]{1,0:T(8,128)S(1)} %get-tuple-element.79), channel_id=1, source_target_pairs={{0,30},{2,4},{4,2},{6,8},{8,6},{10,12},{12,10},{14,16},{16,14},{18... | collective-permute-start | bytes 196616 | tf_op jit(solution)/shard_map/ppermute | solution.py:400
  50.1 0.8 %shard_map.68.result = f32[512,256]{1,0:T(8,128)S(1)} custom-call(f32[384,512]{1,0:T(8,128)S(1)} %get-tuple-element.68.part, f32[128,512]{1,0:T(8,128)S(1)} %get-tuple-element.74.ghosts, bf16[384,384]{1,0:T(8,128)(2,1)S(1)} %get-tuple-element.58.ham_top, bf16[384,384]{1,0:T(8,128)(2,1)S(1)} %get-tuple-element.59.ham_low, ...), custom_call_target="tpu_custom_call" | custom-call | tf_op jit(solution)/shard_map/pallas_call | solution.py:43
  50.9 4.4 %collective-permute-done.14.out_in = f32[32,512]{1,0:T(8,128)S(1)} collective-permute-done((f32[32,512]{1,0:T(8,128)S(1)}, f32[32,512]{1,0:T(8,128)S(1)}, u32[]{:S(2)}, u32[]{:S(2)}) %collective-permute-start.14) | collective-permute-done | bytes 65568 | tf_op jit(solution)/shard_map/ppermute | solution.py:400
  55.3 1.1 %shard_map.70 = f32[512,256]{1,0:T(8,128)} custom-call(f32[512,256]{1,0:T(8,128)S(1)} %shard_map.68.result, bf16[128,256]{1,0:T(8,128)(2,1)S(1)} %get-tuple-element.78.hits, f32[64,512]{1,0:T(8,128)S(1)} %collective-permute-done.13.far_in, f32[32,512]{1,0:T(8,128)S(1)} %collective-permute-done.14.out_in, f32[32,512]{1,0:T(8,128)S(1)} %collective-permute-done.15.near_in), custom_call_target="tpu_custom_call" | custom-call | tf_op jit(solution)/shard_map/pallas_call | solution.py:43
  (28 shorter events, 1.7 us)
Async XLA Ops:
  0.0 12.0 %copy-start.1 = (s32[1,4,32]{2,1,0:T(4,128)S(1)}, s32[1,4,32]{2,1,0:T(4,128)}, u32[]{:S(2)}) copy-start(s32[1,4,32]{2,1,0:T(4,128)} %lists.1) | copy-start | bytes 1540
  0.0 12.0 %copy-start = (s32[16,125]{1,0:T(8,128)S(1)}, s32[16,125]{1,0:T(8,128)}, u32[]{:S(2)}) copy-start(s32[16,125]{1,0:T(8,128)} %connect.1) | copy-start | bytes 24004
  1.9 14.2 %collective-permute-start.1 = (f32[512,128]{1,0:T(8,128)S(1)}, f32[512,128]{1,0:T(8,128)S(1)}, u32[]{:S(2)}, u32[]{:S(2)}) collective-permute-start(f32[512,128]{1,0:T(8,128)S(1)} %get-tuple-element.46), channel_id=1, source_target_pairs={{0,1},{1,0},{2,3},{3,2},{4,5},{5,4},{6,7},{7,6},{8,9},{9,8},{10,11... | collective-permute-start | bytes 786440 | tf_op jit(solution)/shard_map/ppermute | solution.py:407
  4.9 15.4 %collective-permute-start = (f32[512,128]{1,0:T(8,128)S(1)}, f32[512,128]{1,0:T(8,128)S(1)}, u32[]{:S(2)}, u32[]{:S(2)}) collective-permute-start(f32[512,128]{1,0:T(8,128)S(1)} %get-tuple-element.43), channel_id=1, source_target_pairs={{0,1},{1,0},{2,3},{3,2},{4,5},{5,4},{6,7},{7,6},{8,9},{9,8},{10,11... | collective-permute-start | bytes 786440 | tf_op jit(solution)/shard_map/ppermute | solution.py:407
  5.0 18.3 %collective-permute-start.3 = (f32[512,128]{1,0:T(8,128)S(1)}, f32[512,128]{1,0:T(8,128)S(1)}, u32[]{:S(2)}, u32[]{:S(2)}) collective-permute-start(f32[512,128]{1,0:T(8,128)S(1)} %get-tuple-element.54), channel_id=1, source_target_pairs={{0,1},{1,0},{2,3},{3,2},{4,5},{5,4},{6,7},{7,6},{8,9},{9,8},{10,11... | collective-permute-start | bytes 786440 | tf_op jit(solution)/shard_map/ppermute | solution.py:407
  6.9 21.9 %collective-permute-start.2 = (f32[512,128]{1,0:T(8,128)S(1)}, f32[512,128]{1,0:T(8,128)S(1)}, u32[]{:S(2)}, u32[]{:S(2)}) collective-permute-start(f32[512,128]{1,0:T(8,128)S(1)} %get-tuple-element.53), channel_id=1, source_target_pairs={{0,1},{1,0},{2,3},{3,2},{4,5},{5,4},{6,7},{7,6},{8,9},{9,8},{10,11... | collective-permute-start | bytes 786440 | tf_op jit(solution)/shard_map/ppermute | solution.py:407
  17.2 10.9 %collective-permute-start.4 = (f32[64,640]{1,0:T(8,128)S(1)}, f32[64,640]{1,0:T(8,128)S(1)}, u32[]{:S(2)}, u32[]{:S(2)}) collective-permute-start(f32[64,640]{1,0:T(8,128)S(1)} %get-tuple-element.55), channel_id=1, source_target_pairs={{0,16},{2,18},{4,20},{6,22},{8,24},{10,26},{12,28},{14,30},{16,0},... | collective-permute-start | bytes 491528 | tf_op jit(solution)/shard_map/ppermute | solution.py:397
  21.5 6.6 %collective-permute-start.5 = (f32[32,512]{1,0:T(8,128)S(1)}, f32[32,512]{1,0:T(8,128)S(1)}, u32[]{:S(2)}, u32[]{:S(2)}) collective-permute-start(f32[32,512]{1,0:T(8,128)S(1)} %get-tuple-element.56), channel_id=1, source_target_pairs={{0,30},{2,4},{4,2},{6,8},{8,6},{10,12},{12,10},{14,16},{16,14},{18... | collective-permute-start | bytes 196616 | tf_op jit(solution)/shard_map/ppermute | solution.py:400
  21.9 6.2 %collective-permute-start.6 = (f32[32,512]{1,0:T(8,128)S(1)}, f32[32,512]{1,0:T(8,128)S(1)}, u32[]{:S(2)}, u32[]{:S(2)}) collective-permute-start(f32[32,512]{1,0:T(8,128)S(1)} %get-tuple-element.57), channel_id=1, source_target_pairs={{0,2},{2,0},{4,6},{6,4},{8,10},{10,8},{12,14},{14,12},{16,18},{18,... | collective-permute-start | bytes 196616 | tf_op jit(solution)/shard_map/ppermute | solution.py:403
  29.6 12.0 %collective-permute-start.7 = (f32[64,512]{1,0:T(8,128)S(1)}, f32[64,512]{1,0:T(8,128)S(1)}, u32[]{:S(2)}, u32[]{:S(2)}) collective-permute-start(f32[64,512]{1,0:T(8,128)S(1)} %get-tuple-element.63.back_far), channel_id=1, source_target_pairs={{0,16},{2,18},{4,20},{6,22},{8,24},{10,26},{12,28},{14,30},{16,0},... | collective-permute-start | bytes 393224 | tf_op jit(solution)/shard_map/ppermute | solution.py:397
  32.8 6.5 %collective-permute-start.8 = (f32[32,512]{1,0:T(8,128)S(1)}, f32[32,512]{1,0:T(8,128)S(1)}, u32[]{:S(2)}, u32[]{:S(2)}) collective-permute-start(f32[32,512]{1,0:T(8,128)S(1)} %get-tuple-element.65), channel_id=1, source_target_pairs={{0,30},{2,4},{4,2},{6,8},{8,6},{10,12},{12,10},{14,16},{16,14},{18... | collective-permute-start | bytes 196616 | tf_op jit(solution)/shard_map/ppermute | solution.py:400
  32.8 6.5 %collective-permute-start.9 = (f32[32,512]{1,0:T(8,128)S(1)}, f32[32,512]{1,0:T(8,128)S(1)}, u32[]{:S(2)}, u32[]{:S(2)}) collective-permute-start(f32[32,512]{1,0:T(8,128)S(1)} %get-tuple-element.66), channel_id=1, source_target_pairs={{0,2},{2,0},{4,6},{6,4},{8,10},{10,8},{12,14},{14,12},{16,18},{18,... | collective-permute-start | bytes 196616 | tf_op jit(solution)/shard_map/ppermute | solution.py:403
  39.5 9.1 %collective-permute-start.10 = (f32[64,512]{1,0:T(8,128)S(1)}, f32[64,512]{1,0:T(8,128)S(1)}, u32[]{:S(2)}, u32[]{:S(2)}) collective-permute-start(f32[64,512]{1,0:T(8,128)S(1)} %shard_map.65), channel_id=1, source_target_pairs={{0,16},{2,18},{4,20},{6,22},{8,24},{10,26},{12,28},{14,30},{16,0},... | collective-permute-start | bytes 393224 | tf_op jit(solution)/shard_map/ppermute | solution.py:397
  41.8 6.5 %collective-permute-start.11 = (f32[32,512]{1,0:T(8,128)S(1)}, f32[32,512]{1,0:T(8,128)S(1)}, u32[]{:S(2)}, u32[]{:S(2)}) collective-permute-start(f32[32,512]{1,0:T(8,128)S(1)} %get-tuple-element.72), channel_id=1, source_target_pairs={{0,30},{2,4},{4,2},{6,8},{8,6},{10,12},{12,10},{14,16},{16,14},{18... | collective-permute-start | bytes 196616 | tf_op jit(solution)/shard_map/ppermute | solution.py:400
  41.9 6.4 %collective-permute-start.12 = (f32[32,512]{1,0:T(8,128)S(1)}, f32[32,512]{1,0:T(8,128)S(1)}, u32[]{:S(2)}, u32[]{:S(2)}) collective-permute-start(f32[32,512]{1,0:T(8,128)S(1)} %get-tuple-element.73), channel_id=1, source_target_pairs={{0,2},{2,0},{4,6},{6,4},{8,10},{10,8},{12,14},{14,12},{16,18},{18,... | collective-permute-start | bytes 196616 | tf_op jit(solution)/shard_map/ppermute | solution.py:403
  48.5 6.8 %collective-permute-start.13 = (f32[64,512]{1,0:T(8,128)S(1)}, f32[64,512]{1,0:T(8,128)S(1)}, u32[]{:S(2)}, u32[]{:S(2)}) collective-permute-start(f32[64,512]{1,0:T(8,128)S(1)} %shard_map.69), channel_id=1, source_target_pairs={{0,16},{2,18},{4,20},{6,22},{8,24},{10,26},{12,28},{14,30},{16,0},... | collective-permute-start | bytes 393224 | tf_op jit(solution)/shard_map/ppermute | solution.py:397
  48.8 6.5 %collective-permute-start.14 = (f32[32,512]{1,0:T(8,128)S(1)}, f32[32,512]{1,0:T(8,128)S(1)}, u32[]{:S(2)}, u32[]{:S(2)}) collective-permute-start(f32[32,512]{1,0:T(8,128)S(1)} %get-tuple-element.79), channel_id=1, source_target_pairs={{0,30},{2,4},{4,2},{6,8},{8,6},{10,12},{12,10},{14,16},{16,14},{18... | collective-permute-start | bytes 196616 | tf_op jit(solution)/shard_map/ppermute | solution.py:400
  50.1 5.2 %collective-permute-start.15 = (f32[32,512]{1,0:T(8,128)S(1)}, f32[32,512]{1,0:T(8,128)S(1)}, u32[]{:S(2)}, u32[]{:S(2)}) collective-permute-start(f32[32,512]{1,0:T(8,128)S(1)} %get-tuple-element.80), channel_id=1, source_target_pairs={{0,2},{2,0},{4,6},{6,4},{8,10},{10,8},{12,14},{14,12},{16,18},{18,... | collective-permute-start | bytes 196616 | tf_op jit(solution)/shard_map/ppermute | solution.py:403

commit v13 on v12

--- a/solution.py
+++ b/solution.py
@@ -163,40 +163,49 @@
 
 
 def rotate_own(
-    group, shuffle, subspace_in, ritz_in, start_out, top_out, low_out, subspace, ritz, sem, sems
+    group, shuffle, subspace_in, ritz_in, start_out, top_out, low_out, subspace, ritz, sems
 ):
     block, depth = ritz.shape[1:]
     groups = ritz.shape[0]
     parts = sems.shape[1]
-    span = block // parts
-    own_copy = pltpu.make_async_copy(subspace_in, subspace, sem)
-    own_copy.start()
+    span = depth // parts
     copies = []
     for step in range(groups):
         first = lax.rem(group[0] + groups - step, groups) * depth
-        cols = pl.ds(pl.multiple_of(first, depth), depth)
         for part in range(parts):
-            rows = pl.ds(part * span, span)
+            if step == 0:
+                rows = pl.ds(part * span, span)
+                copies.append(
+                    pltpu.make_async_copy(
+                        subspace_in.at[rows], subspace.at[rows], sems.at[groups, part]
+                    )
+                )
+                copies[-1].start()
+            cols = pl.ds(pl.multiple_of(first + part * span, span), span)
             copies.append(
                 pltpu.make_async_copy(
-                    ritz_in.at[rows, cols], ritz.at[step, rows], sems.at[step, part]
+                    ritz_in.at[:, cols],
+                    ritz.at[step, :, pl.ds(part * span, span)],
+                    sems.at[step, part],
                 )
             )
             copies[-1].start()
-    own_copy.wait()
-    own = split(subspace[...])
-    for step in range(groups):
+    total = None
+    for part in range(parts):
+        here = slice(part * span, (part + 1) * span)
+        copies[2 * part].wait()
+        copies[2 * part + 1].wait()
+        term = mul(split(ritz[0, :, here]), split(subspace[here, :]))
+        total = term if total is None else total + term
+    top, low = split(total)
+    start_out[...] = dot(top, shuffle[...], NT) + dot(low, shuffle[...], NT)
+    for step in range(1, groups):
         for part in range(parts):
-            rows = slice(part * span, (part + 1) * span)
-            copies[step * parts + part].wait()
-            top, low = split(ritz[step, rows, :])
-            if step == 0:
-                high, rest = split(mul((top, low), own))
-                start_out[rows, :] = dot(high, shuffle[...], NT) + dot(rest, shuffle[...], NT)
-            else:
-                cols = slice((step - 1) * depth, step * depth)
-                top_out[rows, cols] = top
-                low_out[rows, cols] = low
+            copies[parts + step * parts + part].wait()
+            top, low = split(ritz[step, :, part * span : (part + 1) * span])
+            cols = slice((step - 1) * depth + part * span, (step - 1) * depth + (part + 1) * span)
+            top_out[:, cols] = top
+            low_out[:, cols] = low
 
 
 def rotate(top, low, columns):
@@ -475,8 +484,7 @@
         scratch_shapes=[
             pltpu.VMEM(subspace.shape, F32),
             pltpu.VMEM((groups, block, depth), F32),
-            pltpu.SemaphoreType.DMA,
-            pltpu.SemaphoreType.DMA((groups, 2)),
+            pltpu.SemaphoreType.DMA((groups + 1, 1)),
         ],
     )
 

time: 56.6 us -> 56.6 us (level)
  starting transfers between devices: 17.1 us -> 19.8 us
  Pallas kernels: 19.6 us -> 18.2 us
  waiting for transfers between devices: 19.5 us -> 18.3 us
    ppermute x4, waiting for transfers between devices: 19.5 us -> 16.3 us  [out(): return lax.ppermute(rows, 'mesh', pairs_out)]
    ppermute x4, starting transfers between devices: 1.66 us -> 3.79 us  [out(): return lax.ppermute(rows, 'mesh', pairs_out)]
    ppermute x4, waiting for transfers between devices: 0.07 us -> 1.96 us  [gather(): lax.ppermute(rows, 'state', [(i, (i + step) % groups) for i in range(grou...]
    pallas_call x16, Pallas kernels: 19.6 us -> 18.2 us  [call(): pl.pallas_call(body, out_shape=[jax.ShapeDtypeStruct(*out) for out in out...]
    ppermute x4, starting transfers between devices: 8.42 us -> 9.33 us  [far(): return lax.ppermute(rows, 'mesh', pairs_far)]
  transfers between devices with their start and end apart: 16 -> 16, of which waited for: 5 -> 6; matrix products, arithmetic and copies ran while one was open for 0% -> 0% of each run, Pallas kernels for 28% -> 26%
where the time goes in v13:
time: 56.6 us; the launch traced here: 56.5 us
  starting transfers between devices  19.8 us (35%)
  waiting for transfers between devices  18.3 us (32%)
  Pallas kernels  18.2 us (32%)
    pallas_call x16, Pallas kernels, call(): pl.pallas_call(body, out_shape=[jax.ShapeDtypeStruct(*out) for out in out...  18.2 us
    ppermute x4, waiting for transfers between devices, out(): return lax.ppermute(rows, 'mesh', pairs_out)  16.3 us
    ppermute x4, starting transfers between devices, far(): return lax.ppermute(rows, 'mesh', pairs_far)  9.33 us
    ppermute x4, starting transfers between devices, gather(): lax.ppermute(rows, 'state', [(i, (i + step) % groups) for i in range(grou...  5.14 us
    ppermute x4, starting transfers between devices, out(): return lax.ppermute(rows, 'mesh', pairs_out)  3.79 us
    ppermute x4, waiting for transfers between devices, gather(): lax.ppermute(rows, 'state', [(i, (i + step) % groups) for i in range(grou...  1.96 us
    ppermute x4, starting transfers between devices, near(): return lax.ppermute(rows, 'mesh', pairs_in)  1.53 us
  transfers between devices with their start and end apart: 16, of which 6 were waited for; matrix products, arithmetic and copies ran while one was open for 0% of the time, Pallas kernels for 26%

profile of v13, /device:TPU:0, one launch (start us, length us, event | category | flops | bytes accessed | tf_op | source)
XLA Modules:
  0.0 56.5 jit_solution(9442086095552739463)
XLA Ops:
  0.0 1.8 %shard_map.55 = (f32[512,128]{1,0:T(8,128)S(1)}, f32[512,128]{1,0:T(8,128)S(1)}, f32[512,128]{1,0:T(8,128)S(1)}, f32[512,128]{1,0:T(8,128)S(1)}, bf16[256,256]{1,0:T(8,128)(2,1)S(1)}) custom-call(s32[1,4,32]{2,1,0:T(4,128)} %lists.1, f32[1024,256]{1,0:T(8,128)} %subspace_in.3), custom_call_target="tpu_custom_call" | custom-call | tf_op jit(solution)/shard_map/pallas_call | solution.py:43
  1.9 3.0 %collective-permute-start.1 = (f32[512,128]{1,0:T(8,128)S(1)}, f32[512,128]{1,0:T(8,128)S(1)}, u32[]{:S(2)}, u32[]{:S(2)}) collective-permute-start(f32[512,128]{1,0:T(8,128)S(1)} %get-tuple-element.46), channel_id=1, source_target_pairs={{0,1},{1,0},{2,3},{3,2},{4,5},{5,4},{6,7},{7,6},{8,9},{9,8},{10,11... | collective-permute-start | bytes 786440 | tf_op jit(solution)/shard_map/ppermute | solution.py:416
  5.0 1.9 %collective-permute-start.3 = (f32[512,128]{1,0:T(8,128)S(1)}, f32[512,128]{1,0:T(8,128)S(1)}, u32[]{:S(2)}, u32[]{:S(2)}) collective-permute-start(f32[512,128]{1,0:T(8,128)S(1)} %get-tuple-element.54), channel_id=1, source_target_pairs={{0,1},{1,0},{2,3},{3,2},{4,5},{5,4},{6,7},{7,6},{8,9},{9,8},{10,11... | collective-permute-start | bytes 786440 | tf_op jit(solution)/shard_map/ppermute | solution.py:416
  7.0 3.6 %shard_map.56 = (f32[512,256]{1,0:T(8,128)S(1)}, bf16[512,1024]{1,0:T(8,128)(2,1)S(1)}, bf16[512,1024]{1,0:T(8,128)(2,1)S(1)}) custom-call(s32[1]{0:T(128)} %bitcast.group, bf16[256,256]{1,0:T(8,128)(2,1)S(1)} %get-tuple-element.44.shuffle, f32[1024,256]{1,0:T(8,128)} %subspace_in.3, f32[512,2048]{1,0:T(8,128)} %ritz_in.1), custom_call_target="tpu_custom_call" | custom-call | tf_op jit(solution)/shard_map/pallas_call | solution.py:43
  10.7 4.1 %shard_map.57 = (bf16[384,384]{1,0:T(8,128)(2,1)S(1)}, bf16[384,384]{1,0:T(8,128)(2,1)S(1)}, bf16[128,128]{1,0:T(8,128)(2,1)S(1)}, bf16[128,128]{1,0:T(8,128)(2,...) custom-call(s32[1]{0:T(128)} %bitcast.1.odd, s32[1,4,32]{2,1,0:T(4,128)S(1)} %copy-done.1, ...), custom_call_target="tpu_custom_call" | custom-call | tf_op jit(solution)/shard_map/pallas_call | solution.py:43
  14.8 1.1 %shard_map.58 = (f32[64,512]{1,0:T(8,128)S(1)}, f32[64,640]{1,0:T(8,128)S(1)}) custom-call(f32[512,128]{1,0:T(8,128)S(1)} %collective-permute-done.1.columns, f32[512,256]{1,0:T(8,128)S(1)} %get-tuple-element.45.start_own, bf16[512,1024]{1,0:T(8,128)(2,1)S(1)} %get-tuple-element.47.top, bf16[512,1024]{1,0:T(8,128)(2,1)S(1)} %get-tuple-element.48.low, ...), custom_call_target="tpu_custom_call" | custom-call | tf_op jit(solution)/shard_map/pallas_call | solution.py:43
  15.9 3.1 %collective-permute-start.4 = (f32[64,640]{1,0:T(8,128)S(1)}, f32[64,640]{1,0:T(8,128)S(1)}, u32[]{:S(2)}, u32[]{:S(2)}) collective-permute-start(f32[64,640]{1,0:T(8,128)S(1)} %get-tuple-element.55), channel_id=1, source_target_pairs={{0,16},{2,18},{4,20},{6,22},{8,24},{10,26},{12,28},{14,30},{16,0},... | collective-permute-start | bytes 491528 | tf_op jit(solution)/shard_map/ppermute | solution.py:406
  18.9 1.2 %shard_map.59 = (f32[128,512]{1,0:T(8,128)S(1)}, f32[32,512]{1,0:T(8,128)S(1)}, f32[32,512]{1,0:T(8,128)S(1)}) custom-call(f32[512,128]{1,0:T(8,128)S(1)} %collective-permute-done.columns, f32[512,256]{1,0:T(8,128)S(1)} %get-tuple-element.45.start_own, f32[64,512]{1,0:T(8,128)S(1)} %get-tuple-element.51.start_far, ...), custom_call_target="tpu_custom_call" | custom-call | tf_op jit(solution)/shard_map/pallas_call | solution.py:43
  20.2 1.3 %collective-permute-start.5 = (f32[32,512]{1,0:T(8,128)S(1)}, f32[32,512]{1,0:T(8,128)S(1)}, u32[]{:S(2)}, u32[]{:S(2)}) collective-permute-start(f32[32,512]{1,0:T(8,128)S(1)} %get-tuple-element.56), channel_id=1, source_target_pairs={{0,30},{2,4},{4,2},{6,8},{8,6},{10,12},{12,10},{14,16},{16,14},{18... | collective-permute-start | bytes 196616 | tf_op jit(solution)/shard_map/ppermute | solution.py:409
  21.9 1.4 %collective-permute-done.3.columns = f32[512,128]{1,0:T(8,128)S(1)} collective-permute-done((f32[512,128]{1,0:T(8,128)S(1)}, f32[512,128]{1,0:T(8,128)S(1)}, u32[]{:S(2)}, u32[]{:S(2)}) %collective-permute-start.3) | collective-permute-done | bytes 262176 | tf_op jit(solution)/shard_map/ppermute | solution.py:416
  23.7 3.0 %collective-permute-done.5.out_in = f32[32,512]{1,0:T(8,128)S(1)} collective-permute-done((f32[32,512]{1,0:T(8,128)S(1)}, f32[32,512]{1,0:T(8,128)S(1)}, u32[]{:S(2)}, u32[]{:S(2)}) %collective-permute-start.5) | collective-permute-done | bytes 65568 | tf_op jit(solution)/shard_map/ppermute | solution.py:409
  26.7 0.8 %shard_map.61 = (f32[384,512]{1,0:T(8,128)S(1)}, f32[64,64]{1,0:T(8,128)S(1)}, f32[64,64]{1,0:T(8,128)S(1)}) custom-call(f32[128,512]{1,0:T(8,128)S(1)} %get-tuple-element.52.start_edge, f32[64,640]{1,0:T(8,128)S(1)} %collective-permute-done.4.far_in, f32[32,512]{1,0:T(8,128)S(1)} %collective-permute-done.5.out_in, ...), custom_call_target="tpu_custom_call" | custom-call | tf_op jit(solution)/shard_map/pallas_call | solution.py:43
  28.1 0.8 %shard_map.62 = (f32[128,512]{1,0:T(8,128)S(1)}, f32[64,512]{1,0:T(8,128)S(1)}, f32[32,512]{1,0:T(8,128)S(1)}, f32[32,512]{1,0:T(8,128)S(1)}) custom-call(f32[512,128]{1,0:T(8,128)S(1)} %collective-permute-done.2.columns, f32[512,128]{1,0:T(8,128)S(1)} %shard_map.60.rest_low, bf16[512,1024]{1,0:T(8,128)(2,1)S(1)} %get-tuple-element.47.top, ...), custom_call_target="tpu_custom_call" | custom-call | tf_op jit(solution)/shard_map/pallas_call | solution.py:43
  28.8 2.9 %collective-permute-start.7 = (f32[64,512]{1,0:T(8,128)S(1)}, f32[64,512]{1,0:T(8,128)S(1)}, u32[]{:S(2)}, u32[]{:S(2)}) collective-permute-start(f32[64,512]{1,0:T(8,128)S(1)} %get-tuple-element.63.back_far), channel_id=1, source_target_pairs={{0,16},{2,18},{4,20},{6,22},{8,24},{10,26},{12,28},{14,30},{16,0},... | collective-permute-start | bytes 393224 | tf_op jit(solution)/shard_map/ppermute | solution.py:406
  32.3 1.0 %collective-permute-start.9 = (f32[32,512]{1,0:T(8,128)S(1)}, f32[32,512]{1,0:T(8,128)S(1)}, u32[]{:S(2)}, u32[]{:S(2)}) collective-permute-start(f32[32,512]{1,0:T(8,128)S(1)} %get-tuple-element.66), channel_id=1, source_target_pairs={{0,2},{2,0},{4,6},{6,4},{8,10},{10,8},{12,14},{14,12},{16,18},{18,... | collective-permute-start | bytes 196616 | tf_op jit(solution)/shard_map/ppermute | solution.py:412
  33.3 0.6 %shard_map.63 = (f32[256,512]{1,0:T(8,128)S(1)}, f32[256,512]{1,0:T(8,128)S(1)}, f32[128,512]{1,0:T(8,128)S(1)}, f32[64,512]{1,0:T(8,128)S(1)}) custom-call(f32[128,512]{1,0:T(8,128)S(1)} %get-tuple-element.52.start_edge, f32[128,512]{1,0:T(8,128)S(1)} %get-tuple-element.61.start_rest, f32[384,512]{1,0:T(8,128)S(1)} %get-tuple-element.60.part, ...), custom_call_target="tpu_custom_call" | custom-call | tf_op jit(solution)/shard_map/pallas_call | solution.py:43
  33.9 4.1 %collective-permute-done.8.out_in = f32[32,512]{1,0:T(8,128)S(1)} collective-permute-done((f32[32,512]{1,0:T(8,128)S(1)}, f32[32,512]{1,0:T(8,128)S(1)}, u32[]{:S(2)}, u32[]{:S(2)}) %collective-permute-start.8) | collective-permute-done | bytes 65568 | tf_op jit(solution)/shard_map/ppermute | solution.py:409
  38.3 3.3 %collective-permute-start.10 = (f32[64,512]{1,0:T(8,128)S(1)}, f32[64,512]{1,0:T(8,128)S(1)}, u32[]{:S(2)}, u32[]{:S(2)}) collective-permute-start(f32[64,512]{1,0:T(8,128)S(1)} %shard_map.65), channel_id=1, source_target_pairs={{0,16},{2,18},{4,20},{6,22},{8,24},{10,26},{12,28},{14,30},{16,0},... | collective-permute-start | bytes 393224 | tf_op jit(solution)/shard_map/ppermute | solution.py:406
  42.0 0.9 %shard_map.64 = (f32[256,512]{1,0:T(8,128)S(1)}, f32[384,512]{1,0:T(8,128)S(1)}, f32[64,512]{1,0:T(8,128)S(1)}) custom-call(f32[256,512]{1,0:T(8,128)S(1)} %get-tuple-element.64.base, bf16[128,128]{1,0:T(8,128)(2,1)S(1)} %get-tuple-element.49.pick, f32[64,512]{1,0:T(8,128)S(1)} %collective-permute-done.7.far_in, ...), custom_call_target="tpu_custom_call" | custom-call | tf_op jit(solution)/shard_map/pallas_call | solution.py:43
  42.9 5.4 %collective-permute-done.11.out_in = f32[32,512]{1,0:T(8,128)S(1)} collective-permute-done((f32[32,512]{1,0:T(8,128)S(1)}, f32[32,512]{1,0:T(8,128)S(1)}, u32[]{:S(2)}, u32[]{:S(2)}) %collective-permute-start.11) | collective-permute-done | bytes 65568 | tf_op jit(solution)/shard_map/ppermute | solution.py:409
  48.8 1.9 %collective-permute-start.14 = (f32[32,512]{1,0:T(8,128)S(1)}, f32[32,512]{1,0:T(8,128)S(1)}, u32[]{:S(2)}, u32[]{:S(2)}) collective-permute-start(f32[32,512]{1,0:T(8,128)S(1)} %get-tuple-element.79), channel_id=1, source_target_pairs={{0,30},{2,4},{4,2},{6,8},{8,6},{10,12},{12,10},{14,16},{16,14},{18... | collective-permute-start | bytes 196616 | tf_op jit(solution)/shard_map/ppermute | solution.py:409
  50.7 0.8 %shard_map.68.result = f32[512,256]{1,0:T(8,128)S(1)} custom-call(f32[384,512]{1,0:T(8,128)S(1)} %get-tuple-element.68.part, f32[128,512]{1,0:T(8,128)S(1)} %get-tuple-element.74.ghosts, bf16[384,384]{1,0:T(8,128)(2,1)S(1)} %get-tuple-element.58.ham_top, bf16[384,384]{1,0:T(8,128)(2,1)S(1)} %get-tuple-element.59.ham_low, ...), custom_call_target="tpu_custom_call" | custom-call | tf_op jit(solution)/shard_map/pallas_call | solution.py:43
  51.6 3.7 %collective-permute-done.14.out_in = f32[32,512]{1,0:T(8,128)S(1)} collective-permute-done((f32[32,512]{1,0:T(8,128)S(1)}, f32[32,512]{1,0:T(8,128)S(1)}, u32[]{:S(2)}, u32[]{:S(2)}) %collective-permute-start.14) | collective-permute-done | bytes 65568 | tf_op jit(solution)/shard_map/ppermute | solution.py:409
  55.3 1.1 %shard_map.70 = f32[512,256]{1,0:T(8,128)} custom-call(f32[512,256]{1,0:T(8,128)S(1)} %shard_map.68.result, bf16[128,256]{1,0:T(8,128)(2,1)S(1)} %get-tuple-element.78.hits, f32[64,512]{1,0:T(8,128)S(1)} %collective-permute-done.13.far_in, f32[32,512]{1,0:T(8,128)S(1)} %collective-permute-done.14.out_in, f32[32,512]{1,0:T(8,128)S(1)} %collective-permute-done.15.near_in), custom_call_target="tpu_custom_call" | custom-call | tf_op jit(solution)/shard_map/pallas_call | solution.py:43
  (28 shorter events, 3.3 us)
Async XLA Ops:
  0.0 10.6 %copy-start.1 = (s32[1,4,32]{2,1,0:T(4,128)S(1)}, s32[1,4,32]{2,1,0:T(4,128)}, u32[]{:S(2)}) copy-start(s32[1,4,32]{2,1,0:T(4,128)} %lists.1) | copy-start | bytes 1540
  0.0 10.6 %copy-start = (s32[16,125]{1,0:T(8,128)S(1)}, s32[16,125]{1,0:T(8,128)}, u32[]{:S(2)}) copy-start(s32[16,125]{1,0:T(8,128)} %connect.1) | copy-start | bytes 24004
  1.9 12.9 %collective-permute-start.1 = (f32[512,128]{1,0:T(8,128)S(1)}, f32[512,128]{1,0:T(8,128)S(1)}, u32[]{:S(2)}, u32[]{:S(2)}) collective-permute-start(f32[512,128]{1,0:T(8,128)S(1)} %get-tuple-element.46), channel_id=1, source_target_pairs={{0,1},{1,0},{2,3},{3,2},{4,5},{5,4},{6,7},{7,6},{8,9},{9,8},{10,11... | collective-permute-start | bytes 786440 | tf_op jit(solution)/shard_map/ppermute | solution.py:416
  4.9 14.0 %collective-permute-start = (f32[512,128]{1,0:T(8,128)S(1)}, f32[512,128]{1,0:T(8,128)S(1)}, u32[]{:S(2)}, u32[]{:S(2)}) collective-permute-start(f32[512,128]{1,0:T(8,128)S(1)} %get-tuple-element.43), channel_id=1, source_target_pairs={{0,1},{1,0},{2,3},{3,2},{4,5},{5,4},{6,7},{7,6},{8,9},{9,8},{10,11... | collective-permute-start | bytes 786440 | tf_op jit(solution)/shard_map/ppermute | solution.py:416
  5.0 18.3 %collective-permute-start.3 = (f32[512,128]{1,0:T(8,128)S(1)}, f32[512,128]{1,0:T(8,128)S(1)}, u32[]{:S(2)}, u32[]{:S(2)}) collective-permute-start(f32[512,128]{1,0:T(8,128)S(1)} %get-tuple-element.54), channel_id=1, source_target_pairs={{0,1},{1,0},{2,3},{3,2},{4,5},{5,4},{6,7},{7,6},{8,9},{9,8},{10,11... | collective-permute-start | bytes 786440 | tf_op jit(solution)/shard_map/ppermute | solution.py:416
  6.9 21.1 %collective-permute-start.2 = (f32[512,128]{1,0:T(8,128)S(1)}, f32[512,128]{1,0:T(8,128)S(1)}, u32[]{:S(2)}, u32[]{:S(2)}) collective-permute-start(f32[512,128]{1,0:T(8,128)S(1)} %get-tuple-element.53), channel_id=1, source_target_pairs={{0,1},{1,0},{2,3},{3,2},{4,5},{5,4},{6,7},{7,6},{8,9},{9,8},{10,11... | collective-permute-start | bytes 786440 | tf_op jit(solution)/shard_map/ppermute | solution.py:416
  15.9 10.9 %collective-permute-start.4 = (f32[64,640]{1,0:T(8,128)S(1)}, f32[64,640]{1,0:T(8,128)S(1)}, u32[]{:S(2)}, u32[]{:S(2)}) collective-permute-start(f32[64,640]{1,0:T(8,128)S(1)} %get-tuple-element.55), channel_id=1, source_target_pairs={{0,16},{2,18},{4,20},{6,22},{8,24},{10,26},{12,28},{14,30},{16,0},... | collective-permute-start | bytes 491528 | tf_op jit(solution)/shard_map/ppermute | solution.py:406
  20.2 6.6 %collective-permute-start.5 = (f32[32,512]{1,0:T(8,128)S(1)}, f32[32,512]{1,0:T(8,128)S(1)}, u32[]{:S(2)}, u32[]{:S(2)}) collective-permute-start(f32[32,512]{1,0:T(8,128)S(1)} %get-tuple-element.56), channel_id=1, source_target_pairs={{0,30},{2,4},{4,2},{6,8},{8,6},{10,12},{12,10},{14,16},{16,14},{18... | collective-permute-start | bytes 196616 | tf_op jit(solution)/shard_map/ppermute | solution.py:409
  21.4 5.3 %collective-permute-start.6 = (f32[32,512]{1,0:T(8,128)S(1)}, f32[32,512]{1,0:T(8,128)S(1)}, u32[]{:S(2)}, u32[]{:S(2)}) collective-permute-start(f32[32,512]{1,0:T(8,128)S(1)} %get-tuple-element.57), channel_id=1, source_target_pairs={{0,2},{2,0},{4,6},{6,4},{8,10},{10,8},{12,14},{14,12},{16,18},{18,... | collective-permute-start | bytes 196616 | tf_op jit(solution)/shard_map/ppermute | solution.py:412
  28.8 12.8 %collective-permute-start.7 = (f32[64,512]{1,0:T(8,128)S(1)}, f32[64,512]{1,0:T(8,128)S(1)}, u32[]{:S(2)}, u32[]{:S(2)}) collective-permute-start(f32[64,512]{1,0:T(8,128)S(1)} %get-tuple-element.63.back_far), channel_id=1, source_target_pairs={{0,16},{2,18},{4,20},{6,22},{8,24},{10,26},{12,28},{14,30},{16,0},... | collective-permute-start | bytes 393224 | tf_op jit(solution)/shard_map/ppermute | solution.py:406
  31.7 6.4 %collective-permute-start.8 = (f32[32,512]{1,0:T(8,128)S(1)}, f32[32,512]{1,0:T(8,128)S(1)}, u32[]{:S(2)}, u32[]{:S(2)}) collective-permute-start(f32[32,512]{1,0:T(8,128)S(1)} %get-tuple-element.65), channel_id=1, source_target_pairs={{0,30},{2,4},{4,2},{6,8},{8,6},{10,12},{12,10},{14,16},{16,14},{18... | collective-permute-start | bytes 196616 | tf_op jit(solution)/shard_map/ppermute | solution.py:409
  32.3 5.8 %collective-permute-start.9 = (f32[32,512]{1,0:T(8,128)S(1)}, f32[32,512]{1,0:T(8,128)S(1)}, u32[]{:S(2)}, u32[]{:S(2)}) collective-permute-start(f32[32,512]{1,0:T(8,128)S(1)} %get-tuple-element.66), channel_id=1, source_target_pairs={{0,2},{2,0},{4,6},{6,4},{8,10},{10,8},{12,14},{14,12},{16,18},{18,... | collective-permute-start | bytes 196616 | tf_op jit(solution)/shard_map/ppermute | solution.py:412
  38.3 10.3 %collective-permute-start.10 = (f32[64,512]{1,0:T(8,128)S(1)}, f32[64,512]{1,0:T(8,128)S(1)}, u32[]{:S(2)}, u32[]{:S(2)}) collective-permute-start(f32[64,512]{1,0:T(8,128)S(1)} %shard_map.65), channel_id=1, source_target_pairs={{0,16},{2,18},{4,20},{6,22},{8,24},{10,26},{12,28},{14,30},{16,0},... | collective-permute-start | bytes 393224 | tf_op jit(solution)/shard_map/ppermute | solution.py:406
  41.8 6.5 %collective-permute-start.11 = (f32[32,512]{1,0:T(8,128)S(1)}, f32[32,512]{1,0:T(8,128)S(1)}, u32[]{:S(2)}, u32[]{:S(2)}) collective-permute-start(f32[32,512]{1,0:T(8,128)S(1)} %get-tuple-element.72), channel_id=1, source_target_pairs={{0,30},{2,4},{4,2},{6,8},{8,6},{10,12},{12,10},{14,16},{16,14},{18... | collective-permute-start | bytes 196616 | tf_op jit(solution)/shard_map/ppermute | solution.py:409
  41.9 6.4 %collective-permute-start.12 = (f32[32,512]{1,0:T(8,128)S(1)}, f32[32,512]{1,0:T(8,128)S(1)}, u32[]{:S(2)}, u32[]{:S(2)}) collective-permute-start(f32[32,512]{1,0:T(8,128)S(1)} %get-tuple-element.73), channel_id=1, source_target_pairs={{0,2},{2,0},{4,6},{6,4},{8,10},{10,8},{12,14},{14,12},{16,18},{18,... | collective-permute-start | bytes 196616 | tf_op jit(solution)/shard_map/ppermute | solution.py:412
  48.5 6.8 %collective-permute-start.13 = (f32[64,512]{1,0:T(8,128)S(1)}, f32[64,512]{1,0:T(8,128)S(1)}, u32[]{:S(2)}, u32[]{:S(2)}) collective-permute-start(f32[64,512]{1,0:T(8,128)S(1)} %shard_map.69), channel_id=1, source_target_pairs={{0,16},{2,18},{4,20},{6,22},{8,24},{10,26},{12,28},{14,30},{16,0},... | collective-permute-start | bytes 393224 | tf_op jit(solution)/shard_map/ppermute | solution.py:406
  48.8 6.5 %collective-permute-start.14 = (f32[32,512]{1,0:T(8,128)S(1)}, f32[32,512]{1,0:T(8,128)S(1)}, u32[]{:S(2)}, u32[]{:S(2)}) collective-permute-start(f32[32,512]{1,0:T(8,128)S(1)} %get-tuple-element.79), channel_id=1, source_target_pairs={{0,30},{2,4},{4,2},{6,8},{8,6},{10,12},{12,10},{14,16},{16,14},{18... | collective-permute-start | bytes 196616 | tf_op jit(solution)/shard_map/ppermute | solution.py:409
  50.7 4.6 %collective-permute-start.15 = (f32[32,512]{1,0:T(8,128)S(1)}, f32[32,512]{1,0:T(8,128)S(1)}, u32[]{:S(2)}, u32[]{:S(2)}) collective-permute-start(f32[32,512]{1,0:T(8,128)S(1)} %get-tuple-element.80), channel_id=1, source_target_pairs={{0,2},{2,0},{4,6},{6,4},{8,10},{10,8},{12,14},{14,12},{16,18},{18,... | collective-permute-start | bytes 196616 | tf_op jit(solution)/shard_map/ppermute | solution.py:412

commit v14 on v13

--- a/solution.py
+++ b/solution.py
@@ -112,7 +112,7 @@
     odd, lists, connect, blocks_in, shuffle, top_out, low_out, pick_out, both_out, hits_out, pair_out,
     blocks, sem, spread, rows_both,
 ):
-    copy = pltpu.make_async_copy(blocks_in, blocks, sem)
+    copy = pltpu.make_async_copy(blocks_in, blocks.at[pl.ds(0, blocks_in.shape[0])], sem)
     copy.start()
     elems, size = connect.shape
     slots, halo = lists.shape[1:]
@@ -464,7 +464,7 @@
         limit=12,
         in_specs=[smem, vmem, vmem, hbm, vmem],
         scratch_shapes=[
-            pltpu.VMEM(blocks.shape, F32),
+            pltpu.VMEM((pitch * elems, size), F32),
             pltpu.SemaphoreType.DMA,
             pltpu.VMEM((full, elems * pitch), BF16),
             pltpu.VMEM((elems * pitch, 2 * full), BF16),

time: 56.6 us -> 56.6 us (level)
  no operation moved by 1% of the time
where the time goes in v14:
time: 56.6 us; the launch traced here: 56.5 us
  starting transfers between devices  19.8 us (35%)
  waiting for transfers between devices  18.3 us (32%)
  Pallas kernels  18.2 us (32%)
    pallas_call x16, Pallas kernels, call(): pl.pallas_call(body, out_shape=[jax.ShapeDtypeStruct(*out) for out in out...  18.2 us
    ppermute x4, waiting for transfers between devices, out(): return lax.ppermute(rows, 'mesh', pairs_out)  16.3 us
    ppermute x4, starting transfers between devices, far(): return lax.ppermute(rows, 'mesh', pairs_far)  9.33 us
    ppermute x4, starting transfers between devices, gather(): lax.ppermute(rows, 'state', [(i, (i + step) % groups) for i in range(grou...  5.14 us
    ppermute x4, starting transfers between devices, out(): return lax.ppermute(rows, 'mesh', pairs_out)  3.79 us
    ppermute x4, waiting for transfers between devices, gather(): lax.ppermute(rows, 'state', [(i, (i + step) % groups) for i in range(grou...  1.96 us
    ppermute x4, starting transfers between devices, near(): return lax.ppermute(rows, 'mesh', pairs_in)  1.53 us
  transfers between devices with their start and end apart: 16, of which 6 were waited for; matrix products, arithmetic and copies ran while one was open for 0% of the time, Pallas kernels for 26%

profile of v14, /device:TPU:0, one launch (start us, length us, event | category | flops | bytes accessed | tf_op | source)
XLA Modules:
  0.0 56.5 jit_solution(15537951446613002204)
XLA Ops:
  0.0 1.8 %shard_map.55 = (f32[512,128]{1,0:T(8,128)S(1)}, f32[512,128]{1,0:T(8,128)S(1)}, f32[512,128]{1,0:T(8,128)S(1)}, f32[512,128]{1,0:T(8,128)S(1)}, bf16[256,256]{1,0:T(8,128)(2,1)S(1)}) custom-call(s32[1,4,32]{2,1,0:T(4,128)} %lists.1, f32[1024,256]{1,0:T(8,128)} %subspace_in.3), custom_call_target="tpu_custom_call" | custom-call | tf_op jit(solution)/shard_map/pallas_call | solution.py:43
  1.9 3.0 %collective-permute-start.1 = (f32[512,128]{1,0:T(8,128)S(1)}, f32[512,128]{1,0:T(8,128)S(1)}, u32[]{:S(2)}, u32[]{:S(2)}) collective-permute-start(f32[512,128]{1,0:T(8,128)S(1)} %get-tuple-element.46), channel_id=1, source_target_pairs={{0,1},{1,0},{2,3},{3,2},{4,5},{5,4},{6,7},{7,6},{8,9},{9,8},{10,11... | collective-permute-start | bytes 786440 | tf_op jit(solution)/shard_map/ppermute | solution.py:416
  5.0 1.9 %collective-permute-start.3 = (f32[512,128]{1,0:T(8,128)S(1)}, f32[512,128]{1,0:T(8,128)S(1)}, u32[]{:S(2)}, u32[]{:S(2)}) collective-permute-start(f32[512,128]{1,0:T(8,128)S(1)} %get-tuple-element.54), channel_id=1, source_target_pairs={{0,1},{1,0},{2,3},{3,2},{4,5},{5,4},{6,7},{7,6},{8,9},{9,8},{10,11... | collective-permute-start | bytes 786440 | tf_op jit(solution)/shard_map/ppermute | solution.py:416
  7.0 3.6 %shard_map.56 = (f32[512,256]{1,0:T(8,128)S(1)}, bf16[512,1024]{1,0:T(8,128)(2,1)S(1)}, bf16[512,1024]{1,0:T(8,128)(2,1)S(1)}) custom-call(s32[1]{0:T(128)} %bitcast.group, bf16[256,256]{1,0:T(8,128)(2,1)S(1)} %get-tuple-element.44.shuffle, f32[1024,256]{1,0:T(8,128)} %subspace_in.3, f32[512,2048]{1,0:T(8,128)} %ritz_in.1), custom_call_target="tpu_custom_call" | custom-call | tf_op jit(solution)/shard_map/pallas_call | solution.py:43
  10.7 4.1 %shard_map.57 = (bf16[384,384]{1,0:T(8,128)(2,1)S(1)}, bf16[384,384]{1,0:T(8,128)(2,1)S(1)}, bf16[128,128]{1,0:T(8,128)(2,1)S(1)}, bf16[128,128]{1,0:T(8,128)(2,...) custom-call(s32[1]{0:T(128)} %bitcast.1.odd, s32[1,4,32]{2,1,0:T(4,128)S(1)} %copy-done.1, ...), custom_call_target="tpu_custom_call" | custom-call | tf_op jit(solution)/shard_map/pallas_call | solution.py:43
  14.8 1.1 %shard_map.58 = (f32[64,512]{1,0:T(8,128)S(1)}, f32[64,640]{1,0:T(8,128)S(1)}) custom-call(f32[512,128]{1,0:T(8,128)S(1)} %collective-permute-done.1.columns, f32[512,256]{1,0:T(8,128)S(1)} %get-tuple-element.45.start_own, bf16[512,1024]{1,0:T(8,128)(2,1)S(1)} %get-tuple-element.47.top, bf16[512,1024]{1,0:T(8,128)(2,1)S(1)} %get-tuple-element.48.low, ...), custom_call_target="tpu_custom_call" | custom-call | tf_op jit(solution)/shard_map/pallas_call | solution.py:43
  15.8 3.1 %collective-permute-start.4 = (f32[64,640]{1,0:T(8,128)S(1)}, f32[64,640]{1,0:T(8,128)S(1)}, u32[]{:S(2)}, u32[]{:S(2)}) collective-permute-start(f32[64,640]{1,0:T(8,128)S(1)} %get-tuple-element.55), channel_id=1, source_target_pairs={{0,16},{2,18},{4,20},{6,22},{8,24},{10,26},{12,28},{14,30},{16,0},... | collective-permute-start | bytes 491528 | tf_op jit(solution)/shard_map/ppermute | solution.py:406
  18.9 1.2 %shard_map.59 = (f32[128,512]{1,0:T(8,128)S(1)}, f32[32,512]{1,0:T(8,128)S(1)}, f32[32,512]{1,0:T(8,128)S(1)}) custom-call(f32[512,128]{1,0:T(8,128)S(1)} %collective-permute-done.columns, f32[512,256]{1,0:T(8,128)S(1)} %get-tuple-element.45.start_own, f32[64,512]{1,0:T(8,128)S(1)} %get-tuple-element.51.start_far, ...), custom_call_target="tpu_custom_call" | custom-call | tf_op jit(solution)/shard_map/pallas_call | solution.py:43
  20.2 1.3 %collective-permute-start.5 = (f32[32,512]{1,0:T(8,128)S(1)}, f32[32,512]{1,0:T(8,128)S(1)}, u32[]{:S(2)}, u32[]{:S(2)}) collective-permute-start(f32[32,512]{1,0:T(8,128)S(1)} %get-tuple-element.56), channel_id=1, source_target_pairs={{0,30},{2,4},{4,2},{6,8},{8,6},{10,12},{12,10},{14,16},{16,14},{18... | collective-permute-start | bytes 196616 | tf_op jit(solution)/shard_map/ppermute | solution.py:409
  21.9 1.4 %collective-permute-done.3.columns = f32[512,128]{1,0:T(8,128)S(1)} collective-permute-done((f32[512,128]{1,0:T(8,128)S(1)}, f32[512,128]{1,0:T(8,128)S(1)}, u32[]{:S(2)}, u32[]{:S(2)}) %collective-permute-start.3) | collective-permute-done | bytes 262176 | tf_op jit(solution)/shard_map/ppermute | solution.py:416
  23.7 3.0 %collective-permute-done.5.out_in = f32[32,512]{1,0:T(8,128)S(1)} collective-permute-done((f32[32,512]{1,0:T(8,128)S(1)}, f32[32,512]{1,0:T(8,128)S(1)}, u32[]{:S(2)}, u32[]{:S(2)}) %collective-permute-start.5) | collective-permute-done | bytes 65568 | tf_op jit(solution)/shard_map/ppermute | solution.py:409
  26.7 0.8 %shard_map.61 = (f32[384,512]{1,0:T(8,128)S(1)}, f32[64,64]{1,0:T(8,128)S(1)}, f32[64,64]{1,0:T(8,128)S(1)}) custom-call(f32[128,512]{1,0:T(8,128)S(1)} %get-tuple-element.52.start_edge, f32[64,640]{1,0:T(8,128)S(1)} %collective-permute-done.4.far_in, f32[32,512]{1,0:T(8,128)S(1)} %collective-permute-done.5.out_in, ...), custom_call_target="tpu_custom_call" | custom-call | tf_op jit(solution)/shard_map/pallas_call | solution.py:43
  28.1 0.8 %shard_map.62 = (f32[128,512]{1,0:T(8,128)S(1)}, f32[64,512]{1,0:T(8,128)S(1)}, f32[32,512]{1,0:T(8,128)S(1)}, f32[32,512]{1,0:T(8,128)S(1)}) custom-call(f32[512,128]{1,0:T(8,128)S(1)} %collective-permute-done.2.columns, f32[512,128]{1,0:T(8,128)S(1)} %shard_map.60.rest_low, bf16[512,1024]{1,0:T(8,128)(2,1)S(1)} %get-tuple-element.47.top, ...), custom_call_target="tpu_custom_call" | custom-call | tf_op jit(solution)/shard_map/pallas_call | solution.py:43
  28.8 2.9 %collective-permute-start.7 = (f32[64,512]{1,0:T(8,128)S(1)}, f32[64,512]{1,0:T(8,128)S(1)}, u32[]{:S(2)}, u32[]{:S(2)}) collective-permute-start(f32[64,512]{1,0:T(8,128)S(1)} %get-tuple-element.63.back_far), channel_id=1, source_target_pairs={{0,16},{2,18},{4,20},{6,22},{8,24},{10,26},{12,28},{14,30},{16,0},... | collective-permute-start | bytes 393224 | tf_op jit(solution)/shard_map/ppermute | solution.py:406
  32.3 1.0 %collective-permute-start.9 = (f32[32,512]{1,0:T(8,128)S(1)}, f32[32,512]{1,0:T(8,128)S(1)}, u32[]{:S(2)}, u32[]{:S(2)}) collective-permute-start(f32[32,512]{1,0:T(8,128)S(1)} %get-tuple-element.66), channel_id=1, source_target_pairs={{0,2},{2,0},{4,6},{6,4},{8,10},{10,8},{12,14},{14,12},{16,18},{18,... | collective-permute-start | bytes 196616 | tf_op jit(solution)/shard_map/ppermute | solution.py:412
  33.3 0.6 %shard_map.63 = (f32[256,512]{1,0:T(8,128)S(1)}, f32[256,512]{1,0:T(8,128)S(1)}, f32[128,512]{1,0:T(8,128)S(1)}, f32[64,512]{1,0:T(8,128)S(1)}) custom-call(f32[128,512]{1,0:T(8,128)S(1)} %get-tuple-element.52.start_edge, f32[128,512]{1,0:T(8,128)S(1)} %get-tuple-element.61.start_rest, f32[384,512]{1,0:T(8,128)S(1)} %get-tuple-element.60.part, ...), custom_call_target="tpu_custom_call" | custom-call | tf_op jit(solution)/shard_map/pallas_call | solution.py:43
  33.9 4.1 %collective-permute-done.8.out_in = f32[32,512]{1,0:T(8,128)S(1)} collective-permute-done((f32[32,512]{1,0:T(8,128)S(1)}, f32[32,512]{1,0:T(8,128)S(1)}, u32[]{:S(2)}, u32[]{:S(2)}) %collective-permute-start.8) | collective-permute-done | bytes 65568 | tf_op jit(solution)/shard_map/ppermute | solution.py:409
  38.3 3.3 %collective-permute-start.10 = (f32[64,512]{1,0:T(8,128)S(1)}, f32[64,512]{1,0:T(8,128)S(1)}, u32[]{:S(2)}, u32[]{:S(2)}) collective-permute-start(f32[64,512]{1,0:T(8,128)S(1)} %shard_map.65), channel_id=1, source_target_pairs={{0,16},{2,18},{4,20},{6,22},{8,24},{10,26},{12,28},{14,30},{16,0},... | collective-permute-start | bytes 393224 | tf_op jit(solution)/shard_map/ppermute | solution.py:406
  42.0 0.9 %shard_map.64 = (f32[256,512]{1,0:T(8,128)S(1)}, f32[384,512]{1,0:T(8,128)S(1)}, f32[64,512]{1,0:T(8,128)S(1)}) custom-call(f32[256,512]{1,0:T(8,128)S(1)} %get-tuple-element.64.base, bf16[128,128]{1,0:T(8,128)(2,1)S(1)} %get-tuple-element.49.pick, f32[64,512]{1,0:T(8,128)S(1)} %collective-permute-done.7.far_in, ...), custom_call_target="tpu_custom_call" | custom-call | tf_op jit(solution)/shard_map/pallas_call | solution.py:43
  42.9 5.4 %collective-permute-done.11.out_in = f32[32,512]{1,0:T(8,128)S(1)} collective-permute-done((f32[32,512]{1,0:T(8,128)S(1)}, f32[32,512]{1,0:T(8,128)S(1)}, u32[]{:S(2)}, u32[]{:S(2)}) %collective-permute-start.11) | collective-permute-done | bytes 65568 | tf_op jit(solution)/shard_map/ppermute | solution.py:409
  48.8 1.9 %collective-permute-start.14 = (f32[32,512]{1,0:T(8,128)S(1)}, f32[32,512]{1,0:T(8,128)S(1)}, u32[]{:S(2)}, u32[]{:S(2)}) collective-permute-start(f32[32,512]{1,0:T(8,128)S(1)} %get-tuple-element.79), channel_id=1, source_target_pairs={{0,30},{2,4},{4,2},{6,8},{8,6},{10,12},{12,10},{14,16},{16,14},{18... | collective-permute-start | bytes 196616 | tf_op jit(solution)/shard_map/ppermute | solution.py:409
  50.7 0.8 %shard_map.68.result = f32[512,256]{1,0:T(8,128)S(1)} custom-call(f32[384,512]{1,0:T(8,128)S(1)} %get-tuple-element.68.part, f32[128,512]{1,0:T(8,128)S(1)} %get-tuple-element.74.ghosts, bf16[384,384]{1,0:T(8,128)(2,1)S(1)} %get-tuple-element.58.ham_top, bf16[384,384]{1,0:T(8,128)(2,1)S(1)} %get-tuple-element.59.ham_low, ...), custom_call_target="tpu_custom_call" | custom-call | tf_op jit(solution)/shard_map/pallas_call | solution.py:43
  51.6 3.7 %collective-permute-done.14.out_in = f32[32,512]{1,0:T(8,128)S(1)} collective-permute-done((f32[32,512]{1,0:T(8,128)S(1)}, f32[32,512]{1,0:T(8,128)S(1)}, u32[]{:S(2)}, u32[]{:S(2)}) %collective-permute-start.14) | collective-permute-done | bytes 65568 | tf_op jit(solution)/shard_map/ppermute | solution.py:409
  55.3 1.1 %shard_map.70 = f32[512,256]{1,0:T(8,128)} custom-call(f32[512,256]{1,0:T(8,128)S(1)} %shard_map.68.result, bf16[128,256]{1,0:T(8,128)(2,1)S(1)} %get-tuple-element.78.hits, f32[64,512]{1,0:T(8,128)S(1)} %collective-permute-done.13.far_in, f32[32,512]{1,0:T(8,128)S(1)} %collective-permute-done.14.out_in, f32[32,512]{1,0:T(8,128)S(1)} %collective-permute-done.15.near_in), custom_call_target="tpu_custom_call" | custom-call | tf_op jit(solution)/shard_map/pallas_call | solution.py:43
  (28 shorter events, 3.3 us)
Async XLA Ops:
  0.0 10.6 %copy-start.1 = (s32[1,4,32]{2,1,0:T(4,128)S(1)}, s32[1,4,32]{2,1,0:T(4,128)}, u32[]{:S(2)}) copy-start(s32[1,4,32]{2,1,0:T(4,128)} %lists.1) | copy-start | bytes 1540
  0.0 10.6 %copy-start = (s32[16,125]{1,0:T(8,128)S(1)}, s32[16,125]{1,0:T(8,128)}, u32[]{:S(2)}) copy-start(s32[16,125]{1,0:T(8,128)} %connect.1) | copy-start | bytes 24004
  1.9 12.9 %collective-permute-start.1 = (f32[512,128]{1,0:T(8,128)S(1)}, f32[512,128]{1,0:T(8,128)S(1)}, u32[]{:S(2)}, u32[]{:S(2)}) collective-permute-start(f32[512,128]{1,0:T(8,128)S(1)} %get-tuple-element.46), channel_id=1, source_target_pairs={{0,1},{1,0},{2,3},{3,2},{4,5},{5,4},{6,7},{7,6},{8,9},{9,8},{10,11... | collective-permute-start | bytes 786440 | tf_op jit(solution)/shard_map/ppermute | solution.py:416
  4.9 14.0 %collective-permute-start = (f32[512,128]{1,0:T(8,128)S(1)}, f32[512,128]{1,0:T(8,128)S(1)}, u32[]{:S(2)}, u32[]{:S(2)}) collective-permute-start(f32[512,128]{1,0:T(8,128)S(1)} %get-tuple-element.43), channel_id=1, source_target_pairs={{0,1},{1,0},{2,3},{3,2},{4,5},{5,4},{6,7},{7,6},{8,9},{9,8},{10,11... | collective-permute-start | bytes 786440 | tf_op jit(solution)/shard_map/ppermute | solution.py:416
  5.0 18.3 %collective-permute-start.3 = (f32[512,128]{1,0:T(8,128)S(1)}, f32[512,128]{1,0:T(8,128)S(1)}, u32[]{:S(2)}, u32[]{:S(2)}) collective-permute-start(f32[512,128]{1,0:T(8,128)S(1)} %get-tuple-element.54), channel_id=1, source_target_pairs={{0,1},{1,0},{2,3},{3,2},{4,5},{5,4},{6,7},{7,6},{8,9},{9,8},{10,11... | collective-permute-start | bytes 786440 | tf_op jit(solution)/shard_map/ppermute | solution.py:416
  6.9 21.1 %collective-permute-start.2 = (f32[512,128]{1,0:T(8,128)S(1)}, f32[512,128]{1,0:T(8,128)S(1)}, u32[]{:S(2)}, u32[]{:S(2)}) collective-permute-start(f32[512,128]{1,0:T(8,128)S(1)} %get-tuple-element.53), channel_id=1, source_target_pairs={{0,1},{1,0},{2,3},{3,2},{4,5},{5,4},{6,7},{7,6},{8,9},{9,8},{10,11... | collective-permute-start | bytes 786440 | tf_op jit(solution)/shard_map/ppermute | solution.py:416
  15.8 10.9 %collective-permute-start.4 = (f32[64,640]{1,0:T(8,128)S(1)}, f32[64,640]{1,0:T(8,128)S(1)}, u32[]{:S(2)}, u32[]{:S(2)}) collective-permute-start(f32[64,640]{1,0:T(8,128)S(1)} %get-tuple-element.55), channel_id=1, source_target_pairs={{0,16},{2,18},{4,20},{6,22},{8,24},{10,26},{12,28},{14,30},{16,0},... | collective-permute-start | bytes 491528 | tf_op jit(solution)/shard_map/ppermute | solution.py:406
  20.2 6.6 %collective-permute-start.5 = (f32[32,512]{1,0:T(8,128)S(1)}, f32[32,512]{1,0:T(8,128)S(1)}, u32[]{:S(2)}, u32[]{:S(2)}) collective-permute-start(f32[32,512]{1,0:T(8,128)S(1)} %get-tuple-element.56), channel_id=1, source_target_pairs={{0,30},{2,4},{4,2},{6,8},{8,6},{10,12},{12,10},{14,16},{16,14},{18... | collective-permute-start | bytes 196616 | tf_op jit(solution)/shard_map/ppermute | solution.py:409
  21.4 5.3 %collective-permute-start.6 = (f32[32,512]{1,0:T(8,128)S(1)}, f32[32,512]{1,0:T(8,128)S(1)}, u32[]{:S(2)}, u32[]{:S(2)}) collective-permute-start(f32[32,512]{1,0:T(8,128)S(1)} %get-tuple-element.57), channel_id=1, source_target_pairs={{0,2},{2,0},{4,6},{6,4},{8,10},{10,8},{12,14},{14,12},{16,18},{18,... | collective-permute-start | bytes 196616 | tf_op jit(solution)/shard_map/ppermute | solution.py:412
  28.8 12.8 %collective-permute-start.7 = (f32[64,512]{1,0:T(8,128)S(1)}, f32[64,512]{1,0:T(8,128)S(1)}, u32[]{:S(2)}, u32[]{:S(2)}) collective-permute-start(f32[64,512]{1,0:T(8,128)S(1)} %get-tuple-element.63.back_far), channel_id=1, source_target_pairs={{0,16},{2,18},{4,20},{6,22},{8,24},{10,26},{12,28},{14,30},{16,0},... | collective-permute-start | bytes 393224 | tf_op jit(solution)/shard_map/ppermute | solution.py:406
  31.7 6.4 %collective-permute-start.8 = (f32[32,512]{1,0:T(8,128)S(1)}, f32[32,512]{1,0:T(8,128)S(1)}, u32[]{:S(2)}, u32[]{:S(2)}) collective-permute-start(f32[32,512]{1,0:T(8,128)S(1)} %get-tuple-element.65), channel_id=1, source_target_pairs={{0,30},{2,4},{4,2},{6,8},{8,6},{10,12},{12,10},{14,16},{16,14},{18... | collective-permute-start | bytes 196616 | tf_op jit(solution)/shard_map/ppermute | solution.py:409
  32.3 5.8 %collective-permute-start.9 = (f32[32,512]{1,0:T(8,128)S(1)}, f32[32,512]{1,0:T(8,128)S(1)}, u32[]{:S(2)}, u32[]{:S(2)}) collective-permute-start(f32[32,512]{1,0:T(8,128)S(1)} %get-tuple-element.66), channel_id=1, source_target_pairs={{0,2},{2,0},{4,6},{6,4},{8,10},{10,8},{12,14},{14,12},{16,18},{18,... | collective-permute-start | bytes 196616 | tf_op jit(solution)/shard_map/ppermute | solution.py:412
  38.3 10.3 %collective-permute-start.10 = (f32[64,512]{1,0:T(8,128)S(1)}, f32[64,512]{1,0:T(8,128)S(1)}, u32[]{:S(2)}, u32[]{:S(2)}) collective-permute-start(f32[64,512]{1,0:T(8,128)S(1)} %shard_map.65), channel_id=1, source_target_pairs={{0,16},{2,18},{4,20},{6,22},{8,24},{10,26},{12,28},{14,30},{16,0},... | collective-permute-start | bytes 393224 | tf_op jit(solution)/shard_map/ppermute | solution.py:406
  41.8 6.5 %collective-permute-start.11 = (f32[32,512]{1,0:T(8,128)S(1)}, f32[32,512]{1,0:T(8,128)S(1)}, u32[]{:S(2)}, u32[]{:S(2)}) collective-permute-start(f32[32,512]{1,0:T(8,128)S(1)} %get-tuple-element.72), channel_id=1, source_target_pairs={{0,30},{2,4},{4,2},{6,8},{8,6},{10,12},{12,10},{14,16},{16,14},{18... | collective-permute-start | bytes 196616 | tf_op jit(solution)/shard_map/ppermute | solution.py:409
  41.9 6.4 %collective-permute-start.12 = (f32[32,512]{1,0:T(8,128)S(1)}, f32[32,512]{1,0:T(8,128)S(1)}, u32[]{:S(2)}, u32[]{:S(2)}) collective-permute-start(f32[32,512]{1,0:T(8,128)S(1)} %get-tuple-element.73), channel_id=1, source_target_pairs={{0,2},{2,0},{4,6},{6,4},{8,10},{10,8},{12,14},{14,12},{16,18},{18,... | collective-permute-start | bytes 196616 | tf_op jit(solution)/shard_map/ppermute | solution.py:412
  48.5 6.8 %collective-permute-start.13 = (f32[64,512]{1,0:T(8,128)S(1)}, f32[64,512]{1,0:T(8,128)S(1)}, u32[]{:S(2)}, u32[]{:S(2)}) collective-permute-start(f32[64,512]{1,0:T(8,128)S(1)} %shard_map.69), channel_id=1, source_target_pairs={{0,16},{2,18},{4,20},{6,22},{8,24},{10,26},{12,28},{14,30},{16,0},... | collective-permute-start | bytes 393224 | tf_op jit(solution)/shard_map/ppermute | solution.py:406
  48.8 6.5 %collective-permute-start.14 = (f32[32,512]{1,0:T(8,128)S(1)}, f32[32,512]{1,0:T(8,128)S(1)}, u32[]{:S(2)}, u32[]{:S(2)}) collective-permute-start(f32[32,512]{1,0:T(8,128)S(1)} %get-tuple-element.79), channel_id=1, source_target_pairs={{0,30},{2,4},{4,2},{6,8},{8,6},{10,12},{12,10},{14,16},{16,14},{18... | collective-permute-start | bytes 196616 | tf_op jit(solution)/shard_map/ppermute | solution.py:409
  50.7 4.6 %collective-permute-start.15 = (f32[32,512]{1,0:T(8,128)S(1)}, f32[32,512]{1,0:T(8,128)S(1)}, u32[]{:S(2)}, u32[]{:S(2)}) collective-permute-start(f32[32,512]{1,0:T(8,128)S(1)} %get-tuple-element.80), channel_id=1, source_target_pairs={{0,2},{2,0},{4,6},{6,4},{8,10},{10,8},{12,14},{14,12},{16,18},{18,... | collective-permute-start | bytes 196616 | tf_op jit(solution)/shard_map/ppermute | solution.py:412

commit v15 on v14

--- a/solution.py
+++ b/solution.py
@@ -35,8 +35,7 @@
 
 
 def sift(a, x):
-    top, low = split(x)
-    return dot(a, top) + dot(a, low)
+    return dot(jnp.concatenate([a, a], 1), jnp.concatenate(split(x), 0))
 
 
 def call(body, outs, *args, limit=8, **rest):
@@ -97,11 +96,12 @@
     match = place == down
     shuffle = jnp.where(match, 1.0, 0.0).astype(BF16)
     shuffle_out[...] = shuffle
+    twice = jnp.concatenate([shuffle, shuffle], 1)
     copy.wait()
     halves = []
     for part, rest_out in enumerate((low_out, high_out)):
-        top, low = split(subspace[part * span : (part + 1) * span, :])
-        turned = dot(top, shuffle, NT) + dot(low, shuffle, NT)
+        both_parts = jnp.concatenate(split(subspace[part * span : (part + 1) * span, :]), 1)
+        turned = dot(both_parts, twice, NT)
         rest_out[...] = turned[:, 2 * duo :]
         halves.append(turned)
     far_out[...] = jnp.concatenate([half[:, :duo] for half in halves], 1)
@@ -379,8 +379,8 @@
 
 def finish(result, hits, far_in, out_in, near_in, out):
     back = jnp.concatenate([far_in[...], out_in[...], near_in[...]], 0)
-    top, low = split(SCALE_TWO * back.T)
-    out[...] = result[...] + (dot(top, hits[...]) + dot(low, hits[...]))
+    columns = jnp.concatenate(split(SCALE_TWO * back.T), 1)
+    out[...] = result[...] + dot(columns, jnp.concatenate([hits[...], hits[...]], 0))
 
 
 def per_device(subspace, ritz, element_ham, connect, send_rows):

time: 56.6 us -> 56.5 us (level)
  transfers between devices with their start and end apart: 16 -> 16, of which waited for: 6 -> 6; matrix products, arithmetic and copies ran while one was open for 0% -> 0% of each run, Pallas kernels for 26% -> 25%
where the time goes in v15:
time: 56.5 us; the launch traced here: 56.3 us
  starting transfers between devices  19.9 us (35%)
  waiting for transfers between devices  18.3 us (32%)
  Pallas kernels  18 us (32%)
    pallas_call x16, Pallas kernels, call(): pl.pallas_call(body, out_shape=[jax.ShapeDtypeStruct(*out) for out in out...  18 us
    ppermute x4, waiting for transfers between devices, out(): return lax.ppermute(rows, 'mesh', pairs_out)  16.2 us
    ppermute x4, starting transfers between devices, far(): return lax.ppermute(rows, 'mesh', pairs_far)  9.34 us
    ppermute x4, starting transfers between devices, gather(): lax.ppermute(rows, 'state', [(i, (i + step) % groups) for i in range(grou...  5.14 us
    ppermute x4, starting transfers between devices, out(): return lax.ppermute(rows, 'mesh', pairs_out)  3.9 us
    ppermute x4, waiting for transfers between devices, gather(): lax.ppermute(rows, 'state', [(i, (i + step) % groups) for i in range(grou...  2.02 us
    ppermute x4, starting transfers between devices, near(): return lax.ppermute(rows, 'mesh', pairs_in)  1.48 us
  transfers between devices with their start and end apart: 16, of which 6 were waited for; matrix products, arithmetic and copies ran while one was open for 0% of the time, Pallas kernels for 25%

profile of v15, /device:TPU:0, one launch (start us, length us, event | category | flops | bytes accessed | tf_op | source)
XLA Modules:
  0.0 56.3 jit_solution(6050326542748113146)
XLA Ops:
  0.0 1.8 %shard_map.55 = (f32[512,128]{1,0:T(8,128)S(1)}, f32[512,128]{1,0:T(8,128)S(1)}, f32[512,128]{1,0:T(8,128)S(1)}, f32[512,128]{1,0:T(8,128)S(1)}, bf16[256,256]{1,0:T(8,128)(2,1)S(1)}) custom-call(s32[1,4,32]{2,1,0:T(4,128)} %lists.1, f32[1024,256]{1,0:T(8,128)} %subspace_in.3), custom_call_target="tpu_custom_call" | custom-call | tf_op jit(solution)/shard_map/pallas_call | solution.py:42
  1.8 3.0 %collective-permute-start.1 = (f32[512,128]{1,0:T(8,128)S(1)}, f32[512,128]{1,0:T(8,128)S(1)}, u32[]{:S(2)}, u32[]{:S(2)}) collective-permute-start(f32[512,128]{1,0:T(8,128)S(1)} %get-tuple-element.46), channel_id=1, source_target_pairs={{0,1},{1,0},{2,3},{3,2},{4,5},{5,4},{6,7},{7,6},{8,9},{9,8},{10,11... | collective-permute-start | bytes 786440 | tf_op jit(solution)/shard_map/ppermute | solution.py:416
  5.0 1.9 %collective-permute-start.3 = (f32[512,128]{1,0:T(8,128)S(1)}, f32[512,128]{1,0:T(8,128)S(1)}, u32[]{:S(2)}, u32[]{:S(2)}) collective-permute-start(f32[512,128]{1,0:T(8,128)S(1)} %get-tuple-element.54), channel_id=1, source_target_pairs={{0,1},{1,0},{2,3},{3,2},{4,5},{5,4},{6,7},{7,6},{8,9},{9,8},{10,11... | collective-permute-start | bytes 786440 | tf_op jit(solution)/shard_map/ppermute | solution.py:416
  7.0 3.6 %shard_map.56 = (f32[512,256]{1,0:T(8,128)S(1)}, bf16[512,1024]{1,0:T(8,128)(2,1)S(1)}, bf16[512,1024]{1,0:T(8,128)(2,1)S(1)}) custom-call(s32[1]{0:T(128)} %bitcast.group, bf16[256,256]{1,0:T(8,128)(2,1)S(1)} %get-tuple-element.44.shuffle, f32[1024,256]{1,0:T(8,128)} %subspace_in.3, f32[512,2048]{1,0:T(8,128)} %ritz_in.1), custom_call_target="tpu_custom_call" | custom-call | tf_op jit(solution)/shard_map/pallas_call | solution.py:42
  10.6 4.1 %shard_map.57 = (bf16[384,384]{1,0:T(8,128)(2,1)S(1)}, bf16[384,384]{1,0:T(8,128)(2,1)S(1)}, bf16[128,128]{1,0:T(8,128)(2,1)S(1)}, bf16[128,128]{1,0:T(8,128)(2,...) custom-call(s32[1]{0:T(128)} %bitcast.1.odd, s32[1,4,32]{2,1,0:T(4,128)S(1)} %copy-done.1, ...), custom_call_target="tpu_custom_call" | custom-call | tf_op jit(solution)/shard_map/pallas_call | solution.py:42
  14.7 1.1 %shard_map.58 = (f32[64,512]{1,0:T(8,128)S(1)}, f32[64,640]{1,0:T(8,128)S(1)}) custom-call(f32[512,128]{1,0:T(8,128)S(1)} %collective-permute-done.1.columns, f32[512,256]{1,0:T(8,128)S(1)} %get-tuple-element.45.start_own, bf16[512,1024]{1,0:T(8,128)(2,1)S(1)} %get-tuple-element.47.top, bf16[512,1024]{1,0:T(8,128)(2,1)S(1)} %get-tuple-element.48.low, ...), custom_call_target="tpu_custom_call" | custom-call | tf_op jit(solution)/shard_map/pallas_call | solution.py:42
  15.8 3.1 %collective-permute-start.4 = (f32[64,640]{1,0:T(8,128)S(1)}, f32[64,640]{1,0:T(8,128)S(1)}, u32[]{:S(2)}, u32[]{:S(2)}) collective-permute-start(f32[64,640]{1,0:T(8,128)S(1)} %get-tuple-element.55), channel_id=1, source_target_pairs={{0,16},{2,18},{4,20},{6,22},{8,24},{10,26},{12,28},{14,30},{16,0},... | collective-permute-start | bytes 491528 | tf_op jit(solution)/shard_map/ppermute | solution.py:406
  18.9 1.2 %shard_map.59 = (f32[128,512]{1,0:T(8,128)S(1)}, f32[32,512]{1,0:T(8,128)S(1)}, f32[32,512]{1,0:T(8,128)S(1)}) custom-call(f32[512,128]{1,0:T(8,128)S(1)} %collective-permute-done.columns, f32[512,256]{1,0:T(8,128)S(1)} %get-tuple-element.45.start_own, f32[64,512]{1,0:T(8,128)S(1)} %get-tuple-element.51.start_far, ...), custom_call_target="tpu_custom_call" | custom-call | tf_op jit(solution)/shard_map/pallas_call | solution.py:42
  20.1 1.3 %collective-permute-start.5 = (f32[32,512]{1,0:T(8,128)S(1)}, f32[32,512]{1,0:T(8,128)S(1)}, u32[]{:S(2)}, u32[]{:S(2)}) collective-permute-start(f32[32,512]{1,0:T(8,128)S(1)} %get-tuple-element.56), channel_id=1, source_target_pairs={{0,30},{2,4},{4,2},{6,8},{8,6},{10,12},{12,10},{14,16},{16,14},{18... | collective-permute-start | bytes 196616 | tf_op jit(solution)/shard_map/ppermute | solution.py:409
  21.8 1.4 %collective-permute-done.3.columns = f32[512,128]{1,0:T(8,128)S(1)} collective-permute-done((f32[512,128]{1,0:T(8,128)S(1)}, f32[512,128]{1,0:T(8,128)S(1)}, u32[]{:S(2)}, u32[]{:S(2)}) %collective-permute-start.3) | collective-permute-done | bytes 262176 | tf_op jit(solution)/shard_map/ppermute | solution.py:416
  23.7 3.0 %collective-permute-done.5.out_in = f32[32,512]{1,0:T(8,128)S(1)} collective-permute-done((f32[32,512]{1,0:T(8,128)S(1)}, f32[32,512]{1,0:T(8,128)S(1)}, u32[]{:S(2)}, u32[]{:S(2)}) %collective-permute-start.5) | collective-permute-done | bytes 65568 | tf_op jit(solution)/shard_map/ppermute | solution.py:409
  26.7 0.8 %shard_map.61 = (f32[384,512]{1,0:T(8,128)S(1)}, f32[64,64]{1,0:T(8,128)S(1)}, f32[64,64]{1,0:T(8,128)S(1)}) custom-call(f32[128,512]{1,0:T(8,128)S(1)} %get-tuple-element.52.start_edge, f32[64,640]{1,0:T(8,128)S(1)} %collective-permute-done.4.far_in, f32[32,512]{1,0:T(8,128)S(1)} %collective-permute-done.5.out_in, ...), custom_call_target="tpu_custom_call" | custom-call | tf_op jit(solution)/shard_map/pallas_call | solution.py:42
  28.0 0.8 %shard_map.62 = (f32[128,512]{1,0:T(8,128)S(1)}, f32[64,512]{1,0:T(8,128)S(1)}, f32[32,512]{1,0:T(8,128)S(1)}, f32[32,512]{1,0:T(8,128)S(1)}) custom-call(f32[512,128]{1,0:T(8,128)S(1)} %collective-permute-done.2.columns, f32[512,128]{1,0:T(8,128)S(1)} %shard_map.60.rest_low, bf16[512,1024]{1,0:T(8,128)(2,1)S(1)} %get-tuple-element.47.top, ...), custom_call_target="tpu_custom_call" | custom-call | tf_op jit(solution)/shard_map/pallas_call | solution.py:42
  28.8 2.9 %collective-permute-start.7 = (f32[64,512]{1,0:T(8,128)S(1)}, f32[64,512]{1,0:T(8,128)S(1)}, u32[]{:S(2)}, u32[]{:S(2)}) collective-permute-start(f32[64,512]{1,0:T(8,128)S(1)} %get-tuple-element.63.back_far), channel_id=1, source_target_pairs={{0,16},{2,18},{4,20},{6,22},{8,24},{10,26},{12,28},{14,30},{16,0},... | collective-permute-start | bytes 393224 | tf_op jit(solution)/shard_map/ppermute | solution.py:406
  32.3 1.0 %collective-permute-start.9 = (f32[32,512]{1,0:T(8,128)S(1)}, f32[32,512]{1,0:T(8,128)S(1)}, u32[]{:S(2)}, u32[]{:S(2)}) collective-permute-start(f32[32,512]{1,0:T(8,128)S(1)} %get-tuple-element.66), channel_id=1, source_target_pairs={{0,2},{2,0},{4,6},{6,4},{8,10},{10,8},{12,14},{14,12},{16,18},{18,... | collective-permute-start | bytes 196616 | tf_op jit(solution)/shard_map/ppermute | solution.py:412
  33.3 0.6 %shard_map.63 = (f32[256,512]{1,0:T(8,128)S(1)}, f32[256,512]{1,0:T(8,128)S(1)}, f32[128,512]{1,0:T(8,128)S(1)}, f32[64,512]{1,0:T(8,128)S(1)}) custom-call(f32[128,512]{1,0:T(8,128)S(1)} %get-tuple-element.52.start_edge, f32[128,512]{1,0:T(8,128)S(1)} %get-tuple-element.61.start_rest, f32[384,512]{1,0:T(8,128)S(1)} %get-tuple-element.60.part, ...), custom_call_target="tpu_custom_call" | custom-call | tf_op jit(solution)/shard_map/pallas_call | solution.py:42
  33.9 4.2 %collective-permute-done.8.out_in = f32[32,512]{1,0:T(8,128)S(1)} collective-permute-done((f32[32,512]{1,0:T(8,128)S(1)}, f32[32,512]{1,0:T(8,128)S(1)}, u32[]{:S(2)}, u32[]{:S(2)}) %collective-permute-start.8) | collective-permute-done | bytes 65568 | tf_op jit(solution)/shard_map/ppermute | solution.py:409
  38.3 3.3 %collective-permute-start.10 = (f32[64,512]{1,0:T(8,128)S(1)}, f32[64,512]{1,0:T(8,128)S(1)}, u32[]{:S(2)}, u32[]{:S(2)}) collective-permute-start(f32[64,512]{1,0:T(8,128)S(1)} %shard_map.65), channel_id=1, source_target_pairs={{0,16},{2,18},{4,20},{6,22},{8,24},{10,26},{12,28},{14,30},{16,0},... | collective-permute-start | bytes 393224 | tf_op jit(solution)/shard_map/ppermute | solution.py:406
  41.9 0.9 %shard_map.64 = (f32[256,512]{1,0:T(8,128)S(1)}, f32[384,512]{1,0:T(8,128)S(1)}, f32[64,512]{1,0:T(8,128)S(1)}) custom-call(f32[256,512]{1,0:T(8,128)S(1)} %get-tuple-element.64.base, bf16[128,128]{1,0:T(8,128)(2,1)S(1)} %get-tuple-element.49.pick, f32[64,512]{1,0:T(8,128)S(1)} %collective-permute-done.7.far_in, ...), custom_call_target="tpu_custom_call" | custom-call | tf_op jit(solution)/shard_map/pallas_call | solution.py:42
  42.8 5.4 %collective-permute-done.11.out_in = f32[32,512]{1,0:T(8,128)S(1)} collective-permute-done((f32[32,512]{1,0:T(8,128)S(1)}, f32[32,512]{1,0:T(8,128)S(1)}, u32[]{:S(2)}, u32[]{:S(2)}) %collective-permute-start.11) | collective-permute-done | bytes 65568 | tf_op jit(solution)/shard_map/ppermute | solution.py:409
  48.8 2.0 %collective-permute-start.14 = (f32[32,512]{1,0:T(8,128)S(1)}, f32[32,512]{1,0:T(8,128)S(1)}, u32[]{:S(2)}, u32[]{:S(2)}) collective-permute-start(f32[32,512]{1,0:T(8,128)S(1)} %get-tuple-element.79), channel_id=1, source_target_pairs={{0,30},{2,4},{4,2},{6,8},{8,6},{10,12},{12,10},{14,16},{16,14},{18... | collective-permute-start | bytes 196616 | tf_op jit(solution)/shard_map/ppermute | solution.py:409
  50.8 0.8 %shard_map.68.result = f32[512,256]{1,0:T(8,128)S(1)} custom-call(f32[384,512]{1,0:T(8,128)S(1)} %get-tuple-element.68.part, f32[128,512]{1,0:T(8,128)S(1)} %get-tuple-element.74.ghosts, bf16[384,384]{1,0:T(8,128)(2,1)S(1)} %get-tuple-element.58.ham_top, bf16[384,384]{1,0:T(8,128)(2,1)S(1)} %get-tuple-element.59.ham_low, ...), custom_call_target="tpu_custom_call" | custom-call | tf_op jit(solution)/shard_map/pallas_call | solution.py:42
  51.6 3.6 %collective-permute-done.14.out_in = f32[32,512]{1,0:T(8,128)S(1)} collective-permute-done((f32[32,512]{1,0:T(8,128)S(1)}, f32[32,512]{1,0:T(8,128)S(1)}, u32[]{:S(2)}, u32[]{:S(2)}) %collective-permute-start.14) | collective-permute-done | bytes 65568 | tf_op jit(solution)/shard_map/ppermute | solution.py:409
  55.3 1.1 %shard_map.70 = f32[512,256]{1,0:T(8,128)} custom-call(f32[512,256]{1,0:T(8,128)S(1)} %shard_map.68.result, bf16[128,256]{1,0:T(8,128)(2,1)S(1)} %get-tuple-element.78.hits, f32[64,512]{1,0:T(8,128)S(1)} %collective-permute-done.13.far_in, f32[32,512]{1,0:T(8,128)S(1)} %collective-permute-done.14.out_in, f32[32,512]{1,0:T(8,128)S(1)} %collective-permute-done.15.near_in), custom_call_target="tpu_custom_call" | custom-call | tf_op jit(solution)/shard_map/pallas_call | solution.py:42
  (28 shorter events, 3.2 us)
Async XLA Ops:
  0.0 10.6 %copy-start.1 = (s32[1,4,32]{2,1,0:T(4,128)S(1)}, s32[1,4,32]{2,1,0:T(4,128)}, u32[]{:S(2)}) copy-start(s32[1,4,32]{2,1,0:T(4,128)} %lists.1) | copy-start | bytes 1540
  0.0 10.6 %copy-start = (s32[16,125]{1,0:T(8,128)S(1)}, s32[16,125]{1,0:T(8,128)}, u32[]{:S(2)}) copy-start(s32[16,125]{1,0:T(8,128)} %connect.1) | copy-start | bytes 24004
  1.8 12.9 %collective-permute-start.1 = (f32[512,128]{1,0:T(8,128)S(1)}, f32[512,128]{1,0:T(8,128)S(1)}, u32[]{:S(2)}, u32[]{:S(2)}) collective-permute-start(f32[512,128]{1,0:T(8,128)S(1)} %get-tuple-element.46), channel_id=1, source_target_pairs={{0,1},{1,0},{2,3},{3,2},{4,5},{5,4},{6,7},{7,6},{8,9},{9,8},{10,11... | collective-permute-start | bytes 786440 | tf_op jit(solution)/shard_map/ppermute | solution.py:416
  4.9 14.0 %collective-permute-start = (f32[512,128]{1,0:T(8,128)S(1)}, f32[512,128]{1,0:T(8,128)S(1)}, u32[]{:S(2)}, u32[]{:S(2)}) collective-permute-start(f32[512,128]{1,0:T(8,128)S(1)} %get-tuple-element.43), channel_id=1, source_target_pairs={{0,1},{1,0},{2,3},{3,2},{4,5},{5,4},{6,7},{7,6},{8,9},{9,8},{10,11... | collective-permute-start | bytes 786440 | tf_op jit(solution)/shard_map/ppermute | solution.py:416
  5.0 18.3 %collective-permute-start.3 = (f32[512,128]{1,0:T(8,128)S(1)}, f32[512,128]{1,0:T(8,128)S(1)}, u32[]{:S(2)}, u32[]{:S(2)}) collective-permute-start(f32[512,128]{1,0:T(8,128)S(1)} %get-tuple-element.54), channel_id=1, source_target_pairs={{0,1},{1,0},{2,3},{3,2},{4,5},{5,4},{6,7},{7,6},{8,9},{9,8},{10,11... | collective-permute-start | bytes 786440 | tf_op jit(solution)/shard_map/ppermute | solution.py:416
  6.9 21.1 %collective-permute-start.2 = (f32[512,128]{1,0:T(8,128)S(1)}, f32[512,128]{1,0:T(8,128)S(1)}, u32[]{:S(2)}, u32[]{:S(2)}) collective-permute-start(f32[512,128]{1,0:T(8,128)S(1)} %get-tuple-element.53), channel_id=1, source_target_pairs={{0,1},{1,0},{2,3},{3,2},{4,5},{5,4},{6,7},{7,6},{8,9},{9,8},{10,11... | collective-permute-start | bytes 786440 | tf_op jit(solution)/shard_map/ppermute | solution.py:416
  15.8 10.9 %collective-permute-start.4 = (f32[64,640]{1,0:T(8,128)S(1)}, f32[64,640]{1,0:T(8,128)S(1)}, u32[]{:S(2)}, u32[]{:S(2)}) collective-permute-start(f32[64,640]{1,0:T(8,128)S(1)} %get-tuple-element.55), channel_id=1, source_target_pairs={{0,16},{2,18},{4,20},{6,22},{8,24},{10,26},{12,28},{14,30},{16,0},... | collective-permute-start | bytes 491528 | tf_op jit(solution)/shard_map/ppermute | solution.py:406
  20.1 6.6 %collective-permute-start.5 = (f32[32,512]{1,0:T(8,128)S(1)}, f32[32,512]{1,0:T(8,128)S(1)}, u32[]{:S(2)}, u32[]{:S(2)}) collective-permute-start(f32[32,512]{1,0:T(8,128)S(1)} %get-tuple-element.56), channel_id=1, source_target_pairs={{0,30},{2,4},{4,2},{6,8},{8,6},{10,12},{12,10},{14,16},{16,14},{18... | collective-permute-start | bytes 196616 | tf_op jit(solution)/shard_map/ppermute | solution.py:409
  21.4 5.3 %collective-permute-start.6 = (f32[32,512]{1,0:T(8,128)S(1)}, f32[32,512]{1,0:T(8,128)S(1)}, u32[]{:S(2)}, u32[]{:S(2)}) collective-permute-start(f32[32,512]{1,0:T(8,128)S(1)} %get-tuple-element.57), channel_id=1, source_target_pairs={{0,2},{2,0},{4,6},{6,4},{8,10},{10,8},{12,14},{14,12},{16,18},{18,... | collective-permute-start | bytes 196616 | tf_op jit(solution)/shard_map/ppermute | solution.py:412
  28.8 12.8 %collective-permute-start.7 = (f32[64,512]{1,0:T(8,128)S(1)}, f32[64,512]{1,0:T(8,128)S(1)}, u32[]{:S(2)}, u32[]{:S(2)}) collective-permute-start(f32[64,512]{1,0:T(8,128)S(1)} %get-tuple-element.63.back_far), channel_id=1, source_target_pairs={{0,16},{2,18},{4,20},{6,22},{8,24},{10,26},{12,28},{14,30},{16,0},... | collective-permute-start | bytes 393224 | tf_op jit(solution)/shard_map/ppermute | solution.py:406
  31.7 6.4 %collective-permute-start.8 = (f32[32,512]{1,0:T(8,128)S(1)}, f32[32,512]{1,0:T(8,128)S(1)}, u32[]{:S(2)}, u32[]{:S(2)}) collective-permute-start(f32[32,512]{1,0:T(8,128)S(1)} %get-tuple-element.65), channel_id=1, source_target_pairs={{0,30},{2,4},{4,2},{6,8},{8,6},{10,12},{12,10},{14,16},{16,14},{18... | collective-permute-start | bytes 196616 | tf_op jit(solution)/shard_map/ppermute | solution.py:409
  32.3 5.8 %collective-permute-start.9 = (f32[32,512]{1,0:T(8,128)S(1)}, f32[32,512]{1,0:T(8,128)S(1)}, u32[]{:S(2)}, u32[]{:S(2)}) collective-permute-start(f32[32,512]{1,0:T(8,128)S(1)} %get-tuple-element.66), channel_id=1, source_target_pairs={{0,2},{2,0},{4,6},{6,4},{8,10},{10,8},{12,14},{14,12},{16,18},{18,... | collective-permute-start | bytes 196616 | tf_op jit(solution)/shard_map/ppermute | solution.py:412
  38.3 10.3 %collective-permute-start.10 = (f32[64,512]{1,0:T(8,128)S(1)}, f32[64,512]{1,0:T(8,128)S(1)}, u32[]{:S(2)}, u32[]{:S(2)}) collective-permute-start(f32[64,512]{1,0:T(8,128)S(1)} %shard_map.65), channel_id=1, source_target_pairs={{0,16},{2,18},{4,20},{6,22},{8,24},{10,26},{12,28},{14,30},{16,0},... | collective-permute-start | bytes 393224 | tf_op jit(solution)/shard_map/ppermute | solution.py:406
  41.8 6.5 %collective-permute-start.11 = (f32[32,512]{1,0:T(8,128)S(1)}, f32[32,512]{1,0:T(8,128)S(1)}, u32[]{:S(2)}, u32[]{:S(2)}) collective-permute-start(f32[32,512]{1,0:T(8,128)S(1)} %get-tuple-element.72), channel_id=1, source_target_pairs={{0,30},{2,4},{4,2},{6,8},{8,6},{10,12},{12,10},{14,16},{16,14},{18... | collective-permute-start | bytes 196616 | tf_op jit(solution)/shard_map/ppermute | solution.py:409
  41.9 6.4 %collective-permute-start.12 = (f32[32,512]{1,0:T(8,128)S(1)}, f32[32,512]{1,0:T(8,128)S(1)}, u32[]{:S(2)}, u32[]{:S(2)}) collective-permute-start(f32[32,512]{1,0:T(8,128)S(1)} %get-tuple-element.73), channel_id=1, source_target_pairs={{0,2},{2,0},{4,6},{6,4},{8,10},{10,8},{12,14},{14,12},{16,18},{18,... | collective-permute-start | bytes 196616 | tf_op jit(solution)/shard_map/ppermute | solution.py:412
  48.5 6.8 %collective-permute-start.13 = (f32[64,512]{1,0:T(8,128)S(1)}, f32[64,512]{1,0:T(8,128)S(1)}, u32[]{:S(2)}, u32[]{:S(2)}) collective-permute-start(f32[64,512]{1,0:T(8,128)S(1)} %shard_map.69), channel_id=1, source_target_pairs={{0,16},{2,18},{4,20},{6,22},{8,24},{10,26},{12,28},{14,30},{16,0},... | collective-permute-start | bytes 393224 | tf_op jit(solution)/shard_map/ppermute | solution.py:406
  48.8 6.5 %collective-permute-start.14 = (f32[32,512]{1,0:T(8,128)S(1)}, f32[32,512]{1,0:T(8,128)S(1)}, u32[]{:S(2)}, u32[]{:S(2)}) collective-permute-start(f32[32,512]{1,0:T(8,128)S(1)} %get-tuple-element.79), channel_id=1, source_target_pairs={{0,30},{2,4},{4,2},{6,8},{8,6},{10,12},{12,10},{14,16},{16,14},{18... | collective-permute-start | bytes 196616 | tf_op jit(solution)/shard_map/ppermute | solution.py:409
  50.8 4.5 %collective-permute-start.15 = (f32[32,512]{1,0:T(8,128)S(1)}, f32[32,512]{1,0:T(8,128)S(1)}, u32[]{:S(2)}, u32[]{:S(2)}) collective-permute-start(f32[32,512]{1,0:T(8,128)S(1)} %get-tuple-element.80), channel_id=1, source_target_pairs={{0,2},{2,0},{4,6},{6,4},{8,10},{10,8},{12,14},{14,12},{16,18},{18,... | collective-permute-start | bytes 196616 | tf_op jit(solution)/shard_map/ppermute | solution.py:412

commit v16 on v15

--- a/solution.py
+++ b/solution.py
@@ -269,7 +269,7 @@
     rest_out[...] = start_own[:, edge_nodes:] + rotate_half(columns, top, low, groups, 0)
 
 
-def first_part(start_edge, far_in, out_in, near_in, ham_top, ham_low, part_out, overlap_out, couple_out):
+def first_part(start_edge, far_in, near_in, out_in, ham_top, ham_low, part_out, overlap_out, couple_out):
     edge_nodes = start_edge.shape[0]
     nodes = ham_top.shape[0] - 4 * out_in.shape[0]
     duo = far_in.shape[0]
@@ -315,13 +315,13 @@
     adjust_out[...] = mul(split(overlap[...]), split(back_far[...]))
 
 
-def fetch_far(packed, both, out_in, near_in, far_out):
+def fetch_far(packed, both, near_in, out_in, far_out):
     duo = 2 * out_in.shape[0]
     back = jnp.concatenate([out_in[...], near_in[...]], 0)
     far_out[...] = packed[:duo, :] + SCALE_ONE * sift(both[:duo, duo:], back)
 
 
-def fetch_ring(packed, both, far_in, out_in, near_in, out_out, near_out):
+def fetch_ring(packed, both, far_in, near_in, out_in, out_out, near_out):
     halo = out_in.shape[0]
     back = jnp.concatenate([far_in[...], out_in[...], near_in[...]], 0)
     rows = packed[2 * halo :, :] + SCALE_ONE * sift(both[2 * halo :, :], back)
@@ -330,7 +330,7 @@
 
 
 def first_own(
-    base, pick, far_in, out_in, near_in, ham_top, ham_low, couple, first_out, part_out, known_out
+    base, pick, far_in, near_in, out_in, ham_top, ham_low, couple, first_out, part_out, known_out
 ):
     edge_nodes = pick.shape[1]
     nodes = base.shape[0]
@@ -343,7 +343,7 @@
     known_out[...] = mul(split(couple[...]), split(sift(pick[:duo, :], edge)))
 
 
-def return_far(part, ham_top, ham_low, out_in, near_in, far_out):
+def return_far(part, ham_top, ham_low, near_in, out_in, far_out):
     halo = out_in.shape[0]
     nodes = part.shape[0] - 4 * halo
     far = slice(nodes, nodes + 2 * halo)
@@ -353,7 +353,7 @@
 
 
 def return_ring(
-    part, ham_top, ham_low, far_in, adjust, out_in, near_in, ghosts_out, out_out, near_out
+    part, ham_top, ham_low, far_in, adjust, near_in, out_in, ghosts_out, out_out, near_out
 ):
     halo = out_in.shape[0]
     nodes = part.shape[0] - 4 * halo
@@ -377,7 +377,7 @@
     result_out[...] = result + (dot(top, hits[:duo, :]) + dot(low, hits[:duo, :]))
 
 
-def finish(result, hits, far_in, out_in, near_in, out):
+def finish(result, hits, far_in, near_in, out_in, out):
     back = jnp.concatenate([far_in[...], out_in[...], near_in[...]], 0)
     columns = jnp.concatenate(split(SCALE_TWO * back.T), 1)
     out[...] = result[...] + dot(columns, jnp.concatenate([hits[...], hits[...]], 0))
@@ -499,11 +499,11 @@
         [rows_of(wide), rows_of(halo), rows_of(halo)],
         ring_cols_in, start_own, start_far, ritz_top, ritz_low, pick,
     )
-    out_in, near_in = out(out_rows), near(near_rows)
+    near_in, out_in = near(near_rows), out(out_rows)
     part, overlap, couple = call(
         first_part,
         [rows_of(full), ((duo, duo), F32), ((duo, duo), F32)],
-        start_edge, far_in, out_in, near_in, ham_top, ham_low,
+        start_edge, far_in, near_in, out_in, ham_top, ham_low,
     )
     (rest_low,) = call(
         functools.partial(rotate_low, groups),
@@ -516,41 +516,41 @@
         [rows_of(nodes - wide)] + halo_out,
         high_cols_in, rest_low, ritz_top, ritz_low, part, ham_top, ham_low,
     )
-    far_in, out_in, near_in = far(back_far), out(back_out), near(back_near)
+    far_in, near_in, out_in = far(back_far), near(back_near), out(back_out)
     start, base, packed, adjust = call(
         first_base,
         [rows_of(nodes), rows_of(nodes), rows_of(wide), rows_of(duo)],
         start_edge, start_rest, part, ham_top, ham_low, pick, overlap, back_far,
     )
-    (far_rows,) = call(fetch_far, [rows_of(duo)], packed, both, out_in, near_in)
+    (far_rows,) = call(fetch_far, [rows_of(duo)], packed, both, near_in, out_in)
     fetched_far = far(far_rows)
     out_rows, near_rows = call(
-        fetch_ring, halo_out[1:], packed, both, far_in, out_in, near_in
-    )
-    fetched_out, fetched_near = out(out_rows), near(near_rows)
+        fetch_ring, halo_out[1:], packed, both, far_in, near_in, out_in
+    )
+    fetched_near, fetched_out = near(near_rows), out(out_rows)
     first, part, known = call(
         first_own,
         [rows_of(nodes), rows_of(full), rows_of(duo)],
-        base, pick, far_in, out_in, near_in, ham_top, ham_low, couple,
+        base, pick, far_in, near_in, out_in, ham_top, ham_low, couple,
     )
 
     (far_rows,) = call(
-        return_far, [rows_of(duo)], part, ham_top, ham_low, fetched_out, fetched_near
+        return_far, [rows_of(duo)], part, ham_top, ham_low, fetched_near, fetched_out
     )
     returned_far = far(far_rows)
     ghosts, out_rows, near_rows = call(
         return_ring,
         [rows_of(wide)] + halo_out[1:],
-        part, ham_top, ham_low, fetched_far, adjust, fetched_out, fetched_near,
-    )
-    returned_out, returned_near = out(out_rows), near(near_rows)
+        part, ham_top, ham_low, fetched_far, adjust, fetched_near, fetched_out,
+    )
+    returned_near, returned_out = near(near_rows), out(out_rows)
     (result,) = call(
         second_base,
         [((block, nodes), F32)],
         part, ghosts, ham_top, ham_low, first, start, known, shuffle, hits,
     )
     (result,) = call(
-        finish, [((block, nodes), F32)], result, hits, returned_far, returned_out, returned_near
+        finish, [((block, nodes), F32)], result, hits, returned_far, returned_near, returned_out
     )
     return result
 

time: 56.5 us -> 56.6 us (level)
  starting transfers between devices: 19.9 us -> 23 us
  waiting for transfers between devices: 18.3 us -> 15.2 us
    ppermute x4, starting transfers between devices: 3.9 us -> 8.36 us  [out(): return lax.ppermute(rows, 'mesh', pairs_out)]
    ppermute x4, waiting for transfers between devices: 16.2 us -> 14.7 us  [out(): return lax.ppermute(rows, 'mesh', pairs_out)]
    ppermute x4, waiting for transfers between devices: 2.02 us -> 0.51 us  [gather(): lax.ppermute(rows, 'state', [(i, (i + step) % groups) for i in range(grou...]
    ppermute x4, starting transfers between devices: 1.48 us -> 0.21 us  [near(): return lax.ppermute(rows, 'mesh', pairs_in)]
  transfers between devices with their start and end apart: 16 -> 16, of which waited for: 6 -> 5; matrix products, arithmetic and copies ran while one was open for 0% -> 0% of each run, Pallas kernels for 25% -> 25%
where the time goes in v16:
time: 56.6 us; the launch traced here: 56.5 us
  starting transfers between devices  23 us (41%)
  Pallas kernels  18 us (32%)
  waiting for transfers between devices  15.2 us (27%)
    pallas_call x16, Pallas kernels, call(): pl.pallas_call(body, out_shape=[jax.ShapeDtypeStruct(*out) for out in out...  18 us
    ppermute x4, waiting for transfers between devices, out(): return lax.ppermute(rows, 'mesh', pairs_out)  14.7 us
    ppermute x4, starting transfers between devices, far(): return lax.ppermute(rows, 'mesh', pairs_far)  9.34 us
    ppermute x4, starting transfers between devices, out(): return lax.ppermute(rows, 'mesh', pairs_out)  8.36 us
    ppermute x4, starting transfers between devices, gather(): lax.ppermute(rows, 'state', [(i, (i + step) % groups) for i in range(grou...  5.14 us
  transfers between devices with their start and end apart: 16, of which 5 were waited for; matrix products, arithmetic and copies ran while one was open for 0% of the time, Pallas kernels for 25%

profile of v16, /device:TPU:0, one launch (start us, length us, event | category | flops | bytes accessed | tf_op | source)
XLA Modules:
  0.0 56.5 jit_solution(14203739820442303348)
XLA Ops:
  0.0 1.8 %shard_map.55 = (f32[512,128]{1,0:T(8,128)S(1)}, f32[512,128]{1,0:T(8,128)S(1)}, f32[512,128]{1,0:T(8,128)S(1)}, f32[512,128]{1,0:T(8,128)S(1)}, bf16[256,256]{1,0:T(8,128)(2,1)S(1)}) custom-call(s32[1,4,32]{2,1,0:T(4,128)} %lists.1, f32[1024,256]{1,0:T(8,128)} %subspace_in.3), custom_call_target="tpu_custom_call" | custom-call | tf_op jit(solution)/shard_map/pallas_call | solution.py:42
  1.8 3.0 %collective-permute-start.1 = (f32[512,128]{1,0:T(8,128)S(1)}, f32[512,128]{1,0:T(8,128)S(1)}, u32[]{:S(2)}, u32[]{:S(2)}) collective-permute-start(f32[512,128]{1,0:T(8,128)S(1)} %get-tuple-element.46), channel_id=1, source_target_pairs={{0,1},{1,0},{2,3},{3,2},{4,5},{5,4},{6,7},{7,6},{8,9},{9,8},{10,11... | collective-permute-start | bytes 786440 | tf_op jit(solution)/shard_map/ppermute | solution.py:416
  5.0 1.9 %collective-permute-start.3 = (f32[512,128]{1,0:T(8,128)S(1)}, f32[512,128]{1,0:T(8,128)S(1)}, u32[]{:S(2)}, u32[]{:S(2)}) collective-permute-start(f32[512,128]{1,0:T(8,128)S(1)} %get-tuple-element.54), channel_id=1, source_target_pairs={{0,1},{1,0},{2,3},{3,2},{4,5},{5,4},{6,7},{7,6},{8,9},{9,8},{10,11... | collective-permute-start | bytes 786440 | tf_op jit(solution)/shard_map/ppermute | solution.py:416
  7.0 3.6 %shard_map.56 = (f32[512,256]{1,0:T(8,128)S(1)}, bf16[512,1024]{1,0:T(8,128)(2,1)S(1)}, bf16[512,1024]{1,0:T(8,128)(2,1)S(1)}) custom-call(s32[1]{0:T(128)} %bitcast.group, bf16[256,256]{1,0:T(8,128)(2,1)S(1)} %get-tuple-element.44.shuffle, f32[1024,256]{1,0:T(8,128)} %subspace_in.3, f32[512,2048]{1,0:T(8,128)} %ritz_in.1), custom_call_target="tpu_custom_call" | custom-call | tf_op jit(solution)/shard_map/pallas_call | solution.py:42
  10.6 4.1 %shard_map.57 = (bf16[384,384]{1,0:T(8,128)(2,1)S(1)}, bf16[384,384]{1,0:T(8,128)(2,1)S(1)}, bf16[128,128]{1,0:T(8,128)(2,1)S(1)}, bf16[128,128]{1,0:T(8,128)(2,...) custom-call(s32[1]{0:T(128)} %bitcast.1.odd, s32[1,4,32]{2,1,0:T(4,128)S(1)} %copy-done.1, ...), custom_call_target="tpu_custom_call" | custom-call | tf_op jit(solution)/shard_map/pallas_call | solution.py:42
  14.7 1.1 %shard_map.58 = (f32[64,512]{1,0:T(8,128)S(1)}, f32[64,640]{1,0:T(8,128)S(1)}) custom-call(f32[512,128]{1,0:T(8,128)S(1)} %collective-permute-done.1.columns, f32[512,256]{1,0:T(8,128)S(1)} %get-tuple-element.45.start_own, bf16[512,1024]{1,0:T(8,128)(2,1)S(1)} %get-tuple-element.47.top, bf16[512,1024]{1,0:T(8,128)(2,1)S(1)} %get-tuple-element.48.low, ...), custom_call_target="tpu_custom_call" | custom-call | tf_op jit(solution)/shard_map/pallas_call | solution.py:42
  15.8 3.1 %collective-permute-start.4 = (f32[64,640]{1,0:T(8,128)S(1)}, f32[64,640]{1,0:T(8,128)S(1)}, u32[]{:S(2)}, u32[]{:S(2)}) collective-permute-start(f32[64,640]{1,0:T(8,128)S(1)} %get-tuple-element.55), channel_id=1, source_target_pairs={{0,16},{2,18},{4,20},{6,22},{8,24},{10,26},{12,28},{14,30},{16,0},... | collective-permute-start | bytes 491528 | tf_op jit(solution)/shard_map/ppermute | solution.py:406
  18.9 1.2 %shard_map.59 = (f32[128,512]{1,0:T(8,128)S(1)}, f32[32,512]{1,0:T(8,128)S(1)}, f32[32,512]{1,0:T(8,128)S(1)}) custom-call(f32[512,128]{1,0:T(8,128)S(1)} %collective-permute-done.columns, f32[512,256]{1,0:T(8,128)S(1)} %get-tuple-element.45.start_own, f32[64,512]{1,0:T(8,128)S(1)} %get-tuple-element.51.start_far, ...), custom_call_target="tpu_custom_call" | custom-call | tf_op jit(solution)/shard_map/pallas_call | solution.py:42
  20.2 3.9 %collective-permute-start.6 = (f32[32,512]{1,0:T(8,128)S(1)}, f32[32,512]{1,0:T(8,128)S(1)}, u32[]{:S(2)}, u32[]{:S(2)}) collective-permute-start(f32[32,512]{1,0:T(8,128)S(1)} %get-tuple-element.57), channel_id=1, source_target_pairs={{0,30},{2,4},{4,2},{6,8},{8,6},{10,12},{12,10},{14,16},{16,14},{18... | collective-permute-start | bytes 196616 | tf_op jit(solution)/shard_map/ppermute | solution.py:409
  24.6 2.2 %collective-permute-done.6.out_in = f32[32,512]{1,0:T(8,128)S(1)} collective-permute-done((f32[32,512]{1,0:T(8,128)S(1)}, f32[32,512]{1,0:T(8,128)S(1)}, u32[]{:S(2)}, u32[]{:S(2)}) %collective-permute-start.6) | collective-permute-done | bytes 65568 | tf_op jit(solution)/shard_map/ppermute | solution.py:409
  26.8 0.8 %shard_map.61 = (f32[384,512]{1,0:T(8,128)S(1)}, f32[64,64]{1,0:T(8,128)S(1)}, f32[64,64]{1,0:T(8,128)S(1)}) custom-call(f32[128,512]{1,0:T(8,128)S(1)} %get-tuple-element.52.start_edge, f32[64,640]{1,0:T(8,128)S(1)} %collective-permute-done.4.far_in, f32[32,512]{1,0:T(8,128)S(1)} %collective-permute-done.5.near_in, ...), custom_call_target="tpu_custom_call" | custom-call | tf_op jit(solution)/shard_map/pallas_call | solution.py:42
  28.0 0.8 %shard_map.62 = (f32[128,512]{1,0:T(8,128)S(1)}, f32[64,512]{1,0:T(8,128)S(1)}, f32[32,512]{1,0:T(8,128)S(1)}, f32[32,512]{1,0:T(8,128)S(1)}) custom-call(f32[512,128]{1,0:T(8,128)S(1)} %collective-permute-done.2.columns, f32[512,128]{1,0:T(8,128)S(1)} %shard_map.60.rest_low, bf16[512,1024]{1,0:T(8,128)(2,1)S(1)} %get-tuple-element.47.top, ...), custom_call_target="tpu_custom_call" | custom-call | tf_op jit(solution)/shard_map/pallas_call | solution.py:42
  28.8 2.9 %collective-permute-start.7 = (f32[64,512]{1,0:T(8,128)S(1)}, f32[64,512]{1,0:T(8,128)S(1)}, u32[]{:S(2)}, u32[]{:S(2)}) collective-permute-start(f32[64,512]{1,0:T(8,128)S(1)} %get-tuple-element.63.back_far), channel_id=1, source_target_pairs={{0,16},{2,18},{4,20},{6,22},{8,24},{10,26},{12,28},{14,30},{16,0},... | collective-permute-start | bytes 393224 | tf_op jit(solution)/shard_map/ppermute | solution.py:406
  31.7 2.4 %collective-permute-start.9 = (f32[32,512]{1,0:T(8,128)S(1)}, f32[32,512]{1,0:T(8,128)S(1)}, u32[]{:S(2)}, u32[]{:S(2)}) collective-permute-start(f32[32,512]{1,0:T(8,128)S(1)} %get-tuple-element.66), channel_id=1, source_target_pairs={{0,30},{2,4},{4,2},{6,8},{8,6},{10,12},{12,10},{14,16},{16,14},{18... | collective-permute-start | bytes 196616 | tf_op jit(solution)/shard_map/ppermute | solution.py:409
  34.1 0.6 %shard_map.63 = (f32[256,512]{1,0:T(8,128)S(1)}, f32[256,512]{1,0:T(8,128)S(1)}, f32[128,512]{1,0:T(8,128)S(1)}, f32[64,512]{1,0:T(8,128)S(1)}) custom-call(f32[128,512]{1,0:T(8,128)S(1)} %get-tuple-element.52.start_edge, f32[128,512]{1,0:T(8,128)S(1)} %get-tuple-element.61.start_rest, f32[384,512]{1,0:T(8,128)S(1)} %get-tuple-element.60.part, ...), custom_call_target="tpu_custom_call" | custom-call | tf_op jit(solution)/shard_map/pallas_call | solution.py:42
  34.7 3.4 %collective-permute-done.9.out_in = f32[32,512]{1,0:T(8,128)S(1)} collective-permute-done((f32[32,512]{1,0:T(8,128)S(1)}, f32[32,512]{1,0:T(8,128)S(1)}, u32[]{:S(2)}, u32[]{:S(2)}) %collective-permute-start.9) | collective-permute-done | bytes 65568 | tf_op jit(solution)/shard_map/ppermute | solution.py:409
  38.3 3.3 %collective-permute-start.10 = (f32[64,512]{1,0:T(8,128)S(1)}, f32[64,512]{1,0:T(8,128)S(1)}, u32[]{:S(2)}, u32[]{:S(2)}) collective-permute-start(f32[64,512]{1,0:T(8,128)S(1)} %shard_map.65), channel_id=1, source_target_pairs={{0,16},{2,18},{4,20},{6,22},{8,24},{10,26},{12,28},{14,30},{16,0},... | collective-permute-start | bytes 393224 | tf_op jit(solution)/shard_map/ppermute | solution.py:406
  41.8 0.8 %collective-permute-start.12 = (f32[32,512]{1,0:T(8,128)S(1)}, f32[32,512]{1,0:T(8,128)S(1)}, u32[]{:S(2)}, u32[]{:S(2)}) collective-permute-start(f32[32,512]{1,0:T(8,128)S(1)} %get-tuple-element.73), channel_id=1, source_target_pairs={{0,30},{2,4},{4,2},{6,8},{8,6},{10,12},{12,10},{14,16},{16,14},{18... | collective-permute-start | bytes 196616 | tf_op jit(solution)/shard_map/ppermute | solution.py:409
  42.7 0.9 %shard_map.64 = (f32[256,512]{1,0:T(8,128)S(1)}, f32[384,512]{1,0:T(8,128)S(1)}, f32[64,512]{1,0:T(8,128)S(1)}) custom-call(f32[256,512]{1,0:T(8,128)S(1)} %get-tuple-element.64.base, bf16[128,128]{1,0:T(8,128)(2,1)S(1)} %get-tuple-element.49.pick, f32[64,512]{1,0:T(8,128)S(1)} %collective-permute-done.7.far_in, ...), custom_call_target="tpu_custom_call" | custom-call | tf_op jit(solution)/shard_map/pallas_call | solution.py:42
  43.5 4.8 %collective-permute-done.12.out_in = f32[32,512]{1,0:T(8,128)S(1)} collective-permute-done((f32[32,512]{1,0:T(8,128)S(1)}, f32[32,512]{1,0:T(8,128)S(1)}, u32[]{:S(2)}, u32[]{:S(2)}) %collective-permute-start.12) | collective-permute-done | bytes 65568 | tf_op jit(solution)/shard_map/ppermute | solution.py:409
  48.9 1.3 %collective-permute-start.15 = (f32[32,512]{1,0:T(8,128)S(1)}, f32[32,512]{1,0:T(8,128)S(1)}, u32[]{:S(2)}, u32[]{:S(2)}) collective-permute-start(f32[32,512]{1,0:T(8,128)S(1)} %get-tuple-element.80), channel_id=1, source_target_pairs={{0,30},{2,4},{4,2},{6,8},{8,6},{10,12},{12,10},{14,16},{16,14},{18... | collective-permute-start | bytes 196616 | tf_op jit(solution)/shard_map/ppermute | solution.py:409
  50.2 0.8 %shard_map.68.result = f32[512,256]{1,0:T(8,128)S(1)} custom-call(f32[384,512]{1,0:T(8,128)S(1)} %get-tuple-element.68.part, f32[128,512]{1,0:T(8,128)S(1)} %get-tuple-element.74.ghosts, bf16[384,384]{1,0:T(8,128)(2,1)S(1)} %get-tuple-element.58.ham_top, bf16[384,384]{1,0:T(8,128)(2,1)S(1)} %get-tuple-element.59.ham_low, ...), custom_call_target="tpu_custom_call" | custom-call | tf_op jit(solution)/shard_map/pallas_call | solution.py:42
  51.0 4.4 %collective-permute-done.15.out_in = f32[32,512]{1,0:T(8,128)S(1)} collective-permute-done((f32[32,512]{1,0:T(8,128)S(1)}, f32[32,512]{1,0:T(8,128)S(1)}, u32[]{:S(2)}, u32[]{:S(2)}) %collective-permute-start.15) | collective-permute-done | bytes 65568 | tf_op jit(solution)/shard_map/ppermute | solution.py:409
  55.4 1.1 %shard_map.70 = f32[512,256]{1,0:T(8,128)} custom-call(f32[512,256]{1,0:T(8,128)S(1)} %shard_map.68.result, bf16[128,256]{1,0:T(8,128)(2,1)S(1)} %get-tuple-element.78.hits, f32[64,512]{1,0:T(8,128)S(1)} %collective-permute-done.13.far_in, f32[32,512]{1,0:T(8,128)S(1)} %collective-permute-done.14.near_in, f32[32,512]{1,0:T(8,128)S(1)} %collective-permute-done.15.out_in), custom_call_target="tpu_custom_call" | custom-call | tf_op jit(solution)/shard_map/pallas_call | solution.py:42
  (28 shorter events, 2.3 us)
Async XLA Ops:
  0.0 10.6 %copy-start.1 = (s32[1,4,32]{2,1,0:T(4,128)S(1)}, s32[1,4,32]{2,1,0:T(4,128)}, u32[]{:S(2)}) copy-start(s32[1,4,32]{2,1,0:T(4,128)} %lists.1) | copy-start | bytes 1540
  0.0 10.6 %copy-start = (s32[16,125]{1,0:T(8,128)S(1)}, s32[16,125]{1,0:T(8,128)}, u32[]{:S(2)}) copy-start(s32[16,125]{1,0:T(8,128)} %connect.1) | copy-start | bytes 24004
  1.8 12.9 %collective-permute-start.1 = (f32[512,128]{1,0:T(8,128)S(1)}, f32[512,128]{1,0:T(8,128)S(1)}, u32[]{:S(2)}, u32[]{:S(2)}) collective-permute-start(f32[512,128]{1,0:T(8,128)S(1)} %get-tuple-element.46), channel_id=1, source_target_pairs={{0,1},{1,0},{2,3},{3,2},{4,5},{5,4},{6,7},{7,6},{8,9},{9,8},{10,11... | collective-permute-start | bytes 786440 | tf_op jit(solution)/shard_map/ppermute | solution.py:416
  4.9 14.0 %collective-permute-start = (f32[512,128]{1,0:T(8,128)S(1)}, f32[512,128]{1,0:T(8,128)S(1)}, u32[]{:S(2)}, u32[]{:S(2)}) collective-permute-start(f32[512,128]{1,0:T(8,128)S(1)} %get-tuple-element.43), channel_id=1, source_target_pairs={{0,1},{1,0},{2,3},{3,2},{4,5},{5,4},{6,7},{7,6},{8,9},{9,8},{10,11... | collective-permute-start | bytes 786440 | tf_op jit(solution)/shard_map/ppermute | solution.py:416
  5.0 19.2 %collective-permute-start.3 = (f32[512,128]{1,0:T(8,128)S(1)}, f32[512,128]{1,0:T(8,128)S(1)}, u32[]{:S(2)}, u32[]{:S(2)}) collective-permute-start(f32[512,128]{1,0:T(8,128)S(1)} %get-tuple-element.54), channel_id=1, source_target_pairs={{0,1},{1,0},{2,3},{3,2},{4,5},{5,4},{6,7},{7,6},{8,9},{9,8},{10,11... | collective-permute-start | bytes 786440 | tf_op jit(solution)/shard_map/ppermute | solution.py:416
  6.9 21.1 %collective-permute-start.2 = (f32[512,128]{1,0:T(8,128)S(1)}, f32[512,128]{1,0:T(8,128)S(1)}, u32[]{:S(2)}, u32[]{:S(2)}) collective-permute-start(f32[512,128]{1,0:T(8,128)S(1)} %get-tuple-element.53), channel_id=1, source_target_pairs={{0,1},{1,0},{2,3},{3,2},{4,5},{5,4},{6,7},{7,6},{8,9},{9,8},{10,11... | collective-permute-start | bytes 786440 | tf_op jit(solution)/shard_map/ppermute | solution.py:416
  15.8 11.0 %collective-permute-start.4 = (f32[64,640]{1,0:T(8,128)S(1)}, f32[64,640]{1,0:T(8,128)S(1)}, u32[]{:S(2)}, u32[]{:S(2)}) collective-permute-start(f32[64,640]{1,0:T(8,128)S(1)} %get-tuple-element.55), channel_id=1, source_target_pairs={{0,16},{2,18},{4,20},{6,22},{8,24},{10,26},{12,28},{14,30},{16,0},... | collective-permute-start | bytes 491528 | tf_op jit(solution)/shard_map/ppermute | solution.py:406
  20.1 4.4 %collective-permute-start.5 = (f32[32,512]{1,0:T(8,128)S(1)}, f32[32,512]{1,0:T(8,128)S(1)}, u32[]{:S(2)}, u32[]{:S(2)}) collective-permute-start(f32[32,512]{1,0:T(8,128)S(1)} %get-tuple-element.56), channel_id=1, source_target_pairs={{0,2},{2,0},{4,6},{6,4},{8,10},{10,8},{12,14},{14,12},{16,18},{18,... | collective-permute-start | bytes 196616 | tf_op jit(solution)/shard_map/ppermute | solution.py:412
  20.2 6.6 %collective-permute-start.6 = (f32[32,512]{1,0:T(8,128)S(1)}, f32[32,512]{1,0:T(8,128)S(1)}, u32[]{:S(2)}, u32[]{:S(2)}) collective-permute-start(f32[32,512]{1,0:T(8,128)S(1)} %get-tuple-element.57), channel_id=1, source_target_pairs={{0,30},{2,4},{4,2},{6,8},{8,6},{10,12},{12,10},{14,16},{16,14},{18... | collective-permute-start | bytes 196616 | tf_op jit(solution)/shard_map/ppermute | solution.py:409
  28.8 12.8 %collective-permute-start.7 = (f32[64,512]{1,0:T(8,128)S(1)}, f32[64,512]{1,0:T(8,128)S(1)}, u32[]{:S(2)}, u32[]{:S(2)}) collective-permute-start(f32[64,512]{1,0:T(8,128)S(1)} %get-tuple-element.63.back_far), channel_id=1, source_target_pairs={{0,16},{2,18},{4,20},{6,22},{8,24},{10,26},{12,28},{14,30},{16,0},... | collective-permute-start | bytes 393224 | tf_op jit(solution)/shard_map/ppermute | solution.py:406
  31.7 3.0 %collective-permute-start.8 = (f32[32,512]{1,0:T(8,128)S(1)}, f32[32,512]{1,0:T(8,128)S(1)}, u32[]{:S(2)}, u32[]{:S(2)}) collective-permute-start(f32[32,512]{1,0:T(8,128)S(1)} %get-tuple-element.65), channel_id=1, source_target_pairs={{0,2},{2,0},{4,6},{6,4},{8,10},{10,8},{12,14},{14,12},{16,18},{18,... | collective-permute-start | bytes 196616 | tf_op jit(solution)/shard_map/ppermute | solution.py:412
  31.7 6.4 %collective-permute-start.9 = (f32[32,512]{1,0:T(8,128)S(1)}, f32[32,512]{1,0:T(8,128)S(1)}, u32[]{:S(2)}, u32[]{:S(2)}) collective-permute-start(f32[32,512]{1,0:T(8,128)S(1)} %get-tuple-element.66), channel_id=1, source_target_pairs={{0,30},{2,4},{4,2},{6,8},{8,6},{10,12},{12,10},{14,16},{16,14},{18... | collective-permute-start | bytes 196616 | tf_op jit(solution)/shard_map/ppermute | solution.py:409
  38.3 10.3 %collective-permute-start.10 = (f32[64,512]{1,0:T(8,128)S(1)}, f32[64,512]{1,0:T(8,128)S(1)}, u32[]{:S(2)}, u32[]{:S(2)}) collective-permute-start(f32[64,512]{1,0:T(8,128)S(1)} %shard_map.65), channel_id=1, source_target_pairs={{0,16},{2,18},{4,20},{6,22},{8,24},{10,26},{12,28},{14,30},{16,0},... | collective-permute-start | bytes 393224 | tf_op jit(solution)/shard_map/ppermute | solution.py:406
  41.8 1.7 %collective-permute-start.11 = (f32[32,512]{1,0:T(8,128)S(1)}, f32[32,512]{1,0:T(8,128)S(1)}, u32[]{:S(2)}, u32[]{:S(2)}) collective-permute-start(f32[32,512]{1,0:T(8,128)S(1)} %get-tuple-element.72), channel_id=1, source_target_pairs={{0,2},{2,0},{4,6},{6,4},{8,10},{10,8},{12,14},{14,12},{16,18},{18,... | collective-permute-start | bytes 196616 | tf_op jit(solution)/shard_map/ppermute | solution.py:412
  41.8 6.5 %collective-permute-start.12 = (f32[32,512]{1,0:T(8,128)S(1)}, f32[32,512]{1,0:T(8,128)S(1)}, u32[]{:S(2)}, u32[]{:S(2)}) collective-permute-start(f32[32,512]{1,0:T(8,128)S(1)} %get-tuple-element.73), channel_id=1, source_target_pairs={{0,30},{2,4},{4,2},{6,8},{8,6},{10,12},{12,10},{14,16},{16,14},{18... | collective-permute-start | bytes 196616 | tf_op jit(solution)/shard_map/ppermute | solution.py:409
  48.5 6.9 %collective-permute-start.13 = (f32[64,512]{1,0:T(8,128)S(1)}, f32[64,512]{1,0:T(8,128)S(1)}, u32[]{:S(2)}, u32[]{:S(2)}) collective-permute-start(f32[64,512]{1,0:T(8,128)S(1)} %shard_map.69), channel_id=1, source_target_pairs={{0,16},{2,18},{4,20},{6,22},{8,24},{10,26},{12,28},{14,30},{16,0},... | collective-permute-start | bytes 393224 | tf_op jit(solution)/shard_map/ppermute | solution.py:406
  48.9 2.2 %collective-permute-start.14 = (f32[32,512]{1,0:T(8,128)S(1)}, f32[32,512]{1,0:T(8,128)S(1)}, u32[]{:S(2)}, u32[]{:S(2)}) collective-permute-start(f32[32,512]{1,0:T(8,128)S(1)} %get-tuple-element.79), channel_id=1, source_target_pairs={{0,2},{2,0},{4,6},{6,4},{8,10},{10,8},{12,14},{14,12},{16,18},{18,... | collective-permute-start | bytes 196616 | tf_op jit(solution)/shard_map/ppermute | solution.py:412
  48.9 6.5 %collective-permute-start.15 = (f32[32,512]{1,0:T(8,128)S(1)}, f32[32,512]{1,0:T(8,128)S(1)}, u32[]{:S(2)}, u32[]{:S(2)}) collective-permute-start(f32[32,512]{1,0:T(8,128)S(1)} %get-tuple-element.80), channel_id=1, source_target_pairs={{0,30},{2,4},{4,2},{6,8},{8,6},{10,12},{12,10},{14,16},{16,14},{18... | collective-permute-start | bytes 196616 | tf_op jit(solution)/shard_map/ppermute | solution.py:409

commit v17 on v15

--- a/solution.py
+++ b/solution.py
@@ -31,6 +31,9 @@
 
 
 def mul(a, b, dims=NN):
+    if dims == NN and a[0].shape[1] == 128:
+        left = jnp.concatenate([a[0], a[0], a[1]], 1)
+        return dot(left, jnp.concatenate([b[0], b[1], b[0]], 0))
     return dot(a[0], b[0], dims) + (dot(a[0], b[1], dims) + dot(a[1], b[0], dims))
 
 

time: 56.5 us -> 56.5 us (level)
  no operation moved by 1% of the time
where the time goes in v17:
time: 56.5 us; the launch traced here: 56.3 us
  starting transfers between devices  19.8 us (35%)
  waiting for transfers between devices  18.6 us (33%)
  Pallas kernels  17.7 us (31%)
    pallas_call x16, Pallas kernels, call(): pl.pallas_call(body, out_shape=[jax.ShapeDtypeStruct(*out) for out in out...  17.7 us
    ppermute x4, waiting for transfers between devices, out(): return lax.ppermute(rows, 'mesh', pairs_out)  16.3 us
    ppermute x4, starting transfers between devices, far(): return lax.ppermute(rows, 'mesh', pairs_far)  9.34 us
    ppermute x4, starting transfers between devices, gather(): lax.ppermute(rows, 'state', [(i, (i + step) % groups) for i in range(grou...  5.14 us
    ppermute x4, starting transfers between devices, out(): return lax.ppermute(rows, 'mesh', pairs_out)  3.89 us
    ppermute x4, waiting for transfers between devices, gather(): lax.ppermute(rows, 'state', [(i, (i + step) % groups) for i in range(grou...  2.2 us
    ppermute x4, starting transfers between devices, near(): return lax.ppermute(rows, 'mesh', pairs_in)  1.49 us
  transfers between devices with their start and end apart: 16, of which 6 were waited for; matrix products, arithmetic and copies ran while one was open for 0% of the time, Pallas kernels for 25%

profile of v17, /device:TPU:0, one launch (start us, length us, event | category | flops | bytes accessed | tf_op | source)
XLA Modules:
  0.0 56.3 jit_solution(7178218985912951705)
XLA Ops:
  0.0 1.8 %shard_map.55 = (f32[512,128]{1,0:T(8,128)S(1)}, f32[512,128]{1,0:T(8,128)S(1)}, f32[512,128]{1,0:T(8,128)S(1)}, f32[512,128]{1,0:T(8,128)S(1)}, bf16[256,256]{1,0:T(8,128)(2,1)S(1)}) custom-call(s32[1,4,32]{2,1,0:T(4,128)} %lists.1, f32[1024,256]{1,0:T(8,128)} %subspace_in.3), custom_call_target="tpu_custom_call" | custom-call | tf_op jit(solution)/shard_map/pallas_call | solution.py:45
  1.8 3.0 %collective-permute-start.1 = (f32[512,128]{1,0:T(8,128)S(1)}, f32[512,128]{1,0:T(8,128)S(1)}, u32[]{:S(2)}, u32[]{:S(2)}) collective-permute-start(f32[512,128]{1,0:T(8,128)S(1)} %get-tuple-element.46), channel_id=1, source_target_pairs={{0,1},{1,0},{2,3},{3,2},{4,5},{5,4},{6,7},{7,6},{8,9},{9,8},{10,11... | collective-permute-start | bytes 786440 | tf_op jit(solution)/shard_map/ppermute | solution.py:419
  5.0 1.9 %collective-permute-start.3 = (f32[512,128]{1,0:T(8,128)S(1)}, f32[512,128]{1,0:T(8,128)S(1)}, u32[]{:S(2)}, u32[]{:S(2)}) collective-permute-start(f32[512,128]{1,0:T(8,128)S(1)} %get-tuple-element.54), channel_id=1, source_target_pairs={{0,1},{1,0},{2,3},{3,2},{4,5},{5,4},{6,7},{7,6},{8,9},{9,8},{10,11... | collective-permute-start | bytes 786440 | tf_op jit(solution)/shard_map/ppermute | solution.py:419
  7.0 3.6 %shard_map.56 = (f32[512,256]{1,0:T(8,128)S(1)}, bf16[512,1024]{1,0:T(8,128)(2,1)S(1)}, bf16[512,1024]{1,0:T(8,128)(2,1)S(1)}) custom-call(s32[1]{0:T(128)} %bitcast.group, bf16[256,256]{1,0:T(8,128)(2,1)S(1)} %get-tuple-element.44.shuffle, f32[1024,256]{1,0:T(8,128)} %subspace_in.3, f32[512,2048]{1,0:T(8,128)} %ritz_in.1), custom_call_target="tpu_custom_call" | custom-call | tf_op jit(solution)/shard_map/pallas_call | solution.py:45
  10.6 4.1 %shard_map.57 = (bf16[384,384]{1,0:T(8,128)(2,1)S(1)}, bf16[384,384]{1,0:T(8,128)(2,1)S(1)}, bf16[128,128]{1,0:T(8,128)(2,1)S(1)}, bf16[128,128]{1,0:T(8,128)(2,...) custom-call(s32[1]{0:T(128)} %bitcast.1.odd, s32[1,4,32]{2,1,0:T(4,128)S(1)} %copy-done.1, ...), custom_call_target="tpu_custom_call" | custom-call | tf_op jit(solution)/shard_map/pallas_call | solution.py:45
  14.7 1.1 %shard_map.58 = (f32[64,512]{1,0:T(8,128)S(1)}, f32[64,640]{1,0:T(8,128)S(1)}) custom-call(f32[512,128]{1,0:T(8,128)S(1)} %collective-permute-done.1.columns, f32[512,256]{1,0:T(8,128)S(1)} %get-tuple-element.45.start_own, bf16[512,1024]{1,0:T(8,128)(2,1)S(1)} %get-tuple-element.47.top, bf16[512,1024]{1,0:T(8,128)(2,1)S(1)} %get-tuple-element.48.low, ...), custom_call_target="tpu_custom_call" | custom-call | tf_op jit(solution)/shard_map/pallas_call | solution.py:45
  15.8 3.1 %collective-permute-start.4 = (f32[64,640]{1,0:T(8,128)S(1)}, f32[64,640]{1,0:T(8,128)S(1)}, u32[]{:S(2)}, u32[]{:S(2)}) collective-permute-start(f32[64,640]{1,0:T(8,128)S(1)} %get-tuple-element.55), channel_id=1, source_target_pairs={{0,16},{2,18},{4,20},{6,22},{8,24},{10,26},{12,28},{14,30},{16,0},... | collective-permute-start | bytes 491528 | tf_op jit(solution)/shard_map/ppermute | solution.py:409
  18.9 1.2 %shard_map.59 = (f32[128,512]{1,0:T(8,128)S(1)}, f32[32,512]{1,0:T(8,128)S(1)}, f32[32,512]{1,0:T(8,128)S(1)}) custom-call(f32[512,128]{1,0:T(8,128)S(1)} %collective-permute-done.columns, f32[512,256]{1,0:T(8,128)S(1)} %get-tuple-element.45.start_own, f32[64,512]{1,0:T(8,128)S(1)} %get-tuple-element.51.start_far, ...), custom_call_target="tpu_custom_call" | custom-call | tf_op jit(solution)/shard_map/pallas_call | solution.py:45
  20.1 1.3 %collective-permute-start.5 = (f32[32,512]{1,0:T(8,128)S(1)}, f32[32,512]{1,0:T(8,128)S(1)}, u32[]{:S(2)}, u32[]{:S(2)}) collective-permute-start(f32[32,512]{1,0:T(8,128)S(1)} %get-tuple-element.56), channel_id=1, source_target_pairs={{0,30},{2,4},{4,2},{6,8},{8,6},{10,12},{12,10},{14,16},{16,14},{18... | collective-permute-start | bytes 196616 | tf_op jit(solution)/shard_map/ppermute | solution.py:412
  21.8 1.4 %collective-permute-done.3.columns = f32[512,128]{1,0:T(8,128)S(1)} collective-permute-done((f32[512,128]{1,0:T(8,128)S(1)}, f32[512,128]{1,0:T(8,128)S(1)}, u32[]{:S(2)}, u32[]{:S(2)}) %collective-permute-start.3) | collective-permute-done | bytes 262176 | tf_op jit(solution)/shard_map/ppermute | solution.py:419
  23.7 3.0 %collective-permute-done.5.out_in = f32[32,512]{1,0:T(8,128)S(1)} collective-permute-done((f32[32,512]{1,0:T(8,128)S(1)}, f32[32,512]{1,0:T(8,128)S(1)}, u32[]{:S(2)}, u32[]{:S(2)}) %collective-permute-start.5) | collective-permute-done | bytes 65568 | tf_op jit(solution)/shard_map/ppermute | solution.py:412
  27.3 0.8 %collective-permute-done.2.columns = f32[512,128]{1,0:T(8,128)S(1)} collective-permute-done((f32[512,128]{1,0:T(8,128)S(1)}, f32[512,128]{1,0:T(8,128)S(1)}, u32[]{:S(2)}, u32[]{:S(2)}) %collective-permute-start.2) | collective-permute-done | bytes 262176 | tf_op jit(solution)/shard_map/ppermute | solution.py:419
  28.0 0.7 %shard_map.62 = (f32[128,512]{1,0:T(8,128)S(1)}, f32[64,512]{1,0:T(8,128)S(1)}, f32[32,512]{1,0:T(8,128)S(1)}, f32[32,512]{1,0:T(8,128)S(1)}) custom-call(f32[512,128]{1,0:T(8,128)S(1)} %collective-permute-done.2.columns, f32[512,128]{1,0:T(8,128)S(1)} %shard_map.60.rest_low, bf16[512,1024]{1,0:T(8,128)(2,1)S(1)} %get-tuple-element.47.top, ...), custom_call_target="tpu_custom_call" | custom-call | tf_op jit(solution)/shard_map/pallas_call | solution.py:45
  28.8 2.9 %collective-permute-start.7 = (f32[64,512]{1,0:T(8,128)S(1)}, f32[64,512]{1,0:T(8,128)S(1)}, u32[]{:S(2)}, u32[]{:S(2)}) collective-permute-start(f32[64,512]{1,0:T(8,128)S(1)} %get-tuple-element.63.back_far), channel_id=1, source_target_pairs={{0,16},{2,18},{4,20},{6,22},{8,24},{10,26},{12,28},{14,30},{16,0},... | collective-permute-start | bytes 393224 | tf_op jit(solution)/shard_map/ppermute | solution.py:409
  31.7 0.6 %collective-permute-start.8 = (f32[32,512]{1,0:T(8,128)S(1)}, f32[32,512]{1,0:T(8,128)S(1)}, u32[]{:S(2)}, u32[]{:S(2)}) collective-permute-start(f32[32,512]{1,0:T(8,128)S(1)} %get-tuple-element.65), channel_id=1, source_target_pairs={{0,30},{2,4},{4,2},{6,8},{8,6},{10,12},{12,10},{14,16},{16,14},{18... | collective-permute-start | bytes 196616 | tf_op jit(solution)/shard_map/ppermute | solution.py:412
  32.2 1.0 %collective-permute-start.9 = (f32[32,512]{1,0:T(8,128)S(1)}, f32[32,512]{1,0:T(8,128)S(1)}, u32[]{:S(2)}, u32[]{:S(2)}) collective-permute-start(f32[32,512]{1,0:T(8,128)S(1)} %get-tuple-element.66), channel_id=1, source_target_pairs={{0,2},{2,0},{4,6},{6,4},{8,10},{10,8},{12,14},{14,12},{16,18},{18,... | collective-permute-start | bytes 196616 | tf_op jit(solution)/shard_map/ppermute | solution.py:415
  33.9 4.2 %collective-permute-done.8.out_in = f32[32,512]{1,0:T(8,128)S(1)} collective-permute-done((f32[32,512]{1,0:T(8,128)S(1)}, f32[32,512]{1,0:T(8,128)S(1)}, u32[]{:S(2)}, u32[]{:S(2)}) %collective-permute-start.8) | collective-permute-done | bytes 65568 | tf_op jit(solution)/shard_map/ppermute | solution.py:412
  38.3 3.3 %collective-permute-start.10 = (f32[64,512]{1,0:T(8,128)S(1)}, f32[64,512]{1,0:T(8,128)S(1)}, u32[]{:S(2)}, u32[]{:S(2)}) collective-permute-start(f32[64,512]{1,0:T(8,128)S(1)} %shard_map.65), channel_id=1, source_target_pairs={{0,16},{2,18},{4,20},{6,22},{8,24},{10,26},{12,28},{14,30},{16,0},... | collective-permute-start | bytes 393224 | tf_op jit(solution)/shard_map/ppermute | solution.py:409
  41.9 0.9 %shard_map.64 = (f32[256,512]{1,0:T(8,128)S(1)}, f32[384,512]{1,0:T(8,128)S(1)}, f32[64,512]{1,0:T(8,128)S(1)}) custom-call(f32[256,512]{1,0:T(8,128)S(1)} %get-tuple-element.64.base, bf16[128,128]{1,0:T(8,128)(2,1)S(1)} %get-tuple-element.49.pick, f32[64,512]{1,0:T(8,128)S(1)} %collective-permute-done.7.far_in, ...), custom_call_target="tpu_custom_call" | custom-call | tf_op jit(solution)/shard_map/pallas_call | solution.py:45
  42.8 5.4 %collective-permute-done.11.out_in = f32[32,512]{1,0:T(8,128)S(1)} collective-permute-done((f32[32,512]{1,0:T(8,128)S(1)}, f32[32,512]{1,0:T(8,128)S(1)}, u32[]{:S(2)}, u32[]{:S(2)}) %collective-permute-start.11) | collective-permute-done | bytes 65568 | tf_op jit(solution)/shard_map/ppermute | solution.py:412
  48.8 2.0 %collective-permute-start.14 = (f32[32,512]{1,0:T(8,128)S(1)}, f32[32,512]{1,0:T(8,128)S(1)}, u32[]{:S(2)}, u32[]{:S(2)}) collective-permute-start(f32[32,512]{1,0:T(8,128)S(1)} %get-tuple-element.79), channel_id=1, source_target_pairs={{0,30},{2,4},{4,2},{6,8},{8,6},{10,12},{12,10},{14,16},{16,14},{18... | collective-permute-start | bytes 196616 | tf_op jit(solution)/shard_map/ppermute | solution.py:412
  50.7 0.8 %shard_map.68.result = f32[512,256]{1,0:T(8,128)S(1)} custom-call(f32[384,512]{1,0:T(8,128)S(1)} %get-tuple-element.68.part, f32[128,512]{1,0:T(8,128)S(1)} %get-tuple-element.74.ghosts, bf16[384,384]{1,0:T(8,128)(2,1)S(1)} %get-tuple-element.58.ham_top, bf16[384,384]{1,0:T(8,128)(2,1)S(1)} %get-tuple-element.59.ham_low, ...), custom_call_target="tpu_custom_call" | custom-call | tf_op jit(solution)/shard_map/pallas_call | solution.py:45
  51.5 3.7 %collective-permute-done.14.out_in = f32[32,512]{1,0:T(8,128)S(1)} collective-permute-done((f32[32,512]{1,0:T(8,128)S(1)}, f32[32,512]{1,0:T(8,128)S(1)}, u32[]{:S(2)}, u32[]{:S(2)}) %collective-permute-start.14) | collective-permute-done | bytes 65568 | tf_op jit(solution)/shard_map/ppermute | solution.py:412
  55.2 1.1 %shard_map.70 = f32[512,256]{1,0:T(8,128)} custom-call(f32[512,256]{1,0:T(8,128)S(1)} %shard_map.68.result, bf16[128,256]{1,0:T(8,128)(2,1)S(1)} %get-tuple-element.78.hits, f32[64,512]{1,0:T(8,128)S(1)} %collective-permute-done.13.far_in, f32[32,512]{1,0:T(8,128)S(1)} %collective-permute-done.14.out_in, f32[32,512]{1,0:T(8,128)S(1)} %collective-permute-done.15.near_in), custom_call_target="tpu_custom_call" | custom-call | tf_op jit(solution)/shard_map/pallas_call | solution.py:45
  (28 shorter events, 3.2 us)
Async XLA Ops:
  0.0 10.6 %copy-start.1 = (s32[1,4,32]{2,1,0:T(4,128)S(1)}, s32[1,4,32]{2,1,0:T(4,128)}, u32[]{:S(2)}) copy-start(s32[1,4,32]{2,1,0:T(4,128)} %lists.1) | copy-start | bytes 1540
  0.0 10.6 %copy-start = (s32[16,125]{1,0:T(8,128)S(1)}, s32[16,125]{1,0:T(8,128)}, u32[]{:S(2)}) copy-start(s32[16,125]{1,0:T(8,128)} %connect.1) | copy-start | bytes 24004
  1.8 12.9 %collective-permute-start.1 = (f32[512,128]{1,0:T(8,128)S(1)}, f32[512,128]{1,0:T(8,128)S(1)}, u32[]{:S(2)}, u32[]{:S(2)}) collective-permute-start(f32[512,128]{1,0:T(8,128)S(1)} %get-tuple-element.46), channel_id=1, source_target_pairs={{0,1},{1,0},{2,3},{3,2},{4,5},{5,4},{6,7},{7,6},{8,9},{9,8},{10,11... | collective-permute-start | bytes 786440 | tf_op jit(solution)/shard_map/ppermute | solution.py:419
  4.9 14.0 %collective-permute-start = (f32[512,128]{1,0:T(8,128)S(1)}, f32[512,128]{1,0:T(8,128)S(1)}, u32[]{:S(2)}, u32[]{:S(2)}) collective-permute-start(f32[512,128]{1,0:T(8,128)S(1)} %get-tuple-element.43), channel_id=1, source_target_pairs={{0,1},{1,0},{2,3},{3,2},{4,5},{5,4},{6,7},{7,6},{8,9},{9,8},{10,11... | collective-permute-start | bytes 786440 | tf_op jit(solution)/shard_map/ppermute | solution.py:419
  5.0 18.3 %collective-permute-start.3 = (f32[512,128]{1,0:T(8,128)S(1)}, f32[512,128]{1,0:T(8,128)S(1)}, u32[]{:S(2)}, u32[]{:S(2)}) collective-permute-start(f32[512,128]{1,0:T(8,128)S(1)} %get-tuple-element.54), channel_id=1, source_target_pairs={{0,1},{1,0},{2,3},{3,2},{4,5},{5,4},{6,7},{7,6},{8,9},{9,8},{10,11... | collective-permute-start | bytes 786440 | tf_op jit(solution)/shard_map/ppermute | solution.py:419
  6.9 21.1 %collective-permute-start.2 = (f32[512,128]{1,0:T(8,128)S(1)}, f32[512,128]{1,0:T(8,128)S(1)}, u32[]{:S(2)}, u32[]{:S(2)}) collective-permute-start(f32[512,128]{1,0:T(8,128)S(1)} %get-tuple-element.53), channel_id=1, source_target_pairs={{0,1},{1,0},{2,3},{3,2},{4,5},{5,4},{6,7},{7,6},{8,9},{9,8},{10,11... | collective-permute-start | bytes 786440 | tf_op jit(solution)/shard_map/ppermute | solution.py:419
  15.8 10.9 %collective-permute-start.4 = (f32[64,640]{1,0:T(8,128)S(1)}, f32[64,640]{1,0:T(8,128)S(1)}, u32[]{:S(2)}, u32[]{:S(2)}) collective-permute-start(f32[64,640]{1,0:T(8,128)S(1)} %get-tuple-element.55), channel_id=1, source_target_pairs={{0,16},{2,18},{4,20},{6,22},{8,24},{10,26},{12,28},{14,30},{16,0},... | collective-permute-start | bytes 491528 | tf_op jit(solution)/shard_map/ppermute | solution.py:409
  20.1 6.6 %collective-permute-start.5 = (f32[32,512]{1,0:T(8,128)S(1)}, f32[32,512]{1,0:T(8,128)S(1)}, u32[]{:S(2)}, u32[]{:S(2)}) collective-permute-start(f32[32,512]{1,0:T(8,128)S(1)} %get-tuple-element.56), channel_id=1, source_target_pairs={{0,30},{2,4},{4,2},{6,8},{8,6},{10,12},{12,10},{14,16},{16,14},{18... | collective-permute-start | bytes 196616 | tf_op jit(solution)/shard_map/ppermute | solution.py:412
  21.4 5.3 %collective-permute-start.6 = (f32[32,512]{1,0:T(8,128)S(1)}, f32[32,512]{1,0:T(8,128)S(1)}, u32[]{:S(2)}, u32[]{:S(2)}) collective-permute-start(f32[32,512]{1,0:T(8,128)S(1)} %get-tuple-element.57), channel_id=1, source_target_pairs={{0,2},{2,0},{4,6},{6,4},{8,10},{10,8},{12,14},{14,12},{16,18},{18,... | collective-permute-start | bytes 196616 | tf_op jit(solution)/shard_map/ppermute | solution.py:415
  28.8 12.8 %collective-permute-start.7 = (f32[64,512]{1,0:T(8,128)S(1)}, f32[64,512]{1,0:T(8,128)S(1)}, u32[]{:S(2)}, u32[]{:S(2)}) collective-permute-start(f32[64,512]{1,0:T(8,128)S(1)} %get-tuple-element.63.back_far), channel_id=1, source_target_pairs={{0,16},{2,18},{4,20},{6,22},{8,24},{10,26},{12,28},{14,30},{16,0},... | collective-permute-start | bytes 393224 | tf_op jit(solution)/shard_map/ppermute | solution.py:409
  31.7 6.4 %collective-permute-start.8 = (f32[32,512]{1,0:T(8,128)S(1)}, f32[32,512]{1,0:T(8,128)S(1)}, u32[]{:S(2)}, u32[]{:S(2)}) collective-permute-start(f32[32,512]{1,0:T(8,128)S(1)} %get-tuple-element.65), channel_id=1, source_target_pairs={{0,30},{2,4},{4,2},{6,8},{8,6},{10,12},{12,10},{14,16},{16,14},{18... | collective-permute-start | bytes 196616 | tf_op jit(solution)/shard_map/ppermute | solution.py:412
  32.2 5.8 %collective-permute-start.9 = (f32[32,512]{1,0:T(8,128)S(1)}, f32[32,512]{1,0:T(8,128)S(1)}, u32[]{:S(2)}, u32[]{:S(2)}) collective-permute-start(f32[32,512]{1,0:T(8,128)S(1)} %get-tuple-element.66), channel_id=1, source_target_pairs={{0,2},{2,0},{4,6},{6,4},{8,10},{10,8},{12,14},{14,12},{16,18},{18,... | collective-permute-start | bytes 196616 | tf_op jit(solution)/shard_map/ppermute | solution.py:415
  38.3 10.3 %collective-permute-start.10 = (f32[64,512]{1,0:T(8,128)S(1)}, f32[64,512]{1,0:T(8,128)S(1)}, u32[]{:S(2)}, u32[]{:S(2)}) collective-permute-start(f32[64,512]{1,0:T(8,128)S(1)} %shard_map.65), channel_id=1, source_target_pairs={{0,16},{2,18},{4,20},{6,22},{8,24},{10,26},{12,28},{14,30},{16,0},... | collective-permute-start | bytes 393224 | tf_op jit(solution)/shard_map/ppermute | solution.py:409
  41.7 6.5 %collective-permute-start.11 = (f32[32,512]{1,0:T(8,128)S(1)}, f32[32,512]{1,0:T(8,128)S(1)}, u32[]{:S(2)}, u32[]{:S(2)}) collective-permute-start(f32[32,512]{1,0:T(8,128)S(1)} %get-tuple-element.72), channel_id=1, source_target_pairs={{0,30},{2,4},{4,2},{6,8},{8,6},{10,12},{12,10},{14,16},{16,14},{18... | collective-permute-start | bytes 196616 | tf_op jit(solution)/shard_map/ppermute | solution.py:412
  41.8 6.4 %collective-permute-start.12 = (f32[32,512]{1,0:T(8,128)S(1)}, f32[32,512]{1,0:T(8,128)S(1)}, u32[]{:S(2)}, u32[]{:S(2)}) collective-permute-start(f32[32,512]{1,0:T(8,128)S(1)} %get-tuple-element.73), channel_id=1, source_target_pairs={{0,2},{2,0},{4,6},{6,4},{8,10},{10,8},{12,14},{14,12},{16,18},{18,... | collective-permute-start | bytes 196616 | tf_op jit(solution)/shard_map/ppermute | solution.py:415
  48.5 6.8 %collective-permute-start.13 = (f32[64,512]{1,0:T(8,128)S(1)}, f32[64,512]{1,0:T(8,128)S(1)}, u32[]{:S(2)}, u32[]{:S(2)}) collective-permute-start(f32[64,512]{1,0:T(8,128)S(1)} %shard_map.69), channel_id=1, source_target_pairs={{0,16},{2,18},{4,20},{6,22},{8,24},{10,26},{12,28},{14,30},{16,0},... | collective-permute-start | bytes 393224 | tf_op jit(solution)/shard_map/ppermute | solution.py:409
  48.8 6.5 %collective-permute-start.14 = (f32[32,512]{1,0:T(8,128)S(1)}, f32[32,512]{1,0:T(8,128)S(1)}, u32[]{:S(2)}, u32[]{:S(2)}) collective-permute-start(f32[32,512]{1,0:T(8,128)S(1)} %get-tuple-element.79), channel_id=1, source_target_pairs={{0,30},{2,4},{4,2},{6,8},{8,6},{10,12},{12,10},{14,16},{16,14},{18... | collective-permute-start | bytes 196616 | tf_op jit(solution)/shard_map/ppermute | solution.py:412
  50.7 4.5 %collective-permute-start.15 = (f32[32,512]{1,0:T(8,128)S(1)}, f32[32,512]{1,0:T(8,128)S(1)}, u32[]{:S(2)}, u32[]{:S(2)}) collective-permute-start(f32[32,512]{1,0:T(8,128)S(1)} %get-tuple-element.80), channel_id=1, source_target_pairs={{0,2},{2,0},{4,6},{6,4},{8,10},{10,8},{12,14},{14,12},{16,18},{18,... | collective-permute-start | bytes 196616 | tf_op jit(solution)/shard_map/ppermute | solution.py:415

commit v18 on v17

--- a/solution.py
+++ b/solution.py
@@ -318,7 +318,7 @@
     adjust_out[...] = mul(split(overlap[...]), split(back_far[...]))
 
 
-def fetch_far(packed, both, out_in, near_in, far_out):
+def fetch_far(packed, both, near_in, out_in, far_out):
     duo = 2 * out_in.shape[0]
     back = jnp.concatenate([out_in[...], near_in[...]], 0)
     far_out[...] = packed[:duo, :] + SCALE_ONE * sift(both[:duo, duo:], back)
@@ -519,13 +519,13 @@
         [rows_of(nodes - wide)] + halo_out,
         high_cols_in, rest_low, ritz_top, ritz_low, part, ham_top, ham_low,
     )
-    far_in, out_in, near_in = far(back_far), out(back_out), near(back_near)
+    far_in, near_in, out_in = far(back_far), near(back_near), out(back_out)
     start, base, packed, adjust = call(
         first_base,
         [rows_of(nodes), rows_of(nodes), rows_of(wide), rows_of(duo)],
         start_edge, start_rest, part, ham_top, ham_low, pick, overlap, back_far,
     )
-    (far_rows,) = call(fetch_far, [rows_of(duo)], packed, both, out_in, near_in)
+    (far_rows,) = call(fetch_far, [rows_of(duo)], packed, both, near_in, out_in)
     fetched_far = far(far_rows)
     out_rows, near_rows = call(
         fetch_ring, halo_out[1:], packed, both, far_in, out_in, near_in

time: 56.5 us -> 56.5 us (level)
  no operation moved by 1% of the time
where the time goes in v18:
time: 56.5 us; the launch traced here: 56.3 us
  starting transfers between devices  19.8 us (35%)
  waiting for transfers between devices  18.6 us (33%)
  Pallas kernels  17.7 us (31%)
    pallas_call x16, Pallas kernels, call(): pl.pallas_call(body, out_shape=[jax.ShapeDtypeStruct(*out) for out in out...  17.7 us
    ppermute x4, waiting for transfers between devices, out(): return lax.ppermute(rows, 'mesh', pairs_out)  16.3 us
    ppermute x4, starting transfers between devices, far(): return lax.ppermute(rows, 'mesh', pairs_far)  9.34 us
    ppermute x4, starting transfers between devices, gather(): lax.ppermute(rows, 'state', [(i, (i + step) % groups) for i in range(grou...  5.14 us
    ppermute x4, starting transfers between devices, out(): return lax.ppermute(rows, 'mesh', pairs_out)  3.89 us
    ppermute x4, waiting for transfers between devices, gather(): lax.ppermute(rows, 'state', [(i, (i + step) % groups) for i in range(grou...  2.2 us
    ppermute x4, starting transfers between devices, near(): return lax.ppermute(rows, 'mesh', pairs_in)  1.49 us
  transfers between devices with their start and end apart: 16, of which 6 were waited for; matrix products, arithmetic and copies ran while one was open for 0% of the time, Pallas kernels for 25%

profile of v18, /device:TPU:0, one launch (start us, length us, event | category | flops | bytes accessed | tf_op | source)
XLA Modules:
  0.0 56.3 jit_solution(15767698585704224899)
XLA Ops:
  0.0 1.8 %shard_map.55 = (f32[512,128]{1,0:T(8,128)S(1)}, f32[512,128]{1,0:T(8,128)S(1)}, f32[512,128]{1,0:T(8,128)S(1)}, f32[512,128]{1,0:T(8,128)S(1)}, bf16[256,256]{1,0:T(8,128)(2,1)S(1)}) custom-call(s32[1,4,32]{2,1,0:T(4,128)} %lists.1, f32[1024,256]{1,0:T(8,128)} %subspace_in.3), custom_call_target="tpu_custom_call" | custom-call | tf_op jit(solution)/shard_map/pallas_call | solution.py:45
  1.8 3.0 %collective-permute-start.1 = (f32[512,128]{1,0:T(8,128)S(1)}, f32[512,128]{1,0:T(8,128)S(1)}, u32[]{:S(2)}, u32[]{:S(2)}) collective-permute-start(f32[512,128]{1,0:T(8,128)S(1)} %get-tuple-element.46), channel_id=1, source_target_pairs={{0,1},{1,0},{2,3},{3,2},{4,5},{5,4},{6,7},{7,6},{8,9},{9,8},{10,11... | collective-permute-start | bytes 786440 | tf_op jit(solution)/shard_map/ppermute | solution.py:419
  5.0 1.9 %collective-permute-start.3 = (f32[512,128]{1,0:T(8,128)S(1)}, f32[512,128]{1,0:T(8,128)S(1)}, u32[]{:S(2)}, u32[]{:S(2)}) collective-permute-start(f32[512,128]{1,0:T(8,128)S(1)} %get-tuple-element.54), channel_id=1, source_target_pairs={{0,1},{1,0},{2,3},{3,2},{4,5},{5,4},{6,7},{7,6},{8,9},{9,8},{10,11... | collective-permute-start | bytes 786440 | tf_op jit(solution)/shard_map/ppermute | solution.py:419
  7.0 3.6 %shard_map.56 = (f32[512,256]{1,0:T(8,128)S(1)}, bf16[512,1024]{1,0:T(8,128)(2,1)S(1)}, bf16[512,1024]{1,0:T(8,128)(2,1)S(1)}) custom-call(s32[1]{0:T(128)} %bitcast.group, bf16[256,256]{1,0:T(8,128)(2,1)S(1)} %get-tuple-element.44.shuffle, f32[1024,256]{1,0:T(8,128)} %subspace_in.3, f32[512,2048]{1,0:T(8,128)} %ritz_in.1), custom_call_target="tpu_custom_call" | custom-call | tf_op jit(solution)/shard_map/pallas_call | solution.py:45
  10.6 4.1 %shard_map.57 = (bf16[384,384]{1,0:T(8,128)(2,1)S(1)}, bf16[384,384]{1,0:T(8,128)(2,1)S(1)}, bf16[128,128]{1,0:T(8,128)(2,1)S(1)}, bf16[128,128]{1,0:T(8,128)(2,...) custom-call(s32[1]{0:T(128)} %bitcast.1.odd, s32[1,4,32]{2,1,0:T(4,128)S(1)} %copy-done.1, ...), custom_call_target="tpu_custom_call" | custom-call | tf_op jit(solution)/shard_map/pallas_call | solution.py:45
  14.7 1.1 %shard_map.58 = (f32[64,512]{1,0:T(8,128)S(1)}, f32[64,640]{1,0:T(8,128)S(1)}) custom-call(f32[512,128]{1,0:T(8,128)S(1)} %collective-permute-done.1.columns, f32[512,256]{1,0:T(8,128)S(1)} %get-tuple-element.45.start_own, bf16[512,1024]{1,0:T(8,128)(2,1)S(1)} %get-tuple-element.47.top, bf16[512,1024]{1,0:T(8,128)(2,1)S(1)} %get-tuple-element.48.low, ...), custom_call_target="tpu_custom_call" | custom-call | tf_op jit(solution)/shard_map/pallas_call | solution.py:45
  15.8 3.1 %collective-permute-start.4 = (f32[64,640]{1,0:T(8,128)S(1)}, f32[64,640]{1,0:T(8,128)S(1)}, u32[]{:S(2)}, u32[]{:S(2)}) collective-permute-start(f32[64,640]{1,0:T(8,128)S(1)} %get-tuple-element.55), channel_id=1, source_target_pairs={{0,16},{2,18},{4,20},{6,22},{8,24},{10,26},{12,28},{14,30},{16,0},... | collective-permute-start | bytes 491528 | tf_op jit(solution)/shard_map/ppermute | solution.py:409
  18.9 1.2 %shard_map.59 = (f32[128,512]{1,0:T(8,128)S(1)}, f32[32,512]{1,0:T(8,128)S(1)}, f32[32,512]{1,0:T(8,128)S(1)}) custom-call(f32[512,128]{1,0:T(8,128)S(1)} %collective-permute-done.columns, f32[512,256]{1,0:T(8,128)S(1)} %get-tuple-element.45.start_own, f32[64,512]{1,0:T(8,128)S(1)} %get-tuple-element.51.start_far, ...), custom_call_target="tpu_custom_call" | custom-call | tf_op jit(solution)/shard_map/pallas_call | solution.py:45
  20.1 1.3 %collective-permute-start.5 = (f32[32,512]{1,0:T(8,128)S(1)}, f32[32,512]{1,0:T(8,128)S(1)}, u32[]{:S(2)}, u32[]{:S(2)}) collective-permute-start(f32[32,512]{1,0:T(8,128)S(1)} %get-tuple-element.56), channel_id=1, source_target_pairs={{0,30},{2,4},{4,2},{6,8},{8,6},{10,12},{12,10},{14,16},{16,14},{18... | collective-permute-start | bytes 196616 | tf_op jit(solution)/shard_map/ppermute | solution.py:412
  21.8 1.4 %collective-permute-done.3.columns = f32[512,128]{1,0:T(8,128)S(1)} collective-permute-done((f32[512,128]{1,0:T(8,128)S(1)}, f32[512,128]{1,0:T(8,128)S(1)}, u32[]{:S(2)}, u32[]{:S(2)}) %collective-permute-start.3) | collective-permute-done | bytes 262176 | tf_op jit(solution)/shard_map/ppermute | solution.py:419
  23.7 3.0 %collective-permute-done.5.out_in = f32[32,512]{1,0:T(8,128)S(1)} collective-permute-done((f32[32,512]{1,0:T(8,128)S(1)}, f32[32,512]{1,0:T(8,128)S(1)}, u32[]{:S(2)}, u32[]{:S(2)}) %collective-permute-start.5) | collective-permute-done | bytes 65568 | tf_op jit(solution)/shard_map/ppermute | solution.py:412
  27.3 0.8 %collective-permute-done.2.columns = f32[512,128]{1,0:T(8,128)S(1)} collective-permute-done((f32[512,128]{1,0:T(8,128)S(1)}, f32[512,128]{1,0:T(8,128)S(1)}, u32[]{:S(2)}, u32[]{:S(2)}) %collective-permute-start.2) | collective-permute-done | bytes 262176 | tf_op jit(solution)/shard_map/ppermute | solution.py:419
  28.0 0.7 %shard_map.62 = (f32[128,512]{1,0:T(8,128)S(1)}, f32[64,512]{1,0:T(8,128)S(1)}, f32[32,512]{1,0:T(8,128)S(1)}, f32[32,512]{1,0:T(8,128)S(1)}) custom-call(f32[512,128]{1,0:T(8,128)S(1)} %collective-permute-done.2.columns, f32[512,128]{1,0:T(8,128)S(1)} %shard_map.60.rest_low, bf16[512,1024]{1,0:T(8,128)(2,1)S(1)} %get-tuple-element.47.top, ...), custom_call_target="tpu_custom_call" | custom-call | tf_op jit(solution)/shard_map/pallas_call | solution.py:45
  28.8 2.9 %collective-permute-start.7 = (f32[64,512]{1,0:T(8,128)S(1)}, f32[64,512]{1,0:T(8,128)S(1)}, u32[]{:S(2)}, u32[]{:S(2)}) collective-permute-start(f32[64,512]{1,0:T(8,128)S(1)} %get-tuple-element.63.back_far), channel_id=1, source_target_pairs={{0,16},{2,18},{4,20},{6,22},{8,24},{10,26},{12,28},{14,30},{16,0},... | collective-permute-start | bytes 393224 | tf_op jit(solution)/shard_map/ppermute | solution.py:409
  31.7 0.6 %collective-permute-start.8 = (f32[32,512]{1,0:T(8,128)S(1)}, f32[32,512]{1,0:T(8,128)S(1)}, u32[]{:S(2)}, u32[]{:S(2)}) collective-permute-start(f32[32,512]{1,0:T(8,128)S(1)} %get-tuple-element.65), channel_id=1, source_target_pairs={{0,30},{2,4},{4,2},{6,8},{8,6},{10,12},{12,10},{14,16},{16,14},{18... | collective-permute-start | bytes 196616 | tf_op jit(solution)/shard_map/ppermute | solution.py:412
  32.2 1.0 %collective-permute-start.9 = (f32[32,512]{1,0:T(8,128)S(1)}, f32[32,512]{1,0:T(8,128)S(1)}, u32[]{:S(2)}, u32[]{:S(2)}) collective-permute-start(f32[32,512]{1,0:T(8,128)S(1)} %get-tuple-element.66), channel_id=1, source_target_pairs={{0,2},{2,0},{4,6},{6,4},{8,10},{10,8},{12,14},{14,12},{16,18},{18,... | collective-permute-start | bytes 196616 | tf_op jit(solution)/shard_map/ppermute | solution.py:415
  33.9 4.2 %collective-permute-done.8.out_in = f32[32,512]{1,0:T(8,128)S(1)} collective-permute-done((f32[32,512]{1,0:T(8,128)S(1)}, f32[32,512]{1,0:T(8,128)S(1)}, u32[]{:S(2)}, u32[]{:S(2)}) %collective-permute-start.8) | collective-permute-done | bytes 65568 | tf_op jit(solution)/shard_map/ppermute | solution.py:412
  38.3 3.3 %collective-permute-start.10 = (f32[64,512]{1,0:T(8,128)S(1)}, f32[64,512]{1,0:T(8,128)S(1)}, u32[]{:S(2)}, u32[]{:S(2)}) collective-permute-start(f32[64,512]{1,0:T(8,128)S(1)} %shard_map.65), channel_id=1, source_target_pairs={{0,16},{2,18},{4,20},{6,22},{8,24},{10,26},{12,28},{14,30},{16,0},... | collective-permute-start | bytes 393224 | tf_op jit(solution)/shard_map/ppermute | solution.py:409
  41.9 0.9 %shard_map.64 = (f32[256,512]{1,0:T(8,128)S(1)}, f32[384,512]{1,0:T(8,128)S(1)}, f32[64,512]{1,0:T(8,128)S(1)}) custom-call(f32[256,512]{1,0:T(8,128)S(1)} %get-tuple-element.64.base, bf16[128,128]{1,0:T(8,128)(2,1)S(1)} %get-tuple-element.49.pick, f32[64,512]{1,0:T(8,128)S(1)} %collective-permute-done.7.far_in, ...), custom_call_target="tpu_custom_call" | custom-call | tf_op jit(solution)/shard_map/pallas_call | solution.py:45
  42.8 5.4 %collective-permute-done.11.out_in = f32[32,512]{1,0:T(8,128)S(1)} collective-permute-done((f32[32,512]{1,0:T(8,128)S(1)}, f32[32,512]{1,0:T(8,128)S(1)}, u32[]{:S(2)}, u32[]{:S(2)}) %collective-permute-start.11) | collective-permute-done | bytes 65568 | tf_op jit(solution)/shard_map/ppermute | solution.py:412
  48.8 2.0 %collective-permute-start.14 = (f32[32,512]{1,0:T(8,128)S(1)}, f32[32,512]{1,0:T(8,128)S(1)}, u32[]{:S(2)}, u32[]{:S(2)}) collective-permute-start(f32[32,512]{1,0:T(8,128)S(1)} %get-tuple-element.79), channel_id=1, source_target_pairs={{0,30},{2,4},{4,2},{6,8},{8,6},{10,12},{12,10},{14,16},{16,14},{18... | collective-permute-start | bytes 196616 | tf_op jit(solution)/shard_map/ppermute | solution.py:412
  50.7 0.8 %shard_map.68.result = f32[512,256]{1,0:T(8,128)S(1)} custom-call(f32[384,512]{1,0:T(8,128)S(1)} %get-tuple-element.68.part, f32[128,512]{1,0:T(8,128)S(1)} %get-tuple-element.74.ghosts, bf16[384,384]{1,0:T(8,128)(2,1)S(1)} %get-tuple-element.58.ham_top, bf16[384,384]{1,0:T(8,128)(2,1)S(1)} %get-tuple-element.59.ham_low, ...), custom_call_target="tpu_custom_call" | custom-call | tf_op jit(solution)/shard_map/pallas_call | solution.py:45
  51.5 3.7 %collective-permute-done.14.out_in = f32[32,512]{1,0:T(8,128)S(1)} collective-permute-done((f32[32,512]{1,0:T(8,128)S(1)}, f32[32,512]{1,0:T(8,128)S(1)}, u32[]{:S(2)}, u32[]{:S(2)}) %collective-permute-start.14) | collective-permute-done | bytes 65568 | tf_op jit(solution)/shard_map/ppermute | solution.py:412
  55.2 1.1 %shard_map.70 = f32[512,256]{1,0:T(8,128)} custom-call(f32[512,256]{1,0:T(8,128)S(1)} %shard_map.68.result, bf16[128,256]{1,0:T(8,128)(2,1)S(1)} %get-tuple-element.78.hits, f32[64,512]{1,0:T(8,128)S(1)} %collective-permute-done.13.far_in, f32[32,512]{1,0:T(8,128)S(1)} %collective-permute-done.14.out_in, f32[32,512]{1,0:T(8,128)S(1)} %collective-permute-done.15.near_in), custom_call_target="tpu_custom_call" | custom-call | tf_op jit(solution)/shard_map/pallas_call | solution.py:45
  (28 shorter events, 3.2 us)
Async XLA Ops:
  0.0 10.6 %copy-start.1 = (s32[1,4,32]{2,1,0:T(4,128)S(1)}, s32[1,4,32]{2,1,0:T(4,128)}, u32[]{:S(2)}) copy-start(s32[1,4,32]{2,1,0:T(4,128)} %lists.1) | copy-start | bytes 1540
  0.0 10.6 %copy-start = (s32[16,125]{1,0:T(8,128)S(1)}, s32[16,125]{1,0:T(8,128)}, u32[]{:S(2)}) copy-start(s32[16,125]{1,0:T(8,128)} %connect.1) | copy-start | bytes 24004
  1.8 12.9 %collective-permute-start.1 = (f32[512,128]{1,0:T(8,128)S(1)}, f32[512,128]{1,0:T(8,128)S(1)}, u32[]{:S(2)}, u32[]{:S(2)}) collective-permute-start(f32[512,128]{1,0:T(8,128)S(1)} %get-tuple-element.46), channel_id=1, source_target_pairs={{0,1},{1,0},{2,3},{3,2},{4,5},{5,4},{6,7},{7,6},{8,9},{9,8},{10,11... | collective-permute-start | bytes 786440 | tf_op jit(solution)/shard_map/ppermute | solution.py:419
  4.9 14.0 %collective-permute-start = (f32[512,128]{1,0:T(8,128)S(1)}, f32[512,128]{1,0:T(8,128)S(1)}, u32[]{:S(2)}, u32[]{:S(2)}) collective-permute-start(f32[512,128]{1,0:T(8,128)S(1)} %get-tuple-element.43), channel_id=1, source_target_pairs={{0,1},{1,0},{2,3},{3,2},{4,5},{5,4},{6,7},{7,6},{8,9},{9,8},{10,11... | collective-permute-start | bytes 786440 | tf_op jit(solution)/shard_map/ppermute | solution.py:419
  5.0 18.3 %collective-permute-start.3 = (f32[512,128]{1,0:T(8,128)S(1)}, f32[512,128]{1,0:T(8,128)S(1)}, u32[]{:S(2)}, u32[]{:S(2)}) collective-permute-start(f32[512,128]{1,0:T(8,128)S(1)} %get-tuple-element.54), channel_id=1, source_target_pairs={{0,1},{1,0},{2,3},{3,2},{4,5},{5,4},{6,7},{7,6},{8,9},{9,8},{10,11... | collective-permute-start | bytes 786440 | tf_op jit(solution)/shard_map/ppermute | solution.py:419
  6.9 21.1 %collective-permute-start.2 = (f32[512,128]{1,0:T(8,128)S(1)}, f32[512,128]{1,0:T(8,128)S(1)}, u32[]{:S(2)}, u32[]{:S(2)}) collective-permute-start(f32[512,128]{1,0:T(8,128)S(1)} %get-tuple-element.53), channel_id=1, source_target_pairs={{0,1},{1,0},{2,3},{3,2},{4,5},{5,4},{6,7},{7,6},{8,9},{9,8},{10,11... | collective-permute-start | bytes 786440 | tf_op jit(solution)/shard_map/ppermute | solution.py:419
  15.8 10.9 %collective-permute-start.4 = (f32[64,640]{1,0:T(8,128)S(1)}, f32[64,640]{1,0:T(8,128)S(1)}, u32[]{:S(2)}, u32[]{:S(2)}) collective-permute-start(f32[64,640]{1,0:T(8,128)S(1)} %get-tuple-element.55), channel_id=1, source_target_pairs={{0,16},{2,18},{4,20},{6,22},{8,24},{10,26},{12,28},{14,30},{16,0},... | collective-permute-start | bytes 491528 | tf_op jit(solution)/shard_map/ppermute | solution.py:409
  20.1 6.6 %collective-permute-start.5 = (f32[32,512]{1,0:T(8,128)S(1)}, f32[32,512]{1,0:T(8,128)S(1)}, u32[]{:S(2)}, u32[]{:S(2)}) collective-permute-start(f32[32,512]{1,0:T(8,128)S(1)} %get-tuple-element.56), channel_id=1, source_target_pairs={{0,30},{2,4},{4,2},{6,8},{8,6},{10,12},{12,10},{14,16},{16,14},{18... | collective-permute-start | bytes 196616 | tf_op jit(solution)/shard_map/ppermute | solution.py:412
  21.4 5.3 %collective-permute-start.6 = (f32[32,512]{1,0:T(8,128)S(1)}, f32[32,512]{1,0:T(8,128)S(1)}, u32[]{:S(2)}, u32[]{:S(2)}) collective-permute-start(f32[32,512]{1,0:T(8,128)S(1)} %get-tuple-element.57), channel_id=1, source_target_pairs={{0,2},{2,0},{4,6},{6,4},{8,10},{10,8},{12,14},{14,12},{16,18},{18,... | collective-permute-start | bytes 196616 | tf_op jit(solution)/shard_map/ppermute | solution.py:415
  28.8 12.8 %collective-permute-start.7 = (f32[64,512]{1,0:T(8,128)S(1)}, f32[64,512]{1,0:T(8,128)S(1)}, u32[]{:S(2)}, u32[]{:S(2)}) collective-permute-start(f32[64,512]{1,0:T(8,128)S(1)} %get-tuple-element.63.back_far), channel_id=1, source_target_pairs={{0,16},{2,18},{4,20},{6,22},{8,24},{10,26},{12,28},{14,30},{16,0},... | collective-permute-start | bytes 393224 | tf_op jit(solution)/shard_map/ppermute | solution.py:409
  31.7 6.4 %collective-permute-start.8 = (f32[32,512]{1,0:T(8,128)S(1)}, f32[32,512]{1,0:T(8,128)S(1)}, u32[]{:S(2)}, u32[]{:S(2)}) collective-permute-start(f32[32,512]{1,0:T(8,128)S(1)} %get-tuple-element.65), channel_id=1, source_target_pairs={{0,30},{2,4},{4,2},{6,8},{8,6},{10,12},{12,10},{14,16},{16,14},{18... | collective-permute-start | bytes 196616 | tf_op jit(solution)/shard_map/ppermute | solution.py:412
  32.2 5.8 %collective-permute-start.9 = (f32[32,512]{1,0:T(8,128)S(1)}, f32[32,512]{1,0:T(8,128)S(1)}, u32[]{:S(2)}, u32[]{:S(2)}) collective-permute-start(f32[32,512]{1,0:T(8,128)S(1)} %get-tuple-element.66), channel_id=1, source_target_pairs={{0,2},{2,0},{4,6},{6,4},{8,10},{10,8},{12,14},{14,12},{16,18},{18,... | collective-permute-start | bytes 196616 | tf_op jit(solution)/shard_map/ppermute | solution.py:415
  38.3 10.3 %collective-permute-start.10 = (f32[64,512]{1,0:T(8,128)S(1)}, f32[64,512]{1,0:T(8,128)S(1)}, u32[]{:S(2)}, u32[]{:S(2)}) collective-permute-start(f32[64,512]{1,0:T(8,128)S(1)} %shard_map.65), channel_id=1, source_target_pairs={{0,16},{2,18},{4,20},{6,22},{8,24},{10,26},{12,28},{14,30},{16,0},... | collective-permute-start | bytes 393224 | tf_op jit(solution)/shard_map/ppermute | solution.py:409
  41.7 6.5 %collective-permute-start.11 = (f32[32,512]{1,0:T(8,128)S(1)}, f32[32,512]{1,0:T(8,128)S(1)}, u32[]{:S(2)}, u32[]{:S(2)}) collective-permute-start(f32[32,512]{1,0:T(8,128)S(1)} %get-tuple-element.72), channel_id=1, source_target_pairs={{0,30},{2,4},{4,2},{6,8},{8,6},{10,12},{12,10},{14,16},{16,14},{18... | collective-permute-start | bytes 196616 | tf_op jit(solution)/shard_map/ppermute | solution.py:412
  41.8 6.4 %collective-permute-start.12 = (f32[32,512]{1,0:T(8,128)S(1)}, f32[32,512]{1,0:T(8,128)S(1)}, u32[]{:S(2)}, u32[]{:S(2)}) collective-permute-start(f32[32,512]{1,0:T(8,128)S(1)} %get-tuple-element.73), channel_id=1, source_target_pairs={{0,2},{2,0},{4,6},{6,4},{8,10},{10,8},{12,14},{14,12},{16,18},{18,... | collective-permute-start | bytes 196616 | tf_op jit(solution)/shard_map/ppermute | solution.py:415
  48.5 6.8 %collective-permute-start.13 = (f32[64,512]{1,0:T(8,128)S(1)}, f32[64,512]{1,0:T(8,128)S(1)}, u32[]{:S(2)}, u32[]{:S(2)}) collective-permute-start(f32[64,512]{1,0:T(8,128)S(1)} %shard_map.69), channel_id=1, source_target_pairs={{0,16},{2,18},{4,20},{6,22},{8,24},{10,26},{12,28},{14,30},{16,0},... | collective-permute-start | bytes 393224 | tf_op jit(solution)/shard_map/ppermute | solution.py:409
  48.8 6.5 %collective-permute-start.14 = (f32[32,512]{1,0:T(8,128)S(1)}, f32[32,512]{1,0:T(8,128)S(1)}, u32[]{:S(2)}, u32[]{:S(2)}) collective-permute-start(f32[32,512]{1,0:T(8,128)S(1)} %get-tuple-element.79), channel_id=1, source_target_pairs={{0,30},{2,4},{4,2},{6,8},{8,6},{10,12},{12,10},{14,16},{16,14},{18... | collective-permute-start | bytes 196616 | tf_op jit(solution)/shard_map/ppermute | solution.py:412
  50.7 4.5 %collective-permute-start.15 = (f32[32,512]{1,0:T(8,128)S(1)}, f32[32,512]{1,0:T(8,128)S(1)}, u32[]{:S(2)}, u32[]{:S(2)}) collective-permute-start(f32[32,512]{1,0:T(8,128)S(1)} %get-tuple-element.80), channel_id=1, source_target_pairs={{0,2},{2,0},{4,6},{6,4},{8,10},{10,8},{12,14},{14,12},{16,18},{18,... | collective-permute-start | bytes 196616 | tf_op jit(solution)/shard_map/ppermute | solution.py:415
